TPU v7x, 32 devices: a whole 2x2x4 slice. The times are simulated.
32 devices in a mesh: tiles: 16 (over z, x, core), vec: 2 (over y).
Axes of the slice: x: 2, y: 2, z: 4, core: 2. Of those that a mesh axis runs over, the one named last changes fastest.
Arguments:
- omega: float32 [128, 4, 128, 128], P('vec', None, 'tiles'), may hold values from -24 to 24
- conductance: float32 [3, 4, 128, 128], P(None, None, 'tiles'), may hold values from 0.02 to 0.16
- wet: int32 [128, 128], P('tiles'), may hold values 0 or 1
- volume: float32 [128, 128], P('tiles'), may hold values from 0.3 to 27, as said below
- face_runs: int32 [16, 4], P('tiles'), may hold values from 0 to 128, as said below
Outputs:
- diffused: float32 [128, 4, 128, 128], P('vec', None, 'tiles')
- r_factor: float32 [128, 128], replicated
Inputs may be any that keep to these rules, and one draw needn't show every extreme that they name: `face_runs`: tiles in tile row 0 have a closed lower row face and tiles in tile column 0 a closed lower column face (length 0); every other run lies within its face, covers at least half of it, and some tiles have fully open faces. Positive cell volume weights.
All inputs are finite; a program needn't handle non-finite values. No bound on the sum of `wet` on one device may be relied on, other than what follows from the above.
Results may differ from a plain program's by a relative error of at most 0.00005.
Values sent between devices are 32-bit elements; how exact they have to be, the bound alone decides.
No kernel may reach another device: no remote copies, remote signals or barrier semaphores. Data moves between devices by JAX's collectives and lax.ppermute only.
A program may use at most 64 MiB of HBM per device.

v0:
```python
import jax
import jax.numpy as jnp
from jax import lax
from jax.sharding import PartitionSpec as P

TGY = 8
ITERS = 4


def shifted(value, axis, steps):
    count = lax.axis_size(axis)
    first, last = (max(0, -steps), min(count, count - steps))
    return lax.ppermute(value, axis, [(source, source + steps) for source in range(first, last)])


def diffuse(field, statics):
    cond_x = statics[0]
    cond_y = statics[1]
    cond_z = statics[2]
    wet_cells = statics[3]
    flux_x = cond_x[:, 1:, :] * (field[:, :, 1:, :] - field[:, :, :-1, :])
    flux_y = cond_y[:, :, 1:] * (field[:, :, :, 1:] - field[:, :, :, :-1])
    flux_z = cond_z[1:] * (field[:, 1:] - field[:, :-1])
    zero_level = jnp.zeros_like(field[:, :1])
    flux_z = jnp.concatenate([zero_level, flux_z, zero_level], axis=1)
    change = flux_x[:, :, 1:, 1:-1] - flux_x[:, :, :-1, 1:-1]
    change = change + flux_y[:, :, 1:-1, 1:] - flux_y[:, :, 1:-1, :-1]
    change = change + (flux_z[:, 1:] - flux_z[:, :-1])[:, :, 1:-1, 1:-1]
    return wet_cells[:, 1:-1, 1:-1] * (field[:, :, 1:-1, 1:-1] + change)


def moving(values, offset):
    return shifted(values, "tiles", offset)


def fixed_rim(values, offset):
    return shifted(values, "tiles", offset)


def extend(values, margin, neighbour):
    lower_rim = neighbour(values[:, :, -margin:, :], TGY)
    upper_rim = neighbour(values[:, :, :margin, :], -TGY)
    stacked = jnp.concatenate([lower_rim, values, upper_rim], axis=2)
    left_rim = neighbour(stacked[:, :, :, -margin:], 1)
    right_rim = neighbour(stacked[:, :, :, :margin], -1)
    return jnp.concatenate([left_rim, stacked, right_rim], axis=3)


def shards(omega, conductance, wet, volume, face_runs):
    levels = omega.shape[1]
    tile_rows = omega.shape[2]
    tile_cols = omega.shape[3]
    row_ids = lax.broadcasted_iota(jnp.int32, (tile_rows, tile_cols), 0)
    col_ids = lax.broadcasted_iota(jnp.int32, (tile_rows, tile_cols), 1)
    runs = face_runs[0]
    open_x = (col_ids >= runs[0]) & (col_ids < runs[0] + runs[1])
    factor_x = jnp.where(row_ids == 0, open_x.astype(jnp.float32), jnp.float32(1.0))
    open_y = (row_ids >= runs[2]) & (row_ids < runs[2] + runs[3])
    factor_y = jnp.where(col_ids == 0, open_y.astype(jnp.float32), jnp.float32(1.0))
    level_ids = lax.broadcasted_iota(jnp.int32, (levels, 1, 1), 0)
    cond_z = conductance[2] * (level_ids > 0).astype(jnp.float32)
    wet_float = wet.astype(jnp.float32)
    statics = jnp.stack(
        [
            conductance[0] * factor_x[None],
            conductance[1] * factor_y[None],
            cond_z,
            jnp.broadcast_to(wet_float[None], (levels, tile_rows, tile_cols)),
        ]
    )
    margin = 2
    statics_wide = extend(statics, margin, fixed_rim)
    field = wet_float[None, None] * omega
    for block_index in range(ITERS // margin):
        grown = extend(field, margin, moving)
        current = statics_wide
        for inner_index in range(margin):
            grown = diffuse(grown, current)
            current = current[:, :, 1:-1, 1:-1]
        field = grown
    regrouped = lax.all_to_all(field, "vec", split_axis=1, concat_axis=0, tiled=True)
    all_vectors = regrouped.shape[0]
    total_cells = levels * lax.axis_size("tiles") * tile_rows * tile_cols
    flat_values = regrouped.reshape(all_vectors, -1)
    weighted = (regrouped * volume[None, None]).reshape(all_vectors, -1)
    gram_local = (
        lax.dot_general(
            weighted,
            flat_values,
            (((1,), (1,)), ((), ())),
            precision=lax.Precision.HIGHEST,
            preferred_element_type=jnp.float32,
        )
        / total_cells
    )
    gram = lax.psum(gram_local, ("tiles", "vec"))
    r_factor = jnp.linalg.cholesky(gram).T
    return (field, r_factor)


def solution(mesh):
    in_specs = (
        P("vec", None, "tiles", None),
        P(None, None, "tiles", None),
        P("tiles", None),
        P("tiles", None),
        P("tiles", None),
    )
    out_specs = (P("vec", None, "tiles", None), P())
    return jax.shard_map(shards, mesh=mesh, in_specs=in_specs, out_specs=out_specs, check_vma=False)
```

profile of v0, /device:TPU:0, one launch (start us, length us, event | category | flops | bytes accessed | tf_op | source)
XLA Modules:
  0.0 288.4 jit_solution(13784835235351225855)
XLA Ops:
  7.2 1.5 fusion.30
  14.3 5.9 %collective-permute-start = (f32[4,4,2,128]{3,2,1,0:T(2,128)S(1)}, f32[4,4,2,128]{3,2,1,0:T(2,128)S(1)}, u32[]{:S(2)}, u32[]{:S(2)}) collective-permute-start(f32[4,4,2,128]{3,2,1,0:T(2,128)S(1)} %get-tuple-element.24), channel_id=1, source_target_pairs={{0,16},{2,18},{4,20},{6,22},{8,24},{10,26},{12,28},{14,30},{1,17},... | collective-permute-start | bytes 49160 | tf_op jit(solution)/shard_map/ppermute | solution.py:13
  20.3 1.3 collective-permute-start.1
  21.6 1.8 copy_multiply_fusion
  23.4 3.4 %collective-permute-done.1 = f32[4,4,2,128]{3,2,1,0:T(2,128)S(1)} collective-permute-done((f32[4,4,2,128]{3,2,1,0:T(2,128)S(1)}, f32[4,4,2,128]{3,2,1,0:T(2,128)S(1)}, u32[]{:S(2)}, u32[]{:S(2)}) %collective-permute-start.1) | collective-permute-done | bytes 16416 | tf_op jit(solution)/shard_map/ppermute | solution.py:13
  26.9 1.3 collective-permute-start.2
  28.2 1.3 collective-permute-start.3
  29.6 6.0 %collective-permute-start.4 = (f32[64,4,2,128]{3,0,2,1:T(8,128)S(1)}, f32[64,4,2,128]{3,0,2,1:T(8,128)S(1)}, u32[]{:S(2)}, u32[]{:S(2)}) collective-permute-start(f32[64,4,2,128]{3,0,2,1:T(8,128)S(1)} %get-tuple-element.14), channel_id=1, source_target_pairs={{0,16},{2,18},{4,20},{6,22},{8,24},{10,26},{12,28},{14,30},{1,17},... | collective-permute-start | bytes 786440 | tf_op jit(solution)/shard_map/ppermute | solution.py:13
  35.6 1.3 collective-permute-start.5
  39.3 1.0 collective-permute-done.4
  40.3 10.6 %collective-permute-done.5 = f32[64,4,2,128]{3,0,2,1:T(8,128)S(1)} collective-permute-done((f32[64,4,2,128]{3,0,2,1:T(8,128)S(1)}, f32[64,4,2,128]{3,0,2,1:T(8,128)S(1)}, u32[]{:S(2)}, u32[]{:S(2)}) %collective-permute-start.5) | collective-permute-done | bytes 262176 | tf_op jit(solution)/shard_map/ppermute | solution.py:13
  51.0 1.8 fusion.26
  52.7 2.7 copy.15
  55.5 1.3 copy.16
  56.8 1.3 collective-permute-start.7
  58.1 3.7 %collective-permute-start.6 = (f32[64,4,12,2]{0,2,3,1:T(8,128)}, f32[64,4,12,2]{0,2,3,1:T(8,128)}, u32[]{:S(2)}, u32[]{:S(2)}) collective-permute-start(f32[64,4,12,2]{0,2,3,1:T(8,128)} %copy.15), channel_id=1, source_target_pairs={{0,2},{2,4},{4,6},{6,8},{8,10},{10,12},{12,14},{14,16},{16,18},{18... | collective-permute-start | bytes 73736 | tf_op jit(solution)/shard_map/ppermute | solution.py:13
  62.4 0.9 slice.385
  63.3 0.9 slice.398
  64.3 1.0 slice.414
  66.1 1.4 copy.17
  67.5 2.6 copy.18
  70.1 2.7 pad_maximum_fusion
  73.8 0.9 fusion.1
  74.7 4.1 %fusion.11 = f32[64,4,10,130]{3,0,2,1:T(8,128)S(1)} fusion(f32[64,3,12,132]{3,0,2,1:T(8,128)S(1)} %fusion.15, f32[64,4,12,131]{3,0,2,1:T(8,128)S(1)} %fusion.1, f32[64,4,11,132]{3,0,2,1:T(8,128)S(1)} %fusion.3, f32[64,4,12,132]{3,0,2,1:T(8,128)S(1)} %pad_maximum_fusion, f32[4,10,130]{2,1,0:T(8,128)S(1)} %slice.385), kind=kLoop, calls=%fused_computation.24 | loop fusion | flops 2329600 | bytes 9224512 | tf_op jit(solution)/shard_map/mul | solution.py:29
  80.3 1.6 fusion.23
  82.0 1.5 collective-permute-start.8
  83.5 1.3 collective-permute-start.9
  84.8 5.0 %collective-permute-done.8 = f32[64,4,2,128]{3,0,2,1:T(8,128)S(1)} collective-permute-done((f32[64,4,2,128]{3,0,2,1:T(8,128)S(1)}, f32[64,4,2,128]{3,0,2,1:T(8,128)S(1)}, u32[]{:S(2)}, u32[]{:S(2)}) %collective-permute-start.8) | collective-permute-done | bytes 262176 | tf_op jit(solution)/shard_map/ppermute | solution.py:13
  89.7 10.6 %collective-permute-done.9 = f32[64,4,2,128]{3,0,2,1:T(8,128)S(1)} collective-permute-done((f32[64,4,2,128]{3,0,2,1:T(8,128)S(1)}, f32[64,4,2,128]{3,0,2,1:T(8,128)S(1)}, u32[]{:S(2)}, u32[]{:S(2)}) %collective-permute-start.9) | collective-permute-done | bytes 262176 | tf_op jit(solution)/shard_map/ppermute | solution.py:13
  100.4 1.8 fusion.25
  102.2 2.1 copy.19
  104.3 2.0 collective-permute-start.10
  107.0 1.3 collective-permute-start.11
  108.8 1.4 collective-permute-done.11
  110.2 2.6 copy.22
  112.8 2.7 pad_maximum_fusion.1
  117.2 0.9 fusion
  118.1 4.1 %fusion.7 = f32[64,4,10,130]{3,0,2,1:T(8,128)S(1)} fusion(f32[64,3,12,132]{3,0,2,1:T(8,128)S(1)} %fusion.13, f32[64,4,12,131]{3,0,2,1:T(8,128)S(1)} %fusion, f32[64,4,11,132]{3,0,2,1:T(8,128)S(1)} %fusion.2, f32[64,4,12,132]{3,0,2,1:T(8,128)S(1)} %pad_maximum_fusion.1, f32[4,10,130]{2,1,0:T(8,128)S(1)} %slice.385), kind=kLoop, calls=%fused_computation.15 | loop fusion | flops 2329600 | bytes 9224512 | tf_op jit(solution)/shard_map/mul | solution.py:29
  124.2 1.6 fusion.20
  126.4 16.2 %all_to_all.15 = f32[64,4,8,128]{3,2,0,1:T(8,128)S(1)} all-to-all(f32[64,4,8,128]{3,2,0,1:T(8,128)S(1)} %copy.23), channel_id=1, replica_groups=mesh['tiles'=16,'vec'=2] {'vec'}, dimensions={1} | all-to-all | bytes 2097152 | tf_op jit(solution)/shard_map/all_to_all | solution.py:81
  142.6 1.1 copy.34
  143.8 1.4 reshape.101
  145.2 1.1 mul.199
  146.3 2.9 convolution_multiply_fusion
  149.2 1.6 copy.27
  150.7 115.2 %all-reduce.10.cloned.1.call-done = f32[128,128]{0,1:T(8,128)} async-done(((f32[128,128]{0,1:T(8,128)}), f32[128,128]{0,1:T(8,128)}) %all-reduce.10.cloned.1.call-update) | async-done | bytes 65552 | tf_op jit(solution)/shard_map/psum | solution.py:96
  265.9 0.9 copy.26
  267.7 11.7 %cholesky.18 = f32[128,128]{1,0:T(8,128)S(1)} custom-call(f32[128,128]{1,0:T(8,128)S(1)} %fusion.24), custom_call_target="Cholesky" | custom-call | tf_op jit(solution)/shard_map/jit(cholesky)/cholesky | solution.py:97
  (71 shorter events, 18.4 us)
Async XLA Ops:
  7.2 258.8 %all-reduce.10.cloned.1.call-start = ((), (), s32[]{:S(2)}) async-start(), calls=%async_computation.1 | async-start | bytes 131072 | tf_op jit(solution)/shard_map/psum | solution.py:96
  14.3 9.1 %collective-permute-start = (f32[4,4,2,128]{3,2,1,0:T(2,128)S(1)}, f32[4,4,2,128]{3,2,1,0:T(2,128)S(1)}, u32[]{:S(2)}, u32[]{:S(2)}) collective-permute-start(f32[4,4,2,128]{3,2,1,0:T(2,128)S(1)} %get-tuple-element.24), channel_id=1, source_target_pairs={{0,16},{2,18},{4,20},{6,22},{8,24},{10,26},{12,28},{14,30},{1,17},... | collective-permute-start | bytes 49160 | tf_op jit(solution)/shard_map/ppermute | solution.py:13
  20.3 6.5 %collective-permute-start.1 = (f32[4,4,2,128]{3,2,1,0:T(2,128)S(1)}, f32[4,4,2,128]{3,2,1,0:T(2,128)S(1)}, u32[]{:S(2)}, u32[]{:S(2)}) collective-permute-start(f32[4,4,2,128]{3,2,1,0:T(2,128)S(1)} %get-tuple-element.25), channel_id=1, source_target_pairs={{16,0},{18,2},{20,4},{22,6},{24,8},{26,10},{28,12},{30,14},{17,1},... | collective-permute-start | bytes 49160 | tf_op jit(solution)/shard_map/ppermute | solution.py:13
  26.9 9.9 %collective-permute-start.2 = (f32[4,4,12,2]{3,2,1,0:T(8,128)S(1)}, f32[4,4,12,2]{3,2,1,0:T(8,128)S(1)}, u32[]{:S(2)}, u32[]{:S(2)}) collective-permute-start(f32[4,4,12,2]{3,2,1,0:T(8,128)S(1)} %get-tuple-element.22), channel_id=1, source_target_pairs={{0,2},{2,4},{4,6},{6,8},{8,10},{10,12},{12,14},{14,16},{16,18},{18... | collective-permute-start | bytes 4616 | tf_op jit(solution)/shard_map/ppermute | solution.py:13
  28.2 8.6 %collective-permute-start.3 = (f32[4,4,12,2]{3,2,1,0:T(8,128)S(1)}, f32[4,4,12,2]{3,2,1,0:T(8,128)S(1)}, u32[]{:S(2)}, u32[]{:S(2)}) collective-permute-start(f32[4,4,12,2]{3,2,1,0:T(8,128)S(1)} %get-tuple-element.23), channel_id=1, source_target_pairs={{2,0},{4,2},{6,4},{8,6},{10,8},{12,10},{14,12},{16,14},{18,16},{20... | collective-permute-start | bytes 4616 | tf_op jit(solution)/shard_map/ppermute | solution.py:13
  29.6 10.7 %collective-permute-start.4 = (f32[64,4,2,128]{3,0,2,1:T(8,128)S(1)}, f32[64,4,2,128]{3,0,2,1:T(8,128)S(1)}, u32[]{:S(2)}, u32[]{:S(2)}) collective-permute-start(f32[64,4,2,128]{3,0,2,1:T(8,128)S(1)} %get-tuple-element.14), channel_id=1, source_target_pairs={{0,16},{2,18},{4,20},{6,22},{8,24},{10,26},{12,28},{14,30},{1,17},... | collective-permute-start | bytes 786440 | tf_op jit(solution)/shard_map/ppermute | solution.py:13
  35.6 15.3 %collective-permute-start.5 = (f32[64,4,2,128]{3,0,2,1:T(8,128)S(1)}, f32[64,4,2,128]{3,0,2,1:T(8,128)S(1)}, u32[]{:S(2)}, u32[]{:S(2)}) collective-permute-start(f32[64,4,2,128]{3,0,2,1:T(8,128)S(1)} %get-tuple-element.15), channel_id=1, source_target_pairs={{16,0},{18,2},{20,4},{22,6},{24,8},{26,10},{28,12},{30,14},{17,1},... | collective-permute-start | bytes 786440 | tf_op jit(solution)/shard_map/ppermute | solution.py:13
  56.8 10.7 %collective-permute-start.7 = (f32[64,4,12,2]{0,2,3,1:T(8,128)}, f32[64,4,12,2]{0,2,3,1:T(8,128)}, u32[]{:S(2)}, u32[]{:S(2)}) collective-permute-start(f32[64,4,12,2]{0,2,3,1:T(8,128)} %copy.16), channel_id=1, source_target_pairs={{2,0},{4,2},{6,4},{8,6},{10,8},{12,10},{14,12},{16,14},{18,16},{20... | collective-permute-start | bytes 73736 | tf_op jit(solution)/shard_map/ppermute | solution.py:13
  58.1 8.0 %collective-permute-start.6 = (f32[64,4,12,2]{0,2,3,1:T(8,128)}, f32[64,4,12,2]{0,2,3,1:T(8,128)}, u32[]{:S(2)}, u32[]{:S(2)}) collective-permute-start(f32[64,4,12,2]{0,2,3,1:T(8,128)} %copy.15), channel_id=1, source_target_pairs={{0,2},{2,4},{4,6},{6,8},{8,10},{10,12},{12,14},{14,16},{16,18},{18... | collective-permute-start | bytes 73736 | tf_op jit(solution)/shard_map/ppermute | solution.py:13
  64.3 9.5 %copy-start.2 = (f32[4,12,131]{2,1,0:T(8,128)}, f32[4,12,131]{2,1,0:T(8,128)S(1)}, u32[]{:S(2)}) copy-start(f32[4,12,131]{2,1,0:T(8,128)S(1)} %slice.398) | copy-start | bytes 75460
  64.3 9.0 %copy-start.4 = (f32[4,11,132]{2,1,0:T(8,128)}, f32[4,11,132]{2,1,0:T(8,128)S(1)}, u32[]{:S(2)}) copy-start(f32[4,11,132]{2,1,0:T(8,128)S(1)} %slice.392) | copy-start | bytes 69700
  66.1 13.0 %copy-start = (f32[4,9,130]{2,1,0:T(8,128)}, f32[4,9,130]{2,1,0:T(8,128)S(1)}, u32[]{:S(2)}) copy-start(f32[4,9,130]{2,1,0:T(8,128)S(1)} %slice.408) | copy-start | bytes 56164
  70.1 2.7 copy-start.7
  74.7 4.1 %copy-start.6 = (f32[3,10,130]{2,1,0:T(8,128)S(1)}, f32[3,10,130]{2,1,0:T(8,128)}, u32[]{:S(2)}) copy-start(f32[3,10,130]{2,1,0:T(8,128)} %slice_bitcast_fusion.6) | copy-start | bytes 46804
  82.0 7.8 %collective-permute-start.8 = (f32[64,4,2,128]{3,0,2,1:T(8,128)S(1)}, f32[64,4,2,128]{3,0,2,1:T(8,128)S(1)}, u32[]{:S(2)}, u32[]{:S(2)}) collective-permute-start(f32[64,4,2,128]{3,0,2,1:T(8,128)S(1)} %get-tuple-element.12), channel_id=1, source_target_pairs={{0,16},{2,18},{4,20},{6,22},{8,24},{10,26},{12,28},{14,30},{1,17},... | collective-permute-start | bytes 786440 | tf_op jit(solution)/shard_map/ppermute | solution.py:13
  83.5 16.9 %collective-permute-start.9 = (f32[64,4,2,128]{3,0,2,1:T(8,128)S(1)}, f32[64,4,2,128]{3,0,2,1:T(8,128)S(1)}, u32[]{:S(2)}, u32[]{:S(2)}) collective-permute-start(f32[64,4,2,128]{3,0,2,1:T(8,128)S(1)} %get-tuple-element.13), channel_id=1, source_target_pairs={{16,0},{18,2},{20,4},{22,6},{24,8},{26,10},{28,12},{30,14},{17,1},... | collective-permute-start | bytes 786440 | tf_op jit(solution)/shard_map/ppermute | solution.py:13
  104.3 4.0 %collective-permute-start.10 = (f32[64,4,12,2]{0,2,3,1:T(8,128)S(1)}, f32[64,4,12,2]{0,2,3,1:T(8,128)S(1)}, u32[]{:S(2)}, u32[]{:S(2)}) collective-permute-start(f32[64,4,12,2]{0,2,3,1:T(8,128)S(1)} %copy.19), channel_id=1, source_target_pairs={{0,2},{2,4},{4,6},{6,8},{8,10},{10,12},{12,14},{14,16},{16,18},{18... | collective-permute-start | bytes 73736 | tf_op jit(solution)/shard_map/ppermute | solution.py:13
  107.0 3.3 %collective-permute-start.11 = (f32[64,4,12,2]{0,2,3,1:T(8,128)S(1)}, f32[64,4,12,2]{0,2,3,1:T(8,128)}, u32[]{:S(2)}, u32[]{:S(2)}) collective-permute-start(f32[64,4,12,2]{0,2,3,1:T(8,128)S(1)} %copy.20), channel_id=1, source_target_pairs={{2,0},{4,2},{6,4},{8,6},{10,8},{12,10},{14,12},{16,14},{18,16},{20... | collective-permute-start | bytes 73736 | tf_op jit(solution)/shard_map/ppermute | solution.py:13
  112.8 2.7 copy-start.8
  115.5 0.8 copy-start.5
  116.4 0.8 copy-start.3
  122.2 0.8 copy-start.1
  126.4 17.3 %copy-start.9 = (f32[8,128]{1,0:T(8,128)S(1)}, f32[8,128]{1,0:T(8,128)}, u32[]{:S(2)}) copy-start(f32[8,128]{1,0:T(8,128)} %param.8) | copy-start | bytes 12292
Sparse Core Ops, SparseCore 0:
  149.3 116.6 all-reduce.9
where the time goes:
time: 291 us; the launch traced here: 288 us
  waiting for transfers between devices  147 us (51%)
  other arithmetic  42.6 us (15%)
  local copies, waits for them, and re-layouts  34.1 us (12%)
  starting transfers between devices  28.1 us (10%)
  between operations  17.2 us (6%)
  blocking collectives  16.2 us (6%)
    psum x1, waiting for transfers between devices, shards(): gram = lax.psum(gram_local, ('tiles', 'vec'))  115 us
    ppermute x12, waiting for transfers between devices, shifted(): lax.ppermute(value, axis, [(source, source + steps) for source in range(f...  32 us
    ppermute x12, starting transfers between devices, shifted(): lax.ppermute(value, axis, [(source, source + steps) for source in range(f...  28.1 us
    all_to_all x1, blocking collectives, shards(): lax.all_to_all(field, 'vec', split_axis=1, concat_axis=0, tiled=True)  16.2 us
    another operation x3, other arithmetic, shards(): r_factor = jnp.linalg.cholesky(gram).T  12.4 us
    mul x4, other arithmetic, diffuse(): return wet_cells[:, 1:-1, 1:-1] * (field[:, :, 1:-1, 1:-1] + change)  11.3 us
    slice x5, local copies, waits for them, and re-layouts, extend(): left_rim = neighbour(stacked[:, :, :, -margin:], 1)  8.41 us
    ppermute x4, local copies, waits for them, and re-layouts, shifted(): lax.ppermute(value, axis, [(source, source + steps) for source in range(f...  7.06 us
  transfers between devices with their start and end apart: 13, of which 7 were waited for; matrix products, arithmetic and copies ran while one was open for 4% of the time, Pallas kernels for 0%

commit v1 on v0

--- a/solution.py
+++ b/solution.py
@@ -1,6 +1,9 @@
+import functools
 import jax
 import jax.numpy as jnp
 from jax import lax
+from jax.experimental import pallas as pl
+from jax.experimental.pallas import tpu as pltpu
 from jax.sharding import PartitionSpec as P
 
 TGY = 8
@@ -46,6 +49,50 @@
     return jnp.concatenate([left_rim, stacked, right_rim], axis=3)
 
 
+def swapped(value, axis, bit):
+    count = lax.axis_size(axis)
+    return lax.ppermute(value, axis, [(source, source ^ bit) for source in range(count)])
+
+
+def total_over_mesh(value):
+    for axis in ("tiles", "vec"):
+        bit = 1
+        while bit < lax.axis_size(axis):
+            value = value + swapped(value, axis, bit)
+            bit *= 2
+    return value
+
+
+def factor_kernel(scale, gram_ref, out_ref):
+    order = gram_ref.shape[0]
+    height = 8
+    count = order // height
+    blocks = [gram_ref[height * b : height * (b + 1), :] * scale for b in range(count)]
+    row_ids = lax.broadcasted_iota(jnp.int32, (height, order), 0)
+    col_ids = lax.broadcasted_iota(jnp.int32, (height, order), 1)
+    for p in range(count):
+        rows = jnp.zeros((height, order), jnp.float32)
+        for j in range(height):
+            k = height * p + j
+            current = blocks[p]
+            inverse = jnp.broadcast_to(lax.rsqrt(current[j : j + 1, k : k + 1]), (height, order))
+            pivot_row = jnp.broadcast_to(current[j : j + 1, :], (height, order)) * inverse
+            rows = jnp.where((row_ids == j) & (col_ids >= k), pivot_row, rows)
+            for q in range(p, count):
+                pivot_col = jnp.broadcast_to(blocks[q][:, k : k + 1], (height, order)) * inverse
+                blocks[q] = blocks[q] - pivot_col * pivot_row
+        out_ref[height * p : height * (p + 1), :] = rows
+
+
+def factor(gram, scale):
+    return pl.pallas_call(
+        functools.partial(factor_kernel, scale),
+        out_shape=jax.ShapeDtypeStruct(gram.shape, jnp.float32),
+        in_specs=[pl.BlockSpec(memory_space=pltpu.VMEM)],
+        out_specs=pl.BlockSpec(memory_space=pltpu.VMEM),
+    )(gram)
+
+
 def shards(omega, conductance, wet, volume, face_runs):
     levels = omega.shape[1]
     tile_rows = omega.shape[2]
@@ -83,18 +130,14 @@
     total_cells = levels * lax.axis_size("tiles") * tile_rows * tile_cols
     flat_values = regrouped.reshape(all_vectors, -1)
     weighted = (regrouped * volume[None, None]).reshape(all_vectors, -1)
-    gram_local = (
-        lax.dot_general(
-            weighted,
-            flat_values,
-            (((1,), (1,)), ((), ())),
-            precision=lax.Precision.HIGHEST,
-            preferred_element_type=jnp.float32,
-        )
-        / total_cells
+    gram_local = lax.dot_general(
+        weighted,
+        flat_values,
+        (((1,), (1,)), ((), ())),
+        precision=lax.Precision.HIGHEST,
+        preferred_element_type=jnp.float32,
     )
-    gram = lax.psum(gram_local, ("tiles", "vec"))
-    r_factor = jnp.linalg.cholesky(gram).T
+    r_factor = factor(total_over_mesh(gram_local), 1.0 / total_cells)
     return (field, r_factor)
 
 

time: 291 us -> 183 us (0.63)
  waiting for transfers between devices: 147 us -> 46.5 us
  Pallas kernels: 0 us -> 18.3 us
  between operations: 17.2 us -> 3.7 us
  other arithmetic: 42.6 us -> 29.3 us
  starting transfers between devices: 28.1 us -> 33 us
    psum x1 -> x0, waiting for transfers between devices: 115 us -> none  [shards(): gram = lax.psum(gram_local, ('tiles', 'vec'))]
    pallas_call x0 -> x1, Pallas kernels: none -> 18.3 us  [factor(): pl.pallas_call(functools.partial(factor_kernel, scale), out_shape=jax.Sha...]
    ppermute x0 -> x5, waiting for transfers between devices: none -> 14.7 us  [swapped(): lax.ppermute(value, axis, [(source, source ^ bit) for source in range(cou...]
    another operation x3 -> x0, other arithmetic: 12.4 us -> none  [shards(): r_factor = jnp.linalg.cholesky(gram).T]
    ppermute x0 -> x5, starting transfers between devices: none -> 4.89 us  [swapped(): lax.ppermute(value, axis, [(source, source ^ bit) for source in range(cou...]
  transfers between devices with their start and end apart: 13 -> 17, of which waited for: 7 -> 11; matrix products, arithmetic and copies ran while one was open for 4% -> 7% of each run, Pallas kernels for 0% -> 0%
where the time goes in v1:
time: 183 us; the launch traced here: 182 us
  waiting for transfers between devices  46.5 us (25%)
  starting transfers between devices  33 us (18%)
  local copies, waits for them, and re-layouts  32.5 us (18%)
  other arithmetic  29.3 us (16%)
  Pallas kernels  18.3 us (10%)
  blocking collectives  16.2 us (9%)
  between operations  3.7 us (2%)
  matrix products  2.22 us (1%)
    ppermute x12, waiting for transfers between devices, shifted(): lax.ppermute(value, axis, [(source, source + steps) for source in range(f...  31.8 us
    ppermute x12, starting transfers between devices, shifted(): lax.ppermute(value, axis, [(source, source + steps) for source in range(f...  28.1 us
    pallas_call x1, Pallas kernels, factor(): pl.pallas_call(functools.partial(factor_kernel, scale), out_shape=jax.Sha...  18.3 us
    all_to_all x1, blocking collectives, shards(): lax.all_to_all(field, 'vec', split_axis=1, concat_axis=0, tiled=True)  16.2 us
    ppermute x5, waiting for transfers between devices, swapped(): lax.ppermute(value, axis, [(source, source ^ bit) for source in range(cou...  14.7 us
    mul x4, other arithmetic, diffuse(): return wet_cells[:, 1:-1, 1:-1] * (field[:, :, 1:-1, 1:-1] + change)  11.3 us
    slice x5, local copies, waits for them, and re-layouts, extend(): left_rim = neighbour(stacked[:, :, :, -margin:], 1)  8.42 us
    ppermute x4, local copies, waits for them, and re-layouts, shifted(): lax.ppermute(value, axis, [(source, source + steps) for source in range(f...  7.08 us
  transfers between devices with their start and end apart: 17, of which 11 were waited for; matrix products, arithmetic and copies ran while one was open for 7% of the time, Pallas kernels for 0%

profile of v1, /device:TPU:0, one launch (start us, length us, event | category | flops | bytes accessed | tf_op | source)
XLA Modules:
  0.0 181.7 jit_solution(5802805145210705222)
XLA Ops:
  0.7 1.5 fusion.29
  7.5 5.9 %collective-permute-start = (f32[4,4,2,128]{3,2,1,0:T(2,128)S(1)}, f32[4,4,2,128]{3,2,1,0:T(2,128)S(1)}, u32[]{:S(2)}, u32[]{:S(2)}) collective-permute-start(f32[4,4,2,128]{3,2,1,0:T(2,128)S(1)} %get-tuple-element.20), channel_id=1, source_target_pairs={{0,16},{2,18},{4,20},{6,22},{8,24},{10,26},{12,28},{14,30},{1,17},... | collective-permute-start | bytes 49160 | tf_op jit(solution)/shard_map/ppermute | solution.py:16
  13.5 1.3 collective-permute-start.1
  14.8 1.8 %copy_multiply_fusion = f32[64,4,8,128]{3,0,2,1:T(8,128)S(1)} fusion(f32[64,4,8,128]{3,2,1,0:T(8,128)} %param.5, f32[8,128]{1,0:T(8,128)S(1)} %convert_element_type.24), kind=kLoop, calls=%fused_computation.57 | loop fusion | flops 262144 | bytes 2101248 | tf_op jit(solution)/shard_map/mul | solution.py:120
  16.6 3.4 %collective-permute-done.1 = f32[4,4,2,128]{3,2,1,0:T(2,128)S(1)} collective-permute-done((f32[4,4,2,128]{3,2,1,0:T(2,128)S(1)}, f32[4,4,2,128]{3,2,1,0:T(2,128)S(1)}, u32[]{:S(2)}, u32[]{:S(2)}) %collective-permute-start.1) | collective-permute-done | bytes 16416 | tf_op jit(solution)/shard_map/ppermute | solution.py:16
  20.1 1.3 collective-permute-start.2
  21.4 1.3 collective-permute-start.3
  22.8 6.0 %collective-permute-start.4 = (f32[64,4,2,128]{3,0,2,1:T(8,128)S(1)}, f32[64,4,2,128]{3,0,2,1:T(8,128)S(1)}, u32[]{:S(2)}, u32[]{:S(2)}) collective-permute-start(f32[64,4,2,128]{3,0,2,1:T(8,128)S(1)} %get-tuple-element.10), channel_id=1, source_target_pairs={{0,16},{2,18},{4,20},{6,22},{8,24},{10,26},{12,28},{14,30},{1,17},... | collective-permute-start | bytes 786440 | tf_op jit(solution)/shard_map/ppermute | solution.py:16
  28.7 1.3 collective-permute-start.5
  32.4 1.0 collective-permute-done.4
  33.5 10.6 %collective-permute-done.5 = f32[64,4,2,128]{3,0,2,1:T(8,128)S(1)} collective-permute-done((f32[64,4,2,128]{3,0,2,1:T(8,128)S(1)}, f32[64,4,2,128]{3,0,2,1:T(8,128)S(1)}, u32[]{:S(2)}, u32[]{:S(2)}) %collective-permute-start.5) | collective-permute-done | bytes 262176 | tf_op jit(solution)/shard_map/ppermute | solution.py:16
  44.2 1.8 fusion.25
  45.9 2.7 %copy.9 = f32[64,4,12,2]{0,2,3,1:T(8,128)} copy(f32[64,4,12,2]{3,0,2,1:T(8,128)} %get-tuple-element.6) | data formatting | bytes 49152 | tf_op jit(solution)/shard_map/slice | solution.py:47
  48.7 1.3 copy.10
  50.0 1.3 collective-permute-start.7
  51.3 3.7 %collective-permute-start.6 = (f32[64,4,12,2]{0,2,3,1:T(8,128)}, f32[64,4,12,2]{0,2,3,1:T(8,128)}, u32[]{:S(2)}, u32[]{:S(2)}) collective-permute-start(f32[64,4,12,2]{0,2,3,1:T(8,128)} %copy.9), channel_id=1, source_target_pairs={{0,2},{2,4},{4,6},{6,8},{8,10},{10,12},{12,14},{14,16},{16,18},{18... | collective-permute-start | bytes 73736 | tf_op jit(solution)/shard_map/ppermute | solution.py:16
  57.5 1.0 slice.408
  59.3 1.4 copy.11
  60.7 2.6 %copy.12 = f32[64,4,12,2]{3,0,2,1:T(8,128)} copy(f32[64,4,12,2]{0,2,3,1:T(8,128)} %collective-permute-done.7) | data formatting | bytes 49152 | tf_op jit(solution)/shard_map/ppermute | solution.py:16
  63.3 2.7 %pad_maximum_fusion = f32[64,4,12,132]{3,0,2,1:T(8,128)S(1)} fusion(f32[64,4,12,2]{3,0,2,1:T(8,128)} %copy.12, f32[64,4,2,128]{3,0,2,1:T(8,128)S(1)} %collective-permute-done.5, f32[64,4,8,128]{3,0,2,1:T(8,128)S(1)} %copy_multiply_fusion, f32[64,4,2,128]{3,0,2,1:T(8,128)S(1)} %collective-permute-done.4, f32[64,4,12,2]{3,0,2,1:T(8,128)S(1)} %copy.11), kind=kLoop, calls=%fused_computation.4 | loop fusion | flops 1622016 | bytes 3244032 | tf_op jit(solution)/shard_map/concatenate | solution.py:49
  67.9 4.1 %fusion.11 = f32[64,4,10,130]{3,0,2,1:T(8,128)S(1)} fusion(f32[64,3,12,132]{3,0,2,1:T(8,128)S(1)} %fusion.15, f32[64,4,12,131]{3,0,2,1:T(8,128)S(1)} %fusion.1, f32[64,4,11,132]{3,0,2,1:T(8,128)S(1)} %fusion.3, f32[64,4,12,132]{3,0,2,1:T(8,128)S(1)} %pad_maximum_fusion, f32[4,10,130]{2,1,0:T(8,128)S(1)} %slice.379), kind=kLoop, calls=%fused_computation.24 | loop fusion | flops 2329600 | bytes 9224512 | tf_op jit(solution)/shard_map/mul | solution.py:32
  73.5 1.6 fusion.23
  75.2 1.3 collective-permute-start.8
  76.5 1.5 collective-permute-start.9
  78.0 5.0 %collective-permute-done.8 = f32[64,4,2,128]{3,0,2,1:T(8,128)S(1)} collective-permute-done((f32[64,4,2,128]{3,0,2,1:T(8,128)S(1)}, f32[64,4,2,128]{3,0,2,1:T(8,128)S(1)}, u32[]{:S(2)}, u32[]{:S(2)}) %collective-permute-start.8) | collective-permute-done | bytes 262176 | tf_op jit(solution)/shard_map/ppermute | solution.py:16
  82.9 10.4 %collective-permute-done.9 = f32[64,4,2,128]{3,0,2,1:T(8,128)S(1)} collective-permute-done((f32[64,4,2,128]{3,0,2,1:T(8,128)S(1)}, f32[64,4,2,128]{3,0,2,1:T(8,128)S(1)}, u32[]{:S(2)}, u32[]{:S(2)}) %collective-permute-start.9) | collective-permute-done | bytes 262176 | tf_op jit(solution)/shard_map/ppermute | solution.py:16
  93.4 1.8 fusion.24
  95.2 2.1 %copy.13 = f32[64,4,12,2]{0,2,3,1:T(8,128)S(1)} copy(f32[64,4,12,2]{3,0,2,1:T(8,128)} %get-tuple-element.4) | data formatting | bytes 49152 | tf_op jit(solution)/shard_map/slice | solution.py:47
  97.3 2.0 %collective-permute-start.10 = (f32[64,4,12,2]{0,2,3,1:T(8,128)S(1)}, f32[64,4,12,2]{0,2,3,1:T(8,128)S(1)}, u32[]{:S(2)}, u32[]{:S(2)}) collective-permute-start(f32[64,4,12,2]{0,2,3,1:T(8,128)S(1)} %copy.13), channel_id=1, source_target_pairs={{0,2},{2,4},{4,6},{6,8},{8,10},{10,12},{12,14},{14,16},{16,18},{18... | collective-permute-start | bytes 73736 | tf_op jit(solution)/shard_map/ppermute | solution.py:16
  100.0 1.3 collective-permute-start.11
  101.8 1.4 collective-permute-done.11
  103.3 2.6 %copy.16 = f32[64,4,12,2]{3,0,2,1:T(8,128)} copy(f32[64,4,12,2]{0,2,3,1:T(8,128)} %collective-permute-done.11) | data formatting | bytes 49152 | tf_op jit(solution)/shard_map/ppermute | solution.py:16
  105.8 2.7 %pad_maximum_fusion.1 = f32[64,4,12,132]{3,0,2,1:T(8,128)S(1)} fusion(f32[64,4,12,2]{3,0,2,1:T(8,128)} %copy.16, f32[64,4,2,128]{3,0,2,1:T(8,128)S(1)} %collective-permute-done.9, f32[64,4,8,128]{3,0,2,1:T(8,128)S(1)} %fusion.23, f32[64,4,2,128]{3,0,2,1:T(8,128)S(1)} %collective-permute-done.8, f32[64,4,12,2]{3,0,2,1:T(8,128)S(1)} %copy.15), kind=kLoop, calls=%fused_computation.5 | loop fusion | flops 1622016 | bytes 3244032 | tf_op jit(solution)/shard_map/concatenate | solution.py:49
  111.1 4.1 %fusion.7 = f32[64,4,10,130]{3,0,2,1:T(8,128)S(1)} fusion(f32[64,3,12,132]{3,0,2,1:T(8,128)S(1)} %fusion.13, f32[64,4,12,131]{3,0,2,1:T(8,128)S(1)} %fusion, f32[64,4,11,132]{3,0,2,1:T(8,128)S(1)} %fusion.2, f32[64,4,12,132]{3,0,2,1:T(8,128)S(1)} %pad_maximum_fusion.1, f32[4,10,130]{2,1,0:T(8,128)S(1)} %slice.379), kind=kLoop, calls=%fused_computation.15 | loop fusion | flops 2329600 | bytes 9224512 | tf_op jit(solution)/shard_map/mul | solution.py:32
  117.2 1.6 fusion.20
  119.4 16.2 %all_to_all.15 = f32[64,4,8,128]{3,2,0,1:T(8,128)S(1)} all-to-all(f32[64,4,8,128]{3,2,0,1:T(8,128)S(1)} %copy.17), channel_id=1, replica_groups=mesh['tiles'=16,'vec'=2] {'vec'}, dimensions={1} | all-to-all | bytes 2097152 | tf_op jit(solution)/shard_map/all_to_all | solution.py:128
  135.6 1.1 copy.24
  136.8 1.4 reshape.95
  138.2 1.1 mul.199
  139.3 2.2 %fusion.30 = f32[128,128]{1,0:T(8,128)S(1)} fusion(f32[128,2048]{1,0:T(8,128)} %mul.199, f32[128,2048]{1,0:T(8,128)S(1)} %reshape.95), kind=kOutput, calls=%fused_computation.89 | convolution fusion | flops 402653184 | bytes 2162688 | tf_op jit(solution)/shard_map/dot_general | solution.py:133
  141.5 1.3 collective-permute-start.12
  143.7 2.6 %collective-permute-start.13 = (f32[128,128]{1,0:T(8,128)S(1)}, f32[128,128]{1,0:T(8,128)S(1)}, u32[]{:S(2)}, u32[]{:S(2)}) collective-permute-start(f32[128,128]{1,0:T(8,128)S(1)} %add.87), channel_id=1, source_target_pairs={{0,4},{2,6},{4,0},{6,2},{8,12},{10,14},{12,8},{14,10},{16,20},{18,... | collective-permute-start | bytes 196616 | tf_op jit(solution)/shard_map/ppermute | solution.py:54
  146.3 2.4 %collective-permute-done.13 = f32[128,128]{1,0:T(8,128)S(1)} collective-permute-done((f32[128,128]{1,0:T(8,128)S(1)}, f32[128,128]{1,0:T(8,128)S(1)}, u32[]{:S(2)}, u32[]{:S(2)}) %collective-permute-start.13) | collective-permute-done | bytes 65568 | tf_op jit(solution)/shard_map/ppermute | solution.py:54
  148.8 4.3 %collective-permute-done.14 = f32[128,128]{1,0:T(8,128)S(1)} collective-permute-done((f32[128,128]{1,0:T(8,128)S(1)}, f32[128,128]{1,0:T(8,128)S(1)}, u32[]{:S(2)}, u32[]{:S(2)}) %collective-permute-start.14) | collective-permute-done | bytes 65568 | tf_op jit(solution)/shard_map/ppermute | solution.py:54
  153.9 4.5 %collective-permute-done.15 = f32[128,128]{1,0:T(8,128)S(1)} collective-permute-done((f32[128,128]{1,0:T(8,128)S(1)}, f32[128,128]{1,0:T(8,128)S(1)}, u32[]{:S(2)}, u32[]{:S(2)}) %collective-permute-start.15) | collective-permute-done | bytes 65568 | tf_op jit(solution)/shard_map/ppermute | solution.py:54
  158.6 1.6 copy.19
  160.2 2.6 %collective-permute-done.16 = f32[128,128]{1,0:T(8,128)S(1)} collective-permute-done((f32[128,128]{1,0:T(8,128)S(1)}, f32[128,128]{1,0:T(8,128)S(1)}, u32[]{:S(2)}, u32[]{:S(2)}) %collective-permute-start.16) | collective-permute-done | bytes 65568 | tf_op jit(solution)/shard_map/ppermute | solution.py:54
  163.4 18.3 %shard_map.68 = f32[128,128]{1,0:T(8,128)} custom-call(f32[128,128]{1,0:T(8,128)} %add.91.gram_ref), custom_call_target="tpu_custom_call" | custom-call | tf_op jit(solution)/shard_map/pallas_call | solution.py:88
  (77 shorter events, 21.5 us)
Async XLA Ops:
  7.5 9.1 %collective-permute-start = (f32[4,4,2,128]{3,2,1,0:T(2,128)S(1)}, f32[4,4,2,128]{3,2,1,0:T(2,128)S(1)}, u32[]{:S(2)}, u32[]{:S(2)}) collective-permute-start(f32[4,4,2,128]{3,2,1,0:T(2,128)S(1)} %get-tuple-element.20), channel_id=1, source_target_pairs={{0,16},{2,18},{4,20},{6,22},{8,24},{10,26},{12,28},{14,30},{1,17},... | collective-permute-start | bytes 49160 | tf_op jit(solution)/shard_map/ppermute | solution.py:16
  13.5 6.5 %collective-permute-start.1 = (f32[4,4,2,128]{3,2,1,0:T(2,128)S(1)}, f32[4,4,2,128]{3,2,1,0:T(2,128)S(1)}, u32[]{:S(2)}, u32[]{:S(2)}) collective-permute-start(f32[4,4,2,128]{3,2,1,0:T(2,128)S(1)} %get-tuple-element.21), channel_id=1, source_target_pairs={{16,0},{18,2},{20,4},{22,6},{24,8},{26,10},{28,12},{30,14},{17,1},... | collective-permute-start | bytes 49160 | tf_op jit(solution)/shard_map/ppermute | solution.py:16
  20.1 9.9 %collective-permute-start.2 = (f32[4,4,12,2]{3,2,1,0:T(8,128)S(1)}, f32[4,4,12,2]{3,2,1,0:T(8,128)S(1)}, u32[]{:S(2)}, u32[]{:S(2)}) collective-permute-start(f32[4,4,12,2]{3,2,1,0:T(8,128)S(1)} %get-tuple-element.18), channel_id=1, source_target_pairs={{0,2},{2,4},{4,6},{6,8},{8,10},{10,12},{12,14},{14,16},{16,18},{18... | collective-permute-start | bytes 4616 | tf_op jit(solution)/shard_map/ppermute | solution.py:16
  21.4 8.6 %collective-permute-start.3 = (f32[4,4,12,2]{3,2,1,0:T(8,128)S(1)}, f32[4,4,12,2]{3,2,1,0:T(8,128)S(1)}, u32[]{:S(2)}, u32[]{:S(2)}) collective-permute-start(f32[4,4,12,2]{3,2,1,0:T(8,128)S(1)} %get-tuple-element.19), channel_id=1, source_target_pairs={{2,0},{4,2},{6,4},{8,6},{10,8},{12,10},{14,12},{16,14},{18,16},{20... | collective-permute-start | bytes 4616 | tf_op jit(solution)/shard_map/ppermute | solution.py:16
  22.8 10.7 %collective-permute-start.4 = (f32[64,4,2,128]{3,0,2,1:T(8,128)S(1)}, f32[64,4,2,128]{3,0,2,1:T(8,128)S(1)}, u32[]{:S(2)}, u32[]{:S(2)}) collective-permute-start(f32[64,4,2,128]{3,0,2,1:T(8,128)S(1)} %get-tuple-element.10), channel_id=1, source_target_pairs={{0,16},{2,18},{4,20},{6,22},{8,24},{10,26},{12,28},{14,30},{1,17},... | collective-permute-start | bytes 786440 | tf_op jit(solution)/shard_map/ppermute | solution.py:16
  28.7 15.3 %collective-permute-start.5 = (f32[64,4,2,128]{3,0,2,1:T(8,128)S(1)}, f32[64,4,2,128]{3,0,2,1:T(8,128)S(1)}, u32[]{:S(2)}, u32[]{:S(2)}) collective-permute-start(f32[64,4,2,128]{3,0,2,1:T(8,128)S(1)} %get-tuple-element.11), channel_id=1, source_target_pairs={{16,0},{18,2},{20,4},{22,6},{24,8},{26,10},{28,12},{30,14},{17,1},... | collective-permute-start | bytes 786440 | tf_op jit(solution)/shard_map/ppermute | solution.py:16
  50.0 10.8 %collective-permute-start.7 = (f32[64,4,12,2]{0,2,3,1:T(8,128)}, f32[64,4,12,2]{0,2,3,1:T(8,128)}, u32[]{:S(2)}, u32[]{:S(2)}) collective-permute-start(f32[64,4,12,2]{0,2,3,1:T(8,128)} %copy.10), channel_id=1, source_target_pairs={{2,0},{4,2},{6,4},{8,6},{10,8},{12,10},{14,12},{16,14},{18,16},{20... | collective-permute-start | bytes 73736 | tf_op jit(solution)/shard_map/ppermute | solution.py:16
  51.3 8.1 %collective-permute-start.6 = (f32[64,4,12,2]{0,2,3,1:T(8,128)}, f32[64,4,12,2]{0,2,3,1:T(8,128)}, u32[]{:S(2)}, u32[]{:S(2)}) collective-permute-start(f32[64,4,12,2]{0,2,3,1:T(8,128)} %copy.9), channel_id=1, source_target_pairs={{0,2},{2,4},{4,6},{6,8},{8,10},{10,12},{12,14},{14,16},{16,18},{18... | collective-permute-start | bytes 73736 | tf_op jit(solution)/shard_map/ppermute | solution.py:16
  57.5 9.5 %copy-start.2 = (f32[4,12,131]{2,1,0:T(8,128)}, f32[4,12,131]{2,1,0:T(8,128)S(1)}, u32[]{:S(2)}) copy-start(f32[4,12,131]{2,1,0:T(8,128)S(1)} %slice.392) | copy-start | bytes 75460
  57.5 9.0 %copy-start.4 = (f32[4,11,132]{2,1,0:T(8,128)}, f32[4,11,132]{2,1,0:T(8,128)S(1)}, u32[]{:S(2)}) copy-start(f32[4,11,132]{2,1,0:T(8,128)S(1)} %slice.386) | copy-start | bytes 69700
  59.3 13.0 %copy-start = (f32[4,9,130]{2,1,0:T(8,128)}, f32[4,9,130]{2,1,0:T(8,128)S(1)}, u32[]{:S(2)}) copy-start(f32[4,9,130]{2,1,0:T(8,128)S(1)} %slice.402) | copy-start | bytes 56164
  63.3 2.7 %copy-start.7 = (f32[3,12,132]{2,1,0:T(8,128)S(1)}, f32[3,12,132]{2,1,0:T(8,128)}, u32[]{:S(2)}) copy-start(f32[3,12,132]{2,1,0:T(8,128)} %slice_bitcast_fusion.7) | copy-start | bytes 57028
  67.9 4.1 %copy-start.6 = (f32[3,10,130]{2,1,0:T(8,128)S(1)}, f32[3,10,130]{2,1,0:T(8,128)}, u32[]{:S(2)}) copy-start(f32[3,10,130]{2,1,0:T(8,128)} %slice_bitcast_fusion.6) | copy-start | bytes 46804
  75.2 7.8 %collective-permute-start.8 = (f32[64,4,2,128]{3,0,2,1:T(8,128)S(1)}, f32[64,4,2,128]{3,0,2,1:T(8,128)S(1)}, u32[]{:S(2)}, u32[]{:S(2)}) collective-permute-start(f32[64,4,2,128]{3,0,2,1:T(8,128)S(1)} %get-tuple-element.8), channel_id=1, source_target_pairs={{0,16},{2,18},{4,20},{6,22},{8,24},{10,26},{12,28},{14,30},{1,17},... | collective-permute-start | bytes 786440 | tf_op jit(solution)/shard_map/ppermute | solution.py:16
  76.5 16.9 %collective-permute-start.9 = (f32[64,4,2,128]{3,0,2,1:T(8,128)S(1)}, f32[64,4,2,128]{3,0,2,1:T(8,128)S(1)}, u32[]{:S(2)}, u32[]{:S(2)}) collective-permute-start(f32[64,4,2,128]{3,0,2,1:T(8,128)S(1)} %get-tuple-element.9), channel_id=1, source_target_pairs={{16,0},{18,2},{20,4},{22,6},{24,8},{26,10},{28,12},{30,14},{17,1},... | collective-permute-start | bytes 786440 | tf_op jit(solution)/shard_map/ppermute | solution.py:16
  97.3 4.0 %collective-permute-start.10 = (f32[64,4,12,2]{0,2,3,1:T(8,128)S(1)}, f32[64,4,12,2]{0,2,3,1:T(8,128)S(1)}, u32[]{:S(2)}, u32[]{:S(2)}) collective-permute-start(f32[64,4,12,2]{0,2,3,1:T(8,128)S(1)} %copy.13), channel_id=1, source_target_pairs={{0,2},{2,4},{4,6},{6,8},{8,10},{10,12},{12,14},{14,16},{16,18},{18... | collective-permute-start | bytes 73736 | tf_op jit(solution)/shard_map/ppermute | solution.py:16
  100.0 3.3 %collective-permute-start.11 = (f32[64,4,12,2]{0,2,3,1:T(8,128)S(1)}, f32[64,4,12,2]{0,2,3,1:T(8,128)}, u32[]{:S(2)}, u32[]{:S(2)}) collective-permute-start(f32[64,4,12,2]{0,2,3,1:T(8,128)S(1)} %copy.14), channel_id=1, source_target_pairs={{2,0},{4,2},{6,4},{8,6},{10,8},{12,10},{14,12},{16,14},{18,16},{20... | collective-permute-start | bytes 73736 | tf_op jit(solution)/shard_map/ppermute | solution.py:16
  105.8 2.7 %copy-start.8 = (f32[3,12,132]{2,1,0:T(8,128)S(1)}, f32[3,12,132]{2,1,0:T(8,128)}, u32[]{:S(2)}) copy-start(f32[3,12,132]{2,1,0:T(8,128)} %slice_bitcast_fusion.7) | copy-start | bytes 57028
  108.5 0.8 copy-start.5
  109.4 0.8 copy-start.3
  115.2 0.8 copy-start.1
  119.4 17.3 %copy-start.9 = (f32[8,128]{1,0:T(8,128)S(1)}, f32[8,128]{1,0:T(8,128)}, u32[]{:S(2)}) copy-start(f32[8,128]{1,0:T(8,128)} %param.8) | copy-start | bytes 12292
  141.5 2.2 %collective-permute-start.12 = (f32[128,128]{1,0:T(8,128)S(1)}, f32[128,128]{1,0:T(8,128)S(1)}, u32[]{:S(2)}, u32[]{:S(2)}) collective-permute-start(f32[128,128]{1,0:T(8,128)S(1)} %fusion.30), channel_id=1, source_target_pairs={{0,2},{2,0},{4,6},{6,4},{8,10},{10,8},{12,14},{14,12},{16,18},{18,... | collective-permute-start | bytes 196616 | tf_op jit(solution)/shard_map/ppermute | solution.py:54
  143.7 5.0 %collective-permute-start.13 = (f32[128,128]{1,0:T(8,128)S(1)}, f32[128,128]{1,0:T(8,128)S(1)}, u32[]{:S(2)}, u32[]{:S(2)}) collective-permute-start(f32[128,128]{1,0:T(8,128)S(1)} %add.87), channel_id=1, source_target_pairs={{0,4},{2,6},{4,0},{6,2},{8,12},{10,14},{12,8},{14,10},{16,20},{18,... | collective-permute-start | bytes 196616 | tf_op jit(solution)/shard_map/ppermute | solution.py:54
  148.7 4.3 %collective-permute-start.14 = (f32[128,128]{1,0:T(8,128)S(1)}, f32[128,128]{1,0:T(8,128)S(1)}, u32[]{:S(2)}, u32[]{:S(2)}) collective-permute-start(f32[128,128]{1,0:T(8,128)S(1)} %add.88), channel_id=1, source_target_pairs={{0,8},{2,10},{4,12},{6,14},{8,0},{10,2},{12,4},{14,6},{16,24},{18,... | collective-permute-start | bytes 196616 | tf_op jit(solution)/shard_map/ppermute | solution.py:54
  153.0 5.4 %collective-permute-start.15 = (f32[128,128]{1,0:T(8,128)S(1)}, f32[128,128]{1,0:T(8,128)S(1)}, u32[]{:S(2)}, u32[]{:S(2)}) collective-permute-start(f32[128,128]{1,0:T(8,128)S(1)} %add.89), channel_id=1, source_target_pairs={{0,16},{2,18},{4,20},{6,22},{8,24},{10,26},{12,28},{14,30},{16,0},... | collective-permute-start | bytes 196616 | tf_op jit(solution)/shard_map/ppermute | solution.py:54
  158.4 4.3 %collective-permute-start.16 = (f32[128,128]{1,0:T(8,128)S(1)}, f32[128,128]{1,0:T(8,128)S(1)}, u32[]{:S(2)}, u32[]{:S(2)}) collective-permute-start(f32[128,128]{1,0:T(8,128)S(1)} %add.90), channel_id=1, source_target_pairs={{0,1},{1,0},{2,3},{3,2},{4,5},{5,4},{6,7},{7,6},{8,9},{9,8},{10,11... | collective-permute-start | bytes 196616 | tf_op jit(solution)/shard_map/ppermute | solution.py:54

commit v2 on v1

v2 whole, which is shorter than its diff:
```python
import functools
import jax
import jax.numpy as jnp
from jax import lax
from jax.experimental import pallas as pl
from jax.experimental.pallas import tpu as pltpu
from jax.sharding import PartitionSpec as P

TGY = 8
ITERS = 4
EDGE = 2 * ITERS
VMEM_LIMIT = 32 * 1024 * 1024
MAIN, SLOT = (0, 1)


def ids(shape, axis):
    return lax.broadcasted_iota(jnp.int32, shape, axis)


def turn(value, steps, axis):
    size = value.shape[axis]
    steps = steps % size
    return value if steps == 0 else pltpu.roll(value, steps, axis)


def low_half(shape):
    return ids(shape, 0) < ITERS


def left_lanes(shape):
    return ids(shape, 1) % EDGE < ITERS


def first_pair(a, b):
    return jnp.where(low_half(a.shape), a, turn(b, ITERS, 0))


def last_pair(a, b):
    return jnp.where(low_half(a.shape), turn(a, ITERS, 0), b)


def slots(below, above):
    low = low_half(below.shape)
    return (
        jnp.where(low, below, turn(above, ITERS, 0)),
        jnp.where(low, turn(below, ITERS, 0), above),
    )


def store_pair(outs, index, a, b, is_first_row):
    if len(outs) == 1:
        outs[0][index] = jnp.where(is_first_row, last_pair(a, b), first_pair(a, b))
    else:
        outs[0][index] = first_pair(a, b)
        outs[1][index] = last_pair(a, b)


def add_edge(acc, value, place):
    lanes = ids(value.shape, 1) // EDGE
    moved = turn(value, EDGE * place + ITERS, 1)
    return moved if acc is None else jnp.where(lanes == place, moved, acc)


def prev_row(part, other):
    return jnp.where(ids(part.shape, 0) == 0, turn(other, 1, 0), turn(part, 1, 0))


def next_row(part, other):
    last = part.shape[0] - 1
    return jnp.where(ids(part.shape, 0) == last, turn(other, -1, 0), turn(part, -1, 0))


def prev_col(part, rim):
    return jnp.where(ids(part.shape, 1) == 0, rim, turn(part, 1, 1))


def next_col(part, rim):
    last = part.shape[1] - 1
    return jnp.where(ids(part.shape, 1) == last, rim, turn(part, -1, 1))


def strips(edges, rims):
    left = left_lanes(edges.shape)
    return (jnp.where(left, rims, edges), jnp.where(left, edges, rims))


def crossing(left_strip, right_strip):
    lanes = ids(left_strip.shape, 1) % EDGE
    return jnp.where(lanes == ITERS - 1, turn(right_strip, -1, 1), turn(left_strip, 1, 1))


def rim_of(cross, place):
    return turn(cross, -(EDGE * place + ITERS), 1)


def pack_kernel(chunks, meta, runs, omega, conductance, wet, static_out, edge_out, *row_outs):
    directions = len(row_outs) // chunks
    levels, rows, cols = omega.shape[1:]
    shape = (rows, cols)
    is_first_row = meta[0] == 0
    row_ids, col_ids = (ids(shape, 0), ids(shape, 1))
    wet_cells = wet[...].astype(jnp.float32)
    open_x = (col_ids >= runs[0, 0]) & (col_ids < runs[0, 0] + runs[0, 1])
    open_y = (row_ids >= runs[0, 2]) & (row_ids < runs[0, 2] + runs[0, 3])
    keep_x = (row_ids > 0) | open_x
    keep_y = (col_ids > 0) | open_y
    statics = []
    for level in range(levels):
        statics.append(
            [
                jnp.where(keep_x, conductance[0, level], 0.0),
                jnp.where(keep_y, conductance[1, level], 0.0),
                conductance[2, level] if level else jnp.zeros(shape, jnp.float32),
                wet_cells,
            ]
        )
    kinds = len(statics[0])
    group = cols // EDGE
    for level in range(levels):
        edge = None
        for kind in range(kinds):
            static_out[kind, level] = statics[level][kind]
            edge = add_edge(edge, statics[level][kind], kind)
        edge_out[chunks, level] = edge
        for kind in range(0, kinds, 2):
            outs = row_outs[:directions]
            store_pair(outs, (group // 2 + kind // 2, level), statics[level][kind], statics[level][kind + 1], is_first_row)
        for chunk in range(chunks):
            outs = row_outs[directions * chunk : directions * (chunk + 1)]
            edge = None
            for pair in range(group // 2):
                start = [omega[chunk * group + 2 * pair + i, level] * wet_cells for i in range(2)]
                edge = add_edge(edge, start[0], 2 * pair)
                edge = add_edge(edge, start[1], 2 * pair + 1)
                store_pair(outs, (pair, level), start[0], start[1], is_first_row)
            edge_out[chunk, level] = edge


def corner_kernel(meta, left, right, *outs):
    is_first_row = meta[0] == 0
    groups, levels, rows, cols = left.shape
    take = left_lanes((rows, cols))
    for g in range(groups):
        for level in range(0, levels, 2):
            pair = [jnp.where(take, left[g, level + i], right[g, level + i]) for i in range(2)]
            store_pair(outs, (g, level // 2), pair[0], pair[1], is_first_row)


def rims_of_group(left, right, corner_below, corner_above):
    levels, rows, cols = left.shape[1:]
    take = left_lanes((rows, cols))
    rims = [[jnp.where(take, left[0, level], right[0, level]), None] for level in range(levels)]
    for level in range(0, levels, 2):
        pair = slots(corner_below[0, level // 2], corner_above[0, level // 2])
        rims[level][SLOT], rims[level + 1][SLOT] = pair
    return rims


def weight_kernel(meta, statics, below, above, edges, left, right, corner_below, corner_above, main_out, strip_out):
    kinds, levels, rows, cols = statics.shape
    shape = (rows, cols)
    low = low_half(shape)
    valid = (low & (meta[1] > 0)) | (jnp.logical_not(low) & (meta[0] > 0))
    first = below.shape[0] - kinds // 2
    rims = rims_of_group(left, right, corner_below, corner_above)
    field = [[[statics[kind, level], None] for level in range(levels)] for kind in range(kinds)]
    for level in range(levels):
        for kind in range(0, kinds, 2):
            pair = slots(below[first + kind // 2, level], above[first + kind // 2, level])
            for i in range(2):
                field[kind + i][level][SLOT] = jnp.where(valid, pair[i], 0.0)
    width = cols // EDGE
    lanes = ids(shape, 1) // EDGE

    def spread(strip, kind):
        value = jnp.where(lanes == 0, turn(strip, -EDGE * kind, 1), 0.0)
        span = 1
        while span < width:
            value = value + turn(value, EDGE * span, 1)
            span *= 2
        return value

    side = [[[[None, None] for _ in range(levels)] for _ in range(kinds)] for _ in range(2)]
    cross = [[None, None] for _ in range(levels)]
    for level in range(levels):
        for part in range(2):
            edge = edges[0, level] if part == MAIN else None
            if part == SLOT:
                for kind in range(kinds):
                    edge = add_edge(edge, field[kind][level][SLOT], kind)
            rim = rims[level][part]
            if part == SLOT:
                rim = jnp.where(valid, rim, 0.0)
            pair = strips(edge, rim)
            cross[level][part] = crossing(pair[0], pair[1])
            for s in range(2):
                for kind in range(kinds):
                    side[s][kind][level][part] = spread(pair[s], kind)

    def emit(out, values, after_of):
        for level in range(levels):
            for part in range(2):
                cond_x, cond_y, cond_z, wet = (values[kind][level][part] for kind in range(kinds))
                faces = [
                    cond_x,
                    next_row(cond_x, values[0][level][1 - part]),
                    cond_y,
                    after_of(cond_y, level, part),
                    cond_z,
                    values[2][level + 1][part] if level + 1 < levels else jnp.zeros(shape, jnp.float32),
                ]
                total = faces[0]
                for face in faces[1:]:
                    total = total + face
                out[0, level, part] = wet * (1.0 - total)
                for index, face in enumerate(faces):
                    out[index + 1, level, part] = wet * face

    emit(main_out, field, lambda cond, level, part: next_col(cond, rim_of(cross[level][part], 1)))
    for s in range(2):
        emit(strip_out.at[s], side[s], lambda cond, level, part: turn(cond, -1, 1))


def one_pass(state, weight, parts, rim_at):
    levels = len(state)
    result = [[None, None] for _ in range(levels)]
    for level in range(levels):
        for part in parts:
            value, other = (state[level][part], state[level][1 - part])
            rim = rim_at(level, part)
            before = turn(value, 1, 1) if rim is None else prev_col(value, rim)
            after = turn(value, -1, 1) if rim is None else next_col(value, rim)
            total = weight(0, level, part) * value
            total = total + weight(1, level, part) * prev_row(value, other)
            total = total + weight(2, level, part) * next_row(value, other)
            total = total + weight(3, level, part) * before
            total = total + weight(4, level, part) * after
            if level > 0:
                total = total + weight(5, level, part) * state[level - 1][part]
            if level < levels - 1:
                total = total + weight(6, level, part) * state[level + 1][part]
            result[level][part] = total
    return result


def diffuse_kernel(
    batch, meta, omega, wet, volume, below, above, edges, left, right, corner_below, corner_above,
    main_weights, strip_weights, *rest
):
    field_out, keep_out, send_out, cross_scratch, slot_scratch = rest[-5:]
    group, levels, rows, cols = omega.shape
    shape = (rows, cols)
    wet_cells = wet[...].astype(jnp.float32)
    root = jnp.sqrt(volume[...])
    half = levels // 2
    keeps_low = meta[2] == 0
    rims = rims_of_group(left, right, corner_below, corner_above)
    slot_edges = [None] * levels
    for level in range(levels):
        for pair in range(group // 2):
            two = slots(below[pair, level], above[pair, level])
            for i in range(2):
                slot_scratch[2 * pair + i, level] = two[i]
                slot_edges[level] = add_edge(slot_edges[level], two[i], 2 * pair + i)
    state = [[[None, None] for _ in range(levels)] for _ in range(2)]
    for level in range(levels):
        for part in range(2):
            edge = edges[0, level] if part == MAIN else slot_edges[level]
            pair = strips(edge, rims[level][part])
            for s in range(2):
                state[s][level][part] = pair[s]
    for sweep in range(ITERS):
        for level in range(levels):
            for part in range(2):
                cross_scratch[sweep, level, part] = crossing(state[0][level][part], state[1][level][part])
        if sweep < ITERS - 1:
            for s in range(2):
                state[s] = one_pass(
                    state[s], lambda n, level, part: strip_weights[s, n, level, part], (MAIN, SLOT), lambda level, part: None
                )

    for first in range(0, group, batch):
        fields = []
        for place in range(first, first + batch):
            fields.append([[omega[place, level] * wet_cells, slot_scratch[place, level]] for level in range(levels)])
        for sweep in range(ITERS):
            parts = (MAIN, SLOT) if sweep < ITERS - 1 else (MAIN,)
            for i in range(batch):
                fields[i] = one_pass(
                    fields[i],
                    lambda n, level, part: main_weights[n, level, part],
                    parts,
                    lambda level, part: rim_of(cross_scratch[sweep, level, part], first + i),
                )
        for i in range(batch):
            scaled = []
            for level in range(levels):
                value = fields[i][level][MAIN]
                field_out[first + i, level] = value
                scaled.append(value * root)
            for level in range(half):
                at = ((first + i) * half + level) * rows
                keep_out[at : at + rows, :] = jnp.where(keeps_low, scaled[level], scaled[half + level])
                send_out[at : at + rows, :] = jnp.where(keeps_low, scaled[half + level], scaled[level])


def gram_kernel(chunks, slices, meta, *refs):
    out = refs[-1]
    sources = refs[:-1]
    stride = slices
    group = sources[0].shape[0] // stride
    order = group * len(sources)
    cols = sources[0].shape[1]
    exact = jnp.zeros((order, order), jnp.float32)
    cross = jnp.zeros((order, order), jnp.float32)
    for at in range(0, slices, 2):
        columns = []
        for i in range(2):
            columns.append(jnp.concatenate([ref[pl.ds(at + i, group, stride), :] for ref in sources], axis=0))
        values = jnp.concatenate(columns, axis=1)
        high = values.astype(jnp.bfloat16)
        rest = (values - high.astype(jnp.float32)).astype(jnp.bfloat16)
        dims = (((1,), (1,)), ((), ()))
        exact = exact + lax.dot_general(high, high, dims, preferred_element_type=jnp.float32)
        cross = cross + lax.dot_general(high, rest, dims, preferred_element_type=jnp.float32)
    gram = exact + (cross + cross.T)
    moved = turn(turn(gram, order // 2, 0), order // 2, 1)
    out[...] = jnp.where(meta[2] == 0, gram, moved)


def swapped(value, axis, bit):
    count = lax.axis_size(axis)
    return lax.ppermute(value, axis, [(source, source ^ bit) for source in range(count)])


def total_over_mesh(value):
    for axis in ("tiles", "vec"):
        bit = 1
        while bit < lax.axis_size(axis):
            value = value + swapped(value, axis, bit)
            bit *= 2
    return value


def factor_kernel(scale, gram_ref, out_ref):
    order = gram_ref.shape[0]
    height = 8
    count = order // height
    blocks = [gram_ref[height * b : height * (b + 1), :] * scale for b in range(count)]
    row_ids = lax.broadcasted_iota(jnp.int32, (height, order), 0)
    col_ids = lax.broadcasted_iota(jnp.int32, (height, order), 1)
    for p in range(count):
        rows = jnp.zeros((height, order), jnp.float32)
        for j in range(height):
            k = height * p + j
            current = blocks[p]
            inverse = jnp.broadcast_to(lax.rsqrt(current[j : j + 1, k : k + 1]), (height, order))
            pivot_row = jnp.broadcast_to(current[j : j + 1, :], (height, order)) * inverse
            rows = jnp.where((row_ids == j) & (col_ids >= k), pivot_row, rows)
            for q in range(p, count):
                pivot_col = jnp.broadcast_to(blocks[q][:, k : k + 1], (height, order)) * inverse
                blocks[q] = blocks[q] - pivot_col * pivot_row
        out_ref[height * p : height * (p + 1), :] = rows


def shifted(value, axis, steps):
    count = lax.axis_size(axis)
    first, last = (max(0, -steps), min(count, count - steps))
    return lax.ppermute(value, axis, [(source, source + steps) for source in range(first, last)])


def exchange_rows(messages, grid_rows):
    if len(messages) == 1:
        received = swapped(messages[0], "tiles", TGY)
        return (received, received)
    return (shifted(messages[0], "tiles", -TGY), shifted(messages[1], "tiles", TGY))


def f32(*shape):
    return jax.ShapeDtypeStruct(shape, jnp.float32)


def block(shape, *at):
    return pl.BlockSpec(shape, lambda i: at)


def call(kernel, in_specs, out_specs, out_shape, flops=0, scratch=(), aliases=None):
    return pl.pallas_call(
        kernel,
        grid=(1,),
        in_specs=in_specs,
        out_specs=out_specs,
        out_shape=out_shape,
        scratch_shapes=scratch,
        input_output_aliases=aliases or {},
        compiler_params=pltpu.CompilerParams(vmem_limit_bytes=VMEM_LIMIT),
        cost_estimate=pl.CostEstimate(flops=flops, bytes_accessed=1 << 20, transcendentals=0),
    )


def whole(array):
    zeros = (0,) * array.ndim
    return pl.BlockSpec(array.shape, lambda i: zeros)


def shards(omega, conductance, wet, volume, face_runs):
    vectors, levels, rows, cols = omega.shape
    tiles = lax.axis_size("tiles")
    grid_rows = tiles // TGY
    tile_row = lax.axis_index("tiles") // TGY
    meta = jnp.stack([tile_row, grid_rows - 1 - tile_row, lax.axis_index("vec")]).astype(jnp.int32)
    smem = pl.BlockSpec(memory_space=pltpu.SMEM)
    group = cols // EDGE
    chunks = vectors // group
    directions = 1 if grid_rows == 2 else 2
    kinds = 4
    half = levels // 2

    row_shapes = [f32(group // 2 + (kinds // 2 if c == 0 else 0), levels, rows, cols) for c in range(chunks)]
    row_shapes = [shape for shape in row_shapes for _ in range(directions)]
    packed_shapes = [f32(kinds, levels, rows, cols), f32(chunks + 1, levels, rows, cols)] + row_shapes
    statics, edges, *messages = call(
        functools.partial(pack_kernel, chunks),
        [smem, smem, whole(omega), whole(conductance), whole(wet)],
        [whole(s) for s in packed_shapes],
        packed_shapes,
    )(meta, face_runs, omega, conductance, wet)
    messages = [messages[directions * c : directions * (c + 1)] for c in range(chunks)]
    received = [exchange_rows(messages[0], grid_rows)]
    left = shifted(edges, "tiles", 1)
    right = shifted(edges, "tiles", -1)
    corner_shapes = [f32(chunks + 1, levels // 2, rows, cols)] * directions
    corners = call(
        corner_kernel, [smem, whole(left), whole(right)], [whole(s) for s in corner_shapes], corner_shapes
    )(meta, left, right)
    corners = exchange_rows(corners, grid_rows)
    for c in range(1, chunks):
        received.append(exchange_rows(messages[c], grid_rows))

    def group_specs(c):
        edge = block((1, levels, rows, cols), c, 0, 0, 0)
        corner = block((1, levels // 2, rows, cols), c, 0, 0, 0)
        return [edge, edge, edge, corner, corner]

    around = (edges, left, right, *corners)
    weight_shapes = [f32(7, levels, 2, rows, cols), f32(2, 7, levels, 2, rows, cols)]
    main_weights, strip_weights = call(
        weight_kernel,
        [smem, whole(statics), whole(received[0][0]), whole(received[0][1])] + group_specs(chunks),
        [whole(s) for s in weight_shapes],
        weight_shapes,
    )(meta, statics, *received[0], *around)

    field = None
    kept, sent = ([], [])
    half_shape = f32(group * half * rows, cols)
    for c in range(chunks):
        operands = [meta, omega, wet, volume, *received[c], *around, main_weights, strip_weights]
        row_block = block((group // 2, levels, rows, cols), 0, 0, 0, 0)
        chunk_block = block((group, levels, rows, cols), c, 0, 0, 0)
        specs = [smem, chunk_block, whole(wet), whole(volume), row_block, row_block] + group_specs(c)
        specs += [whole(main_weights), whole(strip_weights)]
        aliases = {}
        if field is not None:
            aliases = {len(operands): 0}
            operands.append(field)
            specs.append(pl.BlockSpec(memory_space=pl.ANY))
        field, keep, send = call(
            functools.partial(diffuse_kernel, 4),
            specs,
            [chunk_block, whole(half_shape), whole(half_shape)],
            [f32(*omega.shape), half_shape, half_shape],
            scratch=[pltpu.VMEM((ITERS, levels, 2, rows, cols), jnp.float32), pltpu.VMEM((group, levels, rows, cols), jnp.float32)],
            aliases=aliases,
        )(*operands)
        kept.append(keep)
        sent.append(swapped(send, "vec", 1))

    order = 2 * vectors
    gram = call(
        functools.partial(gram_kernel, chunks, half * rows),
        [smem] + [whole(half_shape)] * (2 * chunks),
        whole(f32(order, order)),
        f32(order, order),
    )(meta, *kept, *sent)
    total_cells = levels * tiles * rows * cols
    r_factor = call(
        functools.partial(factor_kernel, 1.0 / total_cells),
        [whole(gram)],
        whole(gram),
        f32(order, order),
    )(total_over_mesh(gram))
    return (field, r_factor)


def solution(mesh):
    in_specs = (
        P("vec", None, "tiles", None),
        P(None, None, "tiles", None),
        P("tiles", None),
        P("tiles", None),
        P("tiles", None),
    )
    out_specs = (P("vec", None, "tiles", None), P())
    return jax.shard_map(shards, mesh=mesh, in_specs=in_specs, out_specs=out_specs, check_vma=False)
```

time: 183 us -> 107 us (0.58)
  local copies, waits for them, and re-layouts: 32.5 us -> 2.63 us
  other arithmetic: 29.3 us -> 0.12 us
  waiting for transfers between devices: 46.5 us -> 23 us
  Pallas kernels: 18.3 us -> 34.6 us
  blocking collectives: 16.2 us -> 0 us
  starting transfers between devices: 33 us -> 45.4 us
  between operations: 3.7 us -> 0.79 us
  matrix products: 2.22 us -> 0 us
    ppermute x5 -> x14, starting transfers between devices: 4.89 us -> 42.8 us  [swapped(): lax.ppermute(value, axis, [(source, source ^ bit) for source in range(cou...]
    ppermute x12 -> x2, waiting for transfers between devices: 31.8 us -> 0.9 us  [shifted(): lax.ppermute(value, axis, [(source, source + steps) for source in range(f...]
    ppermute x12 -> x2, starting transfers between devices: 28.1 us -> 2.58 us  [shifted(): lax.ppermute(value, axis, [(source, source + steps) for source in range(f...]
    mul x19 -> x0, other arithmetic: 20.8 us -> none  [the longest x4 11.3 us: diffuse(): return wet_cells[:, 1:-1, 1:-1] * (field[:, :, 1:-1, 1:-1] + change)]
    pallas_call x1 -> x9, Pallas kernels: 18.3 us -> 34.6 us  [the longest x1 17.5 us: shards(): call(functools.partial(factor_kernel, 1.0 / total_cells), [whole(gram)],...]
    all_to_all x1 -> x0, blocking collectives: 16.2 us -> none  [shards(): lax.all_to_all(field, 'vec', split_axis=1, concat_axis=0, tiled=True)]
    slice x16 -> x0, local copies, waits for them, and re-layouts: 15.7 us -> none  [the longest x5 8.42 us: extend(): left_rim = neighbour(stacked[:, :, :, -margin:], 1)]
    ppermute x5 -> x14, waiting for transfers between devices: 14.7 us -> 22.1 us  [swapped(): lax.ppermute(value, axis, [(source, source ^ bit) for source in range(cou...]
  transfers between devices with their start and end apart: 17 -> 16, of which waited for: 11 -> 11; matrix products, arithmetic and copies ran while one was open for 7% -> 0% of each run, Pallas kernels for 0% -> 11%
where the time goes in v2:
time: 107 us; the launch traced here: 106 us
  starting transfers between devices  45.4 us (42%)
  Pallas kernels  34.6 us (32%)
  waiting for transfers between devices  23 us (21%)
  local copies, waits for them, and re-layouts  2.63 us (2%)
    ppermute x14, starting transfers between devices, swapped(): lax.ppermute(value, axis, [(source, source ^ bit) for source in range(cou...  42.8 us
    ppermute x14, waiting for transfers between devices, swapped(): lax.ppermute(value, axis, [(source, source ^ bit) for source in range(cou...  22.1 us
    pallas_call x1, Pallas kernels, shards(): call(functools.partial(factor_kernel, 1.0 / total_cells), [whole(gram)],...  17.5 us
    pallas_call x4, Pallas kernels, shards(): call(functools.partial(diffuse_kernel, 4), specs, [chunk_block, whole(hal...  13 us
    unnamed x12, local copies, waits for them, and re-layouts  2.63 us
    ppermute x2, starting transfers between devices, shifted(): lax.ppermute(value, axis, [(source, source + steps) for source in range(f...  2.58 us
  transfers between devices with their start and end apart: 16, of which 11 were waited for; matrix products, arithmetic and copies ran while one was open for 0% of the time, Pallas kernels for 11%

profile of v2, /device:TPU:0, one launch (start us, length us, event | category | flops | bytes accessed | tf_op | source)
XLA Modules:
  0.0 106.5 jit_solution(15018003934036486200)
XLA Ops:
  0.6 0.0 copy-start.2
  0.7 0.1 pad_add_fusion.meta
  0.7 0.6 copy-done.2
  1.3 1.2 %copy-done = f32[64,4,8,128]{3,2,1,0:T(8,128)S(1)} copy-done((f32[64,4,8,128]{3,2,1,0:T(8,128)S(1)}, f32[64,4,8,128]{3,2,1,0:T(8,128)}, u32[]{:S(2)}) %copy-start) | copy-done | bytes 1048600
  2.6 0.8 copy-done.4
  3.4 0.9 shard_map.68
  4.3 1.3 %collective-permute-start.2 = (f32[5,4,8,128]{3,2,1,0:T(8,128)S(1)}, f32[5,4,8,128]{3,2,1,0:T(8,128)S(1)}, u32[]{:S(2)}, u32[]{:S(2)}) collective-permute-start(f32[5,4,8,128]{3,2,1,0:T(8,128)S(1)} %get-tuple-element.23.edges), channel_id=1, source_target_pairs={{2,0},{4,2},{6,4},{8,6},{10,8},{12,10},{14,12},{16,14},{18,16},{20... | collective-permute-start | bytes 245768 | tf_op jit(solution)/shard_map/ppermute | solution.py:369
  5.6 5.5 %collective-permute-start.4 = (f32[10,4,8,128]{3,2,1,0:T(8,128)S(1)}, f32[10,4,8,128]{3,2,1,0:T(8,128)S(1)}, u32[]{:S(2)}, u32[]{:S(2)}) collective-permute-start(f32[10,4,8,128]{3,2,1,0:T(8,128)S(1)} %get-tuple-element.25), channel_id=1, source_target_pairs={{0,16},{2,18},{4,20},{6,22},{8,24},{10,26},{12,28},{14,30},{16,0},... | collective-permute-start | bytes 491528 | tf_op jit(solution)/shard_map/ppermute | solution.py:333
  11.1 0.1 collective-permute-start.6
  11.2 2.8 %collective-permute-start.5 = (f32[8,4,8,128]{3,2,1,0:T(8,128)S(1)}, f32[8,4,8,128]{3,2,1,0:T(8,128)S(1)}, u32[]{:S(2)}, u32[]{:S(2)}) collective-permute-start(f32[8,4,8,128]{3,2,1,0:T(8,128)S(1)} %get-tuple-element.28), channel_id=1, source_target_pairs={{0,16},{2,18},{4,20},{6,22},{8,24},{10,26},{12,28},{14,30},{16,0},... | collective-permute-start | bytes 393224 | tf_op jit(solution)/shard_map/ppermute | solution.py:333
  14.0 0.1 collective-permute-start
  14.1 0.0 collective-permute-done.2.right
  14.1 1.3 %collective-permute-start.1 = (f32[5,4,8,128]{3,2,1,0:T(8,128)S(1)}, f32[5,4,8,128]{3,2,1,0:T(8,128)S(1)}, u32[]{:S(2)}, u32[]{:S(2)}) collective-permute-start(f32[5,4,8,128]{3,2,1,0:T(8,128)S(1)} %get-tuple-element.23.edges), channel_id=1, source_target_pairs={{0,2},{2,4},{4,6},{6,8},{8,10},{10,12},{12,14},{14,16},{16,18},{18... | collective-permute-start | bytes 245768 | tf_op jit(solution)/shard_map/ppermute | solution.py:369
  15.4 0.9 collective-permute-done.1.left
  16.3 0.6 shard_map.69
  16.9 25.0 %collective-permute-start.3 = (f32[5,2,8,128]{3,2,1,0:T(8,128)S(1)}, f32[5,2,8,128]{3,2,1,0:T(8,128)S(1)}, u32[]{:S(2)}, u32[]{:S(2)}) collective-permute-start(f32[5,2,8,128]{3,2,1,0:T(8,128)S(1)} %shard_map.69), channel_id=1, source_target_pairs={{0,16},{2,18},{4,20},{6,22},{8,24},{10,26},{12,28},{14,30},{16,0},... | collective-permute-start | bytes 122888 | tf_op jit(solution)/shard_map/ppermute | solution.py:333
  41.9 2.0 %collective-permute-done.3.corner_below.corner_above = f32[5,2,8,128]{3,2,1,0:T(8,128)S(1)} collective-permute-done((f32[5,2,8,128]{3,2,1,0:T(8,128)S(1)}, f32[5,2,8,128]{3,2,1,0:T(8,128)S(1)}, u32[]{:S(2)}, u32[]{:S(2)}) %collective-permute-start.3) | collective-permute-done | bytes 40992 | tf_op jit(solution)/shard_map/ppermute | solution.py:333
  43.9 0.0 collective-permute-done.4.below.above
  43.9 1.5 %shard_map.70 = (f32[7,4,2,8,128]{4,3,2,1,0:T(8,128)S(1)}, f32[2,7,4,2,8,128]{5,4,3,2,1,0:T(8,128)S(1)}) custom-call(s32[3]{0:T(128)S(1)} %pad_add_fusion.meta, f32[4,4,8,128]{3,2,1,0:T(8,128)S(1)} %get-tuple-element.24.statics, f32[10,4,8,128]{3,2,1,0:T(8,128)S(1)} %collective-permute-done.4.below.above, ...), custom_call_target="tpu_custom_call" | custom-call | bytes 1048576 | tf_op jit(solution)/shard_map/pallas_call | solution.py:447
  45.4 0.0 copy-done.1
  45.5 0.0 copy-done.3
  45.5 3.2 %shard_map.71 = (f32[64,4,8,128]{3,2,1,0:T(8,128)}, f32[256,128]{1,0:T(8,128)S(1)}, f32[256,128]{1,0:T(8,128)S(1)}) custom-call(s32[3]{0:T(128)S(1)} %pad_add_fusion.meta, f32[64,4,8,128]{3,2,1,0:T(8,128)S(1)} %copy-done.1, s32[8,128]{1,0:T(8,128)S(1)} %copy-done.2, f32[8,128]{1,0:T(8,128)S(1)} %copy-done.3, ...), custom_call_target="tpu_custom_call" | custom-call | bytes 1048576 | tf_op jit(solution)/shard_map/pallas_call | solution.py:468
  48.7 0.0 collective-permute-done.6.below.above
  48.7 3.2 %shard_map.72 = (f32[64,4,8,128]{3,2,1,0:T(8,128)}, f32[256,128]{1,0:T(8,128)S(1)}, f32[256,128]{1,0:T(8,128)S(1)}) custom-call(s32[3]{0:T(128)S(1)} %pad_add_fusion.meta, f32[64,4,8,128]{3,2,1,0:T(8,128)S(1)} %copy-done.1, s32[8,128]{1,0:T(8,128)S(1)} %copy-done.2, f32[8,128]{1,0:T(8,128)S(1)} %copy-done.3, ...), custom_call_target="tpu_custom_call", output_to_operand_aliasing={{0}: (13, {})} | custom-call | bytes 1048576 | tf_op jit(solution)/shard_map/pallas_call | solution.py:468
  52.0 0.0 collective-permute-done.5.below.above
  52.0 3.2 %shard_map.73 = (f32[64,4,8,128]{3,2,1,0:T(8,128)}, f32[256,128]{1,0:T(8,128)S(1)}, f32[256,128]{1,0:T(8,128)S(1)}) custom-call(s32[3]{0:T(128)S(1)} %pad_add_fusion.meta, f32[64,4,8,128]{3,2,1,0:T(8,128)S(1)} %copy-done.1, s32[8,128]{1,0:T(8,128)S(1)} %copy-done.2, f32[8,128]{1,0:T(8,128)S(1)} %copy-done.3, ...), custom_call_target="tpu_custom_call", output_to_operand_aliasing={{0}: (13, {})} | custom-call | bytes 1048576 | tf_op jit(solution)/shard_map/pallas_call | solution.py:468
  55.2 0.0 collective-permute-done.below.above
  55.2 3.2 %shard_map.74 = (f32[64,4,8,128]{3,2,1,0:T(8,128)}, f32[256,128]{1,0:T(8,128)S(1)}, f32[256,128]{1,0:T(8,128)S(1)}) custom-call(s32[3]{0:T(128)S(1)} %pad_add_fusion.meta, f32[64,4,8,128]{3,2,1,0:T(8,128)S(1)} %copy-done.1, s32[8,128]{1,0:T(8,128)S(1)} %copy-done.2, f32[8,128]{1,0:T(8,128)S(1)} %copy-done.3, ...), custom_call_target="tpu_custom_call", output_to_operand_aliasing={{0}: (13, {})} | custom-call | bytes 1048576 | tf_op jit(solution)/shard_map/pallas_call | solution.py:468
  58.4 1.5 %collective-permute-start.10 = (f32[256,128]{1,0:T(8,128)S(1)}, f32[256,128]{1,0:T(8,128)S(1)}, u32[]{:S(2)}, u32[]{:S(2)}) collective-permute-start(f32[256,128]{1,0:T(8,128)S(1)} %get-tuple-element.41), channel_id=1, source_target_pairs={{0,1},{1,0},{2,3},{3,2},{4,5},{5,4},{6,7},{7,6},{8,9},{9,8},{10,11... | collective-permute-start | bytes 393224 | tf_op jit(solution)/shard_map/ppermute | solution.py:333
  60.0 0.5 collective-permute-start.9
  60.5 1.5 %collective-permute-start.8 = (f32[256,128]{1,0:T(8,128)S(1)}, f32[256,128]{1,0:T(8,128)S(1)}, u32[]{:S(2)}, u32[]{:S(2)}) collective-permute-start(f32[256,128]{1,0:T(8,128)S(1)} %get-tuple-element.39), channel_id=1, source_target_pairs={{0,1},{1,0},{2,3},{3,2},{4,5},{5,4},{6,7},{7,6},{8,9},{9,8},{10,11... | collective-permute-start | bytes 393224 | tf_op jit(solution)/shard_map/ppermute | solution.py:333
  62.0 0.5 collective-permute-start.7
  62.5 0.9 collective-permute-done.10.refs_7_
  63.4 1.5 %collective-permute-done.9.refs_6_ = f32[256,128]{1,0:T(8,128)S(1)} collective-permute-done((f32[256,128]{1,0:T(8,128)S(1)}, f32[256,128]{1,0:T(8,128)S(1)}, u32[]{:S(2)}, u32[]{:S(2)}) %collective-permute-start.9) | collective-permute-done | bytes 131104 | tf_op jit(solution)/shard_map/ppermute | solution.py:333
  64.9 1.4 %collective-permute-done.8.refs_5_ = f32[256,128]{1,0:T(8,128)S(1)} collective-permute-done((f32[256,128]{1,0:T(8,128)S(1)}, f32[256,128]{1,0:T(8,128)S(1)}, u32[]{:S(2)}, u32[]{:S(2)}) %collective-permute-start.8) | collective-permute-done | bytes 131104 | tf_op jit(solution)/shard_map/ppermute | solution.py:333
  66.3 1.4 %collective-permute-done.7.refs_4_ = f32[256,128]{1,0:T(8,128)S(1)} collective-permute-done((f32[256,128]{1,0:T(8,128)S(1)}, f32[256,128]{1,0:T(8,128)S(1)}, u32[]{:S(2)}, u32[]{:S(2)}) %collective-permute-start.7) | collective-permute-done | bytes 131104 | tf_op jit(solution)/shard_map/ppermute | solution.py:333
  67.7 1.2 %shard_map.75 = f32[128,128]{1,0:T(8,128)S(1)} custom-call(s32[3]{0:T(128)S(1)} %pad_add_fusion.meta, f32[256,128]{1,0:T(8,128)S(1)} %get-tuple-element.34.refs_0_, f32[256,128]{1,0:T(8,128)S(1)} %get-tuple-element.35.refs_1_, f32[256,128]{1,0:T(8,128)S(1)} %get-tuple-element.36.refs_2_, f32[256,128]{1,0:T(8,128)S(1)} %get-tuple-element.37.refs_3_, ...), custom_call_target="tpu_custom_call" | custom-call | bytes 1048576 | tf_op jit(solution)/shard_map/pallas_call | solution.py:480
  68.9 0.1 collective-permute-start.11
  69.0 1.2 %collective-permute-done.11 = f32[128,128]{1,0:T(8,128)S(1)} collective-permute-done((f32[128,128]{1,0:T(8,128)S(1)}, f32[128,128]{1,0:T(8,128)S(1)}, u32[]{:S(2)}, u32[]{:S(2)}) %collective-permute-start.11) | collective-permute-done | bytes 65568 | tf_op jit(solution)/shard_map/ppermute | solution.py:333
  70.3 0.1 collective-permute-start.12
  70.3 4.3 %collective-permute-done.12 = f32[128,128]{1,0:T(8,128)S(1)} collective-permute-done((f32[128,128]{1,0:T(8,128)S(1)}, f32[128,128]{1,0:T(8,128)S(1)}, u32[]{:S(2)}, u32[]{:S(2)}) %collective-permute-start.12) | collective-permute-done | bytes 65568 | tf_op jit(solution)/shard_map/ppermute | solution.py:333
  74.6 0.1 collective-permute-start.13
  74.7 4.3 %collective-permute-done.13 = f32[128,128]{1,0:T(8,128)S(1)} collective-permute-done((f32[128,128]{1,0:T(8,128)S(1)}, f32[128,128]{1,0:T(8,128)S(1)}, u32[]{:S(2)}, u32[]{:S(2)}) %collective-permute-start.13) | collective-permute-done | bytes 65568 | tf_op jit(solution)/shard_map/ppermute | solution.py:333
  78.9 3.5 %collective-permute-start.14 = (f32[128,128]{1,0:T(8,128)S(1)}, f32[128,128]{1,0:T(8,128)S(1)}, u32[]{:S(2)}, u32[]{:S(2)}) collective-permute-start(f32[128,128]{1,0:T(8,128)S(1)} %add.18), channel_id=1, source_target_pairs={{0,16},{2,18},{4,20},{6,22},{8,24},{10,26},{12,28},{14,30},{16,0},... | collective-permute-start | bytes 196616 | tf_op jit(solution)/shard_map/ppermute | solution.py:333
  82.4 2.2 %collective-permute-done.14 = f32[128,128]{1,0:T(8,128)S(1)} collective-permute-done((f32[128,128]{1,0:T(8,128)S(1)}, f32[128,128]{1,0:T(8,128)S(1)}, u32[]{:S(2)}, u32[]{:S(2)}) %collective-permute-start.14) | collective-permute-done | bytes 65568 | tf_op jit(solution)/shard_map/ppermute | solution.py:333
  84.7 1.5 %collective-permute-start.15 = (f32[128,128]{1,0:T(8,128)S(1)}, f32[128,128]{1,0:T(8,128)S(1)}, u32[]{:S(2)}, u32[]{:S(2)}) collective-permute-start(f32[128,128]{1,0:T(8,128)S(1)} %add.19), channel_id=1, source_target_pairs={{0,1},{1,0},{2,3},{3,2},{4,5},{5,4},{6,7},{7,6},{8,9},{9,8},{10,11... | collective-permute-start | bytes 196616 | tf_op jit(solution)/shard_map/ppermute | solution.py:333
  86.1 2.9 %collective-permute-done.15 = f32[128,128]{1,0:T(8,128)S(1)} collective-permute-done((f32[128,128]{1,0:T(8,128)S(1)}, f32[128,128]{1,0:T(8,128)S(1)}, u32[]{:S(2)}, u32[]{:S(2)}) %collective-permute-start.15) | collective-permute-done | bytes 65568 | tf_op jit(solution)/shard_map/ppermute | solution.py:333
  89.0 17.5 %shard_map.76 = f32[128,128]{1,0:T(8,128)} custom-call(f32[128,128]{1,0:T(8,128)S(1)} %add.20.gram_ref), custom_call_target="tpu_custom_call" | custom-call | bytes 1048576 | tf_op jit(solution)/shard_map/pallas_call | solution.py:487
  (11 shorter events, 0.1 us)
Async XLA Ops:
  0.6 0.7 copy-start.2
  0.7 0.7 copy-start.5
  1.3 1.2 %copy-start = (f32[64,4,8,128]{3,2,1,0:T(8,128)S(1)}, f32[64,4,8,128]{3,2,1,0:T(8,128)}, u32[]{:S(2)}) copy-start(f32[64,4,8,128]{3,2,1,0:T(8,128)} %omega.9) | copy-start | bytes 3145732
  2.6 0.8 copy-start.4
  3.4 42.1 %copy-start.1 = (f32[64,4,8,128]{3,2,1,0:T(8,128)S(1)}, f32[64,4,8,128]{3,2,1,0:T(8,128)}, u32[]{:S(2)}) copy-start(f32[64,4,8,128]{3,2,1,0:T(8,128)} %omega.9) | copy-start | bytes 3145732
  4.3 9.8 %collective-permute-start.2 = (f32[5,4,8,128]{3,2,1,0:T(8,128)S(1)}, f32[5,4,8,128]{3,2,1,0:T(8,128)S(1)}, u32[]{:S(2)}, u32[]{:S(2)}) collective-permute-start(f32[5,4,8,128]{3,2,1,0:T(8,128)S(1)} %get-tuple-element.23.edges), channel_id=1, source_target_pairs={{2,0},{4,2},{6,4},{8,6},{10,8},{12,10},{14,12},{16,14},{18,16},{20... | collective-permute-start | bytes 245768 | tf_op jit(solution)/shard_map/ppermute | solution.py:369
  5.6 38.3 %collective-permute-start.4 = (f32[10,4,8,128]{3,2,1,0:T(8,128)S(1)}, f32[10,4,8,128]{3,2,1,0:T(8,128)S(1)}, u32[]{:S(2)}, u32[]{:S(2)}) collective-permute-start(f32[10,4,8,128]{3,2,1,0:T(8,128)S(1)} %get-tuple-element.25), channel_id=1, source_target_pairs={{0,16},{2,18},{4,20},{6,22},{8,24},{10,26},{12,28},{14,30},{16,0},... | collective-permute-start | bytes 491528 | tf_op jit(solution)/shard_map/ppermute | solution.py:333
  11.1 37.6 %collective-permute-start.6 = (f32[8,4,8,128]{3,2,1,0:T(8,128)S(1)}, f32[8,4,8,128]{3,2,1,0:T(8,128)S(1)}, u32[]{:S(2)}, u32[]{:S(2)}) collective-permute-start(f32[8,4,8,128]{3,2,1,0:T(8,128)S(1)} %get-tuple-element.29), channel_id=1, source_target_pairs={{0,16},{2,18},{4,20},{6,22},{8,24},{10,26},{12,28},{14,30},{16,0},... | collective-permute-start | bytes 393224 | tf_op jit(solution)/shard_map/ppermute | solution.py:333
  11.2 40.8 %collective-permute-start.5 = (f32[8,4,8,128]{3,2,1,0:T(8,128)S(1)}, f32[8,4,8,128]{3,2,1,0:T(8,128)S(1)}, u32[]{:S(2)}, u32[]{:S(2)}) collective-permute-start(f32[8,4,8,128]{3,2,1,0:T(8,128)S(1)} %get-tuple-element.28), channel_id=1, source_target_pairs={{0,16},{2,18},{4,20},{6,22},{8,24},{10,26},{12,28},{14,30},{16,0},... | collective-permute-start | bytes 393224 | tf_op jit(solution)/shard_map/ppermute | solution.py:333
  14.0 41.2 %collective-permute-start = (f32[8,4,8,128]{3,2,1,0:T(8,128)S(1)}, f32[8,4,8,128]{3,2,1,0:T(8,128)S(1)}, u32[]{:S(2)}, u32[]{:S(2)}) collective-permute-start(f32[8,4,8,128]{3,2,1,0:T(8,128)S(1)} %get-tuple-element.22), channel_id=1, source_target_pairs={{0,16},{2,18},{4,20},{6,22},{8,24},{10,26},{12,28},{14,30},{16,0},... | collective-permute-start | bytes 393224 | tf_op jit(solution)/shard_map/ppermute | solution.py:333
  14.1 2.2 %collective-permute-start.1 = (f32[5,4,8,128]{3,2,1,0:T(8,128)S(1)}, f32[5,4,8,128]{3,2,1,0:T(8,128)S(1)}, u32[]{:S(2)}, u32[]{:S(2)}) collective-permute-start(f32[5,4,8,128]{3,2,1,0:T(8,128)S(1)} %get-tuple-element.23.edges), channel_id=1, source_target_pairs={{0,2},{2,4},{4,6},{6,8},{8,10},{10,12},{12,14},{14,16},{16,18},{18... | collective-permute-start | bytes 245768 | tf_op jit(solution)/shard_map/ppermute | solution.py:369
  16.9 27.0 %collective-permute-start.3 = (f32[5,2,8,128]{3,2,1,0:T(8,128)S(1)}, f32[5,2,8,128]{3,2,1,0:T(8,128)S(1)}, u32[]{:S(2)}, u32[]{:S(2)}) collective-permute-start(f32[5,2,8,128]{3,2,1,0:T(8,128)S(1)} %shard_map.69), channel_id=1, source_target_pairs={{0,16},{2,18},{4,20},{6,22},{8,24},{10,26},{12,28},{14,30},{16,0},... | collective-permute-start | bytes 122888 | tf_op jit(solution)/shard_map/ppermute | solution.py:333
  43.9 1.6 %copy-start.3 = (f32[8,128]{1,0:T(8,128)S(1)}, f32[8,128]{1,0:T(8,128)}, u32[]{:S(2)}) copy-start(f32[8,128]{1,0:T(8,128)} %volume.7) | copy-start | bytes 12292
  58.4 5.0 %collective-permute-start.10 = (f32[256,128]{1,0:T(8,128)S(1)}, f32[256,128]{1,0:T(8,128)S(1)}, u32[]{:S(2)}, u32[]{:S(2)}) collective-permute-start(f32[256,128]{1,0:T(8,128)S(1)} %get-tuple-element.41), channel_id=1, source_target_pairs={{0,1},{1,0},{2,3},{3,2},{4,5},{5,4},{6,7},{7,6},{8,9},{9,8},{10,11... | collective-permute-start | bytes 393224 | tf_op jit(solution)/shard_map/ppermute | solution.py:333
  60.0 5.0 %collective-permute-start.9 = (f32[256,128]{1,0:T(8,128)S(1)}, f32[256,128]{1,0:T(8,128)S(1)}, u32[]{:S(2)}, u32[]{:S(2)}) collective-permute-start(f32[256,128]{1,0:T(8,128)S(1)} %get-tuple-element.40), channel_id=1, source_target_pairs={{0,1},{1,0},{2,3},{3,2},{4,5},{5,4},{6,7},{7,6},{8,9},{9,8},{10,11... | collective-permute-start | bytes 393224 | tf_op jit(solution)/shard_map/ppermute | solution.py:333
  60.5 5.9 %collective-permute-start.8 = (f32[256,128]{1,0:T(8,128)S(1)}, f32[256,128]{1,0:T(8,128)S(1)}, u32[]{:S(2)}, u32[]{:S(2)}) collective-permute-start(f32[256,128]{1,0:T(8,128)S(1)} %get-tuple-element.39), channel_id=1, source_target_pairs={{0,1},{1,0},{2,3},{3,2},{4,5},{5,4},{6,7},{7,6},{8,9},{9,8},{10,11... | collective-permute-start | bytes 393224 | tf_op jit(solution)/shard_map/ppermute | solution.py:333
  62.0 5.8 %collective-permute-start.7 = (f32[256,128]{1,0:T(8,128)S(1)}, f32[256,128]{1,0:T(8,128)S(1)}, u32[]{:S(2)}, u32[]{:S(2)}) collective-permute-start(f32[256,128]{1,0:T(8,128)S(1)} %get-tuple-element.38), channel_id=1, source_target_pairs={{0,1},{1,0},{2,3},{3,2},{4,5},{5,4},{6,7},{7,6},{8,9},{9,8},{10,11... | collective-permute-start | bytes 393224 | tf_op jit(solution)/shard_map/ppermute | solution.py:333
  68.9 1.3 %collective-permute-start.11 = (f32[128,128]{1,0:T(8,128)S(1)}, f32[128,128]{1,0:T(8,128)S(1)}, u32[]{:S(2)}, u32[]{:S(2)}) collective-permute-start(f32[128,128]{1,0:T(8,128)S(1)} %shard_map.75), channel_id=1, source_target_pairs={{0,2},{2,0},{4,6},{6,4},{8,10},{10,8},{12,14},{14,12},{16,18},{18,... | collective-permute-start | bytes 196616 | tf_op jit(solution)/shard_map/ppermute | solution.py:333
  70.3 4.3 %collective-permute-start.12 = (f32[128,128]{1,0:T(8,128)S(1)}, f32[128,128]{1,0:T(8,128)S(1)}, u32[]{:S(2)}, u32[]{:S(2)}) collective-permute-start(f32[128,128]{1,0:T(8,128)S(1)} %add.16), channel_id=1, source_target_pairs={{0,4},{2,6},{4,0},{6,2},{8,12},{10,14},{12,8},{14,10},{16,20},{18,... | collective-permute-start | bytes 196616 | tf_op jit(solution)/shard_map/ppermute | solution.py:333
  74.6 4.3 %collective-permute-start.13 = (f32[128,128]{1,0:T(8,128)S(1)}, f32[128,128]{1,0:T(8,128)S(1)}, u32[]{:S(2)}, u32[]{:S(2)}) collective-permute-start(f32[128,128]{1,0:T(8,128)S(1)} %add.17), channel_id=1, source_target_pairs={{0,8},{2,10},{4,12},{6,14},{8,0},{10,2},{12,4},{14,6},{16,24},{18,... | collective-permute-start | bytes 196616 | tf_op jit(solution)/shard_map/ppermute | solution.py:333
  78.9 5.7 %collective-permute-start.14 = (f32[128,128]{1,0:T(8,128)S(1)}, f32[128,128]{1,0:T(8,128)S(1)}, u32[]{:S(2)}, u32[]{:S(2)}) collective-permute-start(f32[128,128]{1,0:T(8,128)S(1)} %add.18), channel_id=1, source_target_pairs={{0,16},{2,18},{4,20},{6,22},{8,24},{10,26},{12,28},{14,30},{16,0},... | collective-permute-start | bytes 196616 | tf_op jit(solution)/shard_map/ppermute | solution.py:333
  84.7 4.3 %collective-permute-start.15 = (f32[128,128]{1,0:T(8,128)S(1)}, f32[128,128]{1,0:T(8,128)S(1)}, u32[]{:S(2)}, u32[]{:S(2)}) collective-permute-start(f32[128,128]{1,0:T(8,128)S(1)} %add.19), channel_id=1, source_target_pairs={{0,1},{1,0},{2,3},{3,2},{4,5},{5,4},{6,7},{7,6},{8,9},{9,8},{10,11... | collective-permute-start | bytes 196616 | tf_op jit(solution)/shard_map/ppermute | solution.py:333

commit v3 on v2

--- a/solution.py
+++ b/solution.py
@@ -369,6 +369,16 @@
     return lax.ppermute(value, axis, [(source, source + steps) for source in range(first, last)])
 
 
+def beside(value, steps):
+    count = lax.axis_size("tiles")
+    pairs = [(source, source + steps) for source in range(count)]
+    return lax.ppermute(value, "tiles", [(a, b) for a, b in pairs if 0 <= b < count and a // TGY == b // TGY])
+
+
+def after(values, *done):
+    return lax.optimization_barrier((values, done))[0]
+
+
 def exchange_rows(messages, grid_rows):
     if len(messages) == 1:
         received = swapped(messages[0], "tiles", TGY)
@@ -427,15 +437,17 @@
     )(meta, face_runs, omega, conductance, wet)
     messages = [messages[directions * c : directions * (c + 1)] for c in range(chunks)]
     received = [exchange_rows(messages[0], grid_rows)]
-    left = shifted(edges, "tiles", 1)
-    right = shifted(edges, "tiles", -1)
+    left = beside(edges, 1)
+    right = beside(edges, -1)
     corner_shapes = [f32(chunks + 1, levels // 2, rows, cols)] * directions
     corners = call(
         corner_kernel, [smem, whole(left), whole(right)], [whole(s) for s in corner_shapes], corner_shapes
     )(meta, left, right)
     corners = exchange_rows(corners, grid_rows)
+    gates = [(left, right), corners]
     for c in range(1, chunks):
-        received.append(exchange_rows(messages[c], grid_rows))
+        gate = gates[c - 1] if c <= 2 else received[c - 2]
+        received.append(exchange_rows(after(messages[c], *gate), grid_rows))
 
     def group_specs(c):
         edge = block((1, levels, rows, cols), c, 0, 0, 0)
@@ -455,7 +467,8 @@
     kept, sent = ([], [])
     half_shape = f32(group * half * rows, cols)
     for c in range(chunks):
-        operands = [meta, omega, wet, volume, *received[c], *around, main_weights, strip_weights]
+        rims = after(received[c], sent[c - 2]) if c >= 2 else received[c]
+        operands = [meta, omega, wet, volume, *rims, *around, main_weights, strip_weights]
         row_block = block((group // 2, levels, rows, cols), 0, 0, 0, 0)
         chunk_block = block((group, levels, rows, cols), c, 0, 0, 0)
         specs = [smem, chunk_block, whole(wet), whole(volume), row_block, row_block] + group_specs(c)
@@ -470,6 +483,7 @@
             specs,
             [chunk_block, whole(half_shape), whole(half_shape)],
             [f32(*omega.shape), half_shape, half_shape],
+            flops=4 * 10**9,
             scratch=[pltpu.VMEM((ITERS, levels, 2, rows, cols), jnp.float32), pltpu.VMEM((group, levels, rows, cols), jnp.float32)],
             aliases=aliases,
         )(*operands)

time: 107 us -> 89.4 us (0.84)
  starting transfers between devices: 45.4 us -> 30 us
  waiting for transfers between devices: 23 us -> 21 us
    ppermute x14, starting transfers between devices: 42.8 us -> 25.7 us  [swapped(): lax.ppermute(value, axis, [(source, source ^ bit) for source in range(cou...]
    ppermute x14, waiting for transfers between devices: 22.1 us -> 20.1 us  [swapped(): lax.ppermute(value, axis, [(source, source ^ bit) for source in range(cou...]
    ppermute x2, starting transfers between devices: 2.58 us -> 4.31 us  [beside(): lax.ppermute(value, 'tiles', [(a, b) for a, b in pairs if 0 <= b < count...]
  transfers between devices with their start and end apart: 16 -> 16, of which waited for: 11 -> 10; matrix products, arithmetic and copies ran while one was open for 0% -> 0% of each run, Pallas kernels for 11% -> 17%
where the time goes in v3:
time: 89.4 us; the launch traced here: 89.1 us
  Pallas kernels  34.6 us (39%)
  starting transfers between devices  30 us (34%)
  waiting for transfers between devices  21 us (23%)
  local copies, waits for them, and re-layouts  2.61 us (3%)
    ppermute x14, starting transfers between devices, swapped(): lax.ppermute(value, axis, [(source, source ^ bit) for source in range(cou...  25.7 us
    ppermute x14, waiting for transfers between devices, swapped(): lax.ppermute(value, axis, [(source, source ^ bit) for source in range(cou...  20.1 us
    pallas_call x1, Pallas kernels, shards(): call(functools.partial(factor_kernel, 1.0 / total_cells), [whole(gram)],...  17.5 us
    pallas_call x4, Pallas kernels, shards(): call(functools.partial(diffuse_kernel, 4), specs, [chunk_block, whole(hal...  13 us
    ppermute x2, starting transfers between devices, beside(): lax.ppermute(value, 'tiles', [(a, b) for a, b in pairs if 0 <= b < count...  4.31 us
    unnamed x12, local copies, waits for them, and re-layouts  2.61 us
  transfers between devices with their start and end apart: 16, of which 10 were waited for; matrix products, arithmetic and copies ran while one was open for 0% of the time, Pallas kernels for 17%

profile of v3, /device:TPU:0, one launch (start us, length us, event | category | flops | bytes accessed | tf_op | source)
XLA Modules:
  0.0 89.1 jit_solution(12560018188317083568)
XLA Ops:
  0.6 0.0 copy-start.2
  0.7 0.0 copy-start.4
  0.7 0.1 pad_add_fusion.meta
  0.7 0.7 copy-done.2
  1.4 0.0 copy-done.4
  1.4 1.2 %copy-done = f32[64,4,8,128]{3,2,1,0:T(8,128)S(1)} copy-done((f32[64,4,8,128]{3,2,1,0:T(8,128)S(1)}, f32[64,4,8,128]{3,2,1,0:T(8,128)}, u32[]{:S(2)}) %copy-start) | copy-done | bytes 1048600
  2.7 0.7 copy-done.3
  3.3 0.9 %shard_map.68 = (f32[4,4,8,128]{3,2,1,0:T(8,128)S(1)}, f32[5,4,8,128]{3,2,1,0:T(8,128)S(1)}, f32[10,4,8,128]{3,2,1,0:T(8,128)S(1)}, f32[8,4,8,128]{3,2,1,0:T(8,1...) custom-call(s32[3]{0:T(128)S(1)} %pad_add_fusion.meta, s32[1,4]{1,0:T(1,128)S(1)} %copy-done.4, ...), custom_call_target="tpu_custom_call" | custom-call | bytes 1048576 | tf_op jit(solution)/shard_map/pallas_call | solution.py:432
  4.3 4.1 %collective-permute-start.5 = (f32[10,4,8,128]{3,2,1,0:T(8,128)S(1)}, f32[10,4,8,128]{3,2,1,0:T(8,128)S(1)}, u32[]{:S(2)}, u32[]{:S(2)}) collective-permute-start(f32[10,4,8,128]{3,2,1,0:T(8,128)S(1)} %get-tuple-element.35), channel_id=1, source_target_pairs={{0,16},{2,18},{4,20},{6,22},{8,24},{10,26},{12,28},{14,30},{16,0},... | collective-permute-start | bytes 491528 | tf_op jit(solution)/shard_map/ppermute | solution.py:333
  8.4 1.3 %collective-permute-start.1 = (f32[5,4,8,128]{3,2,1,0:T(8,128)S(1)}, f32[5,4,8,128]{3,2,1,0:T(8,128)S(1)}, u32[]{:S(2)}, u32[]{:S(2)}) collective-permute-start(f32[5,4,8,128]{3,2,1,0:T(8,128)S(1)} %get-tuple-element.31.edges), channel_id=1, source_target_pairs={{2,0},{4,2},{6,4},{8,6},{10,8},{12,10},{14,12},{18,16},{20,18},{22... | collective-permute-start | bytes 245768 | tf_op jit(solution)/shard_map/ppermute | solution.py:375
  9.6 3.0 %collective-permute-start = (f32[5,4,8,128]{3,2,1,0:T(8,128)S(1)}, f32[5,4,8,128]{3,2,1,0:T(8,128)S(1)}, u32[]{:S(2)}, u32[]{:S(2)}) collective-permute-start(f32[5,4,8,128]{3,2,1,0:T(8,128)S(1)} %get-tuple-element.31.edges), channel_id=1, source_target_pairs={{0,2},{2,4},{4,6},{6,8},{8,10},{10,12},{12,14},{16,18},{18,20},{20... | collective-permute-start | bytes 245768 | tf_op jit(solution)/shard_map/ppermute | solution.py:375
  12.7 0.0 collective-permute-done.1.right
  12.7 0.9 collective-permute-done.left
  13.6 0.6 shard_map.69
  14.1 0.1 collective-permute-start.4
  14.2 2.9 %collective-permute-start.2 = (f32[8,4,8,128]{3,2,1,0:T(8,128)S(1)}, f32[8,4,8,128]{3,2,1,0:T(8,128)S(1)}, u32[]{:S(2)}, u32[]{:S(2)}) collective-permute-start(f32[8,4,8,128]{3,2,1,0:T(8,128)S(1)} %get-tuple-element.32), channel_id=1, source_target_pairs={{0,16},{2,18},{4,20},{6,22},{8,24},{10,26},{12,28},{14,30},{16,0},... | collective-permute-start | bytes 393224 | tf_op jit(solution)/shard_map/ppermute | solution.py:333
  17.1 2.0 %collective-permute-done.4.corner_below.corner_above = f32[5,2,8,128]{3,2,1,0:T(8,128)S(1)} collective-permute-done((f32[5,2,8,128]{3,2,1,0:T(8,128)S(1)}, f32[5,2,8,128]{3,2,1,0:T(8,128)S(1)}, u32[]{:S(2)}, u32[]{:S(2)}) %collective-permute-start.4) | collective-permute-done | bytes 40992 | tf_op jit(solution)/shard_map/ppermute | solution.py:333
  19.1 0.0 collective-permute-start.7
  19.1 0.0 collective-permute-done.5.below.above
  19.1 1.5 %shard_map.70 = (f32[7,4,2,8,128]{4,3,2,1,0:T(8,128)S(1)}, f32[2,7,4,2,8,128]{5,4,3,2,1,0:T(8,128)S(1)}) custom-call(s32[3]{0:T(128)S(1)} %pad_add_fusion.meta, f32[4,4,8,128]{3,2,1,0:T(8,128)S(1)} %get-tuple-element.34.statics, f32[10,4,8,128]{3,2,1,0:T(8,128)S(1)} %collective-permute-done.5.below.above, ...), custom_call_target="tpu_custom_call" | custom-call | bytes 1048576 | tf_op jit(solution)/shard_map/pallas_call | solution.py:459
  20.7 3.2 %shard_map.71 = (f32[64,4,8,128]{3,2,1,0:T(8,128)}, f32[256,128]{1,0:T(8,128)S(1)}, f32[256,128]{1,0:T(8,128)S(1)}) custom-call(s32[3]{0:T(128)S(1)} %pad_add_fusion.meta, f32[64,4,8,128]{3,2,1,0:T(8,128)S(1)} %copy-done.1, s32[8,128]{1,0:T(8,128)S(1)} %copy-done.3, f32[8,128]{1,0:T(8,128)S(1)} %copy-done.5, ...), custom_call_target="tpu_custom_call" | custom-call | flops 4000000000 | bytes 1048576 | tf_op jit(solution)/shard_map/pallas_call | solution.py:481
  24.0 1.8 %collective-permute-start.8 = (f32[256,128]{1,0:T(8,128)S(1)}, f32[256,128]{1,0:T(8,128)S(1)}, u32[]{:S(2)}, u32[]{:S(2)}) collective-permute-start(f32[256,128]{1,0:T(8,128)S(1)} %get-tuple-element.44), channel_id=1, source_target_pairs={{0,1},{1,0},{2,3},{3,2},{4,5},{5,4},{6,7},{7,6},{8,9},{9,8},{10,11... | collective-permute-start | bytes 393224 | tf_op jit(solution)/shard_map/ppermute | solution.py:333
  25.8 0.0 collective-permute-done.2.below.above
  25.8 2.6 %collective-permute-start.3 = (f32[8,4,8,128]{3,2,1,0:T(8,128)S(1)}, f32[8,4,8,128]{3,2,1,0:T(8,128)S(1)}, u32[]{:S(2)}, u32[]{:S(2)}) collective-permute-start(f32[8,4,8,128]{3,2,1,0:T(8,128)S(1)} %get-tuple-element.33), channel_id=1, source_target_pairs={{0,16},{2,18},{4,20},{6,22},{8,24},{10,26},{12,28},{14,30},{16,0},... | collective-permute-start | bytes 393224 | tf_op jit(solution)/shard_map/ppermute | solution.py:333
  28.4 3.2 %shard_map.72 = (f32[64,4,8,128]{3,2,1,0:T(8,128)}, f32[256,128]{1,0:T(8,128)S(1)}, f32[256,128]{1,0:T(8,128)S(1)}) custom-call(s32[3]{0:T(128)S(1)} %pad_add_fusion.meta, f32[64,4,8,128]{3,2,1,0:T(8,128)S(1)} %copy-done.1, s32[8,128]{1,0:T(8,128)S(1)} %copy-done.3, f32[8,128]{1,0:T(8,128)S(1)} %copy-done.5, ...), custom_call_target="tpu_custom_call", output_to_operand_aliasing={{0}: (13, {})} | custom-call | flops 4000000000 | bytes 1048576 | tf_op jit(solution)/shard_map/pallas_call | solution.py:481
  31.6 0.5 collective-permute-start.6
  32.1 0.0 collective-permute-done.7.below.above
  32.1 0.0 collective-permute-done.8.refs_4_
  32.1 3.2 %shard_map.73 = (f32[64,4,8,128]{3,2,1,0:T(8,128)}, f32[256,128]{1,0:T(8,128)S(1)}, f32[256,128]{1,0:T(8,128)S(1)}) custom-call(s32[3]{0:T(128)S(1)} %pad_add_fusion.meta, f32[64,4,8,128]{3,2,1,0:T(8,128)S(1)} %copy-done.1, s32[8,128]{1,0:T(8,128)S(1)} %copy-done.3, f32[8,128]{1,0:T(8,128)S(1)} %copy-done.5, ...), custom_call_target="tpu_custom_call", output_to_operand_aliasing={{0}: (13, {})} | custom-call | flops 4000000000 | bytes 1048576 | tf_op jit(solution)/shard_map/pallas_call | solution.py:481
  35.4 1.5 %collective-permute-start.9 = (f32[256,128]{1,0:T(8,128)S(1)}, f32[256,128]{1,0:T(8,128)S(1)}, u32[]{:S(2)}, u32[]{:S(2)}) collective-permute-start(f32[256,128]{1,0:T(8,128)S(1)} %get-tuple-element.54), channel_id=1, source_target_pairs={{0,1},{1,0},{2,3},{3,2},{4,5},{5,4},{6,7},{7,6},{8,9},{9,8},{10,11... | collective-permute-start | bytes 393224 | tf_op jit(solution)/shard_map/ppermute | solution.py:333
  36.9 0.0 collective-permute-done.3.below.above
  36.9 0.5 collective-permute-done.6.refs_5_
  37.4 3.2 %shard_map.74 = (f32[64,4,8,128]{3,2,1,0:T(8,128)}, f32[256,128]{1,0:T(8,128)S(1)}, f32[256,128]{1,0:T(8,128)S(1)}) custom-call(s32[3]{0:T(128)S(1)} %pad_add_fusion.meta, f32[64,4,8,128]{3,2,1,0:T(8,128)S(1)} %copy-done.1, s32[8,128]{1,0:T(8,128)S(1)} %copy-done.3, f32[8,128]{1,0:T(8,128)S(1)} %copy-done.5, ...), custom_call_target="tpu_custom_call", output_to_operand_aliasing={{0}: (13, {})} | custom-call | flops 4000000000 | bytes 1048576 | tf_op jit(solution)/shard_map/pallas_call | solution.py:481
  40.6 0.5 collective-permute-start.10
  41.1 0.3 collective-permute-done.9.refs_6_
  41.4 5.5 %collective-permute-done.10.refs_7_ = f32[256,128]{1,0:T(8,128)S(1)} collective-permute-done((f32[256,128]{1,0:T(8,128)S(1)}, f32[256,128]{1,0:T(8,128)S(1)}, u32[]{:S(2)}, u32[]{:S(2)}) %collective-permute-start.10) | collective-permute-done | bytes 131104 | tf_op jit(solution)/shard_map/ppermute | solution.py:333
  46.9 1.2 %shard_map.75 = f32[128,128]{1,0:T(8,128)S(1)} custom-call(s32[3]{0:T(128)S(1)} %pad_add_fusion.meta, f32[256,128]{1,0:T(8,128)S(1)} %get-tuple-element.50.refs_0_, f32[256,128]{1,0:T(8,128)S(1)} %get-tuple-element.51.refs_1_, f32[256,128]{1,0:T(8,128)S(1)} %get-tuple-element.52.refs_2_, f32[256,128]{1,0:T(8,128)S(1)} %get-tuple-element.53.refs_3_, ...), custom_call_target="tpu_custom_call" | custom-call | bytes 1048576 | tf_op jit(solution)/shard_map/pallas_call | solution.py:494
  48.1 0.1 collective-permute-start.11
  48.1 1.2 %collective-permute-done.11 = f32[128,128]{1,0:T(8,128)S(1)} collective-permute-done((f32[128,128]{1,0:T(8,128)S(1)}, f32[128,128]{1,0:T(8,128)S(1)}, u32[]{:S(2)}, u32[]{:S(2)}) %collective-permute-start.11) | collective-permute-done | bytes 65568 | tf_op jit(solution)/shard_map/ppermute | solution.py:333
  49.4 2.9 %collective-permute-start.12 = (f32[128,128]{1,0:T(8,128)S(1)}, f32[128,128]{1,0:T(8,128)S(1)}, u32[]{:S(2)}, u32[]{:S(2)}) collective-permute-start(f32[128,128]{1,0:T(8,128)S(1)} %add.16), channel_id=1, source_target_pairs={{0,4},{2,6},{4,0},{6,2},{8,12},{10,14},{12,8},{14,10},{16,20},{18,... | collective-permute-start | bytes 196616 | tf_op jit(solution)/shard_map/ppermute | solution.py:333
  52.3 2.4 %collective-permute-done.12 = f32[128,128]{1,0:T(8,128)S(1)} collective-permute-done((f32[128,128]{1,0:T(8,128)S(1)}, f32[128,128]{1,0:T(8,128)S(1)}, u32[]{:S(2)}, u32[]{:S(2)}) %collective-permute-start.12) | collective-permute-done | bytes 65568 | tf_op jit(solution)/shard_map/ppermute | solution.py:333
  54.7 5.1 %collective-permute-start.13 = (f32[128,128]{1,0:T(8,128)S(1)}, f32[128,128]{1,0:T(8,128)S(1)}, u32[]{:S(2)}, u32[]{:S(2)}) collective-permute-start(f32[128,128]{1,0:T(8,128)S(1)} %add.17), channel_id=1, source_target_pairs={{0,8},{2,10},{4,12},{6,14},{8,0},{10,2},{12,4},{14,6},{16,24},{18,... | collective-permute-start | bytes 196616 | tf_op jit(solution)/shard_map/ppermute | solution.py:333
  59.8 2.2 %collective-permute-done.13 = f32[128,128]{1,0:T(8,128)S(1)} collective-permute-done((f32[128,128]{1,0:T(8,128)S(1)}, f32[128,128]{1,0:T(8,128)S(1)}, u32[]{:S(2)}, u32[]{:S(2)}) %collective-permute-start.13) | collective-permute-done | bytes 65568 | tf_op jit(solution)/shard_map/ppermute | solution.py:333
  62.0 2.9 %collective-permute-start.14 = (f32[128,128]{1,0:T(8,128)S(1)}, f32[128,128]{1,0:T(8,128)S(1)}, u32[]{:S(2)}, u32[]{:S(2)}) collective-permute-start(f32[128,128]{1,0:T(8,128)S(1)} %add.18), channel_id=1, source_target_pairs={{0,16},{2,18},{4,20},{6,22},{8,24},{10,26},{12,28},{14,30},{16,0},... | collective-permute-start | bytes 196616 | tf_op jit(solution)/shard_map/ppermute | solution.py:333
  64.9 2.3 %collective-permute-done.14 = f32[128,128]{1,0:T(8,128)S(1)} collective-permute-done((f32[128,128]{1,0:T(8,128)S(1)}, f32[128,128]{1,0:T(8,128)S(1)}, u32[]{:S(2)}, u32[]{:S(2)}) %collective-permute-start.14) | collective-permute-done | bytes 65568 | tf_op jit(solution)/shard_map/ppermute | solution.py:333
  67.3 0.7 collective-permute-start.15
  68.0 3.6 %collective-permute-done.15 = f32[128,128]{1,0:T(8,128)S(1)} collective-permute-done((f32[128,128]{1,0:T(8,128)S(1)}, f32[128,128]{1,0:T(8,128)S(1)}, u32[]{:S(2)}, u32[]{:S(2)}) %collective-permute-start.15) | collective-permute-done | bytes 65568 | tf_op jit(solution)/shard_map/ppermute | solution.py:333
  71.6 17.5 %shard_map.76 = f32[128,128]{1,0:T(8,128)} custom-call(f32[128,128]{1,0:T(8,128)S(1)} %add.20.gram_ref), custom_call_target="tpu_custom_call" | custom-call | bytes 1048576 | tf_op jit(solution)/shard_map/pallas_call | solution.py:501
  (11 shorter events, 0.1 us)
Async XLA Ops:
  0.6 0.8 copy-start.2
  0.7 0.8 copy-start.4
  1.4 1.2 %copy-start = (f32[64,4,8,128]{3,2,1,0:T(8,128)S(1)}, f32[64,4,8,128]{3,2,1,0:T(8,128)}, u32[]{:S(2)}) copy-start(f32[64,4,8,128]{3,2,1,0:T(8,128)} %omega.9) | copy-start | bytes 3145732
  2.7 0.7 copy-start.3
  3.3 17.3 %copy-start.1 = (f32[64,4,8,128]{3,2,1,0:T(8,128)S(1)}, f32[64,4,8,128]{3,2,1,0:T(8,128)}, u32[]{:S(2)}) copy-start(f32[64,4,8,128]{3,2,1,0:T(8,128)} %omega.9) | copy-start | bytes 3145732
  4.3 14.9 %collective-permute-start.5 = (f32[10,4,8,128]{3,2,1,0:T(8,128)S(1)}, f32[10,4,8,128]{3,2,1,0:T(8,128)S(1)}, u32[]{:S(2)}, u32[]{:S(2)}) collective-permute-start(f32[10,4,8,128]{3,2,1,0:T(8,128)S(1)} %get-tuple-element.35), channel_id=1, source_target_pairs={{0,16},{2,18},{4,20},{6,22},{8,24},{10,26},{12,28},{14,30},{16,0},... | collective-permute-start | bytes 491528 | tf_op jit(solution)/shard_map/ppermute | solution.py:333
  8.4 4.3 %collective-permute-start.1 = (f32[5,4,8,128]{3,2,1,0:T(8,128)S(1)}, f32[5,4,8,128]{3,2,1,0:T(8,128)S(1)}, u32[]{:S(2)}, u32[]{:S(2)}) collective-permute-start(f32[5,4,8,128]{3,2,1,0:T(8,128)S(1)} %get-tuple-element.31.edges), channel_id=1, source_target_pairs={{2,0},{4,2},{6,4},{8,6},{10,8},{12,10},{14,12},{18,16},{20,18},{22... | collective-permute-start | bytes 245768 | tf_op jit(solution)/shard_map/ppermute | solution.py:375
  9.6 3.9 %collective-permute-start = (f32[5,4,8,128]{3,2,1,0:T(8,128)S(1)}, f32[5,4,8,128]{3,2,1,0:T(8,128)S(1)}, u32[]{:S(2)}, u32[]{:S(2)}) collective-permute-start(f32[5,4,8,128]{3,2,1,0:T(8,128)S(1)} %get-tuple-element.31.edges), channel_id=1, source_target_pairs={{0,2},{2,4},{4,6},{6,8},{8,10},{10,12},{12,14},{16,18},{18,20},{20... | collective-permute-start | bytes 245768 | tf_op jit(solution)/shard_map/ppermute | solution.py:375
  14.1 5.0 %collective-permute-start.4 = (f32[5,2,8,128]{3,2,1,0:T(8,128)S(1)}, f32[5,2,8,128]{3,2,1,0:T(8,128)S(1)}, u32[]{:S(2)}, u32[]{:S(2)}) collective-permute-start(f32[5,2,8,128]{3,2,1,0:T(8,128)S(1)} %shard_map.69), channel_id=1, source_target_pairs={{0,16},{2,18},{4,20},{6,22},{8,24},{10,26},{12,28},{14,30},{16,0},... | collective-permute-start | bytes 122888 | tf_op jit(solution)/shard_map/ppermute | solution.py:333
  14.2 11.5 %collective-permute-start.2 = (f32[8,4,8,128]{3,2,1,0:T(8,128)S(1)}, f32[8,4,8,128]{3,2,1,0:T(8,128)S(1)}, u32[]{:S(2)}, u32[]{:S(2)}) collective-permute-start(f32[8,4,8,128]{3,2,1,0:T(8,128)S(1)} %get-tuple-element.32), channel_id=1, source_target_pairs={{0,16},{2,18},{4,20},{6,22},{8,24},{10,26},{12,28},{14,30},{16,0},... | collective-permute-start | bytes 393224 | tf_op jit(solution)/shard_map/ppermute | solution.py:333
  19.1 13.0 %collective-permute-start.7 = (f32[8,4,8,128]{3,2,1,0:T(8,128)S(1)}, f32[8,4,8,128]{3,2,1,0:T(8,128)S(1)}, u32[]{:S(2)}, u32[]{:S(2)}) collective-permute-start(f32[8,4,8,128]{3,2,1,0:T(8,128)S(1)} %get-tuple-element.43), channel_id=1, source_target_pairs={{0,16},{2,18},{4,20},{6,22},{8,24},{10,26},{12,28},{14,30},{16,0},... | collective-permute-start | bytes 393224 | tf_op jit(solution)/shard_map/ppermute | solution.py:333
  19.1 1.6 %copy-start.5 = (f32[8,128]{1,0:T(8,128)S(1)}, f32[8,128]{1,0:T(8,128)}, u32[]{:S(2)}) copy-start(f32[8,128]{1,0:T(8,128)} %volume.7) | copy-start | bytes 12292
  24.0 8.2 %collective-permute-start.8 = (f32[256,128]{1,0:T(8,128)S(1)}, f32[256,128]{1,0:T(8,128)S(1)}, u32[]{:S(2)}, u32[]{:S(2)}) collective-permute-start(f32[256,128]{1,0:T(8,128)S(1)} %get-tuple-element.44), channel_id=1, source_target_pairs={{0,1},{1,0},{2,3},{3,2},{4,5},{5,4},{6,7},{7,6},{8,9},{9,8},{10,11... | collective-permute-start | bytes 393224 | tf_op jit(solution)/shard_map/ppermute | solution.py:333
  25.8 11.1 %collective-permute-start.3 = (f32[8,4,8,128]{3,2,1,0:T(8,128)S(1)}, f32[8,4,8,128]{3,2,1,0:T(8,128)S(1)}, u32[]{:S(2)}, u32[]{:S(2)}) collective-permute-start(f32[8,4,8,128]{3,2,1,0:T(8,128)S(1)} %get-tuple-element.33), channel_id=1, source_target_pairs={{0,16},{2,18},{4,20},{6,22},{8,24},{10,26},{12,28},{14,30},{16,0},... | collective-permute-start | bytes 393224 | tf_op jit(solution)/shard_map/ppermute | solution.py:333
  31.6 5.8 %collective-permute-start.6 = (f32[256,128]{1,0:T(8,128)S(1)}, f32[256,128]{1,0:T(8,128)S(1)}, u32[]{:S(2)}, u32[]{:S(2)}) collective-permute-start(f32[256,128]{1,0:T(8,128)S(1)} %get-tuple-element.39), channel_id=1, source_target_pairs={{0,1},{1,0},{2,3},{3,2},{4,5},{5,4},{6,7},{7,6},{8,9},{9,8},{10,11... | collective-permute-start | bytes 393224 | tf_op jit(solution)/shard_map/ppermute | solution.py:333
  35.4 6.0 %collective-permute-start.9 = (f32[256,128]{1,0:T(8,128)S(1)}, f32[256,128]{1,0:T(8,128)S(1)}, u32[]{:S(2)}, u32[]{:S(2)}) collective-permute-start(f32[256,128]{1,0:T(8,128)S(1)} %get-tuple-element.54), channel_id=1, source_target_pairs={{0,1},{1,0},{2,3},{3,2},{4,5},{5,4},{6,7},{7,6},{8,9},{9,8},{10,11... | collective-permute-start | bytes 393224 | tf_op jit(solution)/shard_map/ppermute | solution.py:333
  40.6 6.3 %collective-permute-start.10 = (f32[256,128]{1,0:T(8,128)S(1)}, f32[256,128]{1,0:T(8,128)S(1)}, u32[]{:S(2)}, u32[]{:S(2)}) collective-permute-start(f32[256,128]{1,0:T(8,128)S(1)} %get-tuple-element.55), channel_id=1, source_target_pairs={{0,1},{1,0},{2,3},{3,2},{4,5},{5,4},{6,7},{7,6},{8,9},{9,8},{10,11... | collective-permute-start | bytes 393224 | tf_op jit(solution)/shard_map/ppermute | solution.py:333
  48.1 1.3 %collective-permute-start.11 = (f32[128,128]{1,0:T(8,128)S(1)}, f32[128,128]{1,0:T(8,128)S(1)}, u32[]{:S(2)}, u32[]{:S(2)}) collective-permute-start(f32[128,128]{1,0:T(8,128)S(1)} %shard_map.75), channel_id=1, source_target_pairs={{0,2},{2,0},{4,6},{6,4},{8,10},{10,8},{12,14},{14,12},{16,18},{18,... | collective-permute-start | bytes 196616 | tf_op jit(solution)/shard_map/ppermute | solution.py:333
  49.4 5.3 %collective-permute-start.12 = (f32[128,128]{1,0:T(8,128)S(1)}, f32[128,128]{1,0:T(8,128)S(1)}, u32[]{:S(2)}, u32[]{:S(2)}) collective-permute-start(f32[128,128]{1,0:T(8,128)S(1)} %add.16), channel_id=1, source_target_pairs={{0,4},{2,6},{4,0},{6,2},{8,12},{10,14},{12,8},{14,10},{16,20},{18,... | collective-permute-start | bytes 196616 | tf_op jit(solution)/shard_map/ppermute | solution.py:333
  54.7 7.3 %collective-permute-start.13 = (f32[128,128]{1,0:T(8,128)S(1)}, f32[128,128]{1,0:T(8,128)S(1)}, u32[]{:S(2)}, u32[]{:S(2)}) collective-permute-start(f32[128,128]{1,0:T(8,128)S(1)} %add.17), channel_id=1, source_target_pairs={{0,8},{2,10},{4,12},{6,14},{8,0},{10,2},{12,4},{14,6},{16,24},{18,... | collective-permute-start | bytes 196616 | tf_op jit(solution)/shard_map/ppermute | solution.py:333
  62.0 5.2 %collective-permute-start.14 = (f32[128,128]{1,0:T(8,128)S(1)}, f32[128,128]{1,0:T(8,128)S(1)}, u32[]{:S(2)}, u32[]{:S(2)}) collective-permute-start(f32[128,128]{1,0:T(8,128)S(1)} %add.18), channel_id=1, source_target_pairs={{0,16},{2,18},{4,20},{6,22},{8,24},{10,26},{12,28},{14,30},{16,0},... | collective-permute-start | bytes 196616 | tf_op jit(solution)/shard_map/ppermute | solution.py:333
  67.3 4.3 %collective-permute-start.15 = (f32[128,128]{1,0:T(8,128)S(1)}, f32[128,128]{1,0:T(8,128)S(1)}, u32[]{:S(2)}, u32[]{:S(2)}) collective-permute-start(f32[128,128]{1,0:T(8,128)S(1)} %add.19), channel_id=1, source_target_pairs={{0,1},{1,0},{2,3},{3,2},{4,5},{5,4},{6,7},{7,6},{8,9},{9,8},{10,11... | collective-permute-start | bytes 196616 | tf_op jit(solution)/shard_map/ppermute | solution.py:333

commit v4 on v3

--- a/solution.py
+++ b/solution.py
@@ -305,8 +305,8 @@
 
 
 def gram_kernel(chunks, slices, meta, *refs):
-    out = refs[-1]
-    sources = refs[:-1]
+    mine, theirs = refs[-2:]
+    sources = refs[:-2]
     stride = slices
     group = sources[0].shape[0] // stride
     order = group * len(sources)
@@ -325,7 +325,10 @@
         cross = cross + lax.dot_general(high, rest, dims, preferred_element_type=jnp.float32)
     gram = exact + (cross + cross.T)
     moved = turn(turn(gram, order // 2, 0), order // 2, 1)
-    out[...] = jnp.where(meta[2] == 0, gram, moved)
+    first, second = halves_of_gram(jnp.where(meta[2] == 0, gram, moved))
+    is_first = meta[3] == 0
+    mine[...] = jnp.where(is_first, first, second)
+    theirs[...] = jnp.where(is_first, second, first)
 
 
 def swapped(value, axis, bit):
@@ -333,34 +336,117 @@
     return lax.ppermute(value, axis, [(source, source ^ bit) for source in range(count)])
 
 
-def total_over_mesh(value):
-    for axis in ("tiles", "vec"):
-        bit = 1
-        while bit < lax.axis_size(axis):
-            value = value + swapped(value, axis, bit)
-            bit *= 2
+def mesh_permute(value, mask):
+    axes = ("tiles", "vec")
+    count = lax.axis_size("tiles") * lax.axis_size("vec")
+    return lax.ppermute(value, axes, [(source, source ^ mask) for source in range(count)])
+
+
+def total_over_chips(value):
+    vec = lax.axis_size("vec")
+    masks = []
+    bit = 1
+    while bit < vec:
+        masks.append(bit)
+        bit *= 2
+    bit = 2
+    while bit < lax.axis_size("tiles"):
+        masks.append(bit * vec)
+        bit *= 2
+    while masks:
+        near, masks = (masks[:2], masks[2:])
+        if len(near) == 1:
+            value = value + mesh_permute(value, near[0])
+        else:
+            one, two, both = (mesh_permute(value, mask) for mask in (near[0], near[1], near[0] ^ near[1]))
+            value = (value + one) + (two + both)
     return value
 
 
-def factor_kernel(scale, gram_ref, out_ref):
-    order = gram_ref.shape[0]
+def fold(a, b):
+    half = a.shape[1] // 2
+    return jnp.where(ids(a.shape, 1) < half, a, b)
+
+
+def flip(value):
+    return turn(value, value.shape[1] // 2, 1)
+
+
+def halves_of_gram(gram):
+    q = gram.shape[0] // 8
+    first = [fold(gram[: 2 * q], flip(gram[2 * q : 4 * q])), fold(flip(gram[:q]), gram[q : 2 * q])]
+    second = [fold(flip(gram[4 * q : 6 * q]), gram[6 * q :]), fold(flip(gram[2 * q : 3 * q]), gram[3 * q : 4 * q])]
+    return (jnp.concatenate(first, axis=0), jnp.concatenate(second, axis=0))
+
+
+def gram_of_halves(first, second):
+    q = first.shape[0] // 3
+    return jnp.concatenate(
+        [
+            fold(first[:q], flip(first[2 * q :])),
+            fold(first[q : 2 * q], first[2 * q :]),
+            fold(flip(first[:q]), flip(second[2 * q :])),
+            fold(flip(first[q : 2 * q]), second[2 * q :]),
+            flip(second[: 2 * q]),
+            second[: 2 * q],
+        ],
+        axis=0,
+    )
+
+
+def spread_lane(value, lane):
+    return jnp.broadcast_to(value[:, lane : lane + 1], value.shape)
+
+
+def squares(rows):
+    high = rows.astype(jnp.bfloat16).astype(jnp.float32)
+    rest = rows - high
+    middle = rest.astype(jnp.bfloat16).astype(jnp.float32)
+    low = rest - middle
+    one = jnp.concatenate([high, high, middle, high, low, middle], axis=0).astype(jnp.bfloat16)
+    two = jnp.concatenate([high, middle, high, low, high, middle], axis=0).astype(jnp.bfloat16)
+    return lax.dot_general(one, two, (((0,), (0,)), ((), ())), preferred_element_type=jnp.float32)
+
+
+def factor_kernel(scale, meta, own, other, out_ref):
+    order = out_ref.shape[0]
     height = 8
     count = order // height
-    blocks = [gram_ref[height * b : height * (b + 1), :] * scale for b in range(count)]
-    row_ids = lax.broadcasted_iota(jnp.int32, (height, order), 0)
-    col_ids = lax.broadcasted_iota(jnp.int32, (height, order), 1)
+    shape = (height, order)
+    is_first = meta[3] == 0
+    mine, theirs = (own[...], other[...])
+    gram = gram_of_halves(jnp.where(is_first, mine, theirs), jnp.where(is_first, theirs, mine)) * scale
+    blocks = [gram[height * b : height * (b + 1), :] for b in range(count)]
+    row_ids, col_ids = (ids(shape, 0), ids(shape, 1))
+    previous = None
     for p in range(count):
-        rows = jnp.zeros((height, order), jnp.float32)
-        for j in range(height):
-            k = height * p + j
-            current = blocks[p]
-            inverse = jnp.broadcast_to(lax.rsqrt(current[j : j + 1, k : k + 1]), (height, order))
-            pivot_row = jnp.broadcast_to(current[j : j + 1, :], (height, order)) * inverse
-            rows = jnp.where((row_ids == j) & (col_ids >= k), pivot_row, rows)
-            for q in range(p, count):
-                pivot_col = jnp.broadcast_to(blocks[q][:, k : k + 1], (height, order)) * inverse
-                blocks[q] = blocks[q] - pivot_col * pivot_row
-        out_ref[height * p : height * (p + 1), :] = rows
+        base = height * p
+        rows = [jnp.broadcast_to(blocks[p][j : j + 1, :], shape) for j in range(height)]
+        corner = {(i, j): spread_lane(rows[j], base + i) for j in range(height) for i in range(j, height)}
+        if previous is not None:
+            for done in previous:
+                lanes = [spread_lane(done, base + j) for j in range(height)]
+                for j in range(height):
+                    rows[j] = rows[j] - lanes[j] * done
+                    for i in range(j, height):
+                        corner[i, j] = corner[i, j] - lanes[i] * lanes[j]
+        panel = jnp.zeros(shape, jnp.float32)
+        for s in range(height):
+            inverse = lax.rsqrt(corner[s, s])
+            rows[s] = rows[s] * inverse
+            lanes = {j: corner[j, s] * inverse for j in range(s + 1, height)}
+            for j in range(s + 1, height):
+                for i in range(j, height):
+                    corner[i, j] = corner[i, j] - lanes[i] * lanes[j]
+                rows[j] = rows[j] - lanes[j] * rows[s]
+            panel = jnp.where(row_ids == s, rows[s], panel)
+        panel = jnp.where(col_ids >= base + row_ids, panel, 0.0)
+        out_ref[base : base + height, :] = panel
+        if p + 2 < count:
+            update = squares(panel)
+            for q in range(p + 2, count):
+                blocks[q] = blocks[q] - update[height * q : height * (q + 1), :]
+        previous = rows
 
 
 def shifted(value, axis, steps):
@@ -418,7 +504,8 @@
     tiles = lax.axis_size("tiles")
     grid_rows = tiles // TGY
     tile_row = lax.axis_index("tiles") // TGY
-    meta = jnp.stack([tile_row, grid_rows - 1 - tile_row, lax.axis_index("vec")]).astype(jnp.int32)
+    core = lax.axis_index("tiles") % 2
+    meta = jnp.stack([tile_row, grid_rows - 1 - tile_row, lax.axis_index("vec"), core]).astype(jnp.int32)
     smem = pl.BlockSpec(memory_space=pltpu.SMEM)
     group = cols // EDGE
     chunks = vectors // group
@@ -491,19 +578,21 @@
         sent.append(swapped(send, "vec", 1))
 
     order = 2 * vectors
-    gram = call(
+    half_gram = f32(3 * order // 8, order)
+    mine, theirs = call(
         functools.partial(gram_kernel, chunks, half * rows),
         [smem] + [whole(half_shape)] * (2 * chunks),
-        whole(f32(order, order)),
-        f32(order, order),
+        [whole(half_gram)] * 2,
+        [half_gram] * 2,
     )(meta, *kept, *sent)
+    mine = total_over_chips(mine + swapped(theirs, "tiles", 1))
     total_cells = levels * tiles * rows * cols
     r_factor = call(
         functools.partial(factor_kernel, 1.0 / total_cells),
-        [whole(gram)],
-        whole(gram),
+        [smem, whole(half_gram), whole(half_gram)],
+        whole(f32(order, order)),
         f32(order, order),
-    )(total_over_mesh(gram))
+    )(meta, mine, swapped(mine, "tiles", 1))
     return (field, r_factor)
 
 

time: 89.4 us -> 74.9 us (0.84)
  Pallas kernels: 34.6 us -> 22.8 us
  waiting for transfers between devices: 21 us -> 18.8 us
    pallas_call x1, Pallas kernels: 17.5 us -> 5.59 us  [shards(): call(functools.partial(factor_kernel, 1.0 / total_cells), [smem, whole(ha...]
    ppermute x0 -> x6, starting transfers between devices: none -> 11.8 us  [mesh_permute(): lax.ppermute(value, axes, [(source, source ^ mask) for source in range(co...]
    ppermute x14 -> x11, starting transfers between devices: 25.7 us -> 14.2 us  [swapped(): lax.ppermute(value, axis, [(source, source ^ bit) for source in range(cou...]
    ppermute x14 -> x11, waiting for transfers between devices: 20.1 us -> 10.6 us  [swapped(): lax.ppermute(value, axis, [(source, source ^ bit) for source in range(cou...]
    ppermute x0 -> x6, waiting for transfers between devices: none -> 7.28 us  [mesh_permute(): lax.ppermute(value, axes, [(source, source ^ mask) for source in range(co...]
  transfers between devices with their start and end apart: 16 -> 19, of which waited for: 10 -> 11; matrix products, arithmetic and copies ran while one was open for 0% -> 0% of each run, Pallas kernels for 17% -> 20%
where the time goes in v4:
time: 74.9 us; the launch traced here: 74.6 us
  starting transfers between devices  30.3 us (40%)
  Pallas kernels  22.8 us (30%)
  waiting for transfers between devices  18.8 us (25%)
  local copies, waits for them, and re-layouts  1.91 us (3%)
  between operations  0.79 us (1%)
    ppermute x11, starting transfers between devices, swapped(): lax.ppermute(value, axis, [(source, source ^ bit) for source in range(cou...  14.2 us
    pallas_call x4, Pallas kernels, shards(): call(functools.partial(diffuse_kernel, 4), specs, [chunk_block, whole(hal...  13 us
    ppermute x6, starting transfers between devices, mesh_permute(): lax.ppermute(value, axes, [(source, source ^ mask) for source in range(co...  11.8 us
    ppermute x11, waiting for transfers between devices, swapped(): lax.ppermute(value, axis, [(source, source ^ bit) for source in range(cou...  10.6 us
    ppermute x6, waiting for transfers between devices, mesh_permute(): lax.ppermute(value, axes, [(source, source ^ mask) for source in range(co...  7.28 us
    pallas_call x1, Pallas kernels, shards(): call(functools.partial(factor_kernel, 1.0 / total_cells), [smem, whole(ha...  5.59 us
    ppermute x2, starting transfers between devices, beside(): lax.ppermute(value, 'tiles', [(a, b) for a, b in pairs if 0 <= b < count...  4.31 us
    unnamed x12, local copies, waits for them, and re-layouts  1.91 us
  transfers between devices with their start and end apart: 19, of which 11 were waited for; matrix products, arithmetic and copies ran while one was open for 0% of the time, Pallas kernels for 20%

profile of v4, /device:TPU:0, one launch (start us, length us, event | category | flops | bytes accessed | tf_op | source)
XLA Modules:
  0.0 74.6 jit_solution(15469225433649457845)
XLA Ops:
  0.7 0.1 pad_add_fusion.meta
  0.8 0.7 copy-done.2
  1.4 1.2 %copy-done = f32[64,4,8,128]{3,2,1,0:T(8,128)S(1)} copy-done((f32[64,4,8,128]{3,2,1,0:T(8,128)S(1)}, f32[64,4,8,128]{3,2,1,0:T(8,128)}, u32[]{:S(2)}) %copy-start) | copy-done | bytes 1048600
  2.7 0.9 %shard_map.68 = (f32[4,4,8,128]{3,2,1,0:T(8,128)S(1)}, f32[5,4,8,128]{3,2,1,0:T(8,128)S(1)}, f32[10,4,8,128]{3,2,1,0:T(8,128)S(1)}, f32[8,4,8,128]{3,2,1,0:T(8,1...) custom-call(s32[4]{0:T(128)S(1)} %pad_add_fusion.meta, s32[1,4]{1,0:T(1,128)S(1)} %copy-done.4, ...), custom_call_target="tpu_custom_call" | custom-call | bytes 1048576 | tf_op jit(solution)/shard_map/pallas_call | solution.py:519
  3.6 4.1 %collective-permute-start.5 = (f32[10,4,8,128]{3,2,1,0:T(8,128)S(1)}, f32[10,4,8,128]{3,2,1,0:T(8,128)S(1)}, u32[]{:S(2)}, u32[]{:S(2)}) collective-permute-start(f32[10,4,8,128]{3,2,1,0:T(8,128)S(1)} %get-tuple-element.37), channel_id=1, source_target_pairs={{0,16},{2,18},{4,20},{6,22},{8,24},{10,26},{12,28},{14,30},{16,0},... | collective-permute-start | bytes 491528 | tf_op jit(solution)/shard_map/ppermute | solution.py:336
  7.7 1.3 %collective-permute-start.1 = (f32[5,4,8,128]{3,2,1,0:T(8,128)S(1)}, f32[5,4,8,128]{3,2,1,0:T(8,128)S(1)}, u32[]{:S(2)}, u32[]{:S(2)}) collective-permute-start(f32[5,4,8,128]{3,2,1,0:T(8,128)S(1)} %get-tuple-element.33.edges), channel_id=1, source_target_pairs={{2,0},{4,2},{6,4},{8,6},{10,8},{12,10},{14,12},{18,16},{20,18},{22... | collective-permute-start | bytes 245768 | tf_op jit(solution)/shard_map/ppermute | solution.py:461
  9.0 3.0 %collective-permute-start = (f32[5,4,8,128]{3,2,1,0:T(8,128)S(1)}, f32[5,4,8,128]{3,2,1,0:T(8,128)S(1)}, u32[]{:S(2)}, u32[]{:S(2)}) collective-permute-start(f32[5,4,8,128]{3,2,1,0:T(8,128)S(1)} %get-tuple-element.33.edges), channel_id=1, source_target_pairs={{0,2},{2,4},{4,6},{6,8},{8,10},{10,12},{12,14},{16,18},{18,20},{20... | collective-permute-start | bytes 245768 | tf_op jit(solution)/shard_map/ppermute | solution.py:461
  12.0 0.0 collective-permute-done.1.right
  12.0 0.9 %collective-permute-done.left = f32[5,4,8,128]{3,2,1,0:T(8,128)S(1)} collective-permute-done((f32[5,4,8,128]{3,2,1,0:T(8,128)S(1)}, f32[5,4,8,128]{3,2,1,0:T(8,128)S(1)}, u32[]{:S(2)}, u32[]{:S(2)}) %collective-permute-start) | collective-permute-done | bytes 81952 | tf_op jit(solution)/shard_map/ppermute | solution.py:461
  12.9 0.6 shard_map.69
  13.5 0.1 collective-permute-start.4
  13.6 2.9 %collective-permute-start.2 = (f32[8,4,8,128]{3,2,1,0:T(8,128)S(1)}, f32[8,4,8,128]{3,2,1,0:T(8,128)S(1)}, u32[]{:S(2)}, u32[]{:S(2)}) collective-permute-start(f32[8,4,8,128]{3,2,1,0:T(8,128)S(1)} %get-tuple-element.34), channel_id=1, source_target_pairs={{0,16},{2,18},{4,20},{6,22},{8,24},{10,26},{12,28},{14,30},{16,0},... | collective-permute-start | bytes 393224 | tf_op jit(solution)/shard_map/ppermute | solution.py:336
  16.5 2.0 %collective-permute-done.4.corner_below.corner_above = f32[5,2,8,128]{3,2,1,0:T(8,128)S(1)} collective-permute-done((f32[5,2,8,128]{3,2,1,0:T(8,128)S(1)}, f32[5,2,8,128]{3,2,1,0:T(8,128)S(1)}, u32[]{:S(2)}, u32[]{:S(2)}) %collective-permute-start.4) | collective-permute-done | bytes 40992 | tf_op jit(solution)/shard_map/ppermute | solution.py:336
  18.4 0.0 collective-permute-start.7
  18.5 0.0 collective-permute-done.5.below.above
  18.5 1.5 %shard_map.70 = (f32[7,4,2,8,128]{4,3,2,1,0:T(8,128)S(1)}, f32[2,7,4,2,8,128]{5,4,3,2,1,0:T(8,128)S(1)}) custom-call(s32[4]{0:T(128)S(1)} %pad_add_fusion.meta, f32[4,4,8,128]{3,2,1,0:T(8,128)S(1)} %get-tuple-element.36.statics, f32[10,4,8,128]{3,2,1,0:T(8,128)S(1)} %collective-permute-done.5.below.above, ...), custom_call_target="tpu_custom_call" | custom-call | bytes 1048576 | tf_op jit(solution)/shard_map/pallas_call | solution.py:546
  20.0 3.2 %shard_map.71 = (f32[64,4,8,128]{3,2,1,0:T(8,128)}, f32[256,128]{1,0:T(8,128)S(1)}, f32[256,128]{1,0:T(8,128)S(1)}) custom-call(s32[4]{0:T(128)S(1)} %pad_add_fusion.meta, f32[64,4,8,128]{3,2,1,0:T(8,128)S(1)} %copy-done.1, s32[8,128]{1,0:T(8,128)S(1)} %copy-done.3, f32[8,128]{1,0:T(8,128)S(1)} %copy-done.5, ...), custom_call_target="tpu_custom_call" | custom-call | flops 4000000000 | bytes 1048576 | tf_op jit(solution)/shard_map/pallas_call | solution.py:568
  23.3 1.8 %collective-permute-start.8 = (f32[256,128]{1,0:T(8,128)S(1)}, f32[256,128]{1,0:T(8,128)S(1)}, u32[]{:S(2)}, u32[]{:S(2)}) collective-permute-start(f32[256,128]{1,0:T(8,128)S(1)} %get-tuple-element.46), channel_id=1, source_target_pairs={{0,1},{1,0},{2,3},{3,2},{4,5},{5,4},{6,7},{7,6},{8,9},{9,8},{10,11... | collective-permute-start | bytes 393224 | tf_op jit(solution)/shard_map/ppermute | solution.py:336
  25.1 0.0 collective-permute-done.2.below.above
  25.1 2.6 %collective-permute-start.3 = (f32[8,4,8,128]{3,2,1,0:T(8,128)S(1)}, f32[8,4,8,128]{3,2,1,0:T(8,128)S(1)}, u32[]{:S(2)}, u32[]{:S(2)}) collective-permute-start(f32[8,4,8,128]{3,2,1,0:T(8,128)S(1)} %get-tuple-element.35), channel_id=1, source_target_pairs={{0,16},{2,18},{4,20},{6,22},{8,24},{10,26},{12,28},{14,30},{16,0},... | collective-permute-start | bytes 393224 | tf_op jit(solution)/shard_map/ppermute | solution.py:336
  27.7 3.2 %shard_map.72 = (f32[64,4,8,128]{3,2,1,0:T(8,128)}, f32[256,128]{1,0:T(8,128)S(1)}, f32[256,128]{1,0:T(8,128)S(1)}) custom-call(s32[4]{0:T(128)S(1)} %pad_add_fusion.meta, f32[64,4,8,128]{3,2,1,0:T(8,128)S(1)} %copy-done.1, s32[8,128]{1,0:T(8,128)S(1)} %copy-done.3, f32[8,128]{1,0:T(8,128)S(1)} %copy-done.5, ...), custom_call_target="tpu_custom_call", output_to_operand_aliasing={{0}: (13, {})} | custom-call | flops 4000000000 | bytes 1048576 | tf_op jit(solution)/shard_map/pallas_call | solution.py:568
  30.9 0.5 collective-permute-start.6
  31.5 0.0 collective-permute-done.7.below.above
  31.5 0.0 collective-permute-done.8.refs_4_
  31.5 3.2 %shard_map.73 = (f32[64,4,8,128]{3,2,1,0:T(8,128)}, f32[256,128]{1,0:T(8,128)S(1)}, f32[256,128]{1,0:T(8,128)S(1)}) custom-call(s32[4]{0:T(128)S(1)} %pad_add_fusion.meta, f32[64,4,8,128]{3,2,1,0:T(8,128)S(1)} %copy-done.1, s32[8,128]{1,0:T(8,128)S(1)} %copy-done.3, f32[8,128]{1,0:T(8,128)S(1)} %copy-done.5, ...), custom_call_target="tpu_custom_call", output_to_operand_aliasing={{0}: (13, {})} | custom-call | flops 4000000000 | bytes 1048576 | tf_op jit(solution)/shard_map/pallas_call | solution.py:568
  34.7 1.5 %collective-permute-start.9 = (f32[256,128]{1,0:T(8,128)S(1)}, f32[256,128]{1,0:T(8,128)S(1)}, u32[]{:S(2)}, u32[]{:S(2)}) collective-permute-start(f32[256,128]{1,0:T(8,128)S(1)} %get-tuple-element.56), channel_id=1, source_target_pairs={{0,1},{1,0},{2,3},{3,2},{4,5},{5,4},{6,7},{7,6},{8,9},{9,8},{10,11... | collective-permute-start | bytes 393224 | tf_op jit(solution)/shard_map/ppermute | solution.py:336
  36.2 0.0 collective-permute-done.3.below.above
  36.2 0.5 collective-permute-done.6.refs_5_
  36.7 3.2 %shard_map.74 = (f32[64,4,8,128]{3,2,1,0:T(8,128)}, f32[256,128]{1,0:T(8,128)S(1)}, f32[256,128]{1,0:T(8,128)S(1)}) custom-call(s32[4]{0:T(128)S(1)} %pad_add_fusion.meta, f32[64,4,8,128]{3,2,1,0:T(8,128)S(1)} %copy-done.1, s32[8,128]{1,0:T(8,128)S(1)} %copy-done.3, f32[8,128]{1,0:T(8,128)S(1)} %copy-done.5, ...), custom_call_target="tpu_custom_call", output_to_operand_aliasing={{0}: (13, {})} | custom-call | flops 4000000000 | bytes 1048576 | tf_op jit(solution)/shard_map/pallas_call | solution.py:568
  39.9 0.5 collective-permute-start.10
  40.4 0.3 collective-permute-done.9.refs_6_
  40.7 5.5 %collective-permute-done.10.refs_7_ = f32[256,128]{1,0:T(8,128)S(1)} collective-permute-done((f32[256,128]{1,0:T(8,128)S(1)}, f32[256,128]{1,0:T(8,128)S(1)}, u32[]{:S(2)}, u32[]{:S(2)}) %collective-permute-start.10) | collective-permute-done | bytes 131104 | tf_op jit(solution)/shard_map/ppermute | solution.py:336
  46.2 1.3 %shard_map.75 = (f32[48,128]{1,0:T(8,128)S(1)}, f32[48,128]{1,0:T(8,128)S(1)}) custom-call(s32[4]{0:T(128)S(1)} %pad_add_fusion.meta, f32[256,128]{1,0:T(8,128)S(1)} %get-tuple-element.52.refs_0_, f32[256,128]{1,0:T(8,128)S(1)} %get-tuple-element.53.refs_1_, f32[256,128]{1,0:T(8,128)S(1)} %get-tuple-element.54.refs_2_, ...), custom_call_target="tpu_custom_call" | custom-call | bytes 1048576 | tf_op jit(solution)/shard_map/pallas_call | solution.py:582
  47.5 0.1 collective-permute-start.11
  47.5 1.2 %collective-permute-done.11 = f32[48,128]{1,0:T(8,128)S(1)} collective-permute-done((f32[48,128]{1,0:T(8,128)S(1)}, f32[48,128]{1,0:T(8,128)S(1)}, u32[]{:S(2)}, u32[]{:S(2)}) %collective-permute-start.11) | collective-permute-done | bytes 24608 | tf_op jit(solution)/shard_map/ppermute | solution.py:336
  48.7 4.0 %collective-permute-start.14 = (f32[48,128]{1,0:T(8,128)S(1)}, f32[48,128]{1,0:T(8,128)S(1)}, u32[]{:S(2)}, u32[]{:S(2)}) collective-permute-start(f32[48,128]{1,0:T(8,128)S(1)} %add.27), channel_id=1, source_target_pairs={{0,5},{1,4},{2,7},{3,6},{4,1},{5,0},{6,3},{7,2},{8,13},{9,12},{10,... | collective-permute-start | bytes 73736 | tf_op jit(solution)/shard_map/ppermute | solution.py:342
  52.7 0.6 collective-permute-start.12
  53.3 1.2 %collective-permute-done.14 = f32[48,128]{1,0:T(8,128)S(1)} collective-permute-done((f32[48,128]{1,0:T(8,128)S(1)}, f32[48,128]{1,0:T(8,128)S(1)}, u32[]{:S(2)}, u32[]{:S(2)}) %collective-permute-start.14) | collective-permute-done | bytes 24608 | tf_op jit(solution)/shard_map/ppermute | solution.py:342
  54.5 2.0 %collective-permute-done.13 = f32[48,128]{1,0:T(8,128)S(1)} collective-permute-done((f32[48,128]{1,0:T(8,128)S(1)}, f32[48,128]{1,0:T(8,128)S(1)}, u32[]{:S(2)}, u32[]{:S(2)}) %collective-permute-start.13) | collective-permute-done | bytes 24608 | tf_op jit(solution)/shard_map/ppermute | solution.py:342
  56.5 0.0 collective-permute-done.12
  56.5 6.5 %collective-permute-start.17 = (f32[48,128]{1,0:T(8,128)S(1)}, f32[48,128]{1,0:T(8,128)S(1)}, u32[]{:S(2)}, u32[]{:S(2)}) collective-permute-start(f32[48,128]{1,0:T(8,128)S(1)} %add_add_fusion.1), channel_id=1, source_target_pairs={{0,24},{1,25},{2,26},{3,27},{4,28},{5,29},{6,30},{7,31},{8,16},{9,... | collective-permute-start | bytes 73736 | tf_op jit(solution)/shard_map/ppermute | solution.py:342
  63.1 0.6 collective-permute-start.15
  63.7 1.2 %collective-permute-done.17 = f32[48,128]{1,0:T(8,128)S(1)} collective-permute-done((f32[48,128]{1,0:T(8,128)S(1)}, f32[48,128]{1,0:T(8,128)S(1)}, u32[]{:S(2)}, u32[]{:S(2)}) %collective-permute-start.17) | collective-permute-done | bytes 24608 | tf_op jit(solution)/shard_map/ppermute | solution.py:342
  64.9 2.9 %collective-permute-done.16 = f32[48,128]{1,0:T(8,128)S(1)} collective-permute-done((f32[48,128]{1,0:T(8,128)S(1)}, f32[48,128]{1,0:T(8,128)S(1)}, u32[]{:S(2)}, u32[]{:S(2)}) %collective-permute-start.16) | collective-permute-done | bytes 24608 | tf_op jit(solution)/shard_map/ppermute | solution.py:342
  67.8 0.0 collective-permute-done.15
  67.8 0.1 collective-permute-start.18
  67.9 1.2 %collective-permute-done.18.other = f32[48,128]{1,0:T(8,128)S(1)} collective-permute-done((f32[48,128]{1,0:T(8,128)S(1)}, f32[48,128]{1,0:T(8,128)S(1)}, u32[]{:S(2)}, u32[]{:S(2)}) %collective-permute-start.18) | collective-permute-done | bytes 24608 | tf_op jit(solution)/shard_map/ppermute | solution.py:336
  69.1 5.6 %shard_map.76 = f32[128,128]{1,0:T(8,128)} custom-call(s32[4]{0:T(128)S(1)} %pad_add_fusion.meta, f32[48,128]{1,0:T(8,128)S(1)} %add_add_fusion.own, f32[48,128]{1,0:T(8,128)S(1)} %collective-permute-done.18.other), custom_call_target="tpu_custom_call" | custom-call | bytes 1048576 | tf_op jit(solution)/shard_map/pallas_call | solution.py:590
  (15 shorter events, 0.0 us)
Async XLA Ops:
  0.6 0.8 %copy-start.2 = (f32[3,4,8,128]{3,2,1,0:T(8,128)S(1)}, f32[3,4,8,128]{3,2,1,0:T(8,128)}, u32[]{:S(2)}) copy-start(f32[3,4,8,128]{3,2,1,0:T(8,128)} %conductance.1) | copy-start | bytes 147460
  0.7 0.8 %copy-start.3 = (s32[8,128]{1,0:T(8,128)S(1)}, s32[8,128]{1,0:T(8,128)}, u32[]{:S(2)}) copy-start(s32[8,128]{1,0:T(8,128)} %wet.9) | copy-start | bytes 12292
  0.7 0.8 %copy-start.4 = (s32[1,4]{1,0:T(1,128)S(1)}, s32[1,4]{1,0:T(1,128)}, u32[]{:S(2)}) copy-start(s32[1,4]{1,0:T(1,128)} %runs.1) | copy-start | bytes 52
  1.4 1.2 %copy-start = (f32[64,4,8,128]{3,2,1,0:T(8,128)S(1)}, f32[64,4,8,128]{3,2,1,0:T(8,128)}, u32[]{:S(2)}) copy-start(f32[64,4,8,128]{3,2,1,0:T(8,128)} %omega.9) | copy-start | bytes 3145732
  2.7 17.3 %copy-start.1 = (f32[64,4,8,128]{3,2,1,0:T(8,128)S(1)}, f32[64,4,8,128]{3,2,1,0:T(8,128)}, u32[]{:S(2)}) copy-start(f32[64,4,8,128]{3,2,1,0:T(8,128)} %omega.9) | copy-start | bytes 3145732
  3.6 14.9 %collective-permute-start.5 = (f32[10,4,8,128]{3,2,1,0:T(8,128)S(1)}, f32[10,4,8,128]{3,2,1,0:T(8,128)S(1)}, u32[]{:S(2)}, u32[]{:S(2)}) collective-permute-start(f32[10,4,8,128]{3,2,1,0:T(8,128)S(1)} %get-tuple-element.37), channel_id=1, source_target_pairs={{0,16},{2,18},{4,20},{6,22},{8,24},{10,26},{12,28},{14,30},{16,0},... | collective-permute-start | bytes 491528 | tf_op jit(solution)/shard_map/ppermute | solution.py:336
  7.7 4.3 %collective-permute-start.1 = (f32[5,4,8,128]{3,2,1,0:T(8,128)S(1)}, f32[5,4,8,128]{3,2,1,0:T(8,128)S(1)}, u32[]{:S(2)}, u32[]{:S(2)}) collective-permute-start(f32[5,4,8,128]{3,2,1,0:T(8,128)S(1)} %get-tuple-element.33.edges), channel_id=1, source_target_pairs={{2,0},{4,2},{6,4},{8,6},{10,8},{12,10},{14,12},{18,16},{20,18},{22... | collective-permute-start | bytes 245768 | tf_op jit(solution)/shard_map/ppermute | solution.py:461
  9.0 3.9 %collective-permute-start = (f32[5,4,8,128]{3,2,1,0:T(8,128)S(1)}, f32[5,4,8,128]{3,2,1,0:T(8,128)S(1)}, u32[]{:S(2)}, u32[]{:S(2)}) collective-permute-start(f32[5,4,8,128]{3,2,1,0:T(8,128)S(1)} %get-tuple-element.33.edges), channel_id=1, source_target_pairs={{0,2},{2,4},{4,6},{6,8},{8,10},{10,12},{12,14},{16,18},{18,20},{20... | collective-permute-start | bytes 245768 | tf_op jit(solution)/shard_map/ppermute | solution.py:461
  13.5 5.0 %collective-permute-start.4 = (f32[5,2,8,128]{3,2,1,0:T(8,128)S(1)}, f32[5,2,8,128]{3,2,1,0:T(8,128)S(1)}, u32[]{:S(2)}, u32[]{:S(2)}) collective-permute-start(f32[5,2,8,128]{3,2,1,0:T(8,128)S(1)} %shard_map.69), channel_id=1, source_target_pairs={{0,16},{2,18},{4,20},{6,22},{8,24},{10,26},{12,28},{14,30},{16,0},... | collective-permute-start | bytes 122888 | tf_op jit(solution)/shard_map/ppermute | solution.py:336
  13.6 11.5 %collective-permute-start.2 = (f32[8,4,8,128]{3,2,1,0:T(8,128)S(1)}, f32[8,4,8,128]{3,2,1,0:T(8,128)S(1)}, u32[]{:S(2)}, u32[]{:S(2)}) collective-permute-start(f32[8,4,8,128]{3,2,1,0:T(8,128)S(1)} %get-tuple-element.34), channel_id=1, source_target_pairs={{0,16},{2,18},{4,20},{6,22},{8,24},{10,26},{12,28},{14,30},{16,0},... | collective-permute-start | bytes 393224 | tf_op jit(solution)/shard_map/ppermute | solution.py:336
  18.4 13.0 %collective-permute-start.7 = (f32[8,4,8,128]{3,2,1,0:T(8,128)S(1)}, f32[8,4,8,128]{3,2,1,0:T(8,128)S(1)}, u32[]{:S(2)}, u32[]{:S(2)}) collective-permute-start(f32[8,4,8,128]{3,2,1,0:T(8,128)S(1)} %get-tuple-element.45), channel_id=1, source_target_pairs={{0,16},{2,18},{4,20},{6,22},{8,24},{10,26},{12,28},{14,30},{16,0},... | collective-permute-start | bytes 393224 | tf_op jit(solution)/shard_map/ppermute | solution.py:336
  18.5 1.6 %copy-start.5 = (f32[8,128]{1,0:T(8,128)S(1)}, f32[8,128]{1,0:T(8,128)}, u32[]{:S(2)}) copy-start(f32[8,128]{1,0:T(8,128)} %volume.7) | copy-start | bytes 12292
  23.3 8.2 %collective-permute-start.8 = (f32[256,128]{1,0:T(8,128)S(1)}, f32[256,128]{1,0:T(8,128)S(1)}, u32[]{:S(2)}, u32[]{:S(2)}) collective-permute-start(f32[256,128]{1,0:T(8,128)S(1)} %get-tuple-element.46), channel_id=1, source_target_pairs={{0,1},{1,0},{2,3},{3,2},{4,5},{5,4},{6,7},{7,6},{8,9},{9,8},{10,11... | collective-permute-start | bytes 393224 | tf_op jit(solution)/shard_map/ppermute | solution.py:336
  25.1 11.1 %collective-permute-start.3 = (f32[8,4,8,128]{3,2,1,0:T(8,128)S(1)}, f32[8,4,8,128]{3,2,1,0:T(8,128)S(1)}, u32[]{:S(2)}, u32[]{:S(2)}) collective-permute-start(f32[8,4,8,128]{3,2,1,0:T(8,128)S(1)} %get-tuple-element.35), channel_id=1, source_target_pairs={{0,16},{2,18},{4,20},{6,22},{8,24},{10,26},{12,28},{14,30},{16,0},... | collective-permute-start | bytes 393224 | tf_op jit(solution)/shard_map/ppermute | solution.py:336
  30.9 5.8 %collective-permute-start.6 = (f32[256,128]{1,0:T(8,128)S(1)}, f32[256,128]{1,0:T(8,128)S(1)}, u32[]{:S(2)}, u32[]{:S(2)}) collective-permute-start(f32[256,128]{1,0:T(8,128)S(1)} %get-tuple-element.41), channel_id=1, source_target_pairs={{0,1},{1,0},{2,3},{3,2},{4,5},{5,4},{6,7},{7,6},{8,9},{9,8},{10,11... | collective-permute-start | bytes 393224 | tf_op jit(solution)/shard_map/ppermute | solution.py:336
  34.7 6.0 %collective-permute-start.9 = (f32[256,128]{1,0:T(8,128)S(1)}, f32[256,128]{1,0:T(8,128)S(1)}, u32[]{:S(2)}, u32[]{:S(2)}) collective-permute-start(f32[256,128]{1,0:T(8,128)S(1)} %get-tuple-element.56), channel_id=1, source_target_pairs={{0,1},{1,0},{2,3},{3,2},{4,5},{5,4},{6,7},{7,6},{8,9},{9,8},{10,11... | collective-permute-start | bytes 393224 | tf_op jit(solution)/shard_map/ppermute | solution.py:336
  39.9 6.3 %collective-permute-start.10 = (f32[256,128]{1,0:T(8,128)S(1)}, f32[256,128]{1,0:T(8,128)S(1)}, u32[]{:S(2)}, u32[]{:S(2)}) collective-permute-start(f32[256,128]{1,0:T(8,128)S(1)} %get-tuple-element.57), channel_id=1, source_target_pairs={{0,1},{1,0},{2,3},{3,2},{4,5},{5,4},{6,7},{7,6},{8,9},{9,8},{10,11... | collective-permute-start | bytes 393224 | tf_op jit(solution)/shard_map/ppermute | solution.py:336
  47.5 1.3 %collective-permute-start.11 = (f32[48,128]{1,0:T(8,128)S(1)}, f32[48,128]{1,0:T(8,128)S(1)}, u32[]{:S(2)}, u32[]{:S(2)}) collective-permute-start(f32[48,128]{1,0:T(8,128)S(1)} %get-tuple-element.59), channel_id=1, source_target_pairs={{0,2},{2,0},{4,6},{6,4},{8,10},{10,8},{12,14},{14,12},{16,18},{18,... | collective-permute-start | bytes 73736 | tf_op jit(solution)/shard_map/ppermute | solution.py:336
  48.7 5.8 %collective-permute-start.14 = (f32[48,128]{1,0:T(8,128)S(1)}, f32[48,128]{1,0:T(8,128)S(1)}, u32[]{:S(2)}, u32[]{:S(2)}) collective-permute-start(f32[48,128]{1,0:T(8,128)S(1)} %add.27), channel_id=1, source_target_pairs={{0,5},{1,4},{2,7},{3,6},{4,1},{5,0},{6,3},{7,2},{8,13},{9,12},{10,... | collective-permute-start | bytes 73736 | tf_op jit(solution)/shard_map/ppermute | solution.py:342
  52.7 3.8 %collective-permute-start.13 = (f32[48,128]{1,0:T(8,128)S(1)}, f32[48,128]{1,0:T(8,128)S(1)}, u32[]{:S(2)}, u32[]{:S(2)}) collective-permute-start(f32[48,128]{1,0:T(8,128)S(1)} %add.27), channel_id=1, source_target_pairs={{0,4},{1,5},{2,6},{3,7},{4,0},{5,1},{6,2},{7,3},{8,12},{9,13},{10,... | collective-permute-start | bytes 73736 | tf_op jit(solution)/shard_map/ppermute | solution.py:342
  52.7 3.8 %collective-permute-start.12 = (f32[48,128]{1,0:T(8,128)S(1)}, f32[48,128]{1,0:T(8,128)S(1)}, u32[]{:S(2)}, u32[]{:S(2)}) collective-permute-start(f32[48,128]{1,0:T(8,128)S(1)} %add.27), channel_id=1, source_target_pairs={{0,1},{1,0},{2,3},{3,2},{4,5},{5,4},{6,7},{7,6},{8,9},{9,8},{10,11... | collective-permute-start | bytes 73736 | tf_op jit(solution)/shard_map/ppermute | solution.py:342
  56.5 8.3 %collective-permute-start.17 = (f32[48,128]{1,0:T(8,128)S(1)}, f32[48,128]{1,0:T(8,128)S(1)}, u32[]{:S(2)}, u32[]{:S(2)}) collective-permute-start(f32[48,128]{1,0:T(8,128)S(1)} %add_add_fusion.1), channel_id=1, source_target_pairs={{0,24},{1,25},{2,26},{3,27},{4,28},{5,29},{6,30},{7,31},{8,16},{9,... | collective-permute-start | bytes 73736 | tf_op jit(solution)/shard_map/ppermute | solution.py:342
  63.1 4.7 %collective-permute-start.16 = (f32[48,128]{1,0:T(8,128)S(1)}, f32[48,128]{1,0:T(8,128)S(1)}, u32[]{:S(2)}, u32[]{:S(2)}) collective-permute-start(f32[48,128]{1,0:T(8,128)S(1)} %add_add_fusion.1), channel_id=1, source_target_pairs={{0,16},{1,17},{2,18},{3,19},{4,20},{5,21},{6,22},{7,23},{8,24},{9,... | collective-permute-start | bytes 73736 | tf_op jit(solution)/shard_map/ppermute | solution.py:342
  63.1 4.7 %collective-permute-start.15 = (f32[48,128]{1,0:T(8,128)S(1)}, f32[48,128]{1,0:T(8,128)S(1)}, u32[]{:S(2)}, u32[]{:S(2)}) collective-permute-start(f32[48,128]{1,0:T(8,128)S(1)} %add_add_fusion.1), channel_id=1, source_target_pairs={{0,8},{1,9},{2,10},{3,11},{4,12},{5,13},{6,14},{7,15},{8,0},{9,1},... | collective-permute-start | bytes 73736 | tf_op jit(solution)/shard_map/ppermute | solution.py:342
  67.8 1.3 %collective-permute-start.18 = (f32[48,128]{1,0:T(8,128)S(1)}, f32[48,128]{1,0:T(8,128)S(1)}, u32[]{:S(2)}, u32[]{:S(2)}) collective-permute-start(f32[48,128]{1,0:T(8,128)S(1)} %add_add_fusion.own), channel_id=1, source_target_pairs={{0,2},{2,0},{4,6},{6,4},{8,10},{10,8},{12,14},{14,12},{16,18},{18,... | collective-permute-start | bytes 73736 | tf_op jit(solution)/shard_map/ppermute | solution.py:336

commit v5 on v4

--- a/solution.py
+++ b/solution.py
@@ -10,6 +10,7 @@
 ITERS = 4
 EDGE = 2 * ITERS
 VMEM_LIMIT = 32 * 1024 * 1024
+EDGE_LIMIT = 63 * 1024 * 1024 + 256 * 1024
 MAIN, SLOT = (0, 1)
 
 
@@ -93,47 +94,52 @@
     return turn(cross, -(EDGE * place + ITERS), 1)
 
 
-def pack_kernel(chunks, meta, runs, omega, conductance, wet, static_out, edge_out, *row_outs):
-    directions = len(row_outs) // chunks
+def edge_kernel(runs, omega, conductance, wet, static_out, edge_out):
     levels, rows, cols = omega.shape[1:]
     shape = (rows, cols)
-    is_first_row = meta[0] == 0
     row_ids, col_ids = (ids(shape, 0), ids(shape, 1))
     wet_cells = wet[...].astype(jnp.float32)
     open_x = (col_ids >= runs[0, 0]) & (col_ids < runs[0, 0] + runs[0, 1])
     open_y = (row_ids >= runs[0, 2]) & (row_ids < runs[0, 2] + runs[0, 3])
     keep_x = (row_ids > 0) | open_x
     keep_y = (col_ids > 0) | open_y
-    statics = []
+    group = cols // EDGE
+    chunks = omega.shape[0] // group
     for level in range(levels):
-        statics.append(
-            [
-                jnp.where(keep_x, conductance[0, level], 0.0),
-                jnp.where(keep_y, conductance[1, level], 0.0),
-                conductance[2, level] if level else jnp.zeros(shape, jnp.float32),
-                wet_cells,
-            ]
-        )
-    kinds = len(statics[0])
+        statics = [
+            jnp.where(keep_x, conductance[0, level], 0.0),
+            jnp.where(keep_y, conductance[1, level], 0.0),
+            conductance[2, level] if level else jnp.zeros(shape, jnp.float32),
+            wet_cells,
+        ]
+        edge = None
+        for kind, value in enumerate(statics):
+            static_out[kind, level] = value
+            edge = add_edge(edge, value, kind)
+        edge_out[chunks, level] = edge
+        for chunk in range(chunks):
+            edge = None
+            for place in range(group):
+                edge = add_edge(edge, omega[chunk * group + place, level] * wet_cells, place)
+            edge_out[chunk, level] = edge
+
+
+def row_kernel(meta, statics, omega, wet, *row_outs):
+    kinds, levels, rows, cols = statics.shape
     group = cols // EDGE
+    chunks = omega.shape[0] // group
+    directions = len(row_outs) // chunks
+    is_first_row = meta[0] == 0
+    wet_cells = wet[...].astype(jnp.float32)
     for level in range(levels):
-        edge = None
-        for kind in range(kinds):
-            static_out[kind, level] = statics[level][kind]
-            edge = add_edge(edge, statics[level][kind], kind)
-        edge_out[chunks, level] = edge
         for kind in range(0, kinds, 2):
-            outs = row_outs[:directions]
-            store_pair(outs, (group // 2 + kind // 2, level), statics[level][kind], statics[level][kind + 1], is_first_row)
+            at = (group // 2 + kind // 2, level)
+            store_pair(row_outs[:directions], at, statics[kind, level], statics[kind + 1, level], is_first_row)
         for chunk in range(chunks):
             outs = row_outs[directions * chunk : directions * (chunk + 1)]
-            edge = None
             for pair in range(group // 2):
                 start = [omega[chunk * group + 2 * pair + i, level] * wet_cells for i in range(2)]
-                edge = add_edge(edge, start[0], 2 * pair)
-                edge = add_edge(edge, start[1], 2 * pair + 1)
                 store_pair(outs, (pair, level), start[0], start[1], is_first_row)
-            edge_out[chunk, level] = edge
 
 
 def corner_kernel(meta, left, right, *outs):
@@ -336,30 +342,11 @@
     return lax.ppermute(value, axis, [(source, source ^ bit) for source in range(count)])
 
 
-def mesh_permute(value, mask):
-    axes = ("tiles", "vec")
-    count = lax.axis_size("tiles") * lax.axis_size("vec")
-    return lax.ppermute(value, axes, [(source, source ^ mask) for source in range(count)])
-
-
 def total_over_chips(value):
-    vec = lax.axis_size("vec")
-    masks = []
-    bit = 1
-    while bit < vec:
-        masks.append(bit)
-        bit *= 2
-    bit = 2
-    while bit < lax.axis_size("tiles"):
-        masks.append(bit * vec)
-        bit *= 2
-    while masks:
-        near, masks = (masks[:2], masks[2:])
-        if len(near) == 1:
-            value = value + mesh_permute(value, near[0])
-        else:
-            one, two, both = (mesh_permute(value, mask) for mask in (near[0], near[1], near[0] ^ near[1]))
-            value = (value + one) + (two + both)
+    for axis, bit in (("tiles", 2), ("vec", 1)):
+        while bit < lax.axis_size(axis):
+            value = value + swapped(value, axis, bit)
+            bit *= 2
     return value
 
 
@@ -480,7 +467,7 @@
     return pl.BlockSpec(shape, lambda i: at)
 
 
-def call(kernel, in_specs, out_specs, out_shape, flops=0, scratch=(), aliases=None):
+def call(kernel, in_specs, out_specs, out_shape, flops=0, scratch=(), aliases=None, limit=VMEM_LIMIT):
     return pl.pallas_call(
         kernel,
         grid=(1,),
@@ -489,7 +476,7 @@
         out_shape=out_shape,
         scratch_shapes=scratch,
         input_output_aliases=aliases or {},
-        compiler_params=pltpu.CompilerParams(vmem_limit_bytes=VMEM_LIMIT),
+        compiler_params=pltpu.CompilerParams(vmem_limit_bytes=limit),
         cost_estimate=pl.CostEstimate(flops=flops, bytes_accessed=1 << 20, transcendentals=0),
     )
 
@@ -515,25 +502,32 @@
 
     row_shapes = [f32(group // 2 + (kinds // 2 if c == 0 else 0), levels, rows, cols) for c in range(chunks)]
     row_shapes = [shape for shape in row_shapes for _ in range(directions)]
-    packed_shapes = [f32(kinds, levels, rows, cols), f32(chunks + 1, levels, rows, cols)] + row_shapes
-    statics, edges, *messages = call(
-        functools.partial(pack_kernel, chunks),
-        [smem, smem, whole(omega), whole(conductance), whole(wet)],
-        [whole(s) for s in packed_shapes],
-        packed_shapes,
-    )(meta, face_runs, omega, conductance, wet)
-    messages = [messages[directions * c : directions * (c + 1)] for c in range(chunks)]
-    received = [exchange_rows(messages[0], grid_rows)]
+    edge_shapes = [f32(kinds, levels, rows, cols), f32(chunks + 1, levels, rows, cols)]
+    statics, edges = call(
+        edge_kernel,
+        [smem, whole(omega), whole(conductance), whole(wet)],
+        [whole(s) for s in edge_shapes],
+        edge_shapes,
+        limit=EDGE_LIMIT,
+    )(face_runs, omega, conductance, wet)
     left = beside(edges, 1)
     right = beside(edges, -1)
+    messages = call(
+        row_kernel,
+        [smem, whole(statics), whole(omega), whole(wet)],
+        [whole(s) for s in row_shapes],
+        row_shapes,
+        flops=10**9,
+    )(meta, statics, omega, wet)
+    messages = [messages[directions * c : directions * (c + 1)] for c in range(chunks)]
+    received = [exchange_rows(after(messages[0], left, right), grid_rows)]
     corner_shapes = [f32(chunks + 1, levels // 2, rows, cols)] * directions
     corners = call(
         corner_kernel, [smem, whole(left), whole(right)], [whole(s) for s in corner_shapes], corner_shapes
     )(meta, left, right)
     corners = exchange_rows(corners, grid_rows)
-    gates = [(left, right), corners]
     for c in range(1, chunks):
-        gate = gates[c - 1] if c <= 2 else received[c - 2]
+        gate = corners if c == 1 else received[c - 2]
         received.append(exchange_rows(after(messages[c], *gate), grid_rows))
 
     def group_specs(c):

time: 74.9 us -> 81.6 us (1.089)
  waiting for transfers between devices: 18.8 us -> 32.4 us
  starting transfers between devices: 30.3 us -> 21.4 us
  Pallas kernels: 22.8 us -> 24.8 us
    ppermute x11 -> x15, waiting for transfers between devices: 10.6 us -> 32.4 us  [swapped(): lax.ppermute(value, axis, [(source, source ^ bit) for source in range(cou...]
    ppermute x6 -> x0, starting transfers between devices: 11.8 us -> none  [mesh_permute(): lax.ppermute(value, axes, [(source, source ^ mask) for source in range(co...]
    ppermute x6 -> x0, waiting for transfers between devices: 7.28 us -> none  [mesh_permute(): lax.ppermute(value, axes, [(source, source ^ mask) for source in range(co...]
    ppermute x11 -> x15, starting transfers between devices: 14.2 us -> 17 us  [swapped(): lax.ppermute(value, axis, [(source, source ^ bit) for source in range(cou...]
    pallas_call x1 -> x2, Pallas kernels: 0.9 us -> 2.93 us  [the longest x1 2.26 us: shards(): call(edge_kernel, [smem, whole(omega), whole(conductance), whole(wet)], [...]
    ppermute x2, waiting for transfers between devices: 0.89 us -> 0.01 us  [beside(): lax.ppermute(value, 'tiles', [(a, b) for a, b in pairs if 0 <= b < count...]
  transfers between devices with their start and end apart: 19 -> 17, of which waited for: 11 -> 10; matrix products, arithmetic and copies ran while one was open for 0% -> 0% of each run, Pallas kernels for 20% -> 19%
where the time goes in v5:
time: 81.6 us; the launch traced here: 81.4 us
  waiting for transfers between devices  32.4 us (40%)
  Pallas kernels  24.8 us (30%)
  starting transfers between devices  21.4 us (26%)
  local copies, waits for them, and re-layouts  1.84 us (2%)
    ppermute x15, waiting for transfers between devices, swapped(): lax.ppermute(value, axis, [(source, source ^ bit) for source in range(cou...  32.4 us
    ppermute x15, starting transfers between devices, swapped(): lax.ppermute(value, axis, [(source, source ^ bit) for source in range(cou...  17 us
    pallas_call x4, Pallas kernels, shards(): call(functools.partial(diffuse_kernel, 4), specs, [chunk_block, whole(hal...  12.9 us
    pallas_call x1, Pallas kernels, shards(): call(functools.partial(factor_kernel, 1.0 / total_cells), [smem, whole(ha...  5.59 us
    ppermute x2, starting transfers between devices, beside(): lax.ppermute(value, 'tiles', [(a, b) for a, b in pairs if 0 <= b < count...  4.45 us
    pallas_call x1, Pallas kernels, shards(): call(edge_kernel, [smem, whole(omega), whole(conductance), whole(wet)], [...  2.26 us
    unnamed x12, local copies, waits for them, and re-layouts  1.84 us
  transfers between devices with their start and end apart: 17, of which 10 were waited for; matrix products, arithmetic and copies ran while one was open for 0% of the time, Pallas kernels for 19%

profile of v5, /device:TPU:0, one launch (start us, length us, event | category | flops | bytes accessed | tf_op | source)
XLA Modules:
  0.0 81.4 jit_solution(770239039945622624)
XLA Ops:
  0.6 2.3 %shard_map.68 = (f32[4,4,8,128]{3,2,1,0:T(8,128)}, f32[5,4,8,128]{3,2,1,0:T(8,128)}) custom-call(s32[1,4]{1,0:T(1,128)} %runs.1, f32[64,4,8,128]{3,2,1,0:T(8,128)} %omega.11, f32[3,4,8,128]{3,2,1,0:T(8,128)} %conductance.1, s32[8,128]{1,0:T(8,128)} %wet.11), custom_call_target="tpu_custom_call" | custom-call | bytes 1048576 | tf_op jit(solution)/shard_map/pallas_call | solution.py:506
  2.9 1.4 %collective-permute-start.1 = (f32[5,4,8,128]{3,2,1,0:T(8,128)}, f32[5,4,8,128]{3,2,1,0:T(8,128)S(1)}, u32[]{:S(2)}, u32[]{:S(2)}) collective-permute-start(f32[5,4,8,128]{3,2,1,0:T(8,128)} %get-tuple-element.35.edges), channel_id=1, source_target_pairs={{2,0},{4,2},{6,4},{8,6},{10,8},{12,10},{14,12},{18,16},{20,18},{22... | collective-permute-start | bytes 245768 | tf_op jit(solution)/shard_map/ppermute | solution.py:448
  4.3 3.0 %collective-permute-start = (f32[5,4,8,128]{3,2,1,0:T(8,128)}, f32[5,4,8,128]{3,2,1,0:T(8,128)S(1)}, u32[]{:S(2)}, u32[]{:S(2)}) collective-permute-start(f32[5,4,8,128]{3,2,1,0:T(8,128)} %get-tuple-element.35.edges), channel_id=1, source_target_pairs={{0,2},{2,4},{4,6},{6,8},{8,10},{10,12},{12,14},{16,18},{18,20},{20... | collective-permute-start | bytes 245768 | tf_op jit(solution)/shard_map/ppermute | solution.py:448
  7.4 0.0 copy-start.4
  7.4 0.1 pad_add_fusion.meta
  7.5 0.6 copy-done.4
  8.1 1.2 %copy-done = f32[64,4,8,128]{3,2,1,0:T(8,128)S(1)} copy-done((f32[64,4,8,128]{3,2,1,0:T(8,128)S(1)}, f32[64,4,8,128]{3,2,1,0:T(8,128)}, u32[]{:S(2)}) %copy-start) | copy-done | bytes 1048600
  9.3 0.7 shard_map.69
  10.0 0.0 collective-permute-done.1.right
  10.0 0.0 collective-permute-done.left
  10.0 0.0 copy-start.2
  10.0 4.1 %collective-permute-start.5 = (f32[10,4,8,128]{3,2,1,0:T(8,128)S(1)}, f32[10,4,8,128]{3,2,1,0:T(8,128)S(1)}, u32[]{:S(2)}, u32[]{:S(2)}) collective-permute-start(f32[10,4,8,128]{3,2,1,0:T(8,128)S(1)} %get-tuple-element.39), channel_id=1, source_target_pairs={{0,16},{2,18},{4,20},{6,22},{8,24},{10,26},{12,28},{14,30},{16,0},... | collective-permute-start | bytes 491528 | tf_op jit(solution)/shard_map/ppermute | solution.py:342
  14.1 0.6 shard_map.70
  14.7 0.1 collective-permute-start.2
  14.7 9.3 %collective-permute-done.2.corner_below.corner_above = f32[5,2,8,128]{3,2,1,0:T(8,128)S(1)} collective-permute-done((f32[5,2,8,128]{3,2,1,0:T(8,128)S(1)}, f32[5,2,8,128]{3,2,1,0:T(8,128)S(1)}, u32[]{:S(2)}, u32[]{:S(2)}) %collective-permute-start.2) | collective-permute-done | bytes 40992 | tf_op jit(solution)/shard_map/ppermute | solution.py:342
  24.0 0.0 collective-permute-start.3
  24.0 0.0 collective-permute-done.5.below.above
  24.0 2.9 %collective-permute-start.7 = (f32[8,4,8,128]{3,2,1,0:T(8,128)S(1)}, f32[8,4,8,128]{3,2,1,0:T(8,128)S(1)}, u32[]{:S(2)}, u32[]{:S(2)}) collective-permute-start(f32[8,4,8,128]{3,2,1,0:T(8,128)S(1)} %get-tuple-element.47), channel_id=1, source_target_pairs={{0,16},{2,18},{4,20},{6,22},{8,24},{10,26},{12,28},{14,30},{16,0},... | collective-permute-start | bytes 393224 | tf_op jit(solution)/shard_map/ppermute | solution.py:342
  27.0 1.5 %shard_map.71 = (f32[7,4,2,8,128]{4,3,2,1,0:T(8,128)S(1)}, f32[2,7,4,2,8,128]{5,4,3,2,1,0:T(8,128)S(1)}) custom-call(s32[4]{0:T(128)S(1)} %pad_add_fusion.meta, f32[4,4,8,128]{3,2,1,0:T(8,128)S(1)} %copy-done.3, f32[10,4,8,128]{3,2,1,0:T(8,128)S(1)} %collective-permute-done.5.below.above, f32[10,4,8,128]{3,2,1,0:T(8,128)S(1)} %collective-permute-done.5.below.above, ...), custom_call_target="tpu_custom_call" | custom-call | bytes 1048576 | tf_op jit(solution)/shard_map/pallas_call | solution.py:540
  28.5 3.2 %shard_map.72 = (f32[64,4,8,128]{3,2,1,0:T(8,128)}, f32[256,128]{1,0:T(8,128)S(1)}, f32[256,128]{1,0:T(8,128)S(1)}) custom-call(s32[4]{0:T(128)S(1)} %pad_add_fusion.meta, f32[64,4,8,128]{3,2,1,0:T(8,128)S(1)} %copy-done.1, s32[8,128]{1,0:T(8,128)S(1)} %copy-done.4, f32[8,128]{1,0:T(8,128)S(1)} %copy-done.5, ...), custom_call_target="tpu_custom_call" | custom-call | flops 4000000000 | bytes 1048576 | tf_op jit(solution)/shard_map/pallas_call | solution.py:562
  31.8 2.1 %collective-permute-start.8 = (f32[256,128]{1,0:T(8,128)S(1)}, f32[256,128]{1,0:T(8,128)S(1)}, u32[]{:S(2)}, u32[]{:S(2)}) collective-permute-start(f32[256,128]{1,0:T(8,128)S(1)} %get-tuple-element.48), channel_id=1, source_target_pairs={{0,1},{1,0},{2,3},{3,2},{4,5},{5,4},{6,7},{7,6},{8,9},{9,8},{10,11... | collective-permute-start | bytes 393224 | tf_op jit(solution)/shard_map/ppermute | solution.py:342
  33.9 3.0 %collective-permute-done.3.below.above = f32[8,4,8,128]{3,2,1,0:T(8,128)S(1)} collective-permute-done((f32[8,4,8,128]{3,2,1,0:T(8,128)S(1)}, f32[8,4,8,128]{3,2,1,0:T(8,128)S(1)}, u32[]{:S(2)}, u32[]{:S(2)}) %collective-permute-start.3) | collective-permute-done | bytes 131104 | tf_op jit(solution)/shard_map/ppermute | solution.py:342
  36.9 0.0 collective-permute-start.4
  36.9 3.2 %shard_map.73 = (f32[64,4,8,128]{3,2,1,0:T(8,128)}, f32[256,128]{1,0:T(8,128)S(1)}, f32[256,128]{1,0:T(8,128)S(1)}) custom-call(s32[4]{0:T(128)S(1)} %pad_add_fusion.meta, f32[64,4,8,128]{3,2,1,0:T(8,128)S(1)} %copy-done.1, s32[8,128]{1,0:T(8,128)S(1)} %copy-done.4, f32[8,128]{1,0:T(8,128)S(1)} %copy-done.5, ...), custom_call_target="tpu_custom_call", output_to_operand_aliasing={{0}: (13, {})} | custom-call | flops 4000000000 | bytes 1048576 | tf_op jit(solution)/shard_map/pallas_call | solution.py:562
  40.1 2.1 %collective-permute-start.6 = (f32[256,128]{1,0:T(8,128)S(1)}, f32[256,128]{1,0:T(8,128)S(1)}, u32[]{:S(2)}, u32[]{:S(2)}) collective-permute-start(f32[256,128]{1,0:T(8,128)S(1)} %get-tuple-element.43), channel_id=1, source_target_pairs={{0,1},{1,0},{2,3},{3,2},{4,5},{5,4},{6,7},{7,6},{8,9},{9,8},{10,11... | collective-permute-start | bytes 393224 | tf_op jit(solution)/shard_map/ppermute | solution.py:342
  42.2 0.1 collective-permute-done.7.below.above
  42.4 0.0 collective-permute-done.8.refs_4_
  42.4 3.2 %shard_map.74 = (f32[64,4,8,128]{3,2,1,0:T(8,128)}, f32[256,128]{1,0:T(8,128)S(1)}, f32[256,128]{1,0:T(8,128)S(1)}) custom-call(s32[4]{0:T(128)S(1)} %pad_add_fusion.meta, f32[64,4,8,128]{3,2,1,0:T(8,128)S(1)} %copy-done.1, s32[8,128]{1,0:T(8,128)S(1)} %copy-done.4, f32[8,128]{1,0:T(8,128)S(1)} %copy-done.5, ...), custom_call_target="tpu_custom_call", output_to_operand_aliasing={{0}: (13, {})} | custom-call | flops 4000000000 | bytes 1048576 | tf_op jit(solution)/shard_map/pallas_call | solution.py:562
  45.6 2.0 %collective-permute-start.9 = (f32[256,128]{1,0:T(8,128)S(1)}, f32[256,128]{1,0:T(8,128)S(1)}, u32[]{:S(2)}, u32[]{:S(2)}) collective-permute-start(f32[256,128]{1,0:T(8,128)S(1)} %get-tuple-element.58), channel_id=1, source_target_pairs={{0,1},{1,0},{2,3},{3,2},{4,5},{5,4},{6,7},{7,6},{8,9},{9,8},{10,11... | collective-permute-start | bytes 393224 | tf_op jit(solution)/shard_map/ppermute | solution.py:342
  47.6 0.0 collective-permute-done.4.below.above
  47.6 0.0 collective-permute-done.6.refs_5_
  47.6 3.2 %shard_map.75 = (f32[64,4,8,128]{3,2,1,0:T(8,128)}, f32[256,128]{1,0:T(8,128)S(1)}, f32[256,128]{1,0:T(8,128)S(1)}) custom-call(s32[4]{0:T(128)S(1)} %pad_add_fusion.meta, f32[64,4,8,128]{3,2,1,0:T(8,128)S(1)} %copy-done.1, s32[8,128]{1,0:T(8,128)S(1)} %copy-done.4, f32[8,128]{1,0:T(8,128)S(1)} %copy-done.5, ...), custom_call_target="tpu_custom_call", output_to_operand_aliasing={{0}: (13, {})} | custom-call | flops 4000000000 | bytes 1048576 | tf_op jit(solution)/shard_map/pallas_call | solution.py:562
  50.9 0.3 collective-permute-start.10
  51.1 0.0 collective-permute-done.9.refs_6_
  51.1 4.7 %collective-permute-done.10.refs_7_ = f32[256,128]{1,0:T(8,128)S(1)} collective-permute-done((f32[256,128]{1,0:T(8,128)S(1)}, f32[256,128]{1,0:T(8,128)S(1)}, u32[]{:S(2)}, u32[]{:S(2)}) %collective-permute-start.10) | collective-permute-done | bytes 131104 | tf_op jit(solution)/shard_map/ppermute | solution.py:342
  55.8 1.3 %shard_map.76 = (f32[48,128]{1,0:T(8,128)S(1)}, f32[48,128]{1,0:T(8,128)S(1)}) custom-call(s32[4]{0:T(128)S(1)} %pad_add_fusion.meta, f32[256,128]{1,0:T(8,128)S(1)} %get-tuple-element.54.refs_0_, f32[256,128]{1,0:T(8,128)S(1)} %get-tuple-element.55.refs_1_, f32[256,128]{1,0:T(8,128)S(1)} %get-tuple-element.56.refs_2_, ...), custom_call_target="tpu_custom_call" | custom-call | bytes 1048576 | tf_op jit(solution)/shard_map/pallas_call | solution.py:576
  57.1 0.1 collective-permute-start.11
  57.2 1.2 %collective-permute-done.11 = f32[48,128]{1,0:T(8,128)S(1)} collective-permute-done((f32[48,128]{1,0:T(8,128)S(1)}, f32[48,128]{1,0:T(8,128)S(1)}, u32[]{:S(2)}, u32[]{:S(2)}) %collective-permute-start.11) | collective-permute-done | bytes 24608 | tf_op jit(solution)/shard_map/ppermute | solution.py:342
  58.4 0.1 collective-permute-start.12
  58.4 3.7 %collective-permute-done.12 = f32[48,128]{1,0:T(8,128)S(1)} collective-permute-done((f32[48,128]{1,0:T(8,128)S(1)}, f32[48,128]{1,0:T(8,128)S(1)}, u32[]{:S(2)}, u32[]{:S(2)}) %collective-permute-start.12) | collective-permute-done | bytes 24608 | tf_op jit(solution)/shard_map/ppermute | solution.py:342
  62.2 1.1 %collective-permute-start.13 = (f32[48,128]{1,0:T(8,128)S(1)}, f32[48,128]{1,0:T(8,128)S(1)}, u32[]{:S(2)}, u32[]{:S(2)}) collective-permute-start(f32[48,128]{1,0:T(8,128)S(1)} %add.22), channel_id=1, source_target_pairs={{0,8},{2,10},{4,12},{6,14},{8,0},{10,2},{12,4},{14,6},{16,24},{18,... | collective-permute-start | bytes 73736 | tf_op jit(solution)/shard_map/ppermute | solution.py:342
  63.3 2.7 %collective-permute-done.13 = f32[48,128]{1,0:T(8,128)S(1)} collective-permute-done((f32[48,128]{1,0:T(8,128)S(1)}, f32[48,128]{1,0:T(8,128)S(1)}, u32[]{:S(2)}, u32[]{:S(2)}) %collective-permute-start.13) | collective-permute-done | bytes 24608 | tf_op jit(solution)/shard_map/ppermute | solution.py:342
  66.0 1.5 %collective-permute-start.14 = (f32[48,128]{1,0:T(8,128)S(1)}, f32[48,128]{1,0:T(8,128)S(1)}, u32[]{:S(2)}, u32[]{:S(2)}) collective-permute-start(f32[48,128]{1,0:T(8,128)S(1)} %add.23), channel_id=1, source_target_pairs={{0,16},{2,18},{4,20},{6,22},{8,24},{10,26},{12,28},{14,30},{16,0},... | collective-permute-start | bytes 73736 | tf_op jit(solution)/shard_map/ppermute | solution.py:342
  67.5 3.2 %collective-permute-done.14 = f32[48,128]{1,0:T(8,128)S(1)} collective-permute-done((f32[48,128]{1,0:T(8,128)S(1)}, f32[48,128]{1,0:T(8,128)S(1)}, u32[]{:S(2)}, u32[]{:S(2)}) %collective-permute-start.14) | collective-permute-done | bytes 24608 | tf_op jit(solution)/shard_map/ppermute | solution.py:342
  70.7 0.6 collective-permute-start.15
  71.3 3.2 %collective-permute-done.15 = f32[48,128]{1,0:T(8,128)S(1)} collective-permute-done((f32[48,128]{1,0:T(8,128)S(1)}, f32[48,128]{1,0:T(8,128)S(1)}, u32[]{:S(2)}, u32[]{:S(2)}) %collective-permute-start.15) | collective-permute-done | bytes 24608 | tf_op jit(solution)/shard_map/ppermute | solution.py:342
  74.6 1.2 %collective-permute-done.16.other = f32[48,128]{1,0:T(8,128)S(1)} collective-permute-done((f32[48,128]{1,0:T(8,128)S(1)}, f32[48,128]{1,0:T(8,128)S(1)}, u32[]{:S(2)}, u32[]{:S(2)}) %collective-permute-start.16) | collective-permute-done | bytes 24608 | tf_op jit(solution)/shard_map/ppermute | solution.py:342
  75.8 5.6 %shard_map.77 = f32[128,128]{1,0:T(8,128)} custom-call(s32[4]{0:T(128)S(1)} %pad_add_fusion.meta, f32[48,128]{1,0:T(8,128)S(1)} %add.25.own, f32[48,128]{1,0:T(8,128)S(1)} %collective-permute-done.16.other), custom_call_target="tpu_custom_call" | custom-call | bytes 1048576 | tf_op jit(solution)/shard_map/pallas_call | solution.py:584
  (14 shorter events, 0.0 us)
Async XLA Ops:
  2.9 4.6 %copy-start.3 = (f32[4,4,8,128]{3,2,1,0:T(8,128)S(1)}, f32[4,4,8,128]{3,2,1,0:T(8,128)}, u32[]{:S(2)}) copy-start(f32[4,4,8,128]{3,2,1,0:T(8,128)} %get-tuple-element.32.statics) | copy-start | bytes 196612
  2.9 7.1 %collective-permute-start.1 = (f32[5,4,8,128]{3,2,1,0:T(8,128)}, f32[5,4,8,128]{3,2,1,0:T(8,128)S(1)}, u32[]{:S(2)}, u32[]{:S(2)}) collective-permute-start(f32[5,4,8,128]{3,2,1,0:T(8,128)} %get-tuple-element.35.edges), channel_id=1, source_target_pairs={{2,0},{4,2},{6,4},{8,6},{10,8},{12,10},{14,12},{18,16},{20,18},{22... | collective-permute-start | bytes 245768 | tf_op jit(solution)/shard_map/ppermute | solution.py:448
  4.3 5.7 %collective-permute-start = (f32[5,4,8,128]{3,2,1,0:T(8,128)}, f32[5,4,8,128]{3,2,1,0:T(8,128)S(1)}, u32[]{:S(2)}, u32[]{:S(2)}) collective-permute-start(f32[5,4,8,128]{3,2,1,0:T(8,128)} %get-tuple-element.35.edges), channel_id=1, source_target_pairs={{0,2},{2,4},{4,6},{6,8},{8,10},{10,12},{12,14},{16,18},{18,20},{20... | collective-permute-start | bytes 245768 | tf_op jit(solution)/shard_map/ppermute | solution.py:448
  7.4 0.7 copy-start.4
  8.1 1.2 %copy-start = (f32[64,4,8,128]{3,2,1,0:T(8,128)S(1)}, f32[64,4,8,128]{3,2,1,0:T(8,128)}, u32[]{:S(2)}) copy-start(f32[64,4,8,128]{3,2,1,0:T(8,128)} %omega.11) | copy-start | bytes 3145732
  9.3 19.2 %copy-start.1 = (f32[64,4,8,128]{3,2,1,0:T(8,128)S(1)}, f32[64,4,8,128]{3,2,1,0:T(8,128)}, u32[]{:S(2)}) copy-start(f32[64,4,8,128]{3,2,1,0:T(8,128)} %omega.11) | copy-start | bytes 3145732
  10.0 17.0 %copy-start.2 = (f32[5,4,8,128]{3,2,1,0:T(8,128)S(1)}, f32[5,4,8,128]{3,2,1,0:T(8,128)}, u32[]{:S(2)}) copy-start(f32[5,4,8,128]{3,2,1,0:T(8,128)} %get-tuple-element.35.edges) | copy-start | bytes 245764
  10.0 14.0 %collective-permute-start.5 = (f32[10,4,8,128]{3,2,1,0:T(8,128)S(1)}, f32[10,4,8,128]{3,2,1,0:T(8,128)S(1)}, u32[]{:S(2)}, u32[]{:S(2)}) collective-permute-start(f32[10,4,8,128]{3,2,1,0:T(8,128)S(1)} %get-tuple-element.39), channel_id=1, source_target_pairs={{0,16},{2,18},{4,20},{6,22},{8,24},{10,26},{12,28},{14,30},{16,0},... | collective-permute-start | bytes 491528 | tf_op jit(solution)/shard_map/ppermute | solution.py:342
  14.7 9.4 %collective-permute-start.2 = (f32[5,2,8,128]{3,2,1,0:T(8,128)S(1)}, f32[5,2,8,128]{3,2,1,0:T(8,128)S(1)}, u32[]{:S(2)}, u32[]{:S(2)}) collective-permute-start(f32[5,2,8,128]{3,2,1,0:T(8,128)S(1)} %shard_map.70), channel_id=1, source_target_pairs={{0,16},{2,18},{4,20},{6,22},{8,24},{10,26},{12,28},{14,30},{16,0},... | collective-permute-start | bytes 122888 | tf_op jit(solution)/shard_map/ppermute | solution.py:342
  24.0 12.8 %collective-permute-start.3 = (f32[8,4,8,128]{3,2,1,0:T(8,128)S(1)}, f32[8,4,8,128]{3,2,1,0:T(8,128)S(1)}, u32[]{:S(2)}, u32[]{:S(2)}) collective-permute-start(f32[8,4,8,128]{3,2,1,0:T(8,128)S(1)} %get-tuple-element.36), channel_id=1, source_target_pairs={{0,16},{2,18},{4,20},{6,22},{8,24},{10,26},{12,28},{14,30},{16,0},... | collective-permute-start | bytes 393224 | tf_op jit(solution)/shard_map/ppermute | solution.py:342
  24.0 4.5 %copy-start.5 = (f32[8,128]{1,0:T(8,128)S(1)}, f32[8,128]{1,0:T(8,128)}, u32[]{:S(2)}) copy-start(f32[8,128]{1,0:T(8,128)} %volume.7) | copy-start | bytes 12292
  24.0 18.3 %collective-permute-start.7 = (f32[8,4,8,128]{3,2,1,0:T(8,128)S(1)}, f32[8,4,8,128]{3,2,1,0:T(8,128)S(1)}, u32[]{:S(2)}, u32[]{:S(2)}) collective-permute-start(f32[8,4,8,128]{3,2,1,0:T(8,128)S(1)} %get-tuple-element.47), channel_id=1, source_target_pairs={{0,16},{2,18},{4,20},{6,22},{8,24},{10,26},{12,28},{14,30},{16,0},... | collective-permute-start | bytes 393224 | tf_op jit(solution)/shard_map/ppermute | solution.py:342
  31.8 10.6 %collective-permute-start.8 = (f32[256,128]{1,0:T(8,128)S(1)}, f32[256,128]{1,0:T(8,128)S(1)}, u32[]{:S(2)}, u32[]{:S(2)}) collective-permute-start(f32[256,128]{1,0:T(8,128)S(1)} %get-tuple-element.48), channel_id=1, source_target_pairs={{0,1},{1,0},{2,3},{3,2},{4,5},{5,4},{6,7},{7,6},{8,9},{9,8},{10,11... | collective-permute-start | bytes 393224 | tf_op jit(solution)/shard_map/ppermute | solution.py:342
  36.9 10.7 %collective-permute-start.4 = (f32[8,4,8,128]{3,2,1,0:T(8,128)S(1)}, f32[8,4,8,128]{3,2,1,0:T(8,128)S(1)}, u32[]{:S(2)}, u32[]{:S(2)}) collective-permute-start(f32[8,4,8,128]{3,2,1,0:T(8,128)S(1)} %get-tuple-element.37), channel_id=1, source_target_pairs={{0,16},{2,18},{4,20},{6,22},{8,24},{10,26},{12,28},{14,30},{16,0},... | collective-permute-start | bytes 393224 | tf_op jit(solution)/shard_map/ppermute | solution.py:342
  40.1 7.5 %collective-permute-start.6 = (f32[256,128]{1,0:T(8,128)S(1)}, f32[256,128]{1,0:T(8,128)S(1)}, u32[]{:S(2)}, u32[]{:S(2)}) collective-permute-start(f32[256,128]{1,0:T(8,128)S(1)} %get-tuple-element.43), channel_id=1, source_target_pairs={{0,1},{1,0},{2,3},{3,2},{4,5},{5,4},{6,7},{7,6},{8,9},{9,8},{10,11... | collective-permute-start | bytes 393224 | tf_op jit(solution)/shard_map/ppermute | solution.py:342
  45.6 5.5 %collective-permute-start.9 = (f32[256,128]{1,0:T(8,128)S(1)}, f32[256,128]{1,0:T(8,128)S(1)}, u32[]{:S(2)}, u32[]{:S(2)}) collective-permute-start(f32[256,128]{1,0:T(8,128)S(1)} %get-tuple-element.58), channel_id=1, source_target_pairs={{0,1},{1,0},{2,3},{3,2},{4,5},{5,4},{6,7},{7,6},{8,9},{9,8},{10,11... | collective-permute-start | bytes 393224 | tf_op jit(solution)/shard_map/ppermute | solution.py:342
  50.9 5.0 %collective-permute-start.10 = (f32[256,128]{1,0:T(8,128)S(1)}, f32[256,128]{1,0:T(8,128)S(1)}, u32[]{:S(2)}, u32[]{:S(2)}) collective-permute-start(f32[256,128]{1,0:T(8,128)S(1)} %get-tuple-element.59), channel_id=1, source_target_pairs={{0,1},{1,0},{2,3},{3,2},{4,5},{5,4},{6,7},{7,6},{8,9},{9,8},{10,11... | collective-permute-start | bytes 393224 | tf_op jit(solution)/shard_map/ppermute | solution.py:342
  57.1 1.3 %collective-permute-start.11 = (f32[48,128]{1,0:T(8,128)S(1)}, f32[48,128]{1,0:T(8,128)S(1)}, u32[]{:S(2)}, u32[]{:S(2)}) collective-permute-start(f32[48,128]{1,0:T(8,128)S(1)} %get-tuple-element.61), channel_id=1, source_target_pairs={{0,2},{2,0},{4,6},{6,4},{8,10},{10,8},{12,14},{14,12},{16,18},{18,... | collective-permute-start | bytes 73736 | tf_op jit(solution)/shard_map/ppermute | solution.py:342
  58.4 3.8 %collective-permute-start.12 = (f32[48,128]{1,0:T(8,128)S(1)}, f32[48,128]{1,0:T(8,128)S(1)}, u32[]{:S(2)}, u32[]{:S(2)}) collective-permute-start(f32[48,128]{1,0:T(8,128)S(1)} %add.21), channel_id=1, source_target_pairs={{0,4},{2,6},{4,0},{6,2},{8,12},{10,14},{12,8},{14,10},{16,20},{18,... | collective-permute-start | bytes 73736 | tf_op jit(solution)/shard_map/ppermute | solution.py:342
  62.2 3.8 %collective-permute-start.13 = (f32[48,128]{1,0:T(8,128)S(1)}, f32[48,128]{1,0:T(8,128)S(1)}, u32[]{:S(2)}, u32[]{:S(2)}) collective-permute-start(f32[48,128]{1,0:T(8,128)S(1)} %add.22), channel_id=1, source_target_pairs={{0,8},{2,10},{4,12},{6,14},{8,0},{10,2},{12,4},{14,6},{16,24},{18,... | collective-permute-start | bytes 73736 | tf_op jit(solution)/shard_map/ppermute | solution.py:342
  66.0 4.7 %collective-permute-start.14 = (f32[48,128]{1,0:T(8,128)S(1)}, f32[48,128]{1,0:T(8,128)S(1)}, u32[]{:S(2)}, u32[]{:S(2)}) collective-permute-start(f32[48,128]{1,0:T(8,128)S(1)} %add.23), channel_id=1, source_target_pairs={{0,16},{2,18},{4,20},{6,22},{8,24},{10,26},{12,28},{14,30},{16,0},... | collective-permute-start | bytes 73736 | tf_op jit(solution)/shard_map/ppermute | solution.py:342
  70.7 3.8 %collective-permute-start.15 = (f32[48,128]{1,0:T(8,128)S(1)}, f32[48,128]{1,0:T(8,128)S(1)}, u32[]{:S(2)}, u32[]{:S(2)}) collective-permute-start(f32[48,128]{1,0:T(8,128)S(1)} %add.24), channel_id=1, source_target_pairs={{0,1},{1,0},{2,3},{3,2},{4,5},{5,4},{6,7},{7,6},{8,9},{9,8},{10,11... | collective-permute-start | bytes 73736 | tf_op jit(solution)/shard_map/ppermute | solution.py:342
  74.6 1.2 %collective-permute-start.16 = (f32[48,128]{1,0:T(8,128)S(1)}, f32[48,128]{1,0:T(8,128)S(1)}, u32[]{:S(2)}, u32[]{:S(2)}) collective-permute-start(f32[48,128]{1,0:T(8,128)S(1)} %add.25.own), channel_id=1, source_target_pairs={{0,2},{2,0},{4,6},{6,4},{8,10},{10,8},{12,14},{14,12},{16,18},{18,... | collective-permute-start | bytes 73736 | tf_op jit(solution)/shard_map/ppermute | solution.py:342

commit v6 on v3

--- a/solution.py
+++ b/solution.py
@@ -334,33 +334,65 @@
 
 
 def total_over_mesh(value):
-    for axis in ("tiles", "vec"):
-        bit = 1
-        while bit < lax.axis_size(axis):
-            value = value + swapped(value, axis, bit)
-            bit *= 2
-    return value
-
-
-def factor_kernel(scale, gram_ref, out_ref):
-    order = gram_ref.shape[0]
+    axes = ("tiles", "vec")
+    devices = lax.axis_size("tiles") * lax.axis_size("vec")
+    rows, cols = value.shape
+    piece = (rows // devices, cols) if rows % devices == 0 else (1, value.size // devices)
+    parts = lax.all_to_all(value.reshape((devices,) + piece), axes, 0, 0, tiled=True)
+    summed = jnp.broadcast_to(jnp.sum(parts, axis=0, keepdims=True), (devices,) + piece)
+    return lax.all_to_all(summed, axes, 0, 0, tiled=True).reshape(value.shape)
+
+
+def spread_lane(value, lane):
+    return jnp.broadcast_to(value[:, lane : lane + 1], value.shape)
+
+
+def squares(rows):
+    high = rows.astype(jnp.bfloat16).astype(jnp.float32)
+    rest = rows - high
+    middle = rest.astype(jnp.bfloat16).astype(jnp.float32)
+    low = rest - middle
+    one = jnp.concatenate([high, high, middle, high, low, middle], axis=0).astype(jnp.bfloat16)
+    two = jnp.concatenate([high, middle, high, low, high, middle], axis=0).astype(jnp.bfloat16)
+    return lax.dot_general(one, two, (((0,), (0,)), ((), ())), preferred_element_type=jnp.float32)
+
+
+def factor_kernel(scale, gram, out_ref):
+    order = out_ref.shape[0]
     height = 8
     count = order // height
-    blocks = [gram_ref[height * b : height * (b + 1), :] * scale for b in range(count)]
-    row_ids = lax.broadcasted_iota(jnp.int32, (height, order), 0)
-    col_ids = lax.broadcasted_iota(jnp.int32, (height, order), 1)
+    shape = (height, order)
+    blocks = [gram[height * b : height * (b + 1), :] * scale for b in range(count)]
+    row_ids, col_ids = (ids(shape, 0), ids(shape, 1))
+    previous = None
     for p in range(count):
-        rows = jnp.zeros((height, order), jnp.float32)
-        for j in range(height):
-            k = height * p + j
-            current = blocks[p]
-            inverse = jnp.broadcast_to(lax.rsqrt(current[j : j + 1, k : k + 1]), (height, order))
-            pivot_row = jnp.broadcast_to(current[j : j + 1, :], (height, order)) * inverse
-            rows = jnp.where((row_ids == j) & (col_ids >= k), pivot_row, rows)
-            for q in range(p, count):
-                pivot_col = jnp.broadcast_to(blocks[q][:, k : k + 1], (height, order)) * inverse
-                blocks[q] = blocks[q] - pivot_col * pivot_row
-        out_ref[height * p : height * (p + 1), :] = rows
+        base = height * p
+        rows = [jnp.broadcast_to(blocks[p][j : j + 1, :], shape) for j in range(height)]
+        corner = {(i, j): spread_lane(rows[j], base + i) for j in range(height) for i in range(j, height)}
+        if previous is not None:
+            for done in previous:
+                lanes = [spread_lane(done, base + j) for j in range(height)]
+                for j in range(height):
+                    rows[j] = rows[j] - lanes[j] * done
+                    for i in range(j, height):
+                        corner[i, j] = corner[i, j] - lanes[i] * lanes[j]
+        panel = jnp.zeros(shape, jnp.float32)
+        for s in range(height):
+            inverse = lax.rsqrt(corner[s, s])
+            rows[s] = rows[s] * inverse
+            lanes = {j: corner[j, s] * inverse for j in range(s + 1, height)}
+            for j in range(s + 1, height):
+                for i in range(j, height):
+                    corner[i, j] = corner[i, j] - lanes[i] * lanes[j]
+                rows[j] = rows[j] - lanes[j] * rows[s]
+            panel = jnp.where(row_ids == s, rows[s], panel)
+        panel = jnp.where(col_ids >= base + row_ids, panel, 0.0)
+        out_ref[base : base + height, :] = panel
+        if p + 2 < count:
+            update = squares(panel)
+            for q in range(p + 2, count):
+                blocks[q] = blocks[q] - update[height * q : height * (q + 1), :]
+        previous = rows
 
 
 def shifted(value, axis, steps):
@@ -491,18 +523,19 @@
         sent.append(swapped(send, "vec", 1))
 
     order = 2 * vectors
+    gram_shape = f32(order, order)
     gram = call(
         functools.partial(gram_kernel, chunks, half * rows),
         [smem] + [whole(half_shape)] * (2 * chunks),
-        whole(f32(order, order)),
-        f32(order, order),
+        whole(gram_shape),
+        gram_shape,
     )(meta, *kept, *sent)
     total_cells = levels * tiles * rows * cols
     r_factor = call(
         functools.partial(factor_kernel, 1.0 / total_cells),
-        [whole(gram)],
-        whole(gram),
-        f32(order, order),
+        [whole(gram_shape)],
+        whole(gram_shape),
+        gram_shape,
     )(total_over_mesh(gram))
     return (field, r_factor)
 

time: 89.4 us -> 78.9 us (0.88)
  blocking collectives: 0 us -> 25.5 us
  Pallas kernels: 34.6 us -> 22.1 us
  waiting for transfers between devices: 21 us -> 9.11 us
  starting transfers between devices: 30 us -> 18.4 us
    all_to_all x0 -> x2, blocking collectives: none -> 25.5 us  [the longest x1 16.2 us: total_over_mesh(): lax.all_to_all(value.reshape((devices,) + piece), axes, 0, 0, tiled=True)]
    pallas_call x1, Pallas kernels: 17.5 us -> 5 us  [shards(): call(functools.partial(factor_kernel, 1.0 / total_cells), [whole(gram_sha...]
    ppermute x14 -> x9, waiting for transfers between devices: 20.1 us -> 8.22 us  [swapped(): lax.ppermute(value, axis, [(source, source ^ bit) for source in range(cou...]
    ppermute x14 -> x9, starting transfers between devices: 25.7 us -> 14.1 us  [swapped(): lax.ppermute(value, axis, [(source, source ^ bit) for source in range(cou...]
  transfers between devices with their start and end apart: 16 -> 11, of which waited for: 10 -> 5; matrix products, arithmetic and copies ran while one was open for 0% -> 0% of each run, Pallas kernels for 17% -> 19%
where the time goes in v6:
time: 78.9 us; the launch traced here: 78.6 us
  blocking collectives  25.5 us (32%)
  Pallas kernels  22.1 us (28%)
  starting transfers between devices  18.4 us (23%)
  waiting for transfers between devices  9.11 us (12%)
  local copies, waits for them, and re-layouts  2.63 us (3%)
    all_to_all x1, blocking collectives, total_over_mesh(): lax.all_to_all(value.reshape((devices,) + piece), axes, 0, 0, tiled=True)  16.2 us
    ppermute x9, starting transfers between devices, swapped(): lax.ppermute(value, axis, [(source, source ^ bit) for source in range(cou...  14.1 us
    pallas_call x4, Pallas kernels, shards(): call(functools.partial(diffuse_kernel, 4), specs, [chunk_block, whole(hal...  13 us
    all_to_all x1, blocking collectives, total_over_mesh(): return lax.all_to_all(summed, axes, 0, 0, tiled=True).reshape(value.shape)  9.3 us
    ppermute x9, waiting for transfers between devices, swapped(): lax.ppermute(value, axis, [(source, source ^ bit) for source in range(cou...  8.22 us
    pallas_call x1, Pallas kernels, shards(): call(functools.partial(factor_kernel, 1.0 / total_cells), [whole(gram_sha...  5 us
    ppermute x2, starting transfers between devices, beside(): lax.ppermute(value, 'tiles', [(a, b) for a, b in pairs if 0 <= b < count...  4.31 us
    unnamed x12, local copies, waits for them, and re-layouts  2.61 us
  transfers between devices with their start and end apart: 11, of which 5 were waited for; matrix products, arithmetic and copies ran while one was open for 0% of the time, Pallas kernels for 19%

profile of v6, /device:TPU:0, one launch (start us, length us, event | category | flops | bytes accessed | tf_op | source)
XLA Modules:
  0.0 78.6 jit_solution(12722210623829381201)
XLA Ops:
  0.6 0.0 copy-start.2
  0.7 0.0 copy-start.4
  0.7 0.1 pad_add_fusion.meta
  0.7 0.7 copy-done.2
  1.4 0.0 copy-done.4
  1.4 0.0 copy-start
  1.4 1.2 %copy-done = f32[64,4,8,128]{3,2,1,0:T(8,128)S(1)} copy-done((f32[64,4,8,128]{3,2,1,0:T(8,128)S(1)}, f32[64,4,8,128]{3,2,1,0:T(8,128)}, u32[]{:S(2)}) %copy-start) | copy-done | bytes 1048600
  2.7 0.0 copy-start.3
  2.7 0.7 copy-done.3
  3.3 0.0 copy-start.1
  3.3 0.9 %shard_map.68 = (f32[4,4,8,128]{3,2,1,0:T(8,128)S(1)}, f32[5,4,8,128]{3,2,1,0:T(8,128)S(1)}, f32[10,4,8,128]{3,2,1,0:T(8,128)S(1)}, f32[8,4,8,128]{3,2,1,0:T(8,1...) custom-call(s32[3]{0:T(128)S(1)} %pad_add_fusion.meta, s32[1,4]{1,0:T(1,128)S(1)} %copy-done.4, ...), custom_call_target="tpu_custom_call" | custom-call | bytes 1048576 | tf_op jit(solution)/shard_map/pallas_call | solution.py:464
  4.3 4.1 %collective-permute-start.5 = (f32[10,4,8,128]{3,2,1,0:T(8,128)S(1)}, f32[10,4,8,128]{3,2,1,0:T(8,128)S(1)}, u32[]{:S(2)}, u32[]{:S(2)}) collective-permute-start(f32[10,4,8,128]{3,2,1,0:T(8,128)S(1)} %get-tuple-element.35), channel_id=1, source_target_pairs={{0,16},{2,18},{4,20},{6,22},{8,24},{10,26},{12,28},{14,30},{16,0},... | collective-permute-start | bytes 491528 | tf_op jit(solution)/shard_map/ppermute | solution.py:333
  8.4 1.3 %collective-permute-start.1 = (f32[5,4,8,128]{3,2,1,0:T(8,128)S(1)}, f32[5,4,8,128]{3,2,1,0:T(8,128)S(1)}, u32[]{:S(2)}, u32[]{:S(2)}) collective-permute-start(f32[5,4,8,128]{3,2,1,0:T(8,128)S(1)} %get-tuple-element.31.edges), channel_id=1, source_target_pairs={{2,0},{4,2},{6,4},{8,6},{10,8},{12,10},{14,12},{18,16},{20,18},{22... | collective-permute-start | bytes 245768 | tf_op jit(solution)/shard_map/ppermute | solution.py:407
  9.6 3.0 %collective-permute-start = (f32[5,4,8,128]{3,2,1,0:T(8,128)S(1)}, f32[5,4,8,128]{3,2,1,0:T(8,128)S(1)}, u32[]{:S(2)}, u32[]{:S(2)}) collective-permute-start(f32[5,4,8,128]{3,2,1,0:T(8,128)S(1)} %get-tuple-element.31.edges), channel_id=1, source_target_pairs={{0,2},{2,4},{4,6},{6,8},{8,10},{10,12},{12,14},{16,18},{18,20},{20... | collective-permute-start | bytes 245768 | tf_op jit(solution)/shard_map/ppermute | solution.py:407
  12.7 0.0 collective-permute-done.1.right
  12.7 0.9 %collective-permute-done.left = f32[5,4,8,128]{3,2,1,0:T(8,128)S(1)} collective-permute-done((f32[5,4,8,128]{3,2,1,0:T(8,128)S(1)}, f32[5,4,8,128]{3,2,1,0:T(8,128)S(1)}, u32[]{:S(2)}, u32[]{:S(2)}) %collective-permute-start) | collective-permute-done | bytes 81952 | tf_op jit(solution)/shard_map/ppermute | solution.py:407
  13.6 0.6 shard_map.69
  14.1 0.1 collective-permute-start.4
  14.2 2.9 %collective-permute-start.2 = (f32[8,4,8,128]{3,2,1,0:T(8,128)S(1)}, f32[8,4,8,128]{3,2,1,0:T(8,128)S(1)}, u32[]{:S(2)}, u32[]{:S(2)}) collective-permute-start(f32[8,4,8,128]{3,2,1,0:T(8,128)S(1)} %get-tuple-element.32), channel_id=1, source_target_pairs={{0,16},{2,18},{4,20},{6,22},{8,24},{10,26},{12,28},{14,30},{16,0},... | collective-permute-start | bytes 393224 | tf_op jit(solution)/shard_map/ppermute | solution.py:333
  17.1 2.0 %collective-permute-done.4.corner_below.corner_above = f32[5,2,8,128]{3,2,1,0:T(8,128)S(1)} collective-permute-done((f32[5,2,8,128]{3,2,1,0:T(8,128)S(1)}, f32[5,2,8,128]{3,2,1,0:T(8,128)S(1)}, u32[]{:S(2)}, u32[]{:S(2)}) %collective-permute-start.4) | collective-permute-done | bytes 40992 | tf_op jit(solution)/shard_map/ppermute | solution.py:333
  19.1 0.0 collective-permute-start.7
  19.1 0.0 collective-permute-done.5.below.above
  19.1 0.0 copy-start.5
  19.1 1.5 %shard_map.70 = (f32[7,4,2,8,128]{4,3,2,1,0:T(8,128)S(1)}, f32[2,7,4,2,8,128]{5,4,3,2,1,0:T(8,128)S(1)}) custom-call(s32[3]{0:T(128)S(1)} %pad_add_fusion.meta, f32[4,4,8,128]{3,2,1,0:T(8,128)S(1)} %get-tuple-element.34.statics, f32[10,4,8,128]{3,2,1,0:T(8,128)S(1)} %collective-permute-done.5.below.above, ...), custom_call_target="tpu_custom_call" | custom-call | bytes 1048576 | tf_op jit(solution)/shard_map/pallas_call | solution.py:491
  20.7 0.0 copy-done.1
  20.7 0.0 copy-done.5
  20.7 3.2 %shard_map.71 = (f32[64,4,8,128]{3,2,1,0:T(8,128)}, f32[256,128]{1,0:T(8,128)S(1)}, f32[256,128]{1,0:T(8,128)S(1)}) custom-call(s32[3]{0:T(128)S(1)} %pad_add_fusion.meta, f32[64,4,8,128]{3,2,1,0:T(8,128)S(1)} %copy-done.1, s32[8,128]{1,0:T(8,128)S(1)} %copy-done.3, f32[8,128]{1,0:T(8,128)S(1)} %copy-done.5, ...), custom_call_target="tpu_custom_call" | custom-call | flops 4000000000 | bytes 1048576 | tf_op jit(solution)/shard_map/pallas_call | solution.py:513
  24.0 1.8 %collective-permute-start.8 = (f32[256,128]{1,0:T(8,128)S(1)}, f32[256,128]{1,0:T(8,128)S(1)}, u32[]{:S(2)}, u32[]{:S(2)}) collective-permute-start(f32[256,128]{1,0:T(8,128)S(1)} %get-tuple-element.44), channel_id=1, source_target_pairs={{0,1},{1,0},{2,3},{3,2},{4,5},{5,4},{6,7},{7,6},{8,9},{9,8},{10,11... | collective-permute-start | bytes 393224 | tf_op jit(solution)/shard_map/ppermute | solution.py:333
  25.8 0.0 collective-permute-done.2.below.above
  25.8 2.6 %collective-permute-start.3 = (f32[8,4,8,128]{3,2,1,0:T(8,128)S(1)}, f32[8,4,8,128]{3,2,1,0:T(8,128)S(1)}, u32[]{:S(2)}, u32[]{:S(2)}) collective-permute-start(f32[8,4,8,128]{3,2,1,0:T(8,128)S(1)} %get-tuple-element.33), channel_id=1, source_target_pairs={{0,16},{2,18},{4,20},{6,22},{8,24},{10,26},{12,28},{14,30},{16,0},... | collective-permute-start | bytes 393224 | tf_op jit(solution)/shard_map/ppermute | solution.py:333
  28.4 3.2 %shard_map.72 = (f32[64,4,8,128]{3,2,1,0:T(8,128)}, f32[256,128]{1,0:T(8,128)S(1)}, f32[256,128]{1,0:T(8,128)S(1)}) custom-call(s32[3]{0:T(128)S(1)} %pad_add_fusion.meta, f32[64,4,8,128]{3,2,1,0:T(8,128)S(1)} %copy-done.1, s32[8,128]{1,0:T(8,128)S(1)} %copy-done.3, f32[8,128]{1,0:T(8,128)S(1)} %copy-done.5, ...), custom_call_target="tpu_custom_call", output_to_operand_aliasing={{0}: (13, {})} | custom-call | flops 4000000000 | bytes 1048576 | tf_op jit(solution)/shard_map/pallas_call | solution.py:513
  31.6 0.5 collective-permute-start.6
  32.1 0.0 collective-permute-done.7.below.above
  32.1 0.0 collective-permute-done.8.refs_4_
  32.1 3.2 %shard_map.73 = (f32[64,4,8,128]{3,2,1,0:T(8,128)}, f32[256,128]{1,0:T(8,128)S(1)}, f32[256,128]{1,0:T(8,128)S(1)}) custom-call(s32[3]{0:T(128)S(1)} %pad_add_fusion.meta, f32[64,4,8,128]{3,2,1,0:T(8,128)S(1)} %copy-done.1, s32[8,128]{1,0:T(8,128)S(1)} %copy-done.3, f32[8,128]{1,0:T(8,128)S(1)} %copy-done.5, ...), custom_call_target="tpu_custom_call", output_to_operand_aliasing={{0}: (13, {})} | custom-call | flops 4000000000 | bytes 1048576 | tf_op jit(solution)/shard_map/pallas_call | solution.py:513
  35.4 1.5 %collective-permute-start.9 = (f32[256,128]{1,0:T(8,128)S(1)}, f32[256,128]{1,0:T(8,128)S(1)}, u32[]{:S(2)}, u32[]{:S(2)}) collective-permute-start(f32[256,128]{1,0:T(8,128)S(1)} %get-tuple-element.54), channel_id=1, source_target_pairs={{0,1},{1,0},{2,3},{3,2},{4,5},{5,4},{6,7},{7,6},{8,9},{9,8},{10,11... | collective-permute-start | bytes 393224 | tf_op jit(solution)/shard_map/ppermute | solution.py:333
  36.9 0.0 collective-permute-done.3.below.above
  36.9 0.5 collective-permute-done.6.refs_5_
  37.4 3.2 %shard_map.74 = (f32[64,4,8,128]{3,2,1,0:T(8,128)}, f32[256,128]{1,0:T(8,128)S(1)}, f32[256,128]{1,0:T(8,128)S(1)}) custom-call(s32[3]{0:T(128)S(1)} %pad_add_fusion.meta, f32[64,4,8,128]{3,2,1,0:T(8,128)S(1)} %copy-done.1, s32[8,128]{1,0:T(8,128)S(1)} %copy-done.3, f32[8,128]{1,0:T(8,128)S(1)} %copy-done.5, ...), custom_call_target="tpu_custom_call", output_to_operand_aliasing={{0}: (13, {})} | custom-call | flops 4000000000 | bytes 1048576 | tf_op jit(solution)/shard_map/pallas_call | solution.py:513
  40.6 0.5 collective-permute-start.10
  41.1 0.3 collective-permute-done.9.refs_6_
  41.4 5.5 %collective-permute-done.10.refs_7_ = f32[256,128]{1,0:T(8,128)S(1)} collective-permute-done((f32[256,128]{1,0:T(8,128)S(1)}, f32[256,128]{1,0:T(8,128)S(1)}, u32[]{:S(2)}, u32[]{:S(2)}) %collective-permute-start.10) | collective-permute-done | bytes 131104 | tf_op jit(solution)/shard_map/ppermute | solution.py:333
  46.9 1.2 %shard_map.75 = f32[128,128]{1,0:T(8,128)S(1)} custom-call(s32[3]{0:T(128)S(1)} %pad_add_fusion.meta, f32[256,128]{1,0:T(8,128)S(1)} %get-tuple-element.50.refs_0_, f32[256,128]{1,0:T(8,128)S(1)} %get-tuple-element.51.refs_1_, f32[256,128]{1,0:T(8,128)S(1)} %get-tuple-element.52.refs_2_, f32[256,128]{1,0:T(8,128)S(1)} %get-tuple-element.53.refs_3_, ...), custom_call_target="tpu_custom_call" | custom-call | bytes 1048576 | tf_op jit(solution)/shard_map/pallas_call | solution.py:527
  48.1 16.2 %all_to_all.10 = f32[32,4,128]{2,1,0:T(4,128)S(1)} all-to-all(f32[32,4,128]{2,1,0:T(4,128)S(1)} %bitcast.5), channel_id=1, replica_groups=mesh['tiles'=16,'vec'=2] {'tiles','vec'}, dimensions={0} | all-to-all | bytes 131072 | tf_op jit(solution)/shard_map/all_to_all | solution.py:341
  64.3 9.3 %all_to_all.11 = f32[32,4,128]{2,1,0:T(4,128)S(1)} all-to-all(f32[32,4,128]{2,1,0:T(4,128)S(1)} %broadcast_in_dim.2), channel_id=1, replica_groups=mesh['tiles'=16,'vec'=2] {'tiles','vec'}, dimensions={0} | all-to-all | bytes 131072 | tf_op jit(solution)/shard_map/all_to_all | solution.py:343
  73.6 5.0 %shard_map.76 = f32[128,128]{1,0:T(8,128)} custom-call(f32[128,128]{1,0:T(8,128)S(1)} %bitcast.6), custom_call_target="tpu_custom_call" | custom-call | bytes 1048576 | tf_op jit(solution)/shard_map/pallas_call | solution.py:534
  (2 shorter events, 0.1 us)
Async XLA Ops:
  0.6 0.8 %copy-start.2 = (f32[3,4,8,128]{3,2,1,0:T(8,128)S(1)}, f32[3,4,8,128]{3,2,1,0:T(8,128)}, u32[]{:S(2)}) copy-start(f32[3,4,8,128]{3,2,1,0:T(8,128)} %conductance.1) | copy-start | bytes 147460
  0.7 0.8 copy-start.4
  1.4 1.2 %copy-start = (f32[64,4,8,128]{3,2,1,0:T(8,128)S(1)}, f32[64,4,8,128]{3,2,1,0:T(8,128)}, u32[]{:S(2)}) copy-start(f32[64,4,8,128]{3,2,1,0:T(8,128)} %omega.9) | copy-start | bytes 3145732
  2.7 0.7 copy-start.3
  3.3 17.3 %copy-start.1 = (f32[64,4,8,128]{3,2,1,0:T(8,128)S(1)}, f32[64,4,8,128]{3,2,1,0:T(8,128)}, u32[]{:S(2)}) copy-start(f32[64,4,8,128]{3,2,1,0:T(8,128)} %omega.9) | copy-start | bytes 3145732
  4.3 14.9 %collective-permute-start.5 = (f32[10,4,8,128]{3,2,1,0:T(8,128)S(1)}, f32[10,4,8,128]{3,2,1,0:T(8,128)S(1)}, u32[]{:S(2)}, u32[]{:S(2)}) collective-permute-start(f32[10,4,8,128]{3,2,1,0:T(8,128)S(1)} %get-tuple-element.35), channel_id=1, source_target_pairs={{0,16},{2,18},{4,20},{6,22},{8,24},{10,26},{12,28},{14,30},{16,0},... | collective-permute-start | bytes 491528 | tf_op jit(solution)/shard_map/ppermute | solution.py:333
  8.4 4.3 %collective-permute-start.1 = (f32[5,4,8,128]{3,2,1,0:T(8,128)S(1)}, f32[5,4,8,128]{3,2,1,0:T(8,128)S(1)}, u32[]{:S(2)}, u32[]{:S(2)}) collective-permute-start(f32[5,4,8,128]{3,2,1,0:T(8,128)S(1)} %get-tuple-element.31.edges), channel_id=1, source_target_pairs={{2,0},{4,2},{6,4},{8,6},{10,8},{12,10},{14,12},{18,16},{20,18},{22... | collective-permute-start | bytes 245768 | tf_op jit(solution)/shard_map/ppermute | solution.py:407
  9.6 3.9 %collective-permute-start = (f32[5,4,8,128]{3,2,1,0:T(8,128)S(1)}, f32[5,4,8,128]{3,2,1,0:T(8,128)S(1)}, u32[]{:S(2)}, u32[]{:S(2)}) collective-permute-start(f32[5,4,8,128]{3,2,1,0:T(8,128)S(1)} %get-tuple-element.31.edges), channel_id=1, source_target_pairs={{0,2},{2,4},{4,6},{6,8},{8,10},{10,12},{12,14},{16,18},{18,20},{20... | collective-permute-start | bytes 245768 | tf_op jit(solution)/shard_map/ppermute | solution.py:407
  14.1 5.0 %collective-permute-start.4 = (f32[5,2,8,128]{3,2,1,0:T(8,128)S(1)}, f32[5,2,8,128]{3,2,1,0:T(8,128)S(1)}, u32[]{:S(2)}, u32[]{:S(2)}) collective-permute-start(f32[5,2,8,128]{3,2,1,0:T(8,128)S(1)} %shard_map.69), channel_id=1, source_target_pairs={{0,16},{2,18},{4,20},{6,22},{8,24},{10,26},{12,28},{14,30},{16,0},... | collective-permute-start | bytes 122888 | tf_op jit(solution)/shard_map/ppermute | solution.py:333
  14.2 11.5 %collective-permute-start.2 = (f32[8,4,8,128]{3,2,1,0:T(8,128)S(1)}, f32[8,4,8,128]{3,2,1,0:T(8,128)S(1)}, u32[]{:S(2)}, u32[]{:S(2)}) collective-permute-start(f32[8,4,8,128]{3,2,1,0:T(8,128)S(1)} %get-tuple-element.32), channel_id=1, source_target_pairs={{0,16},{2,18},{4,20},{6,22},{8,24},{10,26},{12,28},{14,30},{16,0},... | collective-permute-start | bytes 393224 | tf_op jit(solution)/shard_map/ppermute | solution.py:333
  19.1 13.0 %collective-permute-start.7 = (f32[8,4,8,128]{3,2,1,0:T(8,128)S(1)}, f32[8,4,8,128]{3,2,1,0:T(8,128)S(1)}, u32[]{:S(2)}, u32[]{:S(2)}) collective-permute-start(f32[8,4,8,128]{3,2,1,0:T(8,128)S(1)} %get-tuple-element.43), channel_id=1, source_target_pairs={{0,16},{2,18},{4,20},{6,22},{8,24},{10,26},{12,28},{14,30},{16,0},... | collective-permute-start | bytes 393224 | tf_op jit(solution)/shard_map/ppermute | solution.py:333
  19.1 1.6 %copy-start.5 = (f32[8,128]{1,0:T(8,128)S(1)}, f32[8,128]{1,0:T(8,128)}, u32[]{:S(2)}) copy-start(f32[8,128]{1,0:T(8,128)} %volume.7) | copy-start | bytes 12292
  24.0 8.2 %collective-permute-start.8 = (f32[256,128]{1,0:T(8,128)S(1)}, f32[256,128]{1,0:T(8,128)S(1)}, u32[]{:S(2)}, u32[]{:S(2)}) collective-permute-start(f32[256,128]{1,0:T(8,128)S(1)} %get-tuple-element.44), channel_id=1, source_target_pairs={{0,1},{1,0},{2,3},{3,2},{4,5},{5,4},{6,7},{7,6},{8,9},{9,8},{10,11... | collective-permute-start | bytes 393224 | tf_op jit(solution)/shard_map/ppermute | solution.py:333
  25.8 11.1 %collective-permute-start.3 = (f32[8,4,8,128]{3,2,1,0:T(8,128)S(1)}, f32[8,4,8,128]{3,2,1,0:T(8,128)S(1)}, u32[]{:S(2)}, u32[]{:S(2)}) collective-permute-start(f32[8,4,8,128]{3,2,1,0:T(8,128)S(1)} %get-tuple-element.33), channel_id=1, source_target_pairs={{0,16},{2,18},{4,20},{6,22},{8,24},{10,26},{12,28},{14,30},{16,0},... | collective-permute-start | bytes 393224 | tf_op jit(solution)/shard_map/ppermute | solution.py:333
  31.6 5.8 %collective-permute-start.6 = (f32[256,128]{1,0:T(8,128)S(1)}, f32[256,128]{1,0:T(8,128)S(1)}, u32[]{:S(2)}, u32[]{:S(2)}) collective-permute-start(f32[256,128]{1,0:T(8,128)S(1)} %get-tuple-element.39), channel_id=1, source_target_pairs={{0,1},{1,0},{2,3},{3,2},{4,5},{5,4},{6,7},{7,6},{8,9},{9,8},{10,11... | collective-permute-start | bytes 393224 | tf_op jit(solution)/shard_map/ppermute | solution.py:333
  35.4 6.0 %collective-permute-start.9 = (f32[256,128]{1,0:T(8,128)S(1)}, f32[256,128]{1,0:T(8,128)S(1)}, u32[]{:S(2)}, u32[]{:S(2)}) collective-permute-start(f32[256,128]{1,0:T(8,128)S(1)} %get-tuple-element.54), channel_id=1, source_target_pairs={{0,1},{1,0},{2,3},{3,2},{4,5},{5,4},{6,7},{7,6},{8,9},{9,8},{10,11... | collective-permute-start | bytes 393224 | tf_op jit(solution)/shard_map/ppermute | solution.py:333
  40.6 6.3 %collective-permute-start.10 = (f32[256,128]{1,0:T(8,128)S(1)}, f32[256,128]{1,0:T(8,128)S(1)}, u32[]{:S(2)}, u32[]{:S(2)}) collective-permute-start(f32[256,128]{1,0:T(8,128)S(1)} %get-tuple-element.55), channel_id=1, source_target_pairs={{0,1},{1,0},{2,3},{3,2},{4,5},{5,4},{6,7},{7,6},{8,9},{9,8},{10,11... | collective-permute-start | bytes 393224 | tf_op jit(solution)/shard_map/ppermute | solution.py:333

commit v7 on v4

--- a/solution.py
+++ b/solution.py
@@ -10,6 +10,7 @@
 ITERS = 4
 EDGE = 2 * ITERS
 VMEM_LIMIT = 32 * 1024 * 1024
+EDGE_LIMIT = 63 * 1024 * 1024 + 256 * 1024
 MAIN, SLOT = (0, 1)
 
 
@@ -304,31 +305,43 @@
                 send_out[at : at + rows, :] = jnp.where(keeps_low, scaled[half + level], scaled[level])
 
 
-def gram_kernel(chunks, slices, meta, *refs):
-    mine, theirs = refs[-2:]
-    sources = refs[:-2]
-    stride = slices
-    group = sources[0].shape[0] // stride
-    order = group * len(sources)
-    cols = sources[0].shape[1]
+def gram_of_rows(slices, refs):
+    group = refs[0].shape[0] // slices
+    order = group * len(refs)
     exact = jnp.zeros((order, order), jnp.float32)
     cross = jnp.zeros((order, order), jnp.float32)
     for at in range(0, slices, 2):
         columns = []
         for i in range(2):
-            columns.append(jnp.concatenate([ref[pl.ds(at + i, group, stride), :] for ref in sources], axis=0))
+            columns.append(jnp.concatenate([ref[pl.ds(at + i, group, slices), :] for ref in refs], axis=0))
         values = jnp.concatenate(columns, axis=1)
         high = values.astype(jnp.bfloat16)
         rest = (values - high.astype(jnp.float32)).astype(jnp.bfloat16)
         dims = (((1,), (1,)), ((), ()))
         exact = exact + lax.dot_general(high, high, dims, preferred_element_type=jnp.float32)
         cross = cross + lax.dot_general(high, rest, dims, preferred_element_type=jnp.float32)
-    gram = exact + (cross + cross.T)
+    return exact + (cross + cross.T)
+
+
+def store_halves(meta, gram, mine, theirs):
+    order = gram.shape[0]
     moved = turn(turn(gram, order // 2, 0), order // 2, 1)
     first, second = halves_of_gram(jnp.where(meta[2] == 0, gram, moved))
     is_first = meta[3] == 0
     mine[...] = jnp.where(is_first, first, second)
     theirs[...] = jnp.where(is_first, second, first)
+
+
+def gram_kernel(chunks, slices, meta, *refs):
+    store_halves(meta, gram_of_rows(slices, refs[:-2]), *refs[-2:])
+
+
+def far_gram_kernel(slices, kept, received, out):
+    out[...] = gram_of_rows(slices, (kept, received))
+
+
+def near_gram_kernel(slices, meta, far, *refs):
+    store_halves(meta, far[...] + gram_of_rows(slices, refs[:-2]), *refs[-2:])
 
 
 def swapped(value, axis, bit):
@@ -449,6 +462,337 @@
         previous = rows
 
 
+def edge_kernel(runs, omega, conductance, wet, static_out, edge_out):
+    levels, rows, cols = omega.shape[1:]
+    shape = (rows, cols)
+    row_ids, col_ids = (ids(shape, 0), ids(shape, 1))
+    wet_cells = wet[...].astype(jnp.float32)
+    open_x = (col_ids >= runs[0, 0]) & (col_ids < runs[0, 0] + runs[0, 1])
+    open_y = (row_ids >= runs[0, 2]) & (row_ids < runs[0, 2] + runs[0, 3])
+    keep_x = (row_ids > 0) | open_x
+    keep_y = (col_ids > 0) | open_y
+    group = cols // EDGE
+    chunks = omega.shape[0] // group
+    for level in range(levels):
+        statics = [
+            jnp.where(keep_x, conductance[0, level], 0.0),
+            jnp.where(keep_y, conductance[1, level], 0.0),
+            conductance[2, level] if level else jnp.zeros(shape, jnp.float32),
+            wet_cells,
+        ]
+        edge = None
+        for kind, value in enumerate(statics):
+            static_out[kind, level] = value
+            edge = add_edge(edge, value, kind)
+        edge_out[chunks, level] = edge
+        for chunk in range(chunks):
+            edge = None
+            for place in range(group):
+                edge = add_edge(edge, omega[chunk * group + place, level] * wet_cells, place)
+            edge_out[chunk, level] = edge
+
+
+def face_kernel(meta, omega, wet, *row_outs):
+    levels, rows, cols = omega.shape[1:]
+    group = cols // EDGE
+    is_first_row = meta[0] == 0
+    wet_cells = wet[...].astype(jnp.float32)
+    for chunk, out in enumerate(row_outs):
+        for level in range(levels):
+            for pair in range(group // 2):
+                start = [omega[chunk * group + 2 * pair + i, level] * wet_cells for i in range(2)]
+                store_pair((out,), (pair, level), start[0], start[1], is_first_row)
+
+
+def rim_kernel(meta, statics, left, right, out):
+    is_first_row = meta[0] == 0
+    groups, levels, rows, cols = left.shape
+    kinds = statics.shape[0]
+    take = left_lanes((rows, cols))
+    for g in range(groups):
+        for level in range(0, levels, 2):
+            pair = [jnp.where(take, left[g, level + i], right[g, level + i]) for i in range(2)]
+            store_pair((out,), g * levels // 2 + level // 2, pair[0], pair[1], is_first_row)
+    first = groups * levels // 2
+    for kind in range(0, kinds, 2):
+        for level in range(levels):
+            at = first + kind // 2 * levels + level
+            store_pair((out,), at, statics[kind, level], statics[kind + 1, level], is_first_row)
+
+
+def near_rows(is_first_row, a, b, halo):
+    low = low_half(halo.shape)
+    turned = turn(halo, ITERS, 0)
+    result = []
+    for own, across, moved in ((a, halo, turned), (b, turned, halo)):
+        near = turn(own, ITERS, 0)
+        result.append(jnp.where(low, jnp.where(is_first_row, near, across), jnp.where(is_first_row, moved, near)))
+    return result
+
+
+def spread_kind(strip, kind):
+    cols = strip.shape[1]
+    value = jnp.where(ids(strip.shape, 1) // EDGE == 0, turn(strip, -EDGE * kind, 1), 0.0)
+    span = EDGE
+    while span < cols:
+        value = value + turn(value, span, 1)
+        span *= 2
+    return value
+
+
+def store_weights(out, values, after_row, after_col):
+    levels = len(values[0])
+    for level in range(levels):
+        cond_x, cond_y, cond_z, wet = (kind[level] for kind in values)
+        below = values[2][level + 1] if level + 1 < levels else jnp.zeros_like(cond_z)
+        faces = [cond_x, after_row(level), cond_y, after_col(level), cond_z, below]
+        total = faces[0]
+        for face in faces[1:]:
+            total = total + face
+        out[0, level] = wet * (1.0 - total)
+        for index, face in enumerate(faces):
+            out[index + 1, level] = wet * face
+
+
+def plane_pass(state, weight, row_before, row_after, rim_at):
+    levels = len(state)
+    result = []
+    for level in range(levels):
+        value = state[level]
+        rim = rim_at(level)
+        before = turn(value, 1, 1) if rim is None else prev_col(value, rim)
+        after = turn(value, -1, 1) if rim is None else next_col(value, rim)
+        total = weight(0, level) * value
+        total = total + weight(1, level) * row_before(value, level)
+        total = total + weight(2, level) * row_after(value, level)
+        total = total + weight(3, level) * before
+        total = total + weight(4, level) * after
+        if level > 0:
+            total = total + weight(5, level) * state[level - 1]
+        if level < levels - 1:
+            total = total + weight(6, level) * state[level + 1]
+        result.append(total)
+    return result
+
+
+def no_rim(level):
+    return None
+
+
+def pack_levels(values, use_first):
+    pairs = []
+    for level in range(0, len(values), 2):
+        a, b = values[level : level + 2]
+        pairs.append(jnp.where(use_first, first_pair(a, b), last_pair(a, b)))
+    return pairs
+
+
+def store_half(keep, send, place, pairs, keeps_low):
+    rows = pairs[0].shape[0]
+    half = len(pairs) // 2
+    for i in range(half):
+        at = (place * half + i) * rows
+        keep[at : at + rows, :] = jnp.where(keeps_low, pairs[i], pairs[half + i])
+        send[at : at + rows, :] = jnp.where(keeps_low, pairs[half + i], pairs[i])
+
+
+def far_kernel(
+    batch, meta, statics, omega, wet, volume, edges, left, right,
+    final_out, bound_out, strip_bound_out, keep_out, send_out, weights, strip_weights, cross_scratch
+):
+    vectors, levels, rows, cols = omega.shape
+    kinds = statics.shape[0]
+    shape = (rows, cols)
+    group = cols // EDGE
+    chunks = vectors // group
+    is_first_row = meta[0] == 0
+    keeps_low = meta[2] == 0
+    row_ids = ids(shape, 0)
+    take = left_lanes(shape)
+    wet_cells = wet[...].astype(jnp.float32)
+    root = jnp.sqrt(volume[...])
+
+    def sides(g, level):
+        return strips(edges[g, level], jnp.where(take, left[g, level], right[g, level]))
+
+    def roll_before(value, level):
+        return turn(value, 1, 0)
+
+    def roll_after(value, level):
+        return turn(value, -1, 0)
+
+    def closed_after(value):
+        return jnp.where(row_ids == rows - 1, 0.0, turn(value, -1, 0))
+
+    field = [[statics[kind, level] for level in range(levels)] for kind in range(kinds)]
+    pairs = [sides(chunks, level) for level in range(levels)]
+    crosses = [crossing(*pair) for pair in pairs]
+    store_weights(
+        weights, field, lambda level: closed_after(field[0][level]),
+        lambda level: next_col(field[1][level], rim_of(crosses[level], 1)),
+    )
+    for s in range(2):
+        side = [[spread_kind(pairs[level][s], kind) for level in range(levels)] for kind in range(kinds)]
+        store_weights(
+            strip_weights.at[s], side, lambda level: closed_after(side[0][level]), lambda level: turn(side[1][level], -1, 1)
+        )
+
+    def keep_bound(acc, value, sweep):
+        edge = jnp.where(is_first_row, value, turn(value, -1, 0))
+        moved = turn(edge, sweep - (ITERS - 1), 0)
+        return moved if acc is None else jnp.where(row_ids == sweep, moved, acc)
+
+    for g in range(chunks):
+        state = [[sides(g, level)[s] for level in range(levels)] for s in range(2)]
+        bounds = [[None] * levels for _ in range(2)]
+        for sweep in range(ITERS):
+            for level in range(levels):
+                cross_scratch[g, sweep, level] = crossing(state[0][level], state[1][level])
+                for s in range(2):
+                    bounds[s][level] = keep_bound(bounds[s][level], state[s][level], sweep)
+            if sweep < ITERS - 1:
+                for s in range(2):
+                    state[s] = plane_pass(
+                        state[s], lambda n, level: strip_weights[s, n, level], roll_before, roll_after, no_rim
+                    )
+        for s in range(2):
+            for level in range(levels):
+                strip_bound_out[g, s, level] = bounds[s][level]
+
+    for first in range(0, vectors, batch):
+        g = first // group
+        fields = [[omega[place, level] * wet_cells for level in range(levels)] for place in range(first, first + batch)]
+        bounds = [[None] * levels for _ in range(batch)]
+        for sweep in range(ITERS):
+            for i in range(batch):
+                for level in range(levels):
+                    bounds[i][level] = keep_bound(bounds[i][level], fields[i][level], sweep)
+                fields[i] = plane_pass(
+                    fields[i], lambda n, level: weights[n, level], roll_before, roll_after,
+                    lambda level: rim_of(cross_scratch[g, sweep, level], (first + i) % group),
+                )
+        for i in range(batch):
+            for level in range(levels):
+                final_out[first + i, level] = fields[i][level]
+                bound_out[first + i, level] = bounds[i][level]
+            scaled = [value * root for value in fields[i]]
+            store_half(keep_out, send_out, first + i, pack_levels(scaled, is_first_row), keeps_low)
+
+
+def near_weight_kernel(meta, statics, rims, edges, left, right, weights, strip_weights):
+    kinds, levels, rows, cols = statics.shape
+    shape = (rows, cols)
+    is_first_row = meta[0] == 0
+    take = left_lanes(shape)
+    last = ids(shape, 0) == rows - 1
+    g = edges.shape[0] - 1
+    groups = edges.shape[0]
+    first = groups * levels // 2
+    field = [[None] * levels for _ in range(kinds)]
+    for kind in range(0, kinds, 2):
+        for level in range(levels):
+            own = (statics[kind, level], statics[kind + 1, level])
+            pair = near_rows(is_first_row, *own, rims[first + kind // 2 * levels + level])
+            field[kind][level], field[kind + 1][level] = pair
+    rim = [jnp.where(take, left[g, level], right[g, level]) for level in range(levels)]
+    near_rim = []
+    for level in range(0, levels, 2):
+        near_rim += near_rows(is_first_row, rim[level], rim[level + 1], rims[g * levels // 2 + level // 2])
+    near_edge = []
+    for level in range(levels):
+        edge = None
+        for kind in range(kinds):
+            edge = add_edge(edge, field[kind][level], kind)
+        near_edge.append(edge)
+    pairs = [strips(near_edge[level], near_rim[level]) for level in range(levels)]
+    tile_pairs = [strips(edges[g, level], rim[level]) for level in range(levels)]
+    crosses = [crossing(*pair) for pair in pairs]
+
+    def with_next(value, tile_value):
+        beyond = jnp.broadcast_to(tile_value[ITERS : ITERS + 1, :], shape)
+        return jnp.where(last, beyond, turn(value, -1, 0))
+
+    store_weights(
+        weights, field, lambda level: with_next(field[0][level], statics[0, level]),
+        lambda level: next_col(field[1][level], rim_of(crosses[level], 1)),
+    )
+    for s in range(2):
+        side = [[spread_kind(pairs[level][s], kind) for level in range(levels)] for kind in range(kinds)]
+        tile_side = [spread_kind(tile_pairs[level][s], 0) for level in range(levels)]
+        store_weights(
+            strip_weights.at[s], side, lambda level: with_next(side[0][level], tile_side[level]),
+            lambda level: turn(side[1][level], -1, 1),
+        )
+
+
+def near_kernel(
+    batch, chunk, meta, omega, wet, volume, halo, rims, left, right, weights, strip_weights, bound, strip_bound, final, *rest
+):
+    field_out, keep_out, send_out, cross_scratch, start = rest[-5:]
+    group, levels, rows, cols = omega.shape
+    shape = (rows, cols)
+    is_first_row = meta[0] == 0
+    keeps_low = meta[2] == 0
+    row_ids = ids(shape, 0)
+    take = left_lanes(shape)
+    top = (row_ids == 0) & is_first_row
+    bottom = (row_ids == rows - 1) & jnp.logical_not(is_first_row)
+    is_near = low_half(shape) != is_first_row
+    wet_cells = wet[...].astype(jnp.float32)
+    root = jnp.sqrt(volume[...])
+
+    near_edge = [None] * levels
+    for level in range(levels):
+        for pair in range(group // 2):
+            own = [omega[2 * pair + i, level] * wet_cells for i in range(2)]
+            two = near_rows(is_first_row, *own, halo[pair, level])
+            for i in range(2):
+                start[2 * pair + i, level] = two[i]
+                near_edge[level] = add_edge(near_edge[level], two[i], 2 * pair + i)
+    rim = [jnp.where(take, left[0, level], right[0, level]) for level in range(levels)]
+    near_rim = []
+    for level in range(0, levels, 2):
+        near_rim += near_rows(is_first_row, rim[level], rim[level + 1], rims[chunk * levels // 2 + level // 2])
+
+    def around(bound_at, sweep):
+        def kept(level):
+            return jnp.broadcast_to(bound_at(level)[sweep : sweep + 1, :], shape)
+
+        return (
+            lambda value, level: jnp.where(top, kept(level), turn(value, 1, 0)),
+            lambda value, level: jnp.where(bottom, kept(level), turn(value, -1, 0)),
+        )
+
+    pairs = [strips(near_edge[level], near_rim[level]) for level in range(levels)]
+    state = [[pairs[level][s] for level in range(levels)] for s in range(2)]
+    for sweep in range(ITERS):
+        for level in range(levels):
+            cross_scratch[sweep, level] = crossing(state[0][level], state[1][level])
+        if sweep < ITERS - 1:
+            for s in range(2):
+                state[s] = plane_pass(
+                    state[s], lambda n, level: strip_weights[s, n, level],
+                    *around(lambda level: strip_bound[0, s, level], sweep), no_rim,
+                )
+
+    for first in range(0, group, batch):
+        fields = [[start[place, level] for level in range(levels)] for place in range(first, first + batch)]
+        for sweep in range(ITERS):
+            for i in range(batch):
+                fields[i] = plane_pass(
+                    fields[i], lambda n, level: weights[n, level],
+                    *around(lambda level: bound[first + i, level], sweep),
+                    lambda level: rim_of(cross_scratch[sweep, level], first + i),
+                )
+        for i in range(batch):
+            scaled = []
+            for level in range(levels):
+                value = jnp.where(is_near, turn(fields[i][level], ITERS, 0), final[first + i, level])
+                field_out[first + i, level] = value
+                scaled.append(value * root)
+            store_half(keep_out, send_out, first + i, pack_levels(scaled, jnp.logical_not(is_first_row)), keeps_low)
+
+
 def shifted(value, axis, steps):
     count = lax.axis_size(axis)
     first, last = (max(0, -steps), min(count, count - steps))
@@ -480,7 +824,7 @@
     return pl.BlockSpec(shape, lambda i: at)
 
 
-def call(kernel, in_specs, out_specs, out_shape, flops=0, scratch=(), aliases=None):
+def call(kernel, in_specs, out_specs, out_shape, flops=0, scratch=(), aliases=None, limit=VMEM_LIMIT):
     return pl.pallas_call(
         kernel,
         grid=(1,),
@@ -489,7 +833,7 @@
         out_shape=out_shape,
         scratch_shapes=scratch,
         input_output_aliases=aliases or {},
-        compiler_params=pltpu.CompilerParams(vmem_limit_bytes=VMEM_LIMIT),
+        compiler_params=pltpu.CompilerParams(vmem_limit_bytes=limit),
         cost_estimate=pl.CostEstimate(flops=flops, bytes_accessed=1 << 20, transcendentals=0),
     )
 
@@ -499,7 +843,18 @@
     return pl.BlockSpec(array.shape, lambda i: zeros)
 
 
-def shards(omega, conductance, wet, volume, face_runs):
+def factor(meta, mine, theirs, order, scale):
+    mine = total_over_chips(mine + swapped(theirs, "tiles", 1))
+    smem = pl.BlockSpec(memory_space=pltpu.SMEM)
+    return call(
+        functools.partial(factor_kernel, scale),
+        [smem, whole(mine), whole(mine)],
+        whole(f32(order, order)),
+        f32(order, order),
+    )(meta, mine, swapped(mine, "tiles", 1))
+
+
+def shards_any(omega, conductance, wet, volume, face_runs):
     vectors, levels, rows, cols = omega.shape
     tiles = lax.axis_size("tiles")
     grid_rows = tiles // TGY
@@ -585,18 +940,121 @@
         [whole(half_gram)] * 2,
         [half_gram] * 2,
     )(meta, *kept, *sent)
-    mine = total_over_chips(mine + swapped(theirs, "tiles", 1))
-    total_cells = levels * tiles * rows * cols
-    r_factor = call(
-        functools.partial(factor_kernel, 1.0 / total_cells),
-        [smem, whole(half_gram), whole(half_gram)],
-        whole(f32(order, order)),
-        f32(order, order),
-    )(meta, mine, swapped(mine, "tiles", 1))
+    r_factor = factor(meta, mine, theirs, order, 1.0 / (levels * tiles * rows * cols))
     return (field, r_factor)
 
 
+def shards_of_two_rows(omega, conductance, wet, volume, face_runs):
+    vectors, levels, rows, cols = omega.shape
+    tiles = lax.axis_size("tiles")
+    tile_row = lax.axis_index("tiles") // TGY
+    core = lax.axis_index("tiles") % 2
+    meta = jnp.stack([tile_row, 1 - tile_row, lax.axis_index("vec"), core]).astype(jnp.int32)
+    smem = pl.BlockSpec(memory_space=pltpu.SMEM)
+    group = cols // EDGE
+    chunks = vectors // group
+    kinds = 4
+    half = levels // 4
+    plane = (rows, cols)
+
+    def vmem(*lead):
+        return pltpu.VMEM(lead + plane, jnp.float32)
+
+    edge_shapes = [f32(kinds, levels, *plane), f32(chunks + 1, levels, *plane)]
+    statics, edges = call(
+        edge_kernel,
+        [smem, whole(omega), whole(conductance), whole(wet)],
+        [whole(s) for s in edge_shapes],
+        edge_shapes,
+        limit=EDGE_LIMIT,
+    )(face_runs, omega, conductance, wet)
+    left = beside(edges, 1)
+    right = beside(edges, -1)
+    row_shapes = [f32(group // 2, levels, *plane)] * chunks
+    messages = call(
+        face_kernel,
+        [smem, whole(omega), whole(wet)],
+        [whole(s) for s in row_shapes],
+        row_shapes,
+        flops=10**9,
+    )(meta, omega, wet)
+    halos = [swapped(messages[0], "tiles", TGY)]
+    rim_shape = f32((chunks + 1) * levels // 2 + kinds // 2 * levels, *plane)
+    rims = call(rim_kernel, [smem, whole(statics), whole(left), whole(right)], whole(rim_shape), rim_shape)(
+        meta, statics, left, right
+    )
+    rims = swapped(rims, "tiles", TGY)
+    gates = [(left, right), (halos[0], rims)]
+    for c in range(1, chunks):
+        gate = gates[c - 1] if c <= 2 else halos[c - 2]
+        halos.append(swapped(after(messages[c], gate), "tiles", TGY))
+
+    far_shape = f32(vectors * half * rows, cols)
+    far_shapes = [f32(*omega.shape), f32(*omega.shape), f32(chunks, 2, levels, *plane), far_shape, far_shape]
+    final, bound, strip_bound, far_kept, far_sent = call(
+        functools.partial(far_kernel, 4),
+        [smem] + [whole(x) for x in (statics, omega, wet, volume, edges, left, right)],
+        [whole(s) for s in far_shapes],
+        far_shapes,
+        flops=8 * 10**9,
+        scratch=[vmem(7, levels), vmem(2, 7, levels), vmem(chunks, ITERS, levels)],
+    )(meta, statics, omega, wet, volume, edges, left, right)
+    far_received = swapped(far_sent, "vec", 1)
+
+    weight_shapes = [f32(7, levels, *plane), f32(2, 7, levels, *plane)]
+    weights, strip_weights = call(
+        near_weight_kernel,
+        [smem] + [whole(x) for x in (statics, rims, edges, left, right)],
+        [whole(s) for s in weight_shapes],
+        weight_shapes,
+    )(meta, statics, rims, edges, left, right)
+
+    field = None
+    kept, sent = ([], [])
+    near_shape = f32(group * half * rows, cols)
+    for c in range(chunks):
+        waits = [(halos[1],), (far_received,)]
+        halo = after(halos[c], *(waits[c] if c < 2 else sent[c - 2 : c - 1]))
+        chunk_block = block((group, levels, *plane), c, 0, 0, 0)
+        edge_block = block((1, levels, *plane), c, 0, 0, 0)
+        operands = [meta, omega, wet, volume, halo, rims, left, right, weights, strip_weights, bound, strip_bound, final]
+        specs = [smem, chunk_block, whole(wet), whole(volume), whole(halo), whole(rims), edge_block, edge_block]
+        specs += [whole(weights), whole(strip_weights), chunk_block, block((1, 2, levels, *plane), c, 0, 0, 0, 0), chunk_block]
+        aliases = {}
+        if field is not None:
+            aliases = {len(operands): 0}
+            operands.append(field)
+            specs.append(pl.BlockSpec(memory_space=pl.ANY))
+        field, keep, send = call(
+            functools.partial(near_kernel, 4, c),
+            specs,
+            [chunk_block, whole(near_shape), whole(near_shape)],
+            [f32(*omega.shape), near_shape, near_shape],
+            flops=2 * 10**9,
+            scratch=[vmem(ITERS, levels), vmem(group, levels)],
+            aliases=aliases,
+        )(*operands)
+        kept.append(keep)
+        sent.append(swapped(send, "vec", 1))
+
+    order = 2 * vectors
+    gram_shape = f32(order, order)
+    far_gram = call(
+        functools.partial(far_gram_kernel, half * rows), [whole(far_shape)] * 2, whole(gram_shape), gram_shape
+    )(far_kept, far_received)
+    half_gram = f32(3 * order // 8, order)
+    mine, theirs = call(
+        functools.partial(near_gram_kernel, half * rows),
+        [smem, whole(gram_shape)] + [whole(near_shape)] * (2 * chunks),
+        [whole(half_gram)] * 2,
+        [half_gram] * 2,
+    )(meta, far_gram, *kept, *sent)
+    r_factor = factor(meta, mine, theirs, order, 1.0 / (levels * tiles * rows * cols))
+    return (field, r_factor)
+
+
 def solution(mesh):
+    shards = shards_of_two_rows if mesh.shape["tiles"] == 2 * TGY else shards_any
     in_specs = (
         P("vec", None, "tiles", None),
         P(None, None, "tiles", None),

time: 74.9 us -> 79.3 us (1.059)
  Pallas kernels: 22.8 us -> 28.4 us
  waiting for transfers between devices: 18.8 us -> 16.1 us
  starting transfers between devices: 30.3 us -> 31.7 us
    pallas_call x9 -> x12, Pallas kernels: 22.8 us -> 28.4 us  [the longest x4 11 us: shards_of_two_rows(): call(functools.partial(near_kernel, 4, c), specs, [chunk_block, whole(nea...]
    ppermute x11 -> x12, starting transfers between devices: 14.2 us -> 16.1 us  [swapped(): lax.ppermute(value, axis, [(source, source ^ bit) for source in range(cou...]
    ppermute x11 -> x12, waiting for transfers between devices: 10.6 us -> 8.83 us  [swapped(): lax.ppermute(value, axis, [(source, source ^ bit) for source in range(cou...]
    ppermute x2, waiting for transfers between devices: 0.89 us -> 0.01 us  [beside(): lax.ppermute(value, 'tiles', [(a, b) for a, b in pairs if 0 <= b < count...]
  transfers between devices with their start and end apart: 19 -> 20, of which waited for: 11 -> 11; matrix products, arithmetic and copies ran while one was open for 0% -> 0% of each run, Pallas kernels for 20% -> 25%
where the time goes in v7:
time: 79.3 us; the launch traced here: 79 us
  starting transfers between devices  31.7 us (40%)
  Pallas kernels  28.4 us (36%)
  waiting for transfers between devices  16.1 us (20%)
  local copies, waits for them, and re-layouts  1.85 us (2%)
  between operations  0.8 us (1%)
    ppermute x12, starting transfers between devices, swapped(): lax.ppermute(value, axis, [(source, source ^ bit) for source in range(cou...  16.1 us
    ppermute x6, starting transfers between devices, mesh_permute(): lax.ppermute(value, axes, [(source, source ^ mask) for source in range(co...  11.3 us
    pallas_call x4, Pallas kernels, shards_of_two_rows(): call(functools.partial(near_kernel, 4, c), specs, [chunk_block, whole(nea...  11 us
    ppermute x12, waiting for transfers between devices, swapped(): lax.ppermute(value, axis, [(source, source ^ bit) for source in range(cou...  8.83 us
    ppermute x6, waiting for transfers between devices, mesh_permute(): lax.ppermute(value, axes, [(source, source ^ mask) for source in range(co...  7.28 us
    pallas_call x1, Pallas kernels, shards_of_two_rows(): call(functools.partial(far_kernel, 4), [smem] + [whole(x) for x in (stati...  5.88 us
    pallas_call x1, Pallas kernels, factor(): call(functools.partial(factor_kernel, scale), [smem, whole(mine), whole(m...  5.59 us
    ppermute x2, starting transfers between devices, beside(): lax.ppermute(value, 'tiles', [(a, b) for a, b in pairs if 0 <= b < count...  4.31 us
  transfers between devices with their start and end apart: 20, of which 11 were waited for; matrix products, arithmetic and copies ran while one was open for 0% of the time, Pallas kernels for 25%

profile of v7, /device:TPU:0, one launch (start us, length us, event | category | flops | bytes accessed | tf_op | source)
XLA Modules:
  0.0 79.0 jit_solution(9439246450392211257)
XLA Ops:
  0.6 2.3 %shard_map.69 = (f32[4,4,8,128]{3,2,1,0:T(8,128)}, f32[5,4,8,128]{3,2,1,0:T(8,128)}) custom-call(s32[1,4]{1,0:T(1,128)} %runs.1, f32[64,4,8,128]{3,2,1,0:T(8,128)} %omega.13, f32[3,4,8,128]{3,2,1,0:T(8,128)} %conductance.1, s32[8,128]{1,0:T(8,128)} %wet.13), custom_call_target="tpu_custom_call" | custom-call | bytes 1048576 | tf_op jit(solution)/shard_map/pallas_call | solution.py:964
  2.9 1.3 %collective-permute-start.1 = (f32[5,4,8,128]{3,2,1,0:T(8,128)}, f32[5,4,8,128]{3,2,1,0:T(8,128)S(1)}, u32[]{:S(2)}, u32[]{:S(2)}) collective-permute-start(f32[5,4,8,128]{3,2,1,0:T(8,128)} %get-tuple-element.38.edges), channel_id=1, source_target_pairs={{2,0},{4,2},{6,4},{8,6},{10,8},{12,10},{14,12},{18,16},{20,18},{22... | collective-permute-start | bytes 245768 | tf_op jit(solution)/shard_map/ppermute | solution.py:805
  4.2 3.0 %collective-permute-start = (f32[5,4,8,128]{3,2,1,0:T(8,128)}, f32[5,4,8,128]{3,2,1,0:T(8,128)S(1)}, u32[]{:S(2)}, u32[]{:S(2)}) collective-permute-start(f32[5,4,8,128]{3,2,1,0:T(8,128)} %get-tuple-element.38.edges), channel_id=1, source_target_pairs={{0,2},{2,4},{4,6},{6,8},{8,10},{10,12},{12,14},{16,18},{18,20},{20... | collective-permute-start | bytes 245768 | tf_op jit(solution)/shard_map/ppermute | solution.py:805
  7.2 0.0 copy-start.4
  7.2 0.1 pad_add_fusion.meta
  7.3 0.6 copy-done.4
  7.9 1.2 %copy-done = f32[64,4,8,128]{3,2,1,0:T(8,128)S(1)} copy-done((f32[64,4,8,128]{3,2,1,0:T(8,128)S(1)}, f32[64,4,8,128]{3,2,1,0:T(8,128)}, u32[]{:S(2)}) %copy-start) | copy-done | bytes 1048600
  9.2 0.7 shard_map.68
  9.8 4.1 %collective-permute-start.6 = (f32[8,4,8,128]{3,2,1,0:T(8,128)S(1)}, f32[8,4,8,128]{3,2,1,0:T(8,128)S(1)}, u32[]{:S(2)}, u32[]{:S(2)}) collective-permute-start(f32[8,4,8,128]{3,2,1,0:T(8,128)S(1)} %get-tuple-element.49), channel_id=1, source_target_pairs={{0,16},{2,18},{4,20},{6,22},{8,24},{10,26},{12,28},{14,30},{16,0},... | collective-permute-start | bytes 393224 | tf_op jit(solution)/shard_map/ppermute | solution.py:349
  13.9 0.0 collective-permute-done.left
  13.9 0.0 copy-start.3
  14.0 0.0 copy-start.5
  14.0 0.6 shard_map.71
  14.5 0.1 collective-permute-start.5
  14.7 2.8 %collective-permute-start.2 = (f32[8,4,8,128]{3,2,1,0:T(8,128)S(1)}, f32[8,4,8,128]{3,2,1,0:T(8,128)S(1)}, u32[]{:S(2)}, u32[]{:S(2)}) collective-permute-start(f32[8,4,8,128]{3,2,1,0:T(8,128)S(1)} %get-tuple-element.39), channel_id=1, source_target_pairs={{0,16},{2,18},{4,20},{6,22},{8,24},{10,26},{12,28},{14,30},{16,0},... | collective-permute-start | bytes 393224 | tf_op jit(solution)/shard_map/ppermute | solution.py:349
  17.5 5.9 %shard_map.70 = (f32[64,4,8,128]{3,2,1,0:T(8,128)S(1)}, f32[64,4,8,128]{3,2,1,0:T(8,128)S(1)}, f32[4,2,4,8,128]{4,3,2,1,0:T(8,128)S(1)}, f32[512,128]{1,0:T(8,128)S(1)}, f32[512,128]{1,0:T(8,128)S(1)}) custom-call(s32[4]{0:T(128)S(1)} %pad_add_fusion.meta, f32[4,4,8,128]{3,2,1,0:T(8,128)S(1)} %copy-done.2, f32[64,4,8,128]{3,2,1,0:T(8,128)S(1)} %copy-done.1, ...), custom_call_target="tpu_custom_call" | custom-call | flops 8000000000 | bytes 1048576 | tf_op jit(solution)/shard_map/pallas_call | solution.py:994
  23.4 1.6 %collective-permute-start.4 = (f32[512,128]{1,0:T(8,128)S(1)}, f32[512,128]{1,0:T(8,128)S(1)}, u32[]{:S(2)}, u32[]{:S(2)}) collective-permute-start(f32[512,128]{1,0:T(8,128)S(1)} %get-tuple-element.42), channel_id=1, source_target_pairs={{0,1},{1,0},{2,3},{3,2},{4,5},{5,4},{6,7},{7,6},{8,9},{9,8},{10,11... | collective-permute-start | bytes 786440 | tf_op jit(solution)/shard_map/ppermute | solution.py:349
  25.0 0.1 collective-permute-done.6.halo
  25.1 1.6 %collective-permute-done.5.rims = f32[18,8,128]{2,1,0:T(8,128)S(1)} collective-permute-done((f32[18,8,128]{2,1,0:T(8,128)S(1)}, f32[18,8,128]{2,1,0:T(8,128)S(1)}, u32[]{:S(2)}, u32[]{:S(2)}) %collective-permute-start.5) | collective-permute-done | bytes 73760 | tf_op jit(solution)/shard_map/ppermute | solution.py:349
  26.7 0.0 collective-permute-start.8
  26.7 1.1 %shard_map.72 = (f32[7,4,8,128]{3,2,1,0:T(8,128)S(1)}, f32[2,7,4,8,128]{4,3,2,1,0:T(8,128)S(1)}) custom-call(s32[4]{0:T(128)S(1)} %pad_add_fusion.meta, f32[4,4,8,128]{3,2,1,0:T(8,128)S(1)} %copy-done.2, f32[18,8,128]{2,1,0:T(8,128)S(1)} %collective-permute-done.5.rims, f32[5,4,8,128]{3,2,1,0:T(8,128)S(1)} %copy-done.3, ...), custom_call_target="tpu_custom_call" | custom-call | bytes 1048576 | tf_op jit(solution)/shard_map/pallas_call | solution.py:1005
  27.8 1.7 %collective-permute-done.2.halo = f32[8,4,8,128]{3,2,1,0:T(8,128)S(1)} collective-permute-done((f32[8,4,8,128]{3,2,1,0:T(8,128)S(1)}, f32[8,4,8,128]{3,2,1,0:T(8,128)S(1)}, u32[]{:S(2)}, u32[]{:S(2)}) %collective-permute-start.2) | collective-permute-done | bytes 131104 | tf_op jit(solution)/shard_map/ppermute | solution.py:349
  29.5 2.7 %shard_map.73 = (f32[64,4,8,128]{3,2,1,0:T(8,128)}, f32[128,128]{1,0:T(8,128)S(1)}, f32[128,128]{1,0:T(8,128)S(1)}) custom-call(s32[4]{0:T(128)S(1)} %pad_add_fusion.meta, f32[64,4,8,128]{3,2,1,0:T(8,128)S(1)} %copy-done.1, s32[8,128]{1,0:T(8,128)S(1)} %copy-done.4, f32[8,128]{1,0:T(8,128)S(1)} %copy-done.5, ...), custom_call_target="tpu_custom_call" | custom-call | flops 2000000000 | bytes 1048576 | tf_op jit(solution)/shard_map/pallas_call | solution.py:1028
  32.2 2.1 %collective-permute-start.9 = (f32[128,128]{1,0:T(8,128)S(1)}, f32[128,128]{1,0:T(8,128)S(1)}, u32[]{:S(2)}, u32[]{:S(2)}) collective-permute-start(f32[128,128]{1,0:T(8,128)S(1)} %get-tuple-element.56), channel_id=1, source_target_pairs={{0,1},{1,0},{2,3},{3,2},{4,5},{5,4},{6,7},{7,6},{8,9},{9,8},{10,11... | collective-permute-start | bytes 196616 | tf_op jit(solution)/shard_map/ppermute | solution.py:349
  34.3 1.3 %collective-permute-start.3 = (f32[8,4,8,128]{3,2,1,0:T(8,128)S(1)}, f32[8,4,8,128]{3,2,1,0:T(8,128)S(1)}, u32[]{:S(2)}, u32[]{:S(2)}) collective-permute-start(f32[8,4,8,128]{3,2,1,0:T(8,128)S(1)} %get-tuple-element.40), channel_id=1, source_target_pairs={{0,16},{2,18},{4,20},{6,22},{8,24},{10,26},{12,28},{14,30},{16,0},... | collective-permute-start | bytes 393224 | tf_op jit(solution)/shard_map/ppermute | solution.py:349
  35.6 1.1 %collective-permute-done.9.refs_4_ = f32[128,128]{1,0:T(8,128)S(1)} collective-permute-done((f32[128,128]{1,0:T(8,128)S(1)}, f32[128,128]{1,0:T(8,128)S(1)}, u32[]{:S(2)}, u32[]{:S(2)}) %collective-permute-start.9) | collective-permute-done | bytes 65568 | tf_op jit(solution)/shard_map/ppermute | solution.py:349
  36.7 2.7 %shard_map.74 = (f32[64,4,8,128]{3,2,1,0:T(8,128)}, f32[128,128]{1,0:T(8,128)S(1)}, f32[128,128]{1,0:T(8,128)S(1)}) custom-call(s32[4]{0:T(128)S(1)} %pad_add_fusion.meta, f32[64,4,8,128]{3,2,1,0:T(8,128)S(1)} %copy-done.1, s32[8,128]{1,0:T(8,128)S(1)} %copy-done.4, f32[8,128]{1,0:T(8,128)S(1)} %copy-done.5, ...), custom_call_target="tpu_custom_call", output_to_operand_aliasing={{0}: (13, {})} | custom-call | flops 2000000000 | bytes 1048576 | tf_op jit(solution)/shard_map/pallas_call | solution.py:1028
  39.4 1.9 %collective-permute-start.7 = (f32[128,128]{1,0:T(8,128)S(1)}, f32[128,128]{1,0:T(8,128)S(1)}, u32[]{:S(2)}, u32[]{:S(2)}) collective-permute-start(f32[128,128]{1,0:T(8,128)S(1)} %get-tuple-element.52), channel_id=1, source_target_pairs={{0,1},{1,0},{2,3},{3,2},{4,5},{5,4},{6,7},{7,6},{8,9},{9,8},{10,11... | collective-permute-start | bytes 196616 | tf_op jit(solution)/shard_map/ppermute | solution.py:349
  41.3 2.7 %shard_map.75 = (f32[64,4,8,128]{3,2,1,0:T(8,128)}, f32[128,128]{1,0:T(8,128)S(1)}, f32[128,128]{1,0:T(8,128)S(1)}) custom-call(s32[4]{0:T(128)S(1)} %pad_add_fusion.meta, f32[64,4,8,128]{3,2,1,0:T(8,128)S(1)} %copy-done.1, s32[8,128]{1,0:T(8,128)S(1)} %copy-done.4, f32[8,128]{1,0:T(8,128)S(1)} %copy-done.5, ...), custom_call_target="tpu_custom_call", output_to_operand_aliasing={{0}: (13, {})} | custom-call | flops 2000000000 | bytes 1048576 | tf_op jit(solution)/shard_map/pallas_call | solution.py:1028
  44.1 0.1 collective-permute-start.10
  44.2 2.7 %shard_map.76 = (f32[64,4,8,128]{3,2,1,0:T(8,128)}, f32[128,128]{1,0:T(8,128)S(1)}, f32[128,128]{1,0:T(8,128)S(1)}) custom-call(s32[4]{0:T(128)S(1)} %pad_add_fusion.meta, f32[64,4,8,128]{3,2,1,0:T(8,128)S(1)} %copy-done.1, s32[8,128]{1,0:T(8,128)S(1)} %copy-done.4, f32[8,128]{1,0:T(8,128)S(1)} %copy-done.5, ...), custom_call_target="tpu_custom_call", output_to_operand_aliasing={{0}: (13, {})} | custom-call | flops 2000000000 | bytes 1048576 | tf_op jit(solution)/shard_map/pallas_call | solution.py:1028
  46.9 1.9 %collective-permute-start.11 = (f32[128,128]{1,0:T(8,128)S(1)}, f32[128,128]{1,0:T(8,128)S(1)}, u32[]{:S(2)}, u32[]{:S(2)}) collective-permute-start(f32[128,128]{1,0:T(8,128)S(1)} %get-tuple-element.67), channel_id=1, source_target_pairs={{0,1},{1,0},{2,3},{3,2},{4,5},{5,4},{6,7},{7,6},{8,9},{9,8},{10,11... | collective-permute-start | bytes 196616 | tf_op jit(solution)/shard_map/ppermute | solution.py:349
  48.8 0.4 shard_map.77.far
  49.2 2.0 %collective-permute-done.11.refs_7_ = f32[128,128]{1,0:T(8,128)S(1)} collective-permute-done((f32[128,128]{1,0:T(8,128)S(1)}, f32[128,128]{1,0:T(8,128)S(1)}, u32[]{:S(2)}, u32[]{:S(2)}) %collective-permute-start.11) | collective-permute-done | bytes 65568 | tf_op jit(solution)/shard_map/ppermute | solution.py:349
  51.2 1.1 %shard_map.78 = (f32[48,128]{1,0:T(8,128)S(1)}, f32[48,128]{1,0:T(8,128)S(1)}) custom-call(s32[4]{0:T(128)S(1)} %pad_add_fusion.meta, f32[128,128]{1,0:T(8,128)S(1)} %shard_map.77.far, f32[128,128]{1,0:T(8,128)S(1)} %get-tuple-element.62.refs_0_, f32[128,128]{1,0:T(8,128)S(1)} %get-tuple-element.63.refs_1_, f32[128,128]{1,0:T(8,128)S(1)} %get-tuple-element.64.refs_2_, ...), custom_call_target="tpu_custom_call" | custom-call | bytes 1048576 | tf_op jit(solution)/shard_map/pallas_call | solution.py:1046
  52.3 0.1 collective-permute-start.12
  52.4 1.2 %collective-permute-done.12 = f32[48,128]{1,0:T(8,128)S(1)} collective-permute-done((f32[48,128]{1,0:T(8,128)S(1)}, f32[48,128]{1,0:T(8,128)S(1)}, u32[]{:S(2)}, u32[]{:S(2)}) %collective-permute-start.12) | collective-permute-done | bytes 24608 | tf_op jit(solution)/shard_map/ppermute | solution.py:349
  53.5 3.6 %collective-permute-start.15 = (f32[48,128]{1,0:T(8,128)S(1)}, f32[48,128]{1,0:T(8,128)S(1)}, u32[]{:S(2)}, u32[]{:S(2)}) collective-permute-start(f32[48,128]{1,0:T(8,128)S(1)} %add.27), channel_id=1, source_target_pairs={{0,5},{1,4},{2,7},{3,6},{4,1},{5,0},{6,3},{7,2},{8,13},{9,12},{10,... | collective-permute-start | bytes 73736 | tf_op jit(solution)/shard_map/ppermute | solution.py:355
  57.2 0.6 collective-permute-start.13
  57.8 1.2 %collective-permute-done.15 = f32[48,128]{1,0:T(8,128)S(1)} collective-permute-done((f32[48,128]{1,0:T(8,128)S(1)}, f32[48,128]{1,0:T(8,128)S(1)}, u32[]{:S(2)}, u32[]{:S(2)}) %collective-permute-start.15) | collective-permute-done | bytes 24608 | tf_op jit(solution)/shard_map/ppermute | solution.py:355
  59.0 2.0 %collective-permute-done.14 = f32[48,128]{1,0:T(8,128)S(1)} collective-permute-done((f32[48,128]{1,0:T(8,128)S(1)}, f32[48,128]{1,0:T(8,128)S(1)}, u32[]{:S(2)}, u32[]{:S(2)}) %collective-permute-start.14) | collective-permute-done | bytes 24608 | tf_op jit(solution)/shard_map/ppermute | solution.py:355
  61.0 6.4 %collective-permute-start.18 = (f32[48,128]{1,0:T(8,128)S(1)}, f32[48,128]{1,0:T(8,128)S(1)}, u32[]{:S(2)}, u32[]{:S(2)}) collective-permute-start(f32[48,128]{1,0:T(8,128)S(1)} %add_add_fusion.1), channel_id=1, source_target_pairs={{0,24},{1,25},{2,26},{3,27},{4,28},{5,29},{6,30},{7,31},{8,16},{9,... | collective-permute-start | bytes 73736 | tf_op jit(solution)/shard_map/ppermute | solution.py:355
  67.4 0.6 collective-permute-start.16
  68.1 1.2 %collective-permute-done.18 = f32[48,128]{1,0:T(8,128)S(1)} collective-permute-done((f32[48,128]{1,0:T(8,128)S(1)}, f32[48,128]{1,0:T(8,128)S(1)}, u32[]{:S(2)}, u32[]{:S(2)}) %collective-permute-start.18) | collective-permute-done | bytes 24608 | tf_op jit(solution)/shard_map/ppermute | solution.py:355
  69.3 2.9 %collective-permute-done.17 = f32[48,128]{1,0:T(8,128)S(1)} collective-permute-done((f32[48,128]{1,0:T(8,128)S(1)}, f32[48,128]{1,0:T(8,128)S(1)}, u32[]{:S(2)}, u32[]{:S(2)}) %collective-permute-start.17) | collective-permute-done | bytes 24608 | tf_op jit(solution)/shard_map/ppermute | solution.py:355
  72.2 0.1 collective-permute-start.19
  72.3 1.2 %collective-permute-done.19.other = f32[48,128]{1,0:T(8,128)S(1)} collective-permute-done((f32[48,128]{1,0:T(8,128)S(1)}, f32[48,128]{1,0:T(8,128)S(1)}, u32[]{:S(2)}, u32[]{:S(2)}) %collective-permute-start.19) | collective-permute-done | bytes 24608 | tf_op jit(solution)/shard_map/ppermute | solution.py:349
  73.4 5.6 %shard_map.79 = f32[128,128]{1,0:T(8,128)} custom-call(s32[4]{0:T(128)S(1)} %pad_add_fusion.meta, f32[48,128]{1,0:T(8,128)S(1)} %add_add_fusion.own, f32[48,128]{1,0:T(8,128)S(1)} %collective-permute-done.19.other), custom_call_target="tpu_custom_call" | custom-call | bytes 1048576 | tf_op jit(solution)/shard_map/pallas_call | solution.py:849
  (20 shorter events, 0.1 us)
Async XLA Ops:
  2.9 11.0 %collective-permute-start.1 = (f32[5,4,8,128]{3,2,1,0:T(8,128)}, f32[5,4,8,128]{3,2,1,0:T(8,128)S(1)}, u32[]{:S(2)}, u32[]{:S(2)}) collective-permute-start(f32[5,4,8,128]{3,2,1,0:T(8,128)} %get-tuple-element.38.edges), channel_id=1, source_target_pairs={{2,0},{4,2},{6,4},{8,6},{10,8},{12,10},{14,12},{18,16},{20,18},{22... | collective-permute-start | bytes 245768 | tf_op jit(solution)/shard_map/ppermute | solution.py:805
  4.2 9.8 %collective-permute-start = (f32[5,4,8,128]{3,2,1,0:T(8,128)}, f32[5,4,8,128]{3,2,1,0:T(8,128)S(1)}, u32[]{:S(2)}, u32[]{:S(2)}) collective-permute-start(f32[5,4,8,128]{3,2,1,0:T(8,128)} %get-tuple-element.38.edges), channel_id=1, source_target_pairs={{0,2},{2,4},{4,6},{6,8},{8,10},{10,12},{12,14},{16,18},{18,20},{20... | collective-permute-start | bytes 245768 | tf_op jit(solution)/shard_map/ppermute | solution.py:805
  7.2 0.7 copy-start.4
  7.9 1.2 %copy-start = (f32[64,4,8,128]{3,2,1,0:T(8,128)S(1)}, f32[64,4,8,128]{3,2,1,0:T(8,128)}, u32[]{:S(2)}) copy-start(f32[64,4,8,128]{3,2,1,0:T(8,128)} %omega.13) | copy-start | bytes 3145732
  9.2 4.8 %copy-start.2 = (f32[4,4,8,128]{3,2,1,0:T(8,128)S(1)}, f32[4,4,8,128]{3,2,1,0:T(8,128)}, u32[]{:S(2)}) copy-start(f32[4,4,8,128]{3,2,1,0:T(8,128)} %get-tuple-element.41.statics) | copy-start | bytes 196612
  9.2 8.4 %copy-start.1 = (f32[64,4,8,128]{3,2,1,0:T(8,128)S(1)}, f32[64,4,8,128]{3,2,1,0:T(8,128)}, u32[]{:S(2)}) copy-start(f32[64,4,8,128]{3,2,1,0:T(8,128)} %omega.13) | copy-start | bytes 3145732
  9.8 15.3 %collective-permute-start.6 = (f32[8,4,8,128]{3,2,1,0:T(8,128)S(1)}, f32[8,4,8,128]{3,2,1,0:T(8,128)S(1)}, u32[]{:S(2)}, u32[]{:S(2)}) collective-permute-start(f32[8,4,8,128]{3,2,1,0:T(8,128)S(1)} %get-tuple-element.49), channel_id=1, source_target_pairs={{0,16},{2,18},{4,20},{6,22},{8,24},{10,26},{12,28},{14,30},{16,0},... | collective-permute-start | bytes 393224 | tf_op jit(solution)/shard_map/ppermute | solution.py:349
  13.9 3.6 %copy-start.3 = (f32[5,4,8,128]{3,2,1,0:T(8,128)S(1)}, f32[5,4,8,128]{3,2,1,0:T(8,128)}, u32[]{:S(2)}) copy-start(f32[5,4,8,128]{3,2,1,0:T(8,128)} %get-tuple-element.38.edges) | copy-start | bytes 245764
  14.0 3.6 %copy-start.5 = (f32[8,128]{1,0:T(8,128)S(1)}, f32[8,128]{1,0:T(8,128)}, u32[]{:S(2)}) copy-start(f32[8,128]{1,0:T(8,128)} %volume.9) | copy-start | bytes 12292
  14.5 12.1 %collective-permute-start.5 = (f32[18,8,128]{2,1,0:T(8,128)S(1)}, f32[18,8,128]{2,1,0:T(8,128)S(1)}, u32[]{:S(2)}, u32[]{:S(2)}) collective-permute-start(f32[18,8,128]{2,1,0:T(8,128)S(1)} %shard_map.71), channel_id=1, source_target_pairs={{0,16},{2,18},{4,20},{6,22},{8,24},{10,26},{12,28},{14,30},{16,0},... | collective-permute-start | bytes 221192 | tf_op jit(solution)/shard_map/ppermute | solution.py:349
  14.7 14.8 %collective-permute-start.2 = (f32[8,4,8,128]{3,2,1,0:T(8,128)S(1)}, f32[8,4,8,128]{3,2,1,0:T(8,128)S(1)}, u32[]{:S(2)}, u32[]{:S(2)}) collective-permute-start(f32[8,4,8,128]{3,2,1,0:T(8,128)S(1)} %get-tuple-element.39), channel_id=1, source_target_pairs={{0,16},{2,18},{4,20},{6,22},{8,24},{10,26},{12,28},{14,30},{16,0},... | collective-permute-start | bytes 393224 | tf_op jit(solution)/shard_map/ppermute | solution.py:349
  23.4 13.3 %collective-permute-start.4 = (f32[512,128]{1,0:T(8,128)S(1)}, f32[512,128]{1,0:T(8,128)S(1)}, u32[]{:S(2)}, u32[]{:S(2)}) collective-permute-start(f32[512,128]{1,0:T(8,128)S(1)} %get-tuple-element.42), channel_id=1, source_target_pairs={{0,1},{1,0},{2,3},{3,2},{4,5},{5,4},{6,7},{7,6},{8,9},{9,8},{10,11... | collective-permute-start | bytes 786440 | tf_op jit(solution)/shard_map/ppermute | solution.py:349
  26.7 10.0 %collective-permute-start.8 = (f32[8,4,8,128]{3,2,1,0:T(8,128)S(1)}, f32[8,4,8,128]{3,2,1,0:T(8,128)S(1)}, u32[]{:S(2)}, u32[]{:S(2)}) collective-permute-start(f32[8,4,8,128]{3,2,1,0:T(8,128)S(1)} %get-tuple-element.55), channel_id=1, source_target_pairs={{0,16},{2,18},{4,20},{6,22},{8,24},{10,26},{12,28},{14,30},{16,0},... | collective-permute-start | bytes 393224 | tf_op jit(solution)/shard_map/ppermute | solution.py:349
  32.2 4.5 %collective-permute-start.9 = (f32[128,128]{1,0:T(8,128)S(1)}, f32[128,128]{1,0:T(8,128)S(1)}, u32[]{:S(2)}, u32[]{:S(2)}) collective-permute-start(f32[128,128]{1,0:T(8,128)S(1)} %get-tuple-element.56), channel_id=1, source_target_pairs={{0,1},{1,0},{2,3},{3,2},{4,5},{5,4},{6,7},{7,6},{8,9},{9,8},{10,11... | collective-permute-start | bytes 196616 | tf_op jit(solution)/shard_map/ppermute | solution.py:349
  34.3 9.9 %collective-permute-start.3 = (f32[8,4,8,128]{3,2,1,0:T(8,128)S(1)}, f32[8,4,8,128]{3,2,1,0:T(8,128)S(1)}, u32[]{:S(2)}, u32[]{:S(2)}) collective-permute-start(f32[8,4,8,128]{3,2,1,0:T(8,128)S(1)} %get-tuple-element.40), channel_id=1, source_target_pairs={{0,16},{2,18},{4,20},{6,22},{8,24},{10,26},{12,28},{14,30},{16,0},... | collective-permute-start | bytes 393224 | tf_op jit(solution)/shard_map/ppermute | solution.py:349
  39.4 4.8 %collective-permute-start.7 = (f32[128,128]{1,0:T(8,128)S(1)}, f32[128,128]{1,0:T(8,128)S(1)}, u32[]{:S(2)}, u32[]{:S(2)}) collective-permute-start(f32[128,128]{1,0:T(8,128)S(1)} %get-tuple-element.52), channel_id=1, source_target_pairs={{0,1},{1,0},{2,3},{3,2},{4,5},{5,4},{6,7},{7,6},{8,9},{9,8},{10,11... | collective-permute-start | bytes 196616 | tf_op jit(solution)/shard_map/ppermute | solution.py:349
  44.1 5.2 %collective-permute-start.10 = (f32[128,128]{1,0:T(8,128)S(1)}, f32[128,128]{1,0:T(8,128)S(1)}, u32[]{:S(2)}, u32[]{:S(2)}) collective-permute-start(f32[128,128]{1,0:T(8,128)S(1)} %get-tuple-element.66), channel_id=1, source_target_pairs={{0,1},{1,0},{2,3},{3,2},{4,5},{5,4},{6,7},{7,6},{8,9},{9,8},{10,11... | collective-permute-start | bytes 196616 | tf_op jit(solution)/shard_map/ppermute | solution.py:349
  46.9 4.3 %collective-permute-start.11 = (f32[128,128]{1,0:T(8,128)S(1)}, f32[128,128]{1,0:T(8,128)S(1)}, u32[]{:S(2)}, u32[]{:S(2)}) collective-permute-start(f32[128,128]{1,0:T(8,128)S(1)} %get-tuple-element.67), channel_id=1, source_target_pairs={{0,1},{1,0},{2,3},{3,2},{4,5},{5,4},{6,7},{7,6},{8,9},{9,8},{10,11... | collective-permute-start | bytes 196616 | tf_op jit(solution)/shard_map/ppermute | solution.py:349
  52.3 1.3 %collective-permute-start.12 = (f32[48,128]{1,0:T(8,128)S(1)}, f32[48,128]{1,0:T(8,128)S(1)}, u32[]{:S(2)}, u32[]{:S(2)}) collective-permute-start(f32[48,128]{1,0:T(8,128)S(1)} %get-tuple-element.69), channel_id=1, source_target_pairs={{0,2},{2,0},{4,6},{6,4},{8,10},{10,8},{12,14},{14,12},{16,18},{18,... | collective-permute-start | bytes 73736 | tf_op jit(solution)/shard_map/ppermute | solution.py:349
  53.5 5.4 %collective-permute-start.15 = (f32[48,128]{1,0:T(8,128)S(1)}, f32[48,128]{1,0:T(8,128)S(1)}, u32[]{:S(2)}, u32[]{:S(2)}) collective-permute-start(f32[48,128]{1,0:T(8,128)S(1)} %add.27), channel_id=1, source_target_pairs={{0,5},{1,4},{2,7},{3,6},{4,1},{5,0},{6,3},{7,2},{8,13},{9,12},{10,... | collective-permute-start | bytes 73736 | tf_op jit(solution)/shard_map/ppermute | solution.py:355
  57.2 3.8 %collective-permute-start.14 = (f32[48,128]{1,0:T(8,128)S(1)}, f32[48,128]{1,0:T(8,128)S(1)}, u32[]{:S(2)}, u32[]{:S(2)}) collective-permute-start(f32[48,128]{1,0:T(8,128)S(1)} %add.27), channel_id=1, source_target_pairs={{0,4},{1,5},{2,6},{3,7},{4,0},{5,1},{6,2},{7,3},{8,12},{9,13},{10,... | collective-permute-start | bytes 73736 | tf_op jit(solution)/shard_map/ppermute | solution.py:355
  57.2 3.8 %collective-permute-start.13 = (f32[48,128]{1,0:T(8,128)S(1)}, f32[48,128]{1,0:T(8,128)S(1)}, u32[]{:S(2)}, u32[]{:S(2)}) collective-permute-start(f32[48,128]{1,0:T(8,128)S(1)} %add.27), channel_id=1, source_target_pairs={{0,1},{1,0},{2,3},{3,2},{4,5},{5,4},{6,7},{7,6},{8,9},{9,8},{10,11... | collective-permute-start | bytes 73736 | tf_op jit(solution)/shard_map/ppermute | solution.py:355
  61.0 8.2 %collective-permute-start.18 = (f32[48,128]{1,0:T(8,128)S(1)}, f32[48,128]{1,0:T(8,128)S(1)}, u32[]{:S(2)}, u32[]{:S(2)}) collective-permute-start(f32[48,128]{1,0:T(8,128)S(1)} %add_add_fusion.1), channel_id=1, source_target_pairs={{0,24},{1,25},{2,26},{3,27},{4,28},{5,29},{6,30},{7,31},{8,16},{9,... | collective-permute-start | bytes 73736 | tf_op jit(solution)/shard_map/ppermute | solution.py:355
  67.4 4.7 %collective-permute-start.17 = (f32[48,128]{1,0:T(8,128)S(1)}, f32[48,128]{1,0:T(8,128)S(1)}, u32[]{:S(2)}, u32[]{:S(2)}) collective-permute-start(f32[48,128]{1,0:T(8,128)S(1)} %add_add_fusion.1), channel_id=1, source_target_pairs={{0,16},{1,17},{2,18},{3,19},{4,20},{5,21},{6,22},{7,23},{8,24},{9,... | collective-permute-start | bytes 73736 | tf_op jit(solution)/shard_map/ppermute | solution.py:355
  67.4 4.7 %collective-permute-start.16 = (f32[48,128]{1,0:T(8,128)S(1)}, f32[48,128]{1,0:T(8,128)S(1)}, u32[]{:S(2)}, u32[]{:S(2)}) collective-permute-start(f32[48,128]{1,0:T(8,128)S(1)} %add_add_fusion.1), channel_id=1, source_target_pairs={{0,8},{1,9},{2,10},{3,11},{4,12},{5,13},{6,14},{7,15},{8,0},{9,1},... | collective-permute-start | bytes 73736 | tf_op jit(solution)/shard_map/ppermute | solution.py:355
  72.2 1.3 %collective-permute-start.19 = (f32[48,128]{1,0:T(8,128)S(1)}, f32[48,128]{1,0:T(8,128)S(1)}, u32[]{:S(2)}, u32[]{:S(2)}) collective-permute-start(f32[48,128]{1,0:T(8,128)S(1)} %add_add_fusion.own), channel_id=1, source_target_pairs={{0,2},{2,0},{4,6},{6,4},{8,10},{10,8},{12,14},{14,12},{16,18},{18,... | collective-permute-start | bytes 73736 | tf_op jit(solution)/shard_map/ppermute | solution.py:349

commit v8 on v7

--- a/solution.py
+++ b/solution.py
@@ -306,14 +306,15 @@
 
 
 def gram_of_rows(slices, refs):
-    group = refs[0].shape[0] // slices
-    order = group * len(refs)
+    groups = [ref.shape[0] // slices for ref in refs]
+    order = sum(groups)
     exact = jnp.zeros((order, order), jnp.float32)
     cross = jnp.zeros((order, order), jnp.float32)
     for at in range(0, slices, 2):
         columns = []
         for i in range(2):
-            columns.append(jnp.concatenate([ref[pl.ds(at + i, group, slices), :] for ref in refs], axis=0))
+            picked = [ref[pl.ds(at + i, group, slices), :] for ref, group in zip(refs, groups)]
+            columns.append(jnp.concatenate(picked, axis=0))
         values = jnp.concatenate(columns, axis=1)
         high = values.astype(jnp.bfloat16)
         rest = (values - high.astype(jnp.float32)).astype(jnp.bfloat16)
@@ -492,7 +493,7 @@
             edge_out[chunk, level] = edge
 
 
-def face_kernel(meta, omega, wet, *row_outs):
+def face_kernel(first, meta, omega, wet, *row_outs):
     levels, rows, cols = omega.shape[1:]
     group = cols // EDGE
     is_first_row = meta[0] == 0
@@ -500,7 +501,8 @@
     for chunk, out in enumerate(row_outs):
         for level in range(levels):
             for pair in range(group // 2):
-                start = [omega[chunk * group + 2 * pair + i, level] * wet_cells for i in range(2)]
+                at = (first + chunk) * group + 2 * pair
+                start = [omega[at + i, level] * wet_cells for i in range(2)]
                 store_pair((out,), (pair, level), start[0], start[1], is_first_row)
 
 
@@ -726,10 +728,12 @@
 
 
 def near_kernel(
-    batch, chunk, meta, omega, wet, volume, halo, rims, left, right, weights, strip_weights, bound, strip_bound, final, *rest
+    batch, base, parts, meta, omega, wet, volume, rims, left, right, weights, strip_weights, bound, strip_bound, final, *rest
 ):
+    halos = rest[:parts]
     field_out, keep_out, send_out, cross_scratch, start = rest[-5:]
-    group, levels, rows, cols = omega.shape
+    levels, rows, cols = omega.shape[1:]
+    group = omega.shape[0] // parts
     shape = (rows, cols)
     is_first_row = meta[0] == 0
     keeps_low = meta[2] == 0
@@ -741,19 +745,6 @@
     wet_cells = wet[...].astype(jnp.float32)
     root = jnp.sqrt(volume[...])
 
-    near_edge = [None] * levels
-    for level in range(levels):
-        for pair in range(group // 2):
-            own = [omega[2 * pair + i, level] * wet_cells for i in range(2)]
-            two = near_rows(is_first_row, *own, halo[pair, level])
-            for i in range(2):
-                start[2 * pair + i, level] = two[i]
-                near_edge[level] = add_edge(near_edge[level], two[i], 2 * pair + i)
-    rim = [jnp.where(take, left[0, level], right[0, level]) for level in range(levels)]
-    near_rim = []
-    for level in range(0, levels, 2):
-        near_rim += near_rows(is_first_row, rim[level], rim[level + 1], rims[chunk * levels // 2 + level // 2])
-
     def around(bound_at, sweep):
         def kept(level):
             return jnp.broadcast_to(bound_at(level)[sweep : sweep + 1, :], shape)
@@ -763,26 +754,42 @@
             lambda value, level: jnp.where(bottom, kept(level), turn(value, -1, 0)),
         )
 
-    pairs = [strips(near_edge[level], near_rim[level]) for level in range(levels)]
-    state = [[pairs[level][s] for level in range(levels)] for s in range(2)]
-    for sweep in range(ITERS):
+    for part in range(parts):
+        near_edge = [None] * levels
         for level in range(levels):
-            cross_scratch[sweep, level] = crossing(state[0][level], state[1][level])
-        if sweep < ITERS - 1:
-            for s in range(2):
-                state[s] = plane_pass(
-                    state[s], lambda n, level: strip_weights[s, n, level],
-                    *around(lambda level: strip_bound[0, s, level], sweep), no_rim,
-                )
-
-    for first in range(0, group, batch):
+            for pair in range(group // 2):
+                at = part * group + 2 * pair
+                own = [omega[at + i, level] * wet_cells for i in range(2)]
+                two = near_rows(is_first_row, *own, halos[part][pair, level])
+                for i in range(2):
+                    start[at + i, level] = two[i]
+                    near_edge[level] = add_edge(near_edge[level], two[i], 2 * pair + i)
+        rim = [jnp.where(take, left[part, level], right[part, level]) for level in range(levels)]
+        near_rim = []
+        for level in range(0, levels, 2):
+            across = rims[(base + part) * levels // 2 + level // 2]
+            near_rim += near_rows(is_first_row, rim[level], rim[level + 1], across)
+        pairs = [strips(near_edge[level], near_rim[level]) for level in range(levels)]
+        state = [[pairs[level][s] for level in range(levels)] for s in range(2)]
+        for sweep in range(ITERS):
+            for level in range(levels):
+                cross_scratch[part, sweep, level] = crossing(state[0][level], state[1][level])
+            if sweep < ITERS - 1:
+                for s in range(2):
+                    state[s] = plane_pass(
+                        state[s], lambda n, level: strip_weights[s, n, level],
+                        *around(lambda level: strip_bound[part, s, level], sweep), no_rim,
+                    )
+
+    for first in range(0, parts * group, batch):
+        part = first // group
         fields = [[start[place, level] for level in range(levels)] for place in range(first, first + batch)]
         for sweep in range(ITERS):
             for i in range(batch):
                 fields[i] = plane_pass(
                     fields[i], lambda n, level: weights[n, level],
                     *around(lambda level: bound[first + i, level], sweep),
-                    lambda level: rim_of(cross_scratch[sweep, level], first + i),
+                    lambda level: rim_of(cross_scratch[part, sweep, level], (first + i) % group),
                 )
         for i in range(batch):
             scaled = []
@@ -960,6 +967,14 @@
     def vmem(*lead):
         return pltpu.VMEM(lead + plane, jnp.float32)
 
+    row_shape = f32(group // 2, levels, *plane)
+    chunk0 = call(
+        functools.partial(face_kernel, 0),
+        [smem, block((group, levels, *plane), 0, 0, 0, 0), whole(wet)],
+        [whole(row_shape)],
+        [row_shape],
+        limit=EDGE_LIMIT,
+    )(meta, omega, wet)
     edge_shapes = [f32(kinds, levels, *plane), f32(chunks + 1, levels, *plane)]
     statics, edges = call(
         edge_kernel,
@@ -967,12 +982,12 @@
         [whole(s) for s in edge_shapes],
         edge_shapes,
         limit=EDGE_LIMIT,
-    )(face_runs, omega, conductance, wet)
+    )(after(face_runs, chunk0), omega, conductance, wet)
     left = beside(edges, 1)
     right = beside(edges, -1)
-    row_shapes = [f32(group // 2, levels, *plane)] * chunks
-    messages = call(
-        face_kernel,
+    row_shapes = [row_shape] * (chunks - 1)
+    messages = chunk0 + call(
+        functools.partial(face_kernel, 1),
         [smem, whole(omega), whole(wet)],
         [whole(s) for s in row_shapes],
         row_shapes,
@@ -985,9 +1000,8 @@
     )
     rims = swapped(rims, "tiles", TGY)
     gates = [(left, right), (halos[0], rims)]
-    for c in range(1, chunks):
-        gate = gates[c - 1] if c <= 2 else halos[c - 2]
-        halos.append(swapped(after(messages[c], gate), "tiles", TGY))
+    for c in range(1, min(chunks, 3)):
+        halos.append(swapped(after(messages[c], gates[c - 1]), "tiles", TGY))
 
     far_shape = f32(vectors * half * rows, cols)
     far_shapes = [f32(*omega.shape), f32(*omega.shape), f32(chunks, 2, levels, *plane), far_shape, far_shape]
@@ -1011,31 +1025,36 @@
 
     field = None
     kept, sent = ([], [])
-    near_shape = f32(group * half * rows, cols)
-    for c in range(chunks):
-        waits = [(halos[1],), (far_received,)]
-        halo = after(halos[c], *(waits[c] if c < 2 else sent[c - 2 : c - 1]))
-        chunk_block = block((group, levels, *plane), c, 0, 0, 0)
-        edge_block = block((1, levels, *plane), c, 0, 0, 0)
-        operands = [meta, omega, wet, volume, halo, rims, left, right, weights, strip_weights, bound, strip_bound, final]
-        specs = [smem, chunk_block, whole(wet), whole(volume), whole(halo), whole(rims), edge_block, edge_block]
-        specs += [whole(weights), whole(strip_weights), chunk_block, block((1, 2, levels, *plane), c, 0, 0, 0, 0), chunk_block]
+    steps = [(0, 2)] + [(c, 1) for c in range(2, chunks)]
+    for base, parts in steps:
+        waits = [(), (far_received,)]
+        mine = after(halos[base : base + parts], *(waits[len(sent)] if len(sent) < 2 else ()))
+        chunk_block = block((parts * group, levels, *plane), base // parts, 0, 0, 0)
+        edge_block = block((parts, levels, *plane), base // parts, 0, 0, 0)
+        side_block = block((parts, 2, levels, *plane), base // parts, 0, 0, 0, 0)
+        operands = [meta, omega, wet, volume, rims, left, right, weights, strip_weights, bound, strip_bound, final, *mine]
+        specs = [smem, chunk_block, whole(wet), whole(volume), whole(rims), edge_block, edge_block]
+        specs += [whole(weights), whole(strip_weights), chunk_block, side_block, chunk_block]
+        specs += [whole(halo) for halo in mine]
         aliases = {}
         if field is not None:
             aliases = {len(operands): 0}
             operands.append(field)
             specs.append(pl.BlockSpec(memory_space=pl.ANY))
+        near_shape = f32(parts * group * half * rows, cols)
         field, keep, send = call(
-            functools.partial(near_kernel, 4, c),
+            functools.partial(near_kernel, 4, base, parts),
             specs,
             [chunk_block, whole(near_shape), whole(near_shape)],
             [f32(*omega.shape), near_shape, near_shape],
             flops=2 * 10**9,
-            scratch=[vmem(ITERS, levels), vmem(group, levels)],
+            scratch=[vmem(parts, ITERS, levels), vmem(parts * group, levels)],
             aliases=aliases,
         )(*operands)
         kept.append(keep)
         sent.append(swapped(send, "vec", 1))
+        if len(halos) < chunks:
+            halos.append(swapped(after(messages[len(halos)], keep), "tiles", TGY))
 
     order = 2 * vectors
     gram_shape = f32(order, order)
@@ -1045,7 +1064,7 @@
     half_gram = f32(3 * order // 8, order)
     mine, theirs = call(
         functools.partial(near_gram_kernel, half * rows),
-        [smem, whole(gram_shape)] + [whole(near_shape)] * (2 * chunks),
+        [smem, whole(gram_shape)] + [whole(x) for x in kept + sent],
         [whole(half_gram)] * 2,
         [half_gram] * 2,
     )(meta, far_gram, *kept, *sent)

time: 79.3 us -> 72.4 us (0.913)
  starting transfers between devices: 31.7 us -> 25.4 us
  waiting for transfers between devices: 16.1 us -> 15.1 us
    ppermute x6, starting transfers between devices: 11.3 us -> 7.94 us  [mesh_permute(): lax.ppermute(value, axes, [(source, source ^ mask) for source in range(co...]
    ppermute x12 -> x11, starting transfers between devices: 16.1 us -> 13 us  [swapped(): lax.ppermute(value, axis, [(source, source ^ bit) for source in range(cou...]
    ppermute x6, waiting for transfers between devices: 7.28 us -> 5.32 us  [mesh_permute(): lax.ppermute(value, axes, [(source, source ^ mask) for source in range(co...]
    ppermute x12 -> x11, waiting for transfers between devices: 8.83 us -> 9.78 us  [swapped(): lax.ppermute(value, axis, [(source, source ^ bit) for source in range(cou...]
    unnamed x12 -> x14, local copies, waits for them, and re-layouts: 1.85 us -> 1.41 us
  transfers between devices with their start and end apart: 20 -> 19, of which waited for: 11 -> 10; matrix products, arithmetic and copies ran while one was open for 0% -> 0% of each run, Pallas kernels for 25% -> 28%
where the time goes in v8:
time: 72.4 us; the launch traced here: 72.1 us
  Pallas kernels  28.8 us (40%)
  starting transfers between devices  25.4 us (35%)
  waiting for transfers between devices  15.1 us (21%)
  local copies, waits for them, and re-layouts  1.41 us (2%)
  between operations  0.82 us (1%)
    ppermute x11, starting transfers between devices, swapped(): lax.ppermute(value, axis, [(source, source ^ bit) for source in range(cou...  13 us
    ppermute x11, waiting for transfers between devices, swapped(): lax.ppermute(value, axis, [(source, source ^ bit) for source in range(cou...  9.78 us
    pallas_call x3, Pallas kernels, shards_of_two_rows(): call(functools.partial(near_kernel, 4, base, parts), specs, [chunk_block,...  9.53 us
    ppermute x6, starting transfers between devices, mesh_permute(): lax.ppermute(value, axes, [(source, source ^ mask) for source in range(co...  7.94 us
    pallas_call x1, Pallas kernels, shards_of_two_rows(): call(functools.partial(far_kernel, 4), [smem] + [whole(x) for x in (stati...  5.88 us
    pallas_call x1, Pallas kernels, factor(): call(functools.partial(factor_kernel, scale), [smem, whole(mine), whole(m...  5.77 us
    ppermute x6, waiting for transfers between devices, mesh_permute(): lax.ppermute(value, axes, [(source, source ^ mask) for source in range(co...  5.32 us
    ppermute x2, starting transfers between devices, beside(): lax.ppermute(value, 'tiles', [(a, b) for a, b in pairs if 0 <= b < count...  4.45 us
  transfers between devices with their start and end apart: 19, of which 10 were waited for; matrix products, arithmetic and copies ran while one was open for 0% of the time, Pallas kernels for 28%

profile of v8, /device:TPU:0, one launch (start us, length us, event | category | flops | bytes accessed | tf_op | source)
XLA Modules:
  0.0 72.1 jit_solution(1269862807470412674)
XLA Ops:
  0.7 0.6 pad_add_fusion.meta
  1.2 1.6 %shard_map.68 = f32[8,4,8,128]{3,2,1,0:T(8,128)} custom-call(s32[4]{0:T(128)} %pad_add_fusion.meta, f32[64,4,8,128]{3,2,1,0:T(8,128)} %omega.13, s32[8,128]{1,0:T(8,128)} %wet.13), custom_call_target="tpu_custom_call" | custom-call | bytes 1048576 | tf_op jit(solution)/shard_map/pallas_call | solution.py:971
  2.9 4.0 %collective-permute-start.3 = (f32[8,4,8,128]{3,2,1,0:T(8,128)}, f32[8,4,8,128]{3,2,1,0:T(8,128)S(1)}, u32[]{:S(2)}, u32[]{:S(2)}) collective-permute-start(f32[8,4,8,128]{3,2,1,0:T(8,128)} %shard_map.68), channel_id=1, source_target_pairs={{0,16},{2,18},{4,20},{6,22},{8,24},{10,26},{12,28},{14,30},{16,0},... | collective-permute-start | bytes 393224 | tf_op jit(solution)/shard_map/ppermute | solution.py:350
  6.9 2.2 %shard_map.69 = (f32[4,4,8,128]{3,2,1,0:T(8,128)}, f32[5,4,8,128]{3,2,1,0:T(8,128)}) custom-call(s32[1,4]{1,0:T(1,128)} %runs, f32[64,4,8,128]{3,2,1,0:T(8,128)} %omega.13, f32[3,4,8,128]{3,2,1,0:T(8,128)} %conductance.1, s32[8,128]{1,0:T(8,128)} %wet.13), custom_call_target="tpu_custom_call" | custom-call | bytes 1048576 | tf_op jit(solution)/shard_map/pallas_call | solution.py:979
  9.2 1.4 %collective-permute-start.1 = (f32[5,4,8,128]{3,2,1,0:T(8,128)}, f32[5,4,8,128]{3,2,1,0:T(8,128)S(1)}, u32[]{:S(2)}, u32[]{:S(2)}) collective-permute-start(f32[5,4,8,128]{3,2,1,0:T(8,128)} %get-tuple-element.34.edges), channel_id=1, source_target_pairs={{2,0},{4,2},{6,4},{8,6},{10,8},{12,10},{14,12},{18,16},{20,18},{22... | collective-permute-start | bytes 245768 | tf_op jit(solution)/shard_map/ppermute | solution.py:812
  10.6 3.0 %collective-permute-start = (f32[5,4,8,128]{3,2,1,0:T(8,128)}, f32[5,4,8,128]{3,2,1,0:T(8,128)S(1)}, u32[]{:S(2)}, u32[]{:S(2)}) collective-permute-start(f32[5,4,8,128]{3,2,1,0:T(8,128)} %get-tuple-element.34.edges), channel_id=1, source_target_pairs={{0,2},{2,4},{4,6},{6,8},{8,10},{10,12},{12,14},{16,18},{18,20},{20... | collective-permute-start | bytes 245768 | tf_op jit(solution)/shard_map/ppermute | solution.py:812
  13.7 0.0 copy-start
  13.7 1.2 %copy-done = f32[64,4,8,128]{3,2,1,0:T(8,128)S(1)} copy-done((f32[64,4,8,128]{3,2,1,0:T(8,128)S(1)}, f32[64,4,8,128]{3,2,1,0:T(8,128)}, u32[]{:S(2)}) %copy-start) | copy-done | bytes 1048600
  14.9 0.6 shard_map.73
  15.5 0.0 collective-permute-done.left
  15.5 0.2 copy-done.2
  15.7 0.6 shard_map.70
  16.3 0.1 collective-permute-start.2
  16.4 2.9 %collective-permute-start.4 = (f32[8,4,8,128]{3,2,1,0:T(8,128)S(1)}, f32[8,4,8,128]{3,2,1,0:T(8,128)S(1)}, u32[]{:S(2)}, u32[]{:S(2)}) collective-permute-start(f32[8,4,8,128]{3,2,1,0:T(8,128)S(1)} %get-tuple-element.42), channel_id=1, source_target_pairs={{0,16},{2,18},{4,20},{6,22},{8,24},{10,26},{12,28},{14,30},{16,0},... | collective-permute-start | bytes 393224 | tf_op jit(solution)/shard_map/ppermute | solution.py:350
  19.3 5.9 %shard_map.72 = (f32[64,4,8,128]{3,2,1,0:T(8,128)S(1)}, f32[64,4,8,128]{3,2,1,0:T(8,128)S(1)}, f32[4,2,4,8,128]{4,3,2,1,0:T(8,128)S(1)}, f32[512,128]{1,0:T(8,128)S(1)}, f32[512,128]{1,0:T(8,128)S(1)}) custom-call(s32[4]{0:T(128)S(1)} %copy-done.4, f32[4,4,8,128]{3,2,1,0:T(8,128)S(1)} %copy-done.2, f32[64,4,8,128]{3,2,1,0:T(8,128)S(1)} %copy-done.1, ...), custom_call_target="tpu_custom_call" | custom-call | flops 8000000000 | bytes 1048576 | tf_op jit(solution)/shard_map/pallas_call | solution.py:1008
  25.2 1.6 %collective-permute-start.7 = (f32[512,128]{1,0:T(8,128)S(1)}, f32[512,128]{1,0:T(8,128)S(1)}, u32[]{:S(2)}, u32[]{:S(2)}) collective-permute-start(f32[512,128]{1,0:T(8,128)S(1)} %get-tuple-element.49), channel_id=1, source_target_pairs={{0,1},{1,0},{2,3},{3,2},{4,5},{5,4},{6,7},{7,6},{8,9},{9,8},{10,11... | collective-permute-start | bytes 786440 | tf_op jit(solution)/shard_map/ppermute | solution.py:350
  26.8 0.3 collective-permute-start.6
  27.1 1.1 %shard_map.71 = (f32[7,4,8,128]{3,2,1,0:T(8,128)S(1)}, f32[2,7,4,8,128]{4,3,2,1,0:T(8,128)S(1)}) custom-call(s32[4]{0:T(128)S(1)} %copy-done.4, f32[4,4,8,128]{3,2,1,0:T(8,128)S(1)} %copy-done.2, f32[18,8,128]{2,1,0:T(8,128)S(1)} %collective-permute-done.2.rims, f32[5,4,8,128]{3,2,1,0:T(8,128)S(1)} %copy-done.3, ...), custom_call_target="tpu_custom_call" | custom-call | bytes 1048576 | tf_op jit(solution)/shard_map/pallas_call | solution.py:1019
  28.2 1.2 %collective-permute-done.4.rest_1_ = f32[8,4,8,128]{3,2,1,0:T(8,128)S(1)} collective-permute-done((f32[8,4,8,128]{3,2,1,0:T(8,128)S(1)}, f32[8,4,8,128]{3,2,1,0:T(8,128)S(1)}, u32[]{:S(2)}, u32[]{:S(2)}) %collective-permute-start.4) | collective-permute-done | bytes 131104 | tf_op jit(solution)/shard_map/ppermute | solution.py:350
  29.5 4.1 %shard_map.74 = (f32[64,4,8,128]{3,2,1,0:T(8,128)}, f32[256,128]{1,0:T(8,128)S(1)}, f32[256,128]{1,0:T(8,128)S(1)}) custom-call(s32[4]{0:T(128)S(1)} %copy-done.4, f32[64,4,8,128]{3,2,1,0:T(8,128)S(1)} %copy-done.1, s32[8,128]{1,0:T(8,128)S(1)} %copy-done.5, f32[8,128]{1,0:T(8,128)S(1)} %copy-done.6, f32[18,8,128]{2,1,0:T(8,128)S(1)} %collective-permute-done.2.rims, ...), custom_call_target="tpu_custom_call" | custom-call | flops 2000000000 | bytes 1048576 | tf_op jit(solution)/shard_map/pallas_call | solution.py:1045
  33.6 1.4 %collective-permute-start.5 = (f32[8,4,8,128]{3,2,1,0:T(8,128)S(1)}, f32[8,4,8,128]{3,2,1,0:T(8,128)S(1)}, u32[]{:S(2)}, u32[]{:S(2)}) collective-permute-start(f32[8,4,8,128]{3,2,1,0:T(8,128)S(1)} %get-tuple-element.46), channel_id=1, source_target_pairs={{0,16},{2,18},{4,20},{6,22},{8,24},{10,26},{12,28},{14,30},{16,0},... | collective-permute-start | bytes 393224 | tf_op jit(solution)/shard_map/ppermute | solution.py:350
  34.9 0.5 collective-permute-start.8
  35.4 0.0 collective-permute-done.6.rest_0_
  35.4 0.0 collective-permute-done.7.received
  35.4 2.7 %shard_map.75 = (f32[64,4,8,128]{3,2,1,0:T(8,128)}, f32[128,128]{1,0:T(8,128)S(1)}, f32[128,128]{1,0:T(8,128)S(1)}) custom-call(s32[4]{0:T(128)S(1)} %copy-done.4, f32[64,4,8,128]{3,2,1,0:T(8,128)S(1)} %copy-done.1, s32[8,128]{1,0:T(8,128)S(1)} %copy-done.5, f32[8,128]{1,0:T(8,128)S(1)} %copy-done.6, ...), custom_call_target="tpu_custom_call", output_to_operand_aliasing={{0}: (13, {})} | custom-call | flops 2000000000 | bytes 1048576 | tf_op jit(solution)/shard_map/pallas_call | solution.py:1045
  38.2 1.5 %collective-permute-start.9 = (f32[128,128]{1,0:T(8,128)S(1)}, f32[128,128]{1,0:T(8,128)S(1)}, u32[]{:S(2)}, u32[]{:S(2)}) collective-permute-start(f32[128,128]{1,0:T(8,128)S(1)} %get-tuple-element.58), channel_id=1, source_target_pairs={{0,1},{1,0},{2,3},{3,2},{4,5},{5,4},{6,7},{7,6},{8,9},{9,8},{10,11... | collective-permute-start | bytes 196616 | tf_op jit(solution)/shard_map/ppermute | solution.py:350
  39.7 2.8 %collective-permute-done.5.rest_0_ = f32[8,4,8,128]{3,2,1,0:T(8,128)S(1)} collective-permute-done((f32[8,4,8,128]{3,2,1,0:T(8,128)S(1)}, f32[8,4,8,128]{3,2,1,0:T(8,128)S(1)}, u32[]{:S(2)}, u32[]{:S(2)}) %collective-permute-start.5) | collective-permute-done | bytes 131104 | tf_op jit(solution)/shard_map/ppermute | solution.py:350
  42.5 2.7 %shard_map.76 = (f32[64,4,8,128]{3,2,1,0:T(8,128)}, f32[128,128]{1,0:T(8,128)S(1)}, f32[128,128]{1,0:T(8,128)S(1)}) custom-call(s32[4]{0:T(128)S(1)} %copy-done.4, f32[64,4,8,128]{3,2,1,0:T(8,128)S(1)} %copy-done.1, s32[8,128]{1,0:T(8,128)S(1)} %copy-done.5, f32[8,128]{1,0:T(8,128)S(1)} %copy-done.6, ...), custom_call_target="tpu_custom_call", output_to_operand_aliasing={{0}: (13, {})} | custom-call | flops 2000000000 | bytes 1048576 | tf_op jit(solution)/shard_map/pallas_call | solution.py:1045
  45.2 0.5 collective-permute-start.10
  45.7 0.4 shard_map.77.far
  46.1 0.0 collective-permute-done.8.refs_3_
  46.1 3.3 %collective-permute-done.10.refs_5_ = f32[128,128]{1,0:T(8,128)S(1)} collective-permute-done((f32[128,128]{1,0:T(8,128)S(1)}, f32[128,128]{1,0:T(8,128)S(1)}, u32[]{:S(2)}, u32[]{:S(2)}) %collective-permute-start.10) | collective-permute-done | bytes 65568 | tf_op jit(solution)/shard_map/ppermute | solution.py:350
  49.5 1.1 %shard_map.78 = (f32[48,128]{1,0:T(8,128)S(1)}, f32[48,128]{1,0:T(8,128)S(1)}) custom-call(s32[4]{0:T(128)S(1)} %copy-done.4, f32[128,128]{1,0:T(8,128)S(1)} %shard_map.77.far, f32[256,128]{1,0:T(8,128)S(1)} %get-tuple-element.45.refs_0_, f32[128,128]{1,0:T(8,128)S(1)} %get-tuple-element.55.refs_1_, f32[128,128]{1,0:T(8,128)S(1)} %get-tuple-element.56.refs_2_, ...), custom_call_target="tpu_custom_call" | custom-call | bytes 1048576 | tf_op jit(solution)/shard_map/pallas_call | solution.py:1065
  50.5 0.1 collective-permute-start.11
  50.6 1.2 %collective-permute-done.11 = f32[48,128]{1,0:T(8,128)S(1)} collective-permute-done((f32[48,128]{1,0:T(8,128)S(1)}, f32[48,128]{1,0:T(8,128)S(1)}, u32[]{:S(2)}, u32[]{:S(2)}) %collective-permute-start.11) | collective-permute-done | bytes 24608 | tf_op jit(solution)/shard_map/ppermute | solution.py:350
  51.8 2.3 %collective-permute-start.14 = (f32[48,128]{1,0:T(8,128)S(1)}, f32[48,128]{1,0:T(8,128)S(1)}, u32[]{:S(2)}, u32[]{:S(2)}) collective-permute-start(f32[48,128]{1,0:T(8,128)S(1)} %add.27), channel_id=1, source_target_pairs={{0,5},{1,4},{2,7},{3,6},{4,1},{5,0},{6,3},{7,2},{8,13},{9,12},{10,... | collective-permute-start | bytes 73736 | tf_op jit(solution)/shard_map/ppermute | solution.py:356
  54.0 1.2 %collective-permute-start.12 = (f32[48,128]{1,0:T(8,128)S(1)}, f32[48,128]{1,0:T(8,128)S(1)}, u32[]{:S(2)}, u32[]{:S(2)}) collective-permute-start(f32[48,128]{1,0:T(8,128)S(1)} %add.27), channel_id=1, source_target_pairs={{0,1},{1,0},{2,3},{3,2},{4,5},{5,4},{6,7},{7,6},{8,9},{9,8},{10,11... | collective-permute-start | bytes 73736 | tf_op jit(solution)/shard_map/ppermute | solution.py:356
  55.3 1.2 %collective-permute-done.14 = f32[48,128]{1,0:T(8,128)S(1)} collective-permute-done((f32[48,128]{1,0:T(8,128)S(1)}, f32[48,128]{1,0:T(8,128)S(1)}, u32[]{:S(2)}, u32[]{:S(2)}) %collective-permute-start.14) | collective-permute-done | bytes 24608 | tf_op jit(solution)/shard_map/ppermute | solution.py:356
  56.5 1.4 %collective-permute-done.13 = f32[48,128]{1,0:T(8,128)S(1)} collective-permute-done((f32[48,128]{1,0:T(8,128)S(1)}, f32[48,128]{1,0:T(8,128)S(1)}, u32[]{:S(2)}, u32[]{:S(2)}) %collective-permute-start.13) | collective-permute-done | bytes 24608 | tf_op jit(solution)/shard_map/ppermute | solution.py:356
  57.9 2.3 %collective-permute-start.17 = (f32[48,128]{1,0:T(8,128)S(1)}, f32[48,128]{1,0:T(8,128)S(1)}, u32[]{:S(2)}, u32[]{:S(2)}) collective-permute-start(f32[48,128]{1,0:T(8,128)S(1)} %add_add_fusion.1), channel_id=1, source_target_pairs={{0,24},{1,25},{2,26},{3,27},{4,28},{5,29},{6,30},{7,31},{8,16},{9,... | collective-permute-start | bytes 73736 | tf_op jit(solution)/shard_map/ppermute | solution.py:356
  60.2 0.8 %collective-permute-start.16 = (f32[48,128]{1,0:T(8,128)S(1)}, f32[48,128]{1,0:T(8,128)S(1)}, u32[]{:S(2)}, u32[]{:S(2)}) collective-permute-start(f32[48,128]{1,0:T(8,128)S(1)} %add_add_fusion.1), channel_id=1, source_target_pairs={{0,16},{1,17},{2,18},{3,19},{4,20},{5,21},{6,22},{7,23},{8,24},{9,... | collective-permute-start | bytes 73736 | tf_op jit(solution)/shard_map/ppermute | solution.py:356
  61.0 1.4 %collective-permute-start.15 = (f32[48,128]{1,0:T(8,128)S(1)}, f32[48,128]{1,0:T(8,128)S(1)}, u32[]{:S(2)}, u32[]{:S(2)}) collective-permute-start(f32[48,128]{1,0:T(8,128)S(1)} %add_add_fusion.1), channel_id=1, source_target_pairs={{0,8},{1,9},{2,10},{3,11},{4,12},{5,13},{6,14},{7,15},{8,0},{9,1},... | collective-permute-start | bytes 73736 | tf_op jit(solution)/shard_map/ppermute | solution.py:356
  62.3 1.2 %collective-permute-done.17 = f32[48,128]{1,0:T(8,128)S(1)} collective-permute-done((f32[48,128]{1,0:T(8,128)S(1)}, f32[48,128]{1,0:T(8,128)S(1)}, u32[]{:S(2)}, u32[]{:S(2)}) %collective-permute-start.17) | collective-permute-done | bytes 24608 | tf_op jit(solution)/shard_map/ppermute | solution.py:356
  63.6 1.4 %collective-permute-done.16 = f32[48,128]{1,0:T(8,128)S(1)} collective-permute-done((f32[48,128]{1,0:T(8,128)S(1)}, f32[48,128]{1,0:T(8,128)S(1)}, u32[]{:S(2)}, u32[]{:S(2)}) %collective-permute-start.16) | collective-permute-done | bytes 24608 | tf_op jit(solution)/shard_map/ppermute | solution.py:356
  65.0 0.1 collective-permute-done.15
  65.1 0.1 collective-permute-start.18
  65.2 1.2 %collective-permute-done.18.other = f32[48,128]{1,0:T(8,128)S(1)} collective-permute-done((f32[48,128]{1,0:T(8,128)S(1)}, f32[48,128]{1,0:T(8,128)S(1)}, u32[]{:S(2)}, u32[]{:S(2)}) %collective-permute-start.18) | collective-permute-done | bytes 24608 | tf_op jit(solution)/shard_map/ppermute | solution.py:350
  66.3 5.8 %shard_map.79 = f32[128,128]{1,0:T(8,128)} custom-call(s32[4]{0:T(128)S(1)} %copy-done.4, f32[48,128]{1,0:T(8,128)S(1)} %add_add_fusion.own, f32[48,128]{1,0:T(8,128)S(1)} %collective-permute-done.18.other), custom_call_target="tpu_custom_call" | custom-call | bytes 1048576 | tf_op jit(solution)/shard_map/pallas_call | solution.py:856
  (20 shorter events, 0.1 us)
Async XLA Ops:
  2.9 10.8 %copy-start.5 = (s32[8,128]{1,0:T(8,128)S(1)}, s32[8,128]{1,0:T(8,128)}, u32[]{:S(2)}) copy-start(s32[8,128]{1,0:T(8,128)} %wet.13) | copy-start | bytes 12292
  2.9 23.9 %collective-permute-start.3 = (f32[8,4,8,128]{3,2,1,0:T(8,128)}, f32[8,4,8,128]{3,2,1,0:T(8,128)S(1)}, u32[]{:S(2)}, u32[]{:S(2)}) collective-permute-start(f32[8,4,8,128]{3,2,1,0:T(8,128)} %shard_map.68), channel_id=1, source_target_pairs={{0,16},{2,18},{4,20},{6,22},{8,24},{10,26},{12,28},{14,30},{16,0},... | collective-permute-start | bytes 393224 | tf_op jit(solution)/shard_map/ppermute | solution.py:350
  9.2 4.5 %copy-start.4 = (s32[4]{0:T(128)S(1)}, s32[4]{0:T(128)}, u32[]{:S(2)}) copy-start(s32[4]{0:T(128)} %pad_add_fusion.meta) | copy-start | bytes 52
  9.2 6.4 %collective-permute-start.1 = (f32[5,4,8,128]{3,2,1,0:T(8,128)}, f32[5,4,8,128]{3,2,1,0:T(8,128)S(1)}, u32[]{:S(2)}, u32[]{:S(2)}) collective-permute-start(f32[5,4,8,128]{3,2,1,0:T(8,128)} %get-tuple-element.34.edges), channel_id=1, source_target_pairs={{2,0},{4,2},{6,4},{8,6},{10,8},{12,10},{14,12},{18,16},{20,18},{22... | collective-permute-start | bytes 245768 | tf_op jit(solution)/shard_map/ppermute | solution.py:812
  10.6 4.9 %collective-permute-start = (f32[5,4,8,128]{3,2,1,0:T(8,128)}, f32[5,4,8,128]{3,2,1,0:T(8,128)S(1)}, u32[]{:S(2)}, u32[]{:S(2)}) collective-permute-start(f32[5,4,8,128]{3,2,1,0:T(8,128)} %get-tuple-element.34.edges), channel_id=1, source_target_pairs={{0,2},{2,4},{4,6},{6,8},{8,10},{10,12},{12,14},{16,18},{18,20},{20... | collective-permute-start | bytes 245768 | tf_op jit(solution)/shard_map/ppermute | solution.py:812
  13.7 1.2 %copy-start = (f32[64,4,8,128]{3,2,1,0:T(8,128)S(1)}, f32[64,4,8,128]{3,2,1,0:T(8,128)}, u32[]{:S(2)}) copy-start(f32[64,4,8,128]{3,2,1,0:T(8,128)} %omega.13) | copy-start | bytes 3145732
  14.9 0.8 %copy-start.2 = (f32[4,4,8,128]{3,2,1,0:T(8,128)S(1)}, f32[4,4,8,128]{3,2,1,0:T(8,128)}, u32[]{:S(2)}) copy-start(f32[4,4,8,128]{3,2,1,0:T(8,128)} %get-tuple-element.33.statics) | copy-start | bytes 196612
  14.9 4.4 %copy-start.1 = (f32[64,4,8,128]{3,2,1,0:T(8,128)S(1)}, f32[64,4,8,128]{3,2,1,0:T(8,128)}, u32[]{:S(2)}) copy-start(f32[64,4,8,128]{3,2,1,0:T(8,128)} %omega.13) | copy-start | bytes 3145732
  15.7 3.6 %copy-start.3 = (f32[5,4,8,128]{3,2,1,0:T(8,128)S(1)}, f32[5,4,8,128]{3,2,1,0:T(8,128)}, u32[]{:S(2)}) copy-start(f32[5,4,8,128]{3,2,1,0:T(8,128)} %get-tuple-element.34.edges) | copy-start | bytes 245764
  15.7 3.6 %copy-start.6 = (f32[8,128]{1,0:T(8,128)S(1)}, f32[8,128]{1,0:T(8,128)}, u32[]{:S(2)}) copy-start(f32[8,128]{1,0:T(8,128)} %volume.7) | copy-start | bytes 12292
  16.3 10.5 %collective-permute-start.2 = (f32[18,8,128]{2,1,0:T(8,128)S(1)}, f32[18,8,128]{2,1,0:T(8,128)S(1)}, u32[]{:S(2)}, u32[]{:S(2)}) collective-permute-start(f32[18,8,128]{2,1,0:T(8,128)S(1)} %shard_map.70), channel_id=1, source_target_pairs={{0,16},{2,18},{4,20},{6,22},{8,24},{10,26},{12,28},{14,30},{16,0},... | collective-permute-start | bytes 221192 | tf_op jit(solution)/shard_map/ppermute | solution.py:350
  16.4 13.1 %collective-permute-start.4 = (f32[8,4,8,128]{3,2,1,0:T(8,128)S(1)}, f32[8,4,8,128]{3,2,1,0:T(8,128)S(1)}, u32[]{:S(2)}, u32[]{:S(2)}) collective-permute-start(f32[8,4,8,128]{3,2,1,0:T(8,128)S(1)} %get-tuple-element.42), channel_id=1, source_target_pairs={{0,16},{2,18},{4,20},{6,22},{8,24},{10,26},{12,28},{14,30},{16,0},... | collective-permute-start | bytes 393224 | tf_op jit(solution)/shard_map/ppermute | solution.py:350
  25.2 10.3 %collective-permute-start.7 = (f32[512,128]{1,0:T(8,128)S(1)}, f32[512,128]{1,0:T(8,128)S(1)}, u32[]{:S(2)}, u32[]{:S(2)}) collective-permute-start(f32[512,128]{1,0:T(8,128)S(1)} %get-tuple-element.49), channel_id=1, source_target_pairs={{0,1},{1,0},{2,3},{3,2},{4,5},{5,4},{6,7},{7,6},{8,9},{9,8},{10,11... | collective-permute-start | bytes 786440 | tf_op jit(solution)/shard_map/ppermute | solution.py:350
  26.8 8.7 %collective-permute-start.6 = (f32[8,4,8,128]{3,2,1,0:T(8,128)S(1)}, f32[8,4,8,128]{3,2,1,0:T(8,128)S(1)}, u32[]{:S(2)}, u32[]{:S(2)}) collective-permute-start(f32[8,4,8,128]{3,2,1,0:T(8,128)S(1)} %get-tuple-element.48), channel_id=1, source_target_pairs={{0,16},{2,18},{4,20},{6,22},{8,24},{10,26},{12,28},{14,30},{16,0},... | collective-permute-start | bytes 393224 | tf_op jit(solution)/shard_map/ppermute | solution.py:350
  33.6 8.9 %collective-permute-start.5 = (f32[8,4,8,128]{3,2,1,0:T(8,128)S(1)}, f32[8,4,8,128]{3,2,1,0:T(8,128)S(1)}, u32[]{:S(2)}, u32[]{:S(2)}) collective-permute-start(f32[8,4,8,128]{3,2,1,0:T(8,128)S(1)} %get-tuple-element.46), channel_id=1, source_target_pairs={{0,16},{2,18},{4,20},{6,22},{8,24},{10,26},{12,28},{14,30},{16,0},... | collective-permute-start | bytes 393224 | tf_op jit(solution)/shard_map/ppermute | solution.py:350
  34.9 11.2 %collective-permute-start.8 = (f32[256,128]{1,0:T(8,128)S(1)}, f32[256,128]{1,0:T(8,128)S(1)}, u32[]{:S(2)}, u32[]{:S(2)}) collective-permute-start(f32[256,128]{1,0:T(8,128)S(1)} %get-tuple-element.57), channel_id=1, source_target_pairs={{0,1},{1,0},{2,3},{3,2},{4,5},{5,4},{6,7},{7,6},{8,9},{9,8},{10,11... | collective-permute-start | bytes 393224 | tf_op jit(solution)/shard_map/ppermute | solution.py:350
  38.2 7.9 %collective-permute-start.9 = (f32[128,128]{1,0:T(8,128)S(1)}, f32[128,128]{1,0:T(8,128)S(1)}, u32[]{:S(2)}, u32[]{:S(2)}) collective-permute-start(f32[128,128]{1,0:T(8,128)S(1)} %get-tuple-element.58), channel_id=1, source_target_pairs={{0,1},{1,0},{2,3},{3,2},{4,5},{5,4},{6,7},{7,6},{8,9},{9,8},{10,11... | collective-permute-start | bytes 196616 | tf_op jit(solution)/shard_map/ppermute | solution.py:350
  45.2 4.3 %collective-permute-start.10 = (f32[128,128]{1,0:T(8,128)S(1)}, f32[128,128]{1,0:T(8,128)S(1)}, u32[]{:S(2)}, u32[]{:S(2)}) collective-permute-start(f32[128,128]{1,0:T(8,128)S(1)} %get-tuple-element.59), channel_id=1, source_target_pairs={{0,1},{1,0},{2,3},{3,2},{4,5},{5,4},{6,7},{7,6},{8,9},{9,8},{10,11... | collective-permute-start | bytes 196616 | tf_op jit(solution)/shard_map/ppermute | solution.py:350
  50.5 1.3 %collective-permute-start.11 = (f32[48,128]{1,0:T(8,128)S(1)}, f32[48,128]{1,0:T(8,128)S(1)}, u32[]{:S(2)}, u32[]{:S(2)}) collective-permute-start(f32[48,128]{1,0:T(8,128)S(1)} %get-tuple-element.61), channel_id=1, source_target_pairs={{0,2},{2,0},{4,6},{6,4},{8,10},{10,8},{12,14},{14,12},{16,18},{18,... | collective-permute-start | bytes 73736 | tf_op jit(solution)/shard_map/ppermute | solution.py:350
  51.8 4.7 %collective-permute-start.14 = (f32[48,128]{1,0:T(8,128)S(1)}, f32[48,128]{1,0:T(8,128)S(1)}, u32[]{:S(2)}, u32[]{:S(2)}) collective-permute-start(f32[48,128]{1,0:T(8,128)S(1)} %add.27), channel_id=1, source_target_pairs={{0,5},{1,4},{2,7},{3,6},{4,1},{5,0},{6,3},{7,2},{8,13},{9,12},{10,... | collective-permute-start | bytes 73736 | tf_op jit(solution)/shard_map/ppermute | solution.py:356
  54.0 3.8 %collective-permute-start.13 = (f32[48,128]{1,0:T(8,128)S(1)}, f32[48,128]{1,0:T(8,128)S(1)}, u32[]{:S(2)}, u32[]{:S(2)}) collective-permute-start(f32[48,128]{1,0:T(8,128)S(1)} %add.27), channel_id=1, source_target_pairs={{0,4},{1,5},{2,6},{3,7},{4,0},{5,1},{6,2},{7,3},{8,12},{9,13},{10,... | collective-permute-start | bytes 73736 | tf_op jit(solution)/shard_map/ppermute | solution.py:356
  54.0 3.8 %collective-permute-start.12 = (f32[48,128]{1,0:T(8,128)S(1)}, f32[48,128]{1,0:T(8,128)S(1)}, u32[]{:S(2)}, u32[]{:S(2)}) collective-permute-start(f32[48,128]{1,0:T(8,128)S(1)} %add.27), channel_id=1, source_target_pairs={{0,1},{1,0},{2,3},{3,2},{4,5},{5,4},{6,7},{7,6},{8,9},{9,8},{10,11... | collective-permute-start | bytes 73736 | tf_op jit(solution)/shard_map/ppermute | solution.py:356
  57.9 5.7 %collective-permute-start.17 = (f32[48,128]{1,0:T(8,128)S(1)}, f32[48,128]{1,0:T(8,128)S(1)}, u32[]{:S(2)}, u32[]{:S(2)}) collective-permute-start(f32[48,128]{1,0:T(8,128)S(1)} %add_add_fusion.1), channel_id=1, source_target_pairs={{0,24},{1,25},{2,26},{3,27},{4,28},{5,29},{6,30},{7,31},{8,16},{9,... | collective-permute-start | bytes 73736 | tf_op jit(solution)/shard_map/ppermute | solution.py:356
  60.2 4.8 %collective-permute-start.16 = (f32[48,128]{1,0:T(8,128)S(1)}, f32[48,128]{1,0:T(8,128)S(1)}, u32[]{:S(2)}, u32[]{:S(2)}) collective-permute-start(f32[48,128]{1,0:T(8,128)S(1)} %add_add_fusion.1), channel_id=1, source_target_pairs={{0,16},{1,17},{2,18},{3,19},{4,20},{5,21},{6,22},{7,23},{8,24},{9,... | collective-permute-start | bytes 73736 | tf_op jit(solution)/shard_map/ppermute | solution.py:356
  61.0 4.1 %collective-permute-start.15 = (f32[48,128]{1,0:T(8,128)S(1)}, f32[48,128]{1,0:T(8,128)S(1)}, u32[]{:S(2)}, u32[]{:S(2)}) collective-permute-start(f32[48,128]{1,0:T(8,128)S(1)} %add_add_fusion.1), channel_id=1, source_target_pairs={{0,8},{1,9},{2,10},{3,11},{4,12},{5,13},{6,14},{7,15},{8,0},{9,1},... | collective-permute-start | bytes 73736 | tf_op jit(solution)/shard_map/ppermute | solution.py:356
  65.1 1.3 %collective-permute-start.18 = (f32[48,128]{1,0:T(8,128)S(1)}, f32[48,128]{1,0:T(8,128)S(1)}, u32[]{:S(2)}, u32[]{:S(2)}) collective-permute-start(f32[48,128]{1,0:T(8,128)S(1)} %add_add_fusion.own), channel_id=1, source_target_pairs={{0,2},{2,0},{4,6},{6,4},{8,10},{10,8},{12,14},{14,12},{16,18},{18,... | collective-permute-start | bytes 73736 | tf_op jit(solution)/shard_map/ppermute | solution.py:350

commit v9 on v8

--- a/solution.py
+++ b/solution.py
@@ -731,9 +731,10 @@
     batch, base, parts, meta, omega, wet, volume, rims, left, right, weights, strip_weights, bound, strip_bound, final, *rest
 ):
     halos = rest[:parts]
-    field_out, keep_out, send_out, cross_scratch, start = rest[-5:]
+    field_out, keep_out, send_out, cross_scratch, start, done, sems = rest[-7:]
     levels, rows, cols = omega.shape[1:]
-    group = omega.shape[0] // parts
+    group = cols // EDGE
+    offset = base * group
     shape = (rows, cols)
     is_first_row = meta[0] == 0
     keeps_low = meta[2] == 0
@@ -759,12 +760,12 @@
         for level in range(levels):
             for pair in range(group // 2):
                 at = part * group + 2 * pair
-                own = [omega[at + i, level] * wet_cells for i in range(2)]
+                own = [omega[offset + at + i, level] * wet_cells for i in range(2)]
                 two = near_rows(is_first_row, *own, halos[part][pair, level])
                 for i in range(2):
                     start[at + i, level] = two[i]
                     near_edge[level] = add_edge(near_edge[level], two[i], 2 * pair + i)
-        rim = [jnp.where(take, left[part, level], right[part, level]) for level in range(levels)]
+        rim = [jnp.where(take, left[base + part, level], right[base + part, level]) for level in range(levels)]
         near_rim = []
         for level in range(0, levels, 2):
             across = rims[(base + part) * levels // 2 + level // 2]
@@ -778,9 +779,10 @@
                 for s in range(2):
                     state[s] = plane_pass(
                         state[s], lambda n, level: strip_weights[s, n, level],
-                        *around(lambda level: strip_bound[part, s, level], sweep), no_rim,
+                        *around(lambda level: strip_bound[base + part, s, level], sweep), no_rim,
                     )
 
+    copies = []
     for first in range(0, parts * group, batch):
         part = first // group
         fields = [[start[place, level] for level in range(levels)] for place in range(first, first + batch)]
@@ -788,16 +790,24 @@
             for i in range(batch):
                 fields[i] = plane_pass(
                     fields[i], lambda n, level: weights[n, level],
-                    *around(lambda level: bound[first + i, level], sweep),
+                    *around(lambda level: bound[offset + first + i, level], sweep),
                     lambda level: rim_of(cross_scratch[part, sweep, level], (first + i) % group),
                 )
         for i in range(batch):
             scaled = []
             for level in range(levels):
-                value = jnp.where(is_near, turn(fields[i][level], ITERS, 0), final[first + i, level])
-                field_out[first + i, level] = value
+                value = jnp.where(is_near, turn(fields[i][level], ITERS, 0), final[offset + first + i, level])
+                done[first + i, level] = value
                 scaled.append(value * root)
             store_half(keep_out, send_out, first + i, pack_levels(scaled, jnp.logical_not(is_first_row)), keeps_low)
+        copies.append(
+            pltpu.make_async_copy(
+                done.at[pl.ds(first, batch)], field_out.at[pl.ds(offset + first, batch)], sems.at[first // batch]
+            )
+        )
+        copies[-1].start()
+    for copy in copies:
+        copy.wait()
 
 
 def shifted(value, axis, steps):
@@ -831,10 +841,10 @@
     return pl.BlockSpec(shape, lambda i: at)
 
 
-def call(kernel, in_specs, out_specs, out_shape, flops=0, scratch=(), aliases=None, limit=VMEM_LIMIT):
+def call(kernel, in_specs, out_specs, out_shape, flops=0, scratch=(), aliases=None, limit=VMEM_LIMIT, grid=(1,)):
     return pl.pallas_call(
         kernel,
-        grid=(1,),
+        grid=grid,
         in_specs=in_specs,
         out_specs=out_specs,
         out_shape=out_shape,
@@ -845,6 +855,10 @@
     )
 
 
+def resident(count):
+    return [pl.BlockSpec(memory_space=pltpu.VMEM)] * count
+
+
 def whole(array):
     zeros = (0,) * array.ndim
     return pl.BlockSpec(array.shape, lambda i: zeros)
@@ -855,9 +869,10 @@
     smem = pl.BlockSpec(memory_space=pltpu.SMEM)
     return call(
         functools.partial(factor_kernel, scale),
-        [smem, whole(mine), whole(mine)],
-        whole(f32(order, order)),
+        [smem] + resident(2),
+        resident(1)[0],
         f32(order, order),
+        grid=(),
     )(meta, mine, swapped(mine, "tiles", 1))
 
 
@@ -988,14 +1003,15 @@
     row_shapes = [row_shape] * (chunks - 1)
     messages = chunk0 + call(
         functools.partial(face_kernel, 1),
-        [smem, whole(omega), whole(wet)],
-        [whole(s) for s in row_shapes],
+        [smem] + resident(2),
+        resident(len(row_shapes)),
         row_shapes,
         flops=10**9,
+        grid=(),
     )(meta, omega, wet)
     halos = [swapped(messages[0], "tiles", TGY)]
     rim_shape = f32((chunks + 1) * levels // 2 + kinds // 2 * levels, *plane)
-    rims = call(rim_kernel, [smem, whole(statics), whole(left), whole(right)], whole(rim_shape), rim_shape)(
+    rims = call(rim_kernel, [smem] + resident(3), resident(1)[0], rim_shape, grid=())(
         meta, statics, left, right
     )
     rims = swapped(rims, "tiles", TGY)
@@ -1007,9 +1023,10 @@
     far_shapes = [f32(*omega.shape), f32(*omega.shape), f32(chunks, 2, levels, *plane), far_shape, far_shape]
     final, bound, strip_bound, far_kept, far_sent = call(
         functools.partial(far_kernel, 4),
-        [smem] + [whole(x) for x in (statics, omega, wet, volume, edges, left, right)],
-        [whole(s) for s in far_shapes],
+        [smem] + resident(7),
+        resident(len(far_shapes)),
         far_shapes,
+        grid=(),
         flops=8 * 10**9,
         scratch=[vmem(7, levels), vmem(2, 7, levels), vmem(chunks, ITERS, levels)],
     )(meta, statics, omega, wet, volume, edges, left, right)
@@ -1018,9 +1035,10 @@
     weight_shapes = [f32(7, levels, *plane), f32(2, 7, levels, *plane)]
     weights, strip_weights = call(
         near_weight_kernel,
-        [smem] + [whole(x) for x in (statics, rims, edges, left, right)],
-        [whole(s) for s in weight_shapes],
+        [smem] + resident(5),
+        resident(2),
         weight_shapes,
+        grid=(),
     )(meta, statics, rims, edges, left, right)
 
     field = None
@@ -1029,27 +1047,28 @@
     for base, parts in steps:
         waits = [(), (far_received,)]
         mine = after(halos[base : base + parts], *(waits[len(sent)] if len(sent) < 2 else ()))
-        chunk_block = block((parts * group, levels, *plane), base // parts, 0, 0, 0)
-        edge_block = block((parts, levels, *plane), base // parts, 0, 0, 0)
-        side_block = block((parts, 2, levels, *plane), base // parts, 0, 0, 0, 0)
         operands = [meta, omega, wet, volume, rims, left, right, weights, strip_weights, bound, strip_bound, final, *mine]
-        specs = [smem, chunk_block, whole(wet), whole(volume), whole(rims), edge_block, edge_block]
-        specs += [whole(weights), whole(strip_weights), chunk_block, side_block, chunk_block]
-        specs += [whole(halo) for halo in mine]
+        specs = [smem] + resident(len(operands) - 1)
         aliases = {}
         if field is not None:
             aliases = {len(operands): 0}
             operands.append(field)
             specs.append(pl.BlockSpec(memory_space=pl.ANY))
         near_shape = f32(parts * group * half * rows, cols)
+        batch = 4
+        count = parts * group
         field, keep, send = call(
-            functools.partial(near_kernel, 4, base, parts),
+            functools.partial(near_kernel, batch, base, parts),
             specs,
-            [chunk_block, whole(near_shape), whole(near_shape)],
+            [pl.BlockSpec(memory_space=pl.ANY)] + resident(2),
             [f32(*omega.shape), near_shape, near_shape],
             flops=2 * 10**9,
-            scratch=[vmem(parts, ITERS, levels), vmem(parts * group, levels)],
+            scratch=[
+                vmem(parts, ITERS, levels), vmem(count, levels), vmem(count, levels),
+                pltpu.SemaphoreType.DMA((count // batch,)),
+            ],
             aliases=aliases,
+            grid=(),
         )(*operands)
         kept.append(keep)
         sent.append(swapped(send, "vec", 1))
@@ -1059,14 +1078,15 @@
     order = 2 * vectors
     gram_shape = f32(order, order)
     far_gram = call(
-        functools.partial(far_gram_kernel, half * rows), [whole(far_shape)] * 2, whole(gram_shape), gram_shape
+        functools.partial(far_gram_kernel, half * rows), resident(2), resident(1)[0], gram_shape, grid=()
     )(far_kept, far_received)
     half_gram = f32(3 * order // 8, order)
     mine, theirs = call(
         functools.partial(near_gram_kernel, half * rows),
-        [smem, whole(gram_shape)] + [whole(x) for x in kept + sent],
-        [whole(half_gram)] * 2,
+        [smem] + resident(1 + len(kept + sent)),
+        resident(2),
         [half_gram] * 2,
+        grid=(),
     )(meta, far_gram, *kept, *sent)
     r_factor = factor(meta, mine, theirs, order, 1.0 / (levels * tiles * rows * cols))
     return (field, r_factor)

time: 72.4 us -> 72.4 us (level)
  no operation moved by 1% of the time
where the time goes in v9:
time: 72.4 us; the launch traced here: 72.2 us
  Pallas kernels  28.5 us (39%)
  starting transfers between devices  25.7 us (35%)
  waiting for transfers between devices  15.1 us (21%)
  local copies, waits for them, and re-layouts  1.41 us (2%)
  between operations  0.84 us (1%)
    ppermute x11, starting transfers between devices, swapped(): lax.ppermute(value, axis, [(source, source ^ bit) for source in range(cou...  13.4 us
    ppermute x11, waiting for transfers between devices, swapped(): lax.ppermute(value, axis, [(source, source ^ bit) for source in range(cou...  9.74 us
    pallas_call x3, Pallas kernels, shards_of_two_rows(): call(functools.partial(near_kernel, batch, base, parts), specs, [pl.Block...  9.37 us
    ppermute x6, starting transfers between devices, mesh_permute(): lax.ppermute(value, axes, [(source, source ^ mask) for source in range(co...  7.94 us
    pallas_call x1, Pallas kernels, shards_of_two_rows(): call(functools.partial(far_kernel, 4), [smem] + resident(7), resident(len...  5.88 us
    pallas_call x1, Pallas kernels, factor(): call(functools.partial(factor_kernel, scale), [smem] + resident(2), resid...  5.59 us
    ppermute x6, waiting for transfers between devices, mesh_permute(): lax.ppermute(value, axes, [(source, source ^ mask) for source in range(co...  5.36 us
    ppermute x2, starting transfers between devices, beside(): lax.ppermute(value, 'tiles', [(a, b) for a, b in pairs if 0 <= b < count...  4.45 us
  transfers between devices with their start and end apart: 19, of which 10 were waited for; matrix products, arithmetic and copies ran while one was open for 0% of the time, Pallas kernels for 28%

profile of v9, /device:TPU:0, one launch (start us, length us, event | category | flops | bytes accessed | tf_op | source)
XLA Modules:
  0.0 72.2 jit_solution(16409432729602491115)
XLA Ops:
  0.7 0.6 pad_add_fusion.meta
  1.2 1.6 %shard_map.68 = f32[8,4,8,128]{3,2,1,0:T(8,128)} custom-call(s32[4]{0:T(128)} %pad_add_fusion.meta, f32[64,4,8,128]{3,2,1,0:T(8,128)} %omega.13, s32[8,128]{1,0:T(8,128)} %wet.13), custom_call_target="tpu_custom_call" | custom-call | bytes 1048576 | tf_op jit(solution)/shard_map/pallas_call | solution.py:986
  2.9 4.0 %collective-permute-start.3 = (f32[8,4,8,128]{3,2,1,0:T(8,128)}, f32[8,4,8,128]{3,2,1,0:T(8,128)S(1)}, u32[]{:S(2)}, u32[]{:S(2)}) collective-permute-start(f32[8,4,8,128]{3,2,1,0:T(8,128)} %shard_map.68), channel_id=1, source_target_pairs={{0,16},{2,18},{4,20},{6,22},{8,24},{10,26},{12,28},{14,30},{16,0},... | collective-permute-start | bytes 393224 | tf_op jit(solution)/shard_map/ppermute | solution.py:350
  6.9 2.2 %shard_map.69 = (f32[4,4,8,128]{3,2,1,0:T(8,128)}, f32[5,4,8,128]{3,2,1,0:T(8,128)}) custom-call(s32[1,4]{1,0:T(1,128)} %runs, f32[64,4,8,128]{3,2,1,0:T(8,128)} %omega.13, f32[3,4,8,128]{3,2,1,0:T(8,128)} %conductance.1, s32[8,128]{1,0:T(8,128)} %wet.13), custom_call_target="tpu_custom_call" | custom-call | bytes 1048576 | tf_op jit(solution)/shard_map/pallas_call | solution.py:994
  9.2 1.4 %collective-permute-start.1 = (f32[5,4,8,128]{3,2,1,0:T(8,128)}, f32[5,4,8,128]{3,2,1,0:T(8,128)S(1)}, u32[]{:S(2)}, u32[]{:S(2)}) collective-permute-start(f32[5,4,8,128]{3,2,1,0:T(8,128)} %get-tuple-element.34.edges), channel_id=1, source_target_pairs={{2,0},{4,2},{6,4},{8,6},{10,8},{12,10},{14,12},{18,16},{20,18},{22... | collective-permute-start | bytes 245768 | tf_op jit(solution)/shard_map/ppermute | solution.py:822
  10.6 3.0 %collective-permute-start = (f32[5,4,8,128]{3,2,1,0:T(8,128)}, f32[5,4,8,128]{3,2,1,0:T(8,128)S(1)}, u32[]{:S(2)}, u32[]{:S(2)}) collective-permute-start(f32[5,4,8,128]{3,2,1,0:T(8,128)} %get-tuple-element.34.edges), channel_id=1, source_target_pairs={{0,2},{2,4},{4,6},{6,8},{8,10},{10,12},{12,14},{16,18},{18,20},{20... | collective-permute-start | bytes 245768 | tf_op jit(solution)/shard_map/ppermute | solution.py:822
  13.7 0.0 copy-start
  13.7 1.2 %copy-done = f32[64,4,8,128]{3,2,1,0:T(8,128)S(1)} copy-done((f32[64,4,8,128]{3,2,1,0:T(8,128)S(1)}, f32[64,4,8,128]{3,2,1,0:T(8,128)}, u32[]{:S(2)}) %copy-start) | copy-done | bytes 1048600
  14.9 0.6 shard_map.73
  15.5 0.0 collective-permute-done.1.right
  15.5 0.2 copy-done.2
  15.7 0.6 shard_map.70
  16.3 0.1 collective-permute-start.2
  16.4 2.9 %collective-permute-start.4 = (f32[8,4,8,128]{3,2,1,0:T(8,128)S(1)}, f32[8,4,8,128]{3,2,1,0:T(8,128)S(1)}, u32[]{:S(2)}, u32[]{:S(2)}) collective-permute-start(f32[8,4,8,128]{3,2,1,0:T(8,128)S(1)} %get-tuple-element.42), channel_id=1, source_target_pairs={{0,16},{2,18},{4,20},{6,22},{8,24},{10,26},{12,28},{14,30},{16,0},... | collective-permute-start | bytes 393224 | tf_op jit(solution)/shard_map/ppermute | solution.py:350
  19.3 5.9 %shard_map.72 = (f32[64,4,8,128]{3,2,1,0:T(8,128)S(1)}, f32[64,4,8,128]{3,2,1,0:T(8,128)S(1)}, f32[4,2,4,8,128]{4,3,2,1,0:T(8,128)S(1)}, f32[512,128]{1,0:T(8,128)S(1)}, f32[512,128]{1,0:T(8,128)S(1)}) custom-call(s32[4]{0:T(128)S(1)} %copy-done.4, f32[4,4,8,128]{3,2,1,0:T(8,128)S(1)} %copy-done.2, f32[64,4,8,128]{3,2,1,0:T(8,128)S(1)} %copy-done.1, ...), custom_call_target="tpu_custom_call" | custom-call | flops 8000000000 | bytes 1048576 | tf_op jit(solution)/shard_map/pallas_call | solution.py:1024
  25.2 1.6 %collective-permute-start.7 = (f32[512,128]{1,0:T(8,128)S(1)}, f32[512,128]{1,0:T(8,128)S(1)}, u32[]{:S(2)}, u32[]{:S(2)}) collective-permute-start(f32[512,128]{1,0:T(8,128)S(1)} %get-tuple-element.49), channel_id=1, source_target_pairs={{0,1},{1,0},{2,3},{3,2},{4,5},{5,4},{6,7},{7,6},{8,9},{9,8},{10,11... | collective-permute-start | bytes 786440 | tf_op jit(solution)/shard_map/ppermute | solution.py:350
  26.8 0.0 collective-permute-done.2.rims
  26.8 0.3 collective-permute-start.6
  27.1 1.1 %shard_map.71 = (f32[7,4,8,128]{3,2,1,0:T(8,128)S(1)}, f32[2,7,4,8,128]{4,3,2,1,0:T(8,128)S(1)}) custom-call(s32[4]{0:T(128)S(1)} %copy-done.4, f32[4,4,8,128]{3,2,1,0:T(8,128)S(1)} %copy-done.2, f32[18,8,128]{2,1,0:T(8,128)S(1)} %collective-permute-done.2.rims, f32[5,4,8,128]{3,2,1,0:T(8,128)S(1)} %copy-done.3, ...), custom_call_target="tpu_custom_call" | custom-call | bytes 1048576 | tf_op jit(solution)/shard_map/pallas_call | solution.py:1036
  28.2 1.2 %collective-permute-done.4.rest_1_ = f32[8,4,8,128]{3,2,1,0:T(8,128)S(1)} collective-permute-done((f32[8,4,8,128]{3,2,1,0:T(8,128)S(1)}, f32[8,4,8,128]{3,2,1,0:T(8,128)S(1)}, u32[]{:S(2)}, u32[]{:S(2)}) %collective-permute-start.4) | collective-permute-done | bytes 131104 | tf_op jit(solution)/shard_map/ppermute | solution.py:350
  29.5 4.0 %shard_map.74 = (f32[64,4,8,128]{3,2,1,0:T(8,128)}, f32[256,128]{1,0:T(8,128)S(1)}, f32[256,128]{1,0:T(8,128)S(1)}) custom-call(s32[4]{0:T(128)S(1)} %copy-done.4, f32[64,4,8,128]{3,2,1,0:T(8,128)S(1)} %copy-done.1, s32[8,128]{1,0:T(8,128)S(1)} %copy-done.5, f32[8,128]{1,0:T(8,128)S(1)} %copy-done.6, f32[18,8,128]{2,1,0:T(8,128)S(1)} %collective-permute-done.2.rims, ...), custom_call_target="tpu_custom_call" | custom-call | flops 2000000000 | bytes 1048576 | tf_op jit(solution)/shard_map/pallas_call | solution.py:1060
  33.5 1.4 %collective-permute-start.5 = (f32[8,4,8,128]{3,2,1,0:T(8,128)S(1)}, f32[8,4,8,128]{3,2,1,0:T(8,128)S(1)}, u32[]{:S(2)}, u32[]{:S(2)}) collective-permute-start(f32[8,4,8,128]{3,2,1,0:T(8,128)S(1)} %get-tuple-element.46), channel_id=1, source_target_pairs={{0,16},{2,18},{4,20},{6,22},{8,24},{10,26},{12,28},{14,30},{16,0},... | collective-permute-start | bytes 393224 | tf_op jit(solution)/shard_map/ppermute | solution.py:350
  34.9 0.5 collective-permute-start.8
  35.4 2.7 %shard_map.75 = (f32[64,4,8,128]{3,2,1,0:T(8,128)}, f32[128,128]{1,0:T(8,128)S(1)}, f32[128,128]{1,0:T(8,128)S(1)}) custom-call(s32[4]{0:T(128)S(1)} %copy-done.4, f32[64,4,8,128]{3,2,1,0:T(8,128)S(1)} %copy-done.1, s32[8,128]{1,0:T(8,128)S(1)} %copy-done.5, f32[8,128]{1,0:T(8,128)S(1)} %copy-done.6, ...), custom_call_target="tpu_custom_call", output_to_operand_aliasing={{0}: (13, {})} | custom-call | flops 2000000000 | bytes 1048576 | tf_op jit(solution)/shard_map/pallas_call | solution.py:1060
  38.1 1.6 %collective-permute-start.9 = (f32[128,128]{1,0:T(8,128)S(1)}, f32[128,128]{1,0:T(8,128)S(1)}, u32[]{:S(2)}, u32[]{:S(2)}) collective-permute-start(f32[128,128]{1,0:T(8,128)S(1)} %get-tuple-element.58), channel_id=1, source_target_pairs={{0,1},{1,0},{2,3},{3,2},{4,5},{5,4},{6,7},{7,6},{8,9},{9,8},{10,11... | collective-permute-start | bytes 196616 | tf_op jit(solution)/shard_map/ppermute | solution.py:350
  39.7 2.8 %collective-permute-done.5.rest_0_ = f32[8,4,8,128]{3,2,1,0:T(8,128)S(1)} collective-permute-done((f32[8,4,8,128]{3,2,1,0:T(8,128)S(1)}, f32[8,4,8,128]{3,2,1,0:T(8,128)S(1)}, u32[]{:S(2)}, u32[]{:S(2)}) %collective-permute-start.5) | collective-permute-done | bytes 131104 | tf_op jit(solution)/shard_map/ppermute | solution.py:350
  42.5 2.7 %shard_map.76 = (f32[64,4,8,128]{3,2,1,0:T(8,128)}, f32[128,128]{1,0:T(8,128)S(1)}, f32[128,128]{1,0:T(8,128)S(1)}) custom-call(s32[4]{0:T(128)S(1)} %copy-done.4, f32[64,4,8,128]{3,2,1,0:T(8,128)S(1)} %copy-done.1, s32[8,128]{1,0:T(8,128)S(1)} %copy-done.5, f32[8,128]{1,0:T(8,128)S(1)} %copy-done.6, ...), custom_call_target="tpu_custom_call", output_to_operand_aliasing={{0}: (13, {})} | custom-call | flops 2000000000 | bytes 1048576 | tf_op jit(solution)/shard_map/pallas_call | solution.py:1060
  45.1 0.6 collective-permute-start.10
  45.7 0.4 shard_map.77.far
  46.1 0.0 collective-permute-done.8.refs_3_
  46.1 3.3 %collective-permute-done.10.refs_5_ = f32[128,128]{1,0:T(8,128)S(1)} collective-permute-done((f32[128,128]{1,0:T(8,128)S(1)}, f32[128,128]{1,0:T(8,128)S(1)}, u32[]{:S(2)}, u32[]{:S(2)}) %collective-permute-start.10) | collective-permute-done | bytes 65568 | tf_op jit(solution)/shard_map/ppermute | solution.py:350
  49.5 1.1 %shard_map.78 = (f32[48,128]{1,0:T(8,128)S(1)}, f32[48,128]{1,0:T(8,128)S(1)}) custom-call(s32[4]{0:T(128)S(1)} %copy-done.4, f32[128,128]{1,0:T(8,128)S(1)} %shard_map.77.far, f32[256,128]{1,0:T(8,128)S(1)} %get-tuple-element.45.refs_0_, f32[128,128]{1,0:T(8,128)S(1)} %get-tuple-element.55.refs_1_, f32[128,128]{1,0:T(8,128)S(1)} %get-tuple-element.56.refs_2_, ...), custom_call_target="tpu_custom_call" | custom-call | bytes 1048576 | tf_op jit(solution)/shard_map/pallas_call | solution.py:1084
  50.5 0.1 collective-permute-start.11
  50.6 1.2 %collective-permute-done.11 = f32[48,128]{1,0:T(8,128)S(1)} collective-permute-done((f32[48,128]{1,0:T(8,128)S(1)}, f32[48,128]{1,0:T(8,128)S(1)}, u32[]{:S(2)}, u32[]{:S(2)}) %collective-permute-start.11) | collective-permute-done | bytes 24608 | tf_op jit(solution)/shard_map/ppermute | solution.py:350
  51.8 2.3 %collective-permute-start.14 = (f32[48,128]{1,0:T(8,128)S(1)}, f32[48,128]{1,0:T(8,128)S(1)}, u32[]{:S(2)}, u32[]{:S(2)}) collective-permute-start(f32[48,128]{1,0:T(8,128)S(1)} %add.27), channel_id=1, source_target_pairs={{0,5},{1,4},{2,7},{3,6},{4,1},{5,0},{6,3},{7,2},{8,13},{9,12},{10,... | collective-permute-start | bytes 73736 | tf_op jit(solution)/shard_map/ppermute | solution.py:356
  54.1 1.2 %collective-permute-start.12 = (f32[48,128]{1,0:T(8,128)S(1)}, f32[48,128]{1,0:T(8,128)S(1)}, u32[]{:S(2)}, u32[]{:S(2)}) collective-permute-start(f32[48,128]{1,0:T(8,128)S(1)} %add.27), channel_id=1, source_target_pairs={{0,1},{1,0},{2,3},{3,2},{4,5},{5,4},{6,7},{7,6},{8,9},{9,8},{10,11... | collective-permute-start | bytes 73736 | tf_op jit(solution)/shard_map/ppermute | solution.py:356
  55.3 1.2 %collective-permute-done.14 = f32[48,128]{1,0:T(8,128)S(1)} collective-permute-done((f32[48,128]{1,0:T(8,128)S(1)}, f32[48,128]{1,0:T(8,128)S(1)}, u32[]{:S(2)}, u32[]{:S(2)}) %collective-permute-start.14) | collective-permute-done | bytes 24608 | tf_op jit(solution)/shard_map/ppermute | solution.py:356
  56.5 1.4 %collective-permute-done.13 = f32[48,128]{1,0:T(8,128)S(1)} collective-permute-done((f32[48,128]{1,0:T(8,128)S(1)}, f32[48,128]{1,0:T(8,128)S(1)}, u32[]{:S(2)}, u32[]{:S(2)}) %collective-permute-start.13) | collective-permute-done | bytes 24608 | tf_op jit(solution)/shard_map/ppermute | solution.py:356
  57.9 0.0 collective-permute-done.12
  57.9 2.3 %collective-permute-start.17 = (f32[48,128]{1,0:T(8,128)S(1)}, f32[48,128]{1,0:T(8,128)S(1)}, u32[]{:S(2)}, u32[]{:S(2)}) collective-permute-start(f32[48,128]{1,0:T(8,128)S(1)} %add_add_fusion.1), channel_id=1, source_target_pairs={{0,24},{1,25},{2,26},{3,27},{4,28},{5,29},{6,30},{7,31},{8,16},{9,... | collective-permute-start | bytes 73736 | tf_op jit(solution)/shard_map/ppermute | solution.py:356
  60.2 0.8 %collective-permute-start.16 = (f32[48,128]{1,0:T(8,128)S(1)}, f32[48,128]{1,0:T(8,128)S(1)}, u32[]{:S(2)}, u32[]{:S(2)}) collective-permute-start(f32[48,128]{1,0:T(8,128)S(1)} %add_add_fusion.1), channel_id=1, source_target_pairs={{0,16},{1,17},{2,18},{3,19},{4,20},{5,21},{6,22},{7,23},{8,24},{9,... | collective-permute-start | bytes 73736 | tf_op jit(solution)/shard_map/ppermute | solution.py:356
  61.0 1.3 %collective-permute-start.15 = (f32[48,128]{1,0:T(8,128)S(1)}, f32[48,128]{1,0:T(8,128)S(1)}, u32[]{:S(2)}, u32[]{:S(2)}) collective-permute-start(f32[48,128]{1,0:T(8,128)S(1)} %add_add_fusion.1), channel_id=1, source_target_pairs={{0,8},{1,9},{2,10},{3,11},{4,12},{5,13},{6,14},{7,15},{8,0},{9,1},... | collective-permute-start | bytes 73736 | tf_op jit(solution)/shard_map/ppermute | solution.py:356
  62.4 1.2 %collective-permute-done.17 = f32[48,128]{1,0:T(8,128)S(1)} collective-permute-done((f32[48,128]{1,0:T(8,128)S(1)}, f32[48,128]{1,0:T(8,128)S(1)}, u32[]{:S(2)}, u32[]{:S(2)}) %collective-permute-start.17) | collective-permute-done | bytes 24608 | tf_op jit(solution)/shard_map/ppermute | solution.py:356
  63.6 1.4 %collective-permute-done.16 = f32[48,128]{1,0:T(8,128)S(1)} collective-permute-done((f32[48,128]{1,0:T(8,128)S(1)}, f32[48,128]{1,0:T(8,128)S(1)}, u32[]{:S(2)}, u32[]{:S(2)}) %collective-permute-start.16) | collective-permute-done | bytes 24608 | tf_op jit(solution)/shard_map/ppermute | solution.py:356
  65.0 0.1 collective-permute-done.15
  65.1 0.3 collective-permute-start.18
  65.4 1.2 %collective-permute-done.18.other = f32[48,128]{1,0:T(8,128)S(1)} collective-permute-done((f32[48,128]{1,0:T(8,128)S(1)}, f32[48,128]{1,0:T(8,128)S(1)}, u32[]{:S(2)}, u32[]{:S(2)}) %collective-permute-start.18) | collective-permute-done | bytes 24608 | tf_op jit(solution)/shard_map/ppermute | solution.py:350
  66.6 5.6 %shard_map.79 = f32[128,128]{1,0:T(8,128)} custom-call(s32[4]{0:T(128)S(1)} %copy-done.4, f32[48,128]{1,0:T(8,128)S(1)} %add_add_fusion.own, f32[48,128]{1,0:T(8,128)S(1)} %collective-permute-done.18.other), custom_call_target="tpu_custom_call" | custom-call | bytes 1048576 | tf_op jit(solution)/shard_map/pallas_call | solution.py:870
  (20 shorter events, 0.1 us)
Async XLA Ops:
  2.9 10.8 %copy-start.5 = (s32[8,128]{1,0:T(8,128)S(1)}, s32[8,128]{1,0:T(8,128)}, u32[]{:S(2)}) copy-start(s32[8,128]{1,0:T(8,128)} %wet.13) | copy-start | bytes 12292
  2.9 23.9 %collective-permute-start.3 = (f32[8,4,8,128]{3,2,1,0:T(8,128)}, f32[8,4,8,128]{3,2,1,0:T(8,128)S(1)}, u32[]{:S(2)}, u32[]{:S(2)}) collective-permute-start(f32[8,4,8,128]{3,2,1,0:T(8,128)} %shard_map.68), channel_id=1, source_target_pairs={{0,16},{2,18},{4,20},{6,22},{8,24},{10,26},{12,28},{14,30},{16,0},... | collective-permute-start | bytes 393224 | tf_op jit(solution)/shard_map/ppermute | solution.py:350
  9.2 4.5 %copy-start.4 = (s32[4]{0:T(128)S(1)}, s32[4]{0:T(128)}, u32[]{:S(2)}) copy-start(s32[4]{0:T(128)} %pad_add_fusion.meta) | copy-start | bytes 52
  9.2 6.4 %collective-permute-start.1 = (f32[5,4,8,128]{3,2,1,0:T(8,128)}, f32[5,4,8,128]{3,2,1,0:T(8,128)S(1)}, u32[]{:S(2)}, u32[]{:S(2)}) collective-permute-start(f32[5,4,8,128]{3,2,1,0:T(8,128)} %get-tuple-element.34.edges), channel_id=1, source_target_pairs={{2,0},{4,2},{6,4},{8,6},{10,8},{12,10},{14,12},{18,16},{20,18},{22... | collective-permute-start | bytes 245768 | tf_op jit(solution)/shard_map/ppermute | solution.py:822
  10.6 4.9 %collective-permute-start = (f32[5,4,8,128]{3,2,1,0:T(8,128)}, f32[5,4,8,128]{3,2,1,0:T(8,128)S(1)}, u32[]{:S(2)}, u32[]{:S(2)}) collective-permute-start(f32[5,4,8,128]{3,2,1,0:T(8,128)} %get-tuple-element.34.edges), channel_id=1, source_target_pairs={{0,2},{2,4},{4,6},{6,8},{8,10},{10,12},{12,14},{16,18},{18,20},{20... | collective-permute-start | bytes 245768 | tf_op jit(solution)/shard_map/ppermute | solution.py:822
  13.7 1.2 %copy-start = (f32[64,4,8,128]{3,2,1,0:T(8,128)S(1)}, f32[64,4,8,128]{3,2,1,0:T(8,128)}, u32[]{:S(2)}) copy-start(f32[64,4,8,128]{3,2,1,0:T(8,128)} %omega.13) | copy-start | bytes 3145732
  14.9 0.8 %copy-start.2 = (f32[4,4,8,128]{3,2,1,0:T(8,128)S(1)}, f32[4,4,8,128]{3,2,1,0:T(8,128)}, u32[]{:S(2)}) copy-start(f32[4,4,8,128]{3,2,1,0:T(8,128)} %get-tuple-element.33.statics) | copy-start | bytes 196612
  14.9 4.4 %copy-start.1 = (f32[64,4,8,128]{3,2,1,0:T(8,128)S(1)}, f32[64,4,8,128]{3,2,1,0:T(8,128)}, u32[]{:S(2)}) copy-start(f32[64,4,8,128]{3,2,1,0:T(8,128)} %omega.13) | copy-start | bytes 3145732
  15.7 3.6 %copy-start.3 = (f32[5,4,8,128]{3,2,1,0:T(8,128)S(1)}, f32[5,4,8,128]{3,2,1,0:T(8,128)}, u32[]{:S(2)}) copy-start(f32[5,4,8,128]{3,2,1,0:T(8,128)} %get-tuple-element.34.edges) | copy-start | bytes 245764
  15.7 3.6 %copy-start.6 = (f32[8,128]{1,0:T(8,128)S(1)}, f32[8,128]{1,0:T(8,128)}, u32[]{:S(2)}) copy-start(f32[8,128]{1,0:T(8,128)} %volume.7) | copy-start | bytes 12292
  16.3 10.5 %collective-permute-start.2 = (f32[18,8,128]{2,1,0:T(8,128)S(1)}, f32[18,8,128]{2,1,0:T(8,128)S(1)}, u32[]{:S(2)}, u32[]{:S(2)}) collective-permute-start(f32[18,8,128]{2,1,0:T(8,128)S(1)} %shard_map.70), channel_id=1, source_target_pairs={{0,16},{2,18},{4,20},{6,22},{8,24},{10,26},{12,28},{14,30},{16,0},... | collective-permute-start | bytes 221192 | tf_op jit(solution)/shard_map/ppermute | solution.py:350
  16.4 13.1 %collective-permute-start.4 = (f32[8,4,8,128]{3,2,1,0:T(8,128)S(1)}, f32[8,4,8,128]{3,2,1,0:T(8,128)S(1)}, u32[]{:S(2)}, u32[]{:S(2)}) collective-permute-start(f32[8,4,8,128]{3,2,1,0:T(8,128)S(1)} %get-tuple-element.42), channel_id=1, source_target_pairs={{0,16},{2,18},{4,20},{6,22},{8,24},{10,26},{12,28},{14,30},{16,0},... | collective-permute-start | bytes 393224 | tf_op jit(solution)/shard_map/ppermute | solution.py:350
  25.2 10.3 %collective-permute-start.7 = (f32[512,128]{1,0:T(8,128)S(1)}, f32[512,128]{1,0:T(8,128)S(1)}, u32[]{:S(2)}, u32[]{:S(2)}) collective-permute-start(f32[512,128]{1,0:T(8,128)S(1)} %get-tuple-element.49), channel_id=1, source_target_pairs={{0,1},{1,0},{2,3},{3,2},{4,5},{5,4},{6,7},{7,6},{8,9},{9,8},{10,11... | collective-permute-start | bytes 786440 | tf_op jit(solution)/shard_map/ppermute | solution.py:350
  26.8 8.7 %collective-permute-start.6 = (f32[8,4,8,128]{3,2,1,0:T(8,128)S(1)}, f32[8,4,8,128]{3,2,1,0:T(8,128)S(1)}, u32[]{:S(2)}, u32[]{:S(2)}) collective-permute-start(f32[8,4,8,128]{3,2,1,0:T(8,128)S(1)} %get-tuple-element.48), channel_id=1, source_target_pairs={{0,16},{2,18},{4,20},{6,22},{8,24},{10,26},{12,28},{14,30},{16,0},... | collective-permute-start | bytes 393224 | tf_op jit(solution)/shard_map/ppermute | solution.py:350
  33.5 9.0 %collective-permute-start.5 = (f32[8,4,8,128]{3,2,1,0:T(8,128)S(1)}, f32[8,4,8,128]{3,2,1,0:T(8,128)S(1)}, u32[]{:S(2)}, u32[]{:S(2)}) collective-permute-start(f32[8,4,8,128]{3,2,1,0:T(8,128)S(1)} %get-tuple-element.46), channel_id=1, source_target_pairs={{0,16},{2,18},{4,20},{6,22},{8,24},{10,26},{12,28},{14,30},{16,0},... | collective-permute-start | bytes 393224 | tf_op jit(solution)/shard_map/ppermute | solution.py:350
  34.9 11.2 %collective-permute-start.8 = (f32[256,128]{1,0:T(8,128)S(1)}, f32[256,128]{1,0:T(8,128)S(1)}, u32[]{:S(2)}, u32[]{:S(2)}) collective-permute-start(f32[256,128]{1,0:T(8,128)S(1)} %get-tuple-element.57), channel_id=1, source_target_pairs={{0,1},{1,0},{2,3},{3,2},{4,5},{5,4},{6,7},{7,6},{8,9},{9,8},{10,11... | collective-permute-start | bytes 393224 | tf_op jit(solution)/shard_map/ppermute | solution.py:350
  38.1 8.0 %collective-permute-start.9 = (f32[128,128]{1,0:T(8,128)S(1)}, f32[128,128]{1,0:T(8,128)S(1)}, u32[]{:S(2)}, u32[]{:S(2)}) collective-permute-start(f32[128,128]{1,0:T(8,128)S(1)} %get-tuple-element.58), channel_id=1, source_target_pairs={{0,1},{1,0},{2,3},{3,2},{4,5},{5,4},{6,7},{7,6},{8,9},{9,8},{10,11... | collective-permute-start | bytes 196616 | tf_op jit(solution)/shard_map/ppermute | solution.py:350
  45.1 4.3 %collective-permute-start.10 = (f32[128,128]{1,0:T(8,128)S(1)}, f32[128,128]{1,0:T(8,128)S(1)}, u32[]{:S(2)}, u32[]{:S(2)}) collective-permute-start(f32[128,128]{1,0:T(8,128)S(1)} %get-tuple-element.59), channel_id=1, source_target_pairs={{0,1},{1,0},{2,3},{3,2},{4,5},{5,4},{6,7},{7,6},{8,9},{9,8},{10,11... | collective-permute-start | bytes 196616 | tf_op jit(solution)/shard_map/ppermute | solution.py:350
  50.5 1.3 %collective-permute-start.11 = (f32[48,128]{1,0:T(8,128)S(1)}, f32[48,128]{1,0:T(8,128)S(1)}, u32[]{:S(2)}, u32[]{:S(2)}) collective-permute-start(f32[48,128]{1,0:T(8,128)S(1)} %get-tuple-element.61), channel_id=1, source_target_pairs={{0,2},{2,0},{4,6},{6,4},{8,10},{10,8},{12,14},{14,12},{16,18},{18,... | collective-permute-start | bytes 73736 | tf_op jit(solution)/shard_map/ppermute | solution.py:350
  51.8 4.7 %collective-permute-start.14 = (f32[48,128]{1,0:T(8,128)S(1)}, f32[48,128]{1,0:T(8,128)S(1)}, u32[]{:S(2)}, u32[]{:S(2)}) collective-permute-start(f32[48,128]{1,0:T(8,128)S(1)} %add.27), channel_id=1, source_target_pairs={{0,5},{1,4},{2,7},{3,6},{4,1},{5,0},{6,3},{7,2},{8,13},{9,12},{10,... | collective-permute-start | bytes 73736 | tf_op jit(solution)/shard_map/ppermute | solution.py:356
  54.1 3.8 %collective-permute-start.13 = (f32[48,128]{1,0:T(8,128)S(1)}, f32[48,128]{1,0:T(8,128)S(1)}, u32[]{:S(2)}, u32[]{:S(2)}) collective-permute-start(f32[48,128]{1,0:T(8,128)S(1)} %add.27), channel_id=1, source_target_pairs={{0,4},{1,5},{2,6},{3,7},{4,0},{5,1},{6,2},{7,3},{8,12},{9,13},{10,... | collective-permute-start | bytes 73736 | tf_op jit(solution)/shard_map/ppermute | solution.py:356
  54.1 3.8 %collective-permute-start.12 = (f32[48,128]{1,0:T(8,128)S(1)}, f32[48,128]{1,0:T(8,128)S(1)}, u32[]{:S(2)}, u32[]{:S(2)}) collective-permute-start(f32[48,128]{1,0:T(8,128)S(1)} %add.27), channel_id=1, source_target_pairs={{0,1},{1,0},{2,3},{3,2},{4,5},{5,4},{6,7},{7,6},{8,9},{9,8},{10,11... | collective-permute-start | bytes 73736 | tf_op jit(solution)/shard_map/ppermute | solution.py:356
  57.9 5.7 %collective-permute-start.17 = (f32[48,128]{1,0:T(8,128)S(1)}, f32[48,128]{1,0:T(8,128)S(1)}, u32[]{:S(2)}, u32[]{:S(2)}) collective-permute-start(f32[48,128]{1,0:T(8,128)S(1)} %add_add_fusion.1), channel_id=1, source_target_pairs={{0,24},{1,25},{2,26},{3,27},{4,28},{5,29},{6,30},{7,31},{8,16},{9,... | collective-permute-start | bytes 73736 | tf_op jit(solution)/shard_map/ppermute | solution.py:356
  60.2 4.8 %collective-permute-start.16 = (f32[48,128]{1,0:T(8,128)S(1)}, f32[48,128]{1,0:T(8,128)S(1)}, u32[]{:S(2)}, u32[]{:S(2)}) collective-permute-start(f32[48,128]{1,0:T(8,128)S(1)} %add_add_fusion.1), channel_id=1, source_target_pairs={{0,16},{1,17},{2,18},{3,19},{4,20},{5,21},{6,22},{7,23},{8,24},{9,... | collective-permute-start | bytes 73736 | tf_op jit(solution)/shard_map/ppermute | solution.py:356
  61.0 4.1 %collective-permute-start.15 = (f32[48,128]{1,0:T(8,128)S(1)}, f32[48,128]{1,0:T(8,128)S(1)}, u32[]{:S(2)}, u32[]{:S(2)}) collective-permute-start(f32[48,128]{1,0:T(8,128)S(1)} %add_add_fusion.1), channel_id=1, source_target_pairs={{0,8},{1,9},{2,10},{3,11},{4,12},{5,13},{6,14},{7,15},{8,0},{9,1},... | collective-permute-start | bytes 73736 | tf_op jit(solution)/shard_map/ppermute | solution.py:356
  65.1 1.4 %collective-permute-start.18 = (f32[48,128]{1,0:T(8,128)S(1)}, f32[48,128]{1,0:T(8,128)S(1)}, u32[]{:S(2)}, u32[]{:S(2)}) collective-permute-start(f32[48,128]{1,0:T(8,128)S(1)} %add_add_fusion.own), channel_id=1, source_target_pairs={{0,2},{2,0},{4,6},{6,4},{8,10},{10,8},{12,14},{14,12},{16,18},{18,... | collective-permute-start | bytes 73736 | tf_op jit(solution)/shard_map/ppermute | solution.py:350

commit v10 on v9

--- a/solution.py
+++ b/solution.py
@@ -1022,7 +1022,7 @@
     far_shape = f32(vectors * half * rows, cols)
     far_shapes = [f32(*omega.shape), f32(*omega.shape), f32(chunks, 2, levels, *plane), far_shape, far_shape]
     final, bound, strip_bound, far_kept, far_sent = call(
-        functools.partial(far_kernel, 4),
+        functools.partial(far_kernel, 8),
         [smem] + resident(7),
         resident(len(far_shapes)),
         far_shapes,
@@ -1055,7 +1055,7 @@
             operands.append(field)
             specs.append(pl.BlockSpec(memory_space=pl.ANY))
         near_shape = f32(parts * group * half * rows, cols)
-        batch = 4
+        batch = 8
         count = parts * group
         field, keep, send = call(
             functools.partial(near_kernel, batch, base, parts),

time: 72.4 us -> 72.5 us (level)
  starting transfers between devices: 25.7 us -> 28.6 us
  Pallas kernels: 28.5 us -> 26.3 us
    ppermute x11, starting transfers between devices: 13.4 us -> 16.2 us  [swapped(): lax.ppermute(value, axis, [(source, source ^ bit) for source in range(cou...]
    pallas_call x3, Pallas kernels: 9.37 us -> 8.12 us  [shards_of_two_rows(): call(functools.partial(near_kernel, batch, base, parts), specs, [pl.Block...]
    pallas_call x1, Pallas kernels: 5.88 us -> 4.84 us  [shards_of_two_rows(): call(functools.partial(far_kernel, 8), [smem] + resident(7), resident(len...]
    ppermute x11, waiting for transfers between devices: 9.74 us -> 8.77 us  [swapped(): lax.ppermute(value, axis, [(source, source ^ bit) for source in range(cou...]
  transfers between devices with their start and end apart: 19 -> 19, of which waited for: 10 -> 11; matrix products, arithmetic and copies ran while one was open for 0% -> 0% of each run, Pallas kernels for 28% -> 25%
where the time goes in v10:
time: 72.5 us; the launch traced here: 72.3 us
  starting transfers between devices  28.6 us (39%)
  Pallas kernels  26.3 us (36%)
  waiting for transfers between devices  14.5 us (20%)
  local copies, waits for them, and re-layouts  1.41 us (2%)
  between operations  0.84 us (1%)
    ppermute x11, starting transfers between devices, swapped(): lax.ppermute(value, axis, [(source, source ^ bit) for source in range(cou...  16.2 us
    ppermute x11, waiting for transfers between devices, swapped(): lax.ppermute(value, axis, [(source, source ^ bit) for source in range(cou...  8.77 us
    pallas_call x3, Pallas kernels, shards_of_two_rows(): call(functools.partial(near_kernel, batch, base, parts), specs, [pl.Block...  8.12 us
    ppermute x6, starting transfers between devices, mesh_permute(): lax.ppermute(value, axes, [(source, source ^ mask) for source in range(co...  7.94 us
    pallas_call x1, Pallas kernels, factor(): call(functools.partial(factor_kernel, scale), [smem] + resident(2), resid...  5.77 us
    ppermute x6, waiting for transfers between devices, mesh_permute(): lax.ppermute(value, axes, [(source, source ^ mask) for source in range(co...  5.72 us
    pallas_call x1, Pallas kernels, shards_of_two_rows(): call(functools.partial(far_kernel, 8), [smem] + resident(7), resident(len...  4.84 us
    ppermute x2, starting transfers between devices, beside(): lax.ppermute(value, 'tiles', [(a, b) for a, b in pairs if 0 <= b < count...  4.45 us
  transfers between devices with their start and end apart: 19, of which 11 were waited for; matrix products, arithmetic and copies ran while one was open for 0% of the time, Pallas kernels for 25%

profile of v10, /device:TPU:0, one launch (start us, length us, event | category | flops | bytes accessed | tf_op | source)
XLA Modules:
  0.0 72.3 jit_solution(6563282930465293945)
XLA Ops:
  0.7 0.6 pad_add_fusion.meta
  1.2 1.6 %shard_map.68 = f32[8,4,8,128]{3,2,1,0:T(8,128)} custom-call(s32[4]{0:T(128)} %pad_add_fusion.meta, f32[64,4,8,128]{3,2,1,0:T(8,128)} %omega.13, s32[8,128]{1,0:T(8,128)} %wet.13), custom_call_target="tpu_custom_call" | custom-call | bytes 1048576 | tf_op jit(solution)/shard_map/pallas_call | solution.py:986
  2.9 4.0 %collective-permute-start.3 = (f32[8,4,8,128]{3,2,1,0:T(8,128)}, f32[8,4,8,128]{3,2,1,0:T(8,128)S(1)}, u32[]{:S(2)}, u32[]{:S(2)}) collective-permute-start(f32[8,4,8,128]{3,2,1,0:T(8,128)} %shard_map.68), channel_id=1, source_target_pairs={{0,16},{2,18},{4,20},{6,22},{8,24},{10,26},{12,28},{14,30},{16,0},... | collective-permute-start | bytes 393224 | tf_op jit(solution)/shard_map/ppermute | solution.py:350
  6.9 2.2 %shard_map.69 = (f32[4,4,8,128]{3,2,1,0:T(8,128)}, f32[5,4,8,128]{3,2,1,0:T(8,128)}) custom-call(s32[1,4]{1,0:T(1,128)} %runs, f32[64,4,8,128]{3,2,1,0:T(8,128)} %omega.13, f32[3,4,8,128]{3,2,1,0:T(8,128)} %conductance.1, s32[8,128]{1,0:T(8,128)} %wet.13), custom_call_target="tpu_custom_call" | custom-call | bytes 1048576 | tf_op jit(solution)/shard_map/pallas_call | solution.py:994
  9.2 1.4 %collective-permute-start.1 = (f32[5,4,8,128]{3,2,1,0:T(8,128)}, f32[5,4,8,128]{3,2,1,0:T(8,128)S(1)}, u32[]{:S(2)}, u32[]{:S(2)}) collective-permute-start(f32[5,4,8,128]{3,2,1,0:T(8,128)} %get-tuple-element.34.edges), channel_id=1, source_target_pairs={{2,0},{4,2},{6,4},{8,6},{10,8},{12,10},{14,12},{18,16},{20,18},{22... | collective-permute-start | bytes 245768 | tf_op jit(solution)/shard_map/ppermute | solution.py:822
  10.6 3.0 %collective-permute-start = (f32[5,4,8,128]{3,2,1,0:T(8,128)}, f32[5,4,8,128]{3,2,1,0:T(8,128)S(1)}, u32[]{:S(2)}, u32[]{:S(2)}) collective-permute-start(f32[5,4,8,128]{3,2,1,0:T(8,128)} %get-tuple-element.34.edges), channel_id=1, source_target_pairs={{0,2},{2,4},{4,6},{6,8},{8,10},{10,12},{12,14},{16,18},{18,20},{20... | collective-permute-start | bytes 245768 | tf_op jit(solution)/shard_map/ppermute | solution.py:822
  13.7 0.0 copy-start
  13.7 1.2 %copy-done = f32[64,4,8,128]{3,2,1,0:T(8,128)S(1)} copy-done((f32[64,4,8,128]{3,2,1,0:T(8,128)S(1)}, f32[64,4,8,128]{3,2,1,0:T(8,128)}, u32[]{:S(2)}) %copy-start) | copy-done | bytes 1048600
  14.9 0.6 shard_map.73
  15.5 0.0 collective-permute-done.left
  15.5 0.2 copy-done.2
  15.7 0.6 shard_map.70
  16.3 0.1 collective-permute-start.2
  16.4 2.9 %collective-permute-start.4 = (f32[8,4,8,128]{3,2,1,0:T(8,128)S(1)}, f32[8,4,8,128]{3,2,1,0:T(8,128)S(1)}, u32[]{:S(2)}, u32[]{:S(2)}) collective-permute-start(f32[8,4,8,128]{3,2,1,0:T(8,128)S(1)} %get-tuple-element.42), channel_id=1, source_target_pairs={{0,16},{2,18},{4,20},{6,22},{8,24},{10,26},{12,28},{14,30},{16,0},... | collective-permute-start | bytes 393224 | tf_op jit(solution)/shard_map/ppermute | solution.py:350
  19.3 4.8 %shard_map.72 = (f32[64,4,8,128]{3,2,1,0:T(8,128)S(1)}, f32[64,4,8,128]{3,2,1,0:T(8,128)S(1)}, f32[4,2,4,8,128]{4,3,2,1,0:T(8,128)S(1)}, f32[512,128]{1,0:T(8,128)S(1)}, f32[512,128]{1,0:T(8,128)S(1)}) custom-call(s32[4]{0:T(128)S(1)} %copy-done.4, f32[4,4,8,128]{3,2,1,0:T(8,128)S(1)} %copy-done.2, f32[64,4,8,128]{3,2,1,0:T(8,128)S(1)} %copy-done.1, ...), custom_call_target="tpu_custom_call" | custom-call | flops 8000000000 | bytes 1048576 | tf_op jit(solution)/shard_map/pallas_call | solution.py:1024
  24.1 1.6 %collective-permute-start.7 = (f32[512,128]{1,0:T(8,128)S(1)}, f32[512,128]{1,0:T(8,128)S(1)}, u32[]{:S(2)}, u32[]{:S(2)}) collective-permute-start(f32[512,128]{1,0:T(8,128)S(1)} %get-tuple-element.49), channel_id=1, source_target_pairs={{0,1},{1,0},{2,3},{3,2},{4,5},{5,4},{6,7},{7,6},{8,9},{9,8},{10,11... | collective-permute-start | bytes 786440 | tf_op jit(solution)/shard_map/ppermute | solution.py:350
  25.7 0.3 collective-permute-start.6
  26.1 1.1 %shard_map.71 = (f32[7,4,8,128]{3,2,1,0:T(8,128)S(1)}, f32[2,7,4,8,128]{4,3,2,1,0:T(8,128)S(1)}) custom-call(s32[4]{0:T(128)S(1)} %copy-done.4, f32[4,4,8,128]{3,2,1,0:T(8,128)S(1)} %copy-done.2, f32[18,8,128]{2,1,0:T(8,128)S(1)} %collective-permute-done.2.rims, f32[5,4,8,128]{3,2,1,0:T(8,128)S(1)} %copy-done.3, ...), custom_call_target="tpu_custom_call" | custom-call | bytes 1048576 | tf_op jit(solution)/shard_map/pallas_call | solution.py:1036
  27.2 2.3 %collective-permute-done.4.rest_1_ = f32[8,4,8,128]{3,2,1,0:T(8,128)S(1)} collective-permute-done((f32[8,4,8,128]{3,2,1,0:T(8,128)S(1)}, f32[8,4,8,128]{3,2,1,0:T(8,128)S(1)}, u32[]{:S(2)}, u32[]{:S(2)}) %collective-permute-start.4) | collective-permute-done | bytes 131104 | tf_op jit(solution)/shard_map/ppermute | solution.py:350
  29.5 3.5 %shard_map.74 = (f32[64,4,8,128]{3,2,1,0:T(8,128)}, f32[256,128]{1,0:T(8,128)S(1)}, f32[256,128]{1,0:T(8,128)S(1)}) custom-call(s32[4]{0:T(128)S(1)} %copy-done.4, f32[64,4,8,128]{3,2,1,0:T(8,128)S(1)} %copy-done.1, s32[8,128]{1,0:T(8,128)S(1)} %copy-done.5, f32[8,128]{1,0:T(8,128)S(1)} %copy-done.6, f32[18,8,128]{2,1,0:T(8,128)S(1)} %collective-permute-done.2.rims, ...), custom_call_target="tpu_custom_call" | custom-call | flops 2000000000 | bytes 1048576 | tf_op jit(solution)/shard_map/pallas_call | solution.py:1060
  32.9 0.4 collective-permute-start.5
  33.3 1.3 %collective-permute-start.8 = (f32[256,128]{1,0:T(8,128)S(1)}, f32[256,128]{1,0:T(8,128)S(1)}, u32[]{:S(2)}, u32[]{:S(2)}) collective-permute-start(f32[256,128]{1,0:T(8,128)S(1)} %get-tuple-element.57), channel_id=1, source_target_pairs={{0,1},{1,0},{2,3},{3,2},{4,5},{5,4},{6,7},{7,6},{8,9},{9,8},{10,11... | collective-permute-start | bytes 393224 | tf_op jit(solution)/shard_map/ppermute | solution.py:350
  34.6 0.0 collective-permute-done.6.rest_0_
  34.6 2.3 %shard_map.75 = (f32[64,4,8,128]{3,2,1,0:T(8,128)}, f32[128,128]{1,0:T(8,128)S(1)}, f32[128,128]{1,0:T(8,128)S(1)}) custom-call(s32[4]{0:T(128)S(1)} %copy-done.4, f32[64,4,8,128]{3,2,1,0:T(8,128)S(1)} %copy-done.1, s32[8,128]{1,0:T(8,128)S(1)} %copy-done.5, f32[8,128]{1,0:T(8,128)S(1)} %copy-done.6, ...), custom_call_target="tpu_custom_call", output_to_operand_aliasing={{0}: (13, {})} | custom-call | flops 2000000000 | bytes 1048576 | tf_op jit(solution)/shard_map/pallas_call | solution.py:1060
  36.9 2.1 %collective-permute-start.9 = (f32[128,128]{1,0:T(8,128)S(1)}, f32[128,128]{1,0:T(8,128)S(1)}, u32[]{:S(2)}, u32[]{:S(2)}) collective-permute-start(f32[128,128]{1,0:T(8,128)S(1)} %get-tuple-element.58), channel_id=1, source_target_pairs={{0,1},{1,0},{2,3},{3,2},{4,5},{5,4},{6,7},{7,6},{8,9},{9,8},{10,11... | collective-permute-start | bytes 196616 | tf_op jit(solution)/shard_map/ppermute | solution.py:350
  39.0 2.1 %collective-permute-done.5.rest_0_ = f32[8,4,8,128]{3,2,1,0:T(8,128)S(1)} collective-permute-done((f32[8,4,8,128]{3,2,1,0:T(8,128)S(1)}, f32[8,4,8,128]{3,2,1,0:T(8,128)S(1)}, u32[]{:S(2)}, u32[]{:S(2)}) %collective-permute-start.5) | collective-permute-done | bytes 131104 | tf_op jit(solution)/shard_map/ppermute | solution.py:350
  41.1 2.3 %shard_map.76 = (f32[64,4,8,128]{3,2,1,0:T(8,128)}, f32[128,128]{1,0:T(8,128)S(1)}, f32[128,128]{1,0:T(8,128)S(1)}) custom-call(s32[4]{0:T(128)S(1)} %copy-done.4, f32[64,4,8,128]{3,2,1,0:T(8,128)S(1)} %copy-done.1, s32[8,128]{1,0:T(8,128)S(1)} %copy-done.5, f32[8,128]{1,0:T(8,128)S(1)} %copy-done.6, ...), custom_call_target="tpu_custom_call", output_to_operand_aliasing={{0}: (13, {})} | custom-call | flops 2000000000 | bytes 1048576 | tf_op jit(solution)/shard_map/pallas_call | solution.py:1060
  43.5 3.4 %collective-permute-start.10 = (f32[128,128]{1,0:T(8,128)S(1)}, f32[128,128]{1,0:T(8,128)S(1)}, u32[]{:S(2)}, u32[]{:S(2)}) collective-permute-start(f32[128,128]{1,0:T(8,128)S(1)} %get-tuple-element.59), channel_id=1, source_target_pairs={{0,1},{1,0},{2,3},{3,2},{4,5},{5,4},{6,7},{7,6},{8,9},{9,8},{10,11... | collective-permute-start | bytes 196616 | tf_op jit(solution)/shard_map/ppermute | solution.py:350
  46.9 0.4 shard_map.77.far
  47.3 2.0 %collective-permute-done.10.refs_5_ = f32[128,128]{1,0:T(8,128)S(1)} collective-permute-done((f32[128,128]{1,0:T(8,128)S(1)}, f32[128,128]{1,0:T(8,128)S(1)}, u32[]{:S(2)}, u32[]{:S(2)}) %collective-permute-start.10) | collective-permute-done | bytes 65568 | tf_op jit(solution)/shard_map/ppermute | solution.py:350
  49.2 1.1 %shard_map.78 = (f32[48,128]{1,0:T(8,128)S(1)}, f32[48,128]{1,0:T(8,128)S(1)}) custom-call(s32[4]{0:T(128)S(1)} %copy-done.4, f32[128,128]{1,0:T(8,128)S(1)} %shard_map.77.far, f32[256,128]{1,0:T(8,128)S(1)} %get-tuple-element.45.refs_0_, f32[128,128]{1,0:T(8,128)S(1)} %get-tuple-element.55.refs_1_, f32[128,128]{1,0:T(8,128)S(1)} %get-tuple-element.56.refs_2_, ...), custom_call_target="tpu_custom_call" | custom-call | bytes 1048576 | tf_op jit(solution)/shard_map/pallas_call | solution.py:1084
  50.3 0.1 collective-permute-start.11
  50.4 1.2 %collective-permute-done.11 = f32[48,128]{1,0:T(8,128)S(1)} collective-permute-done((f32[48,128]{1,0:T(8,128)S(1)}, f32[48,128]{1,0:T(8,128)S(1)}, u32[]{:S(2)}, u32[]{:S(2)}) %collective-permute-start.11) | collective-permute-done | bytes 24608 | tf_op jit(solution)/shard_map/ppermute | solution.py:350
  51.6 1.6 %collective-permute-start.14 = (f32[48,128]{1,0:T(8,128)S(1)}, f32[48,128]{1,0:T(8,128)S(1)}, u32[]{:S(2)}, u32[]{:S(2)}) collective-permute-start(f32[48,128]{1,0:T(8,128)S(1)} %add.27), channel_id=1, source_target_pairs={{0,5},{1,4},{2,7},{3,6},{4,1},{5,0},{6,3},{7,2},{8,13},{9,12},{10,... | collective-permute-start | bytes 73736 | tf_op jit(solution)/shard_map/ppermute | solution.py:356
  53.2 1.7 %collective-permute-start.13 = (f32[48,128]{1,0:T(8,128)S(1)}, f32[48,128]{1,0:T(8,128)S(1)}, u32[]{:S(2)}, u32[]{:S(2)}) collective-permute-start(f32[48,128]{1,0:T(8,128)S(1)} %add.27), channel_id=1, source_target_pairs={{0,4},{1,5},{2,6},{3,7},{4,0},{5,1},{6,2},{7,3},{8,12},{9,13},{10,... | collective-permute-start | bytes 73736 | tf_op jit(solution)/shard_map/ppermute | solution.py:356
  54.9 0.1 collective-permute-start.12
  55.0 1.2 %collective-permute-done.14 = f32[48,128]{1,0:T(8,128)S(1)} collective-permute-done((f32[48,128]{1,0:T(8,128)S(1)}, f32[48,128]{1,0:T(8,128)S(1)}, u32[]{:S(2)}, u32[]{:S(2)}) %collective-permute-start.14) | collective-permute-done | bytes 24608 | tf_op jit(solution)/shard_map/ppermute | solution.py:356
  56.3 0.7 collective-permute-done.13
  57.0 1.7 %collective-permute-done.12 = f32[48,128]{1,0:T(8,128)S(1)} collective-permute-done((f32[48,128]{1,0:T(8,128)S(1)}, f32[48,128]{1,0:T(8,128)S(1)}, u32[]{:S(2)}, u32[]{:S(2)}) %collective-permute-start.12) | collective-permute-done | bytes 24608 | tf_op jit(solution)/shard_map/ppermute | solution.py:356
  58.8 1.1 %collective-permute-start.17 = (f32[48,128]{1,0:T(8,128)S(1)}, f32[48,128]{1,0:T(8,128)S(1)}, u32[]{:S(2)}, u32[]{:S(2)}) collective-permute-start(f32[48,128]{1,0:T(8,128)S(1)} %add_add_fusion.1), channel_id=1, source_target_pairs={{0,24},{1,25},{2,26},{3,27},{4,28},{5,29},{6,30},{7,31},{8,16},{9,... | collective-permute-start | bytes 73736 | tf_op jit(solution)/shard_map/ppermute | solution.py:356
  59.9 0.6 collective-permute-start.16
  60.4 2.8 %collective-permute-start.15 = (f32[48,128]{1,0:T(8,128)S(1)}, f32[48,128]{1,0:T(8,128)S(1)}, u32[]{:S(2)}, u32[]{:S(2)}) collective-permute-start(f32[48,128]{1,0:T(8,128)S(1)} %add_add_fusion.1), channel_id=1, source_target_pairs={{0,8},{1,9},{2,10},{3,11},{4,12},{5,13},{6,14},{7,15},{8,0},{9,1},... | collective-permute-start | bytes 73736 | tf_op jit(solution)/shard_map/ppermute | solution.py:356
  63.2 1.2 %collective-permute-done.17 = f32[48,128]{1,0:T(8,128)S(1)} collective-permute-done((f32[48,128]{1,0:T(8,128)S(1)}, f32[48,128]{1,0:T(8,128)S(1)}, u32[]{:S(2)}, u32[]{:S(2)}) %collective-permute-start.17) | collective-permute-done | bytes 24608 | tf_op jit(solution)/shard_map/ppermute | solution.py:356
  64.5 0.5 collective-permute-done.16
  65.0 0.2 collective-permute-done.15
  65.2 0.1 collective-permute-start.18
  65.3 1.2 %collective-permute-done.18.other = f32[48,128]{1,0:T(8,128)S(1)} collective-permute-done((f32[48,128]{1,0:T(8,128)S(1)}, f32[48,128]{1,0:T(8,128)S(1)}, u32[]{:S(2)}, u32[]{:S(2)}) %collective-permute-start.18) | collective-permute-done | bytes 24608 | tf_op jit(solution)/shard_map/ppermute | solution.py:350
  66.5 5.8 %shard_map.79 = f32[128,128]{1,0:T(8,128)} custom-call(s32[4]{0:T(128)S(1)} %copy-done.4, f32[48,128]{1,0:T(8,128)S(1)} %add_add_fusion.own, f32[48,128]{1,0:T(8,128)S(1)} %collective-permute-done.18.other), custom_call_target="tpu_custom_call" | custom-call | bytes 1048576 | tf_op jit(solution)/shard_map/pallas_call | solution.py:870
  (20 shorter events, 0.1 us)
Async XLA Ops:
  2.9 10.8 %copy-start.5 = (s32[8,128]{1,0:T(8,128)S(1)}, s32[8,128]{1,0:T(8,128)}, u32[]{:S(2)}) copy-start(s32[8,128]{1,0:T(8,128)} %wet.13) | copy-start | bytes 12292
  2.9 22.8 %collective-permute-start.3 = (f32[8,4,8,128]{3,2,1,0:T(8,128)}, f32[8,4,8,128]{3,2,1,0:T(8,128)S(1)}, u32[]{:S(2)}, u32[]{:S(2)}) collective-permute-start(f32[8,4,8,128]{3,2,1,0:T(8,128)} %shard_map.68), channel_id=1, source_target_pairs={{0,16},{2,18},{4,20},{6,22},{8,24},{10,26},{12,28},{14,30},{16,0},... | collective-permute-start | bytes 393224 | tf_op jit(solution)/shard_map/ppermute | solution.py:350
  9.2 4.5 %copy-start.4 = (s32[4]{0:T(128)S(1)}, s32[4]{0:T(128)}, u32[]{:S(2)}) copy-start(s32[4]{0:T(128)} %pad_add_fusion.meta) | copy-start | bytes 52
  9.2 6.4 %collective-permute-start.1 = (f32[5,4,8,128]{3,2,1,0:T(8,128)}, f32[5,4,8,128]{3,2,1,0:T(8,128)S(1)}, u32[]{:S(2)}, u32[]{:S(2)}) collective-permute-start(f32[5,4,8,128]{3,2,1,0:T(8,128)} %get-tuple-element.34.edges), channel_id=1, source_target_pairs={{2,0},{4,2},{6,4},{8,6},{10,8},{12,10},{14,12},{18,16},{20,18},{22... | collective-permute-start | bytes 245768 | tf_op jit(solution)/shard_map/ppermute | solution.py:822
  10.6 4.9 %collective-permute-start = (f32[5,4,8,128]{3,2,1,0:T(8,128)}, f32[5,4,8,128]{3,2,1,0:T(8,128)S(1)}, u32[]{:S(2)}, u32[]{:S(2)}) collective-permute-start(f32[5,4,8,128]{3,2,1,0:T(8,128)} %get-tuple-element.34.edges), channel_id=1, source_target_pairs={{0,2},{2,4},{4,6},{6,8},{8,10},{10,12},{12,14},{16,18},{18,20},{20... | collective-permute-start | bytes 245768 | tf_op jit(solution)/shard_map/ppermute | solution.py:822
  13.7 1.2 %copy-start = (f32[64,4,8,128]{3,2,1,0:T(8,128)S(1)}, f32[64,4,8,128]{3,2,1,0:T(8,128)}, u32[]{:S(2)}) copy-start(f32[64,4,8,128]{3,2,1,0:T(8,128)} %omega.13) | copy-start | bytes 3145732
  14.9 0.8 %copy-start.2 = (f32[4,4,8,128]{3,2,1,0:T(8,128)S(1)}, f32[4,4,8,128]{3,2,1,0:T(8,128)}, u32[]{:S(2)}) copy-start(f32[4,4,8,128]{3,2,1,0:T(8,128)} %get-tuple-element.33.statics) | copy-start | bytes 196612
  14.9 4.4 %copy-start.1 = (f32[64,4,8,128]{3,2,1,0:T(8,128)S(1)}, f32[64,4,8,128]{3,2,1,0:T(8,128)}, u32[]{:S(2)}) copy-start(f32[64,4,8,128]{3,2,1,0:T(8,128)} %omega.13) | copy-start | bytes 3145732
  15.7 3.6 %copy-start.3 = (f32[5,4,8,128]{3,2,1,0:T(8,128)S(1)}, f32[5,4,8,128]{3,2,1,0:T(8,128)}, u32[]{:S(2)}) copy-start(f32[5,4,8,128]{3,2,1,0:T(8,128)} %get-tuple-element.34.edges) | copy-start | bytes 245764
  15.7 3.6 %copy-start.6 = (f32[8,128]{1,0:T(8,128)S(1)}, f32[8,128]{1,0:T(8,128)}, u32[]{:S(2)}) copy-start(f32[8,128]{1,0:T(8,128)} %volume.7) | copy-start | bytes 12292
  16.3 9.4 %collective-permute-start.2 = (f32[18,8,128]{2,1,0:T(8,128)S(1)}, f32[18,8,128]{2,1,0:T(8,128)S(1)}, u32[]{:S(2)}, u32[]{:S(2)}) collective-permute-start(f32[18,8,128]{2,1,0:T(8,128)S(1)} %shard_map.70), channel_id=1, source_target_pairs={{0,16},{2,18},{4,20},{6,22},{8,24},{10,26},{12,28},{14,30},{16,0},... | collective-permute-start | bytes 221192 | tf_op jit(solution)/shard_map/ppermute | solution.py:350
  16.4 13.1 %collective-permute-start.4 = (f32[8,4,8,128]{3,2,1,0:T(8,128)S(1)}, f32[8,4,8,128]{3,2,1,0:T(8,128)S(1)}, u32[]{:S(2)}, u32[]{:S(2)}) collective-permute-start(f32[8,4,8,128]{3,2,1,0:T(8,128)S(1)} %get-tuple-element.42), channel_id=1, source_target_pairs={{0,16},{2,18},{4,20},{6,22},{8,24},{10,26},{12,28},{14,30},{16,0},... | collective-permute-start | bytes 393224 | tf_op jit(solution)/shard_map/ppermute | solution.py:350
  24.1 10.5 %collective-permute-start.7 = (f32[512,128]{1,0:T(8,128)S(1)}, f32[512,128]{1,0:T(8,128)S(1)}, u32[]{:S(2)}, u32[]{:S(2)}) collective-permute-start(f32[512,128]{1,0:T(8,128)S(1)} %get-tuple-element.49), channel_id=1, source_target_pairs={{0,1},{1,0},{2,3},{3,2},{4,5},{5,4},{6,7},{7,6},{8,9},{9,8},{10,11... | collective-permute-start | bytes 786440 | tf_op jit(solution)/shard_map/ppermute | solution.py:350
  25.7 8.9 %collective-permute-start.6 = (f32[8,4,8,128]{3,2,1,0:T(8,128)S(1)}, f32[8,4,8,128]{3,2,1,0:T(8,128)S(1)}, u32[]{:S(2)}, u32[]{:S(2)}) collective-permute-start(f32[8,4,8,128]{3,2,1,0:T(8,128)S(1)} %get-tuple-element.48), channel_id=1, source_target_pairs={{0,16},{2,18},{4,20},{6,22},{8,24},{10,26},{12,28},{14,30},{16,0},... | collective-permute-start | bytes 393224 | tf_op jit(solution)/shard_map/ppermute | solution.py:350
  32.9 8.2 %collective-permute-start.5 = (f32[8,4,8,128]{3,2,1,0:T(8,128)S(1)}, f32[8,4,8,128]{3,2,1,0:T(8,128)S(1)}, u32[]{:S(2)}, u32[]{:S(2)}) collective-permute-start(f32[8,4,8,128]{3,2,1,0:T(8,128)S(1)} %get-tuple-element.46), channel_id=1, source_target_pairs={{0,16},{2,18},{4,20},{6,22},{8,24},{10,26},{12,28},{14,30},{16,0},... | collective-permute-start | bytes 393224 | tf_op jit(solution)/shard_map/ppermute | solution.py:350
  33.3 13.9 %collective-permute-start.8 = (f32[256,128]{1,0:T(8,128)S(1)}, f32[256,128]{1,0:T(8,128)S(1)}, u32[]{:S(2)}, u32[]{:S(2)}) collective-permute-start(f32[256,128]{1,0:T(8,128)S(1)} %get-tuple-element.57), channel_id=1, source_target_pairs={{0,1},{1,0},{2,3},{3,2},{4,5},{5,4},{6,7},{7,6},{8,9},{9,8},{10,11... | collective-permute-start | bytes 393224 | tf_op jit(solution)/shard_map/ppermute | solution.py:350
  36.9 10.3 %collective-permute-start.9 = (f32[128,128]{1,0:T(8,128)S(1)}, f32[128,128]{1,0:T(8,128)S(1)}, u32[]{:S(2)}, u32[]{:S(2)}) collective-permute-start(f32[128,128]{1,0:T(8,128)S(1)} %get-tuple-element.58), channel_id=1, source_target_pairs={{0,1},{1,0},{2,3},{3,2},{4,5},{5,4},{6,7},{7,6},{8,9},{9,8},{10,11... | collective-permute-start | bytes 196616 | tf_op jit(solution)/shard_map/ppermute | solution.py:350
  43.5 5.8 %collective-permute-start.10 = (f32[128,128]{1,0:T(8,128)S(1)}, f32[128,128]{1,0:T(8,128)S(1)}, u32[]{:S(2)}, u32[]{:S(2)}) collective-permute-start(f32[128,128]{1,0:T(8,128)S(1)} %get-tuple-element.59), channel_id=1, source_target_pairs={{0,1},{1,0},{2,3},{3,2},{4,5},{5,4},{6,7},{7,6},{8,9},{9,8},{10,11... | collective-permute-start | bytes 196616 | tf_op jit(solution)/shard_map/ppermute | solution.py:350
  50.3 1.3 %collective-permute-start.11 = (f32[48,128]{1,0:T(8,128)S(1)}, f32[48,128]{1,0:T(8,128)S(1)}, u32[]{:S(2)}, u32[]{:S(2)}) collective-permute-start(f32[48,128]{1,0:T(8,128)S(1)} %get-tuple-element.61), channel_id=1, source_target_pairs={{0,2},{2,0},{4,6},{6,4},{8,10},{10,8},{12,14},{14,12},{16,18},{18,... | collective-permute-start | bytes 73736 | tf_op jit(solution)/shard_map/ppermute | solution.py:350
  51.6 4.7 %collective-permute-start.14 = (f32[48,128]{1,0:T(8,128)S(1)}, f32[48,128]{1,0:T(8,128)S(1)}, u32[]{:S(2)}, u32[]{:S(2)}) collective-permute-start(f32[48,128]{1,0:T(8,128)S(1)} %add.27), channel_id=1, source_target_pairs={{0,5},{1,4},{2,7},{3,6},{4,1},{5,0},{6,3},{7,2},{8,13},{9,12},{10,... | collective-permute-start | bytes 73736 | tf_op jit(solution)/shard_map/ppermute | solution.py:356
  53.2 3.8 %collective-permute-start.13 = (f32[48,128]{1,0:T(8,128)S(1)}, f32[48,128]{1,0:T(8,128)S(1)}, u32[]{:S(2)}, u32[]{:S(2)}) collective-permute-start(f32[48,128]{1,0:T(8,128)S(1)} %add.27), channel_id=1, source_target_pairs={{0,4},{1,5},{2,6},{3,7},{4,0},{5,1},{6,2},{7,3},{8,12},{9,13},{10,... | collective-permute-start | bytes 73736 | tf_op jit(solution)/shard_map/ppermute | solution.py:356
  54.9 3.8 %collective-permute-start.12 = (f32[48,128]{1,0:T(8,128)S(1)}, f32[48,128]{1,0:T(8,128)S(1)}, u32[]{:S(2)}, u32[]{:S(2)}) collective-permute-start(f32[48,128]{1,0:T(8,128)S(1)} %add.27), channel_id=1, source_target_pairs={{0,1},{1,0},{2,3},{3,2},{4,5},{5,4},{6,7},{7,6},{8,9},{9,8},{10,11... | collective-permute-start | bytes 73736 | tf_op jit(solution)/shard_map/ppermute | solution.py:356
  58.8 5.7 %collective-permute-start.17 = (f32[48,128]{1,0:T(8,128)S(1)}, f32[48,128]{1,0:T(8,128)S(1)}, u32[]{:S(2)}, u32[]{:S(2)}) collective-permute-start(f32[48,128]{1,0:T(8,128)S(1)} %add_add_fusion.1), channel_id=1, source_target_pairs={{0,24},{1,25},{2,26},{3,27},{4,28},{5,29},{6,30},{7,31},{8,16},{9,... | collective-permute-start | bytes 73736 | tf_op jit(solution)/shard_map/ppermute | solution.py:356
  59.9 5.1 %collective-permute-start.16 = (f32[48,128]{1,0:T(8,128)S(1)}, f32[48,128]{1,0:T(8,128)S(1)}, u32[]{:S(2)}, u32[]{:S(2)}) collective-permute-start(f32[48,128]{1,0:T(8,128)S(1)} %add_add_fusion.1), channel_id=1, source_target_pairs={{0,16},{1,17},{2,18},{3,19},{4,20},{5,21},{6,22},{7,23},{8,24},{9,... | collective-permute-start | bytes 73736 | tf_op jit(solution)/shard_map/ppermute | solution.py:356
  60.4 4.8 %collective-permute-start.15 = (f32[48,128]{1,0:T(8,128)S(1)}, f32[48,128]{1,0:T(8,128)S(1)}, u32[]{:S(2)}, u32[]{:S(2)}) collective-permute-start(f32[48,128]{1,0:T(8,128)S(1)} %add_add_fusion.1), channel_id=1, source_target_pairs={{0,8},{1,9},{2,10},{3,11},{4,12},{5,13},{6,14},{7,15},{8,0},{9,1},... | collective-permute-start | bytes 73736 | tf_op jit(solution)/shard_map/ppermute | solution.py:356
  65.2 1.3 %collective-permute-start.18 = (f32[48,128]{1,0:T(8,128)S(1)}, f32[48,128]{1,0:T(8,128)S(1)}, u32[]{:S(2)}, u32[]{:S(2)}) collective-permute-start(f32[48,128]{1,0:T(8,128)S(1)} %add_add_fusion.own), channel_id=1, source_target_pairs={{0,2},{2,0},{4,6},{6,4},{8,10},{10,8},{12,14},{14,12},{16,18},{18,... | collective-permute-start | bytes 73736 | tf_op jit(solution)/shard_map/ppermute | solution.py:350

commit v11 on v10

--- a/solution.py
+++ b/solution.py
@@ -1015,7 +1015,7 @@
         meta, statics, left, right
     )
     rims = swapped(rims, "tiles", TGY)
-    gates = [(left, right), (halos[0], rims)]
+    gates = [(), (halos[0], rims)]
     for c in range(1, min(chunks, 3)):
         halos.append(swapped(after(messages[c], gates[c - 1]), "tiles", TGY))
 

time: 72.5 us -> 80.1 us (1.10)
  waiting for transfers between devices: 14.5 us -> 22.9 us
    ppermute x11, waiting for transfers between devices: 8.77 us -> 17.9 us  [swapped(): lax.ppermute(value, axis, [(source, source ^ bit) for source in range(cou...]
    ppermute x11, starting transfers between devices: 16.2 us -> 15.4 us  [swapped(): lax.ppermute(value, axis, [(source, source ^ bit) for source in range(cou...]
  transfers between devices with their start and end apart: 19 -> 19, of which waited for: 11 -> 11; matrix products, arithmetic and copies ran while one was open for 0% -> 0% of each run, Pallas kernels for 25% -> 22%
where the time goes in v11:
time: 80.1 us; the launch traced here: 79.8 us
  starting transfers between devices  27.8 us (35%)
  Pallas kernels  26.4 us (33%)
  waiting for transfers between devices  22.9 us (29%)
  local copies, waits for them, and re-layouts  1.33 us (2%)
  between operations  0.85 us (1%)
    ppermute x11, waiting for transfers between devices, swapped(): lax.ppermute(value, axis, [(source, source ^ bit) for source in range(cou...  17.9 us
    ppermute x11, starting transfers between devices, swapped(): lax.ppermute(value, axis, [(source, source ^ bit) for source in range(cou...  15.4 us
    pallas_call x3, Pallas kernels, shards_of_two_rows(): call(functools.partial(near_kernel, batch, base, parts), specs, [pl.Block...  8.14 us
    ppermute x6, starting transfers between devices, mesh_permute(): lax.ppermute(value, axes, [(source, source ^ mask) for source in range(co...  7.94 us
    pallas_call x1, Pallas kernels, factor(): call(functools.partial(factor_kernel, scale), [smem] + resident(2), resid...  5.77 us
    ppermute x6, waiting for transfers between devices, mesh_permute(): lax.ppermute(value, axes, [(source, source ^ mask) for source in range(co...  4.96 us
    pallas_call x1, Pallas kernels, shards_of_two_rows(): call(functools.partial(far_kernel, 8), [smem] + resident(7), resident(len...  4.84 us
    ppermute x2, starting transfers between devices, beside(): lax.ppermute(value, 'tiles', [(a, b) for a, b in pairs if 0 <= b < count...  4.45 us
  transfers between devices with their start and end apart: 19, of which 11 were waited for; matrix products, arithmetic and copies ran while one was open for 0% of the time, Pallas kernels for 22%

profile of v11, /device:TPU:0, one launch (start us, length us, event | category | flops | bytes accessed | tf_op | source)
XLA Modules:
  0.0 79.8 jit_solution(4441906544584660586)
XLA Ops:
  0.7 0.6 pad_add_fusion.meta
  1.2 1.6 %shard_map.68 = f32[8,4,8,128]{3,2,1,0:T(8,128)} custom-call(s32[4]{0:T(128)} %pad_add_fusion.meta, f32[64,4,8,128]{3,2,1,0:T(8,128)} %omega.13, s32[8,128]{1,0:T(8,128)} %wet.13), custom_call_target="tpu_custom_call" | custom-call | bytes 1048576 | tf_op jit(solution)/shard_map/pallas_call | solution.py:986
  2.9 4.0 %collective-permute-start.3 = (f32[8,4,8,128]{3,2,1,0:T(8,128)}, f32[8,4,8,128]{3,2,1,0:T(8,128)S(1)}, u32[]{:S(2)}, u32[]{:S(2)}) collective-permute-start(f32[8,4,8,128]{3,2,1,0:T(8,128)} %shard_map.68), channel_id=1, source_target_pairs={{0,16},{2,18},{4,20},{6,22},{8,24},{10,26},{12,28},{14,30},{16,0},... | collective-permute-start | bytes 393224 | tf_op jit(solution)/shard_map/ppermute | solution.py:350
  6.9 2.2 %shard_map.69 = (f32[4,4,8,128]{3,2,1,0:T(8,128)}, f32[5,4,8,128]{3,2,1,0:T(8,128)}) custom-call(s32[1,4]{1,0:T(1,128)} %runs, f32[64,4,8,128]{3,2,1,0:T(8,128)} %omega.13, f32[3,4,8,128]{3,2,1,0:T(8,128)} %conductance.1, s32[8,128]{1,0:T(8,128)} %wet.13), custom_call_target="tpu_custom_call" | custom-call | bytes 1048576 | tf_op jit(solution)/shard_map/pallas_call | solution.py:994
  9.2 1.4 %collective-permute-start.1 = (f32[5,4,8,128]{3,2,1,0:T(8,128)}, f32[5,4,8,128]{3,2,1,0:T(8,128)S(1)}, u32[]{:S(2)}, u32[]{:S(2)}) collective-permute-start(f32[5,4,8,128]{3,2,1,0:T(8,128)} %get-tuple-element.33.edges), channel_id=1, source_target_pairs={{2,0},{4,2},{6,4},{8,6},{10,8},{12,10},{14,12},{18,16},{20,18},{22... | collective-permute-start | bytes 245768 | tf_op jit(solution)/shard_map/ppermute | solution.py:822
  10.6 3.0 %collective-permute-start = (f32[5,4,8,128]{3,2,1,0:T(8,128)}, f32[5,4,8,128]{3,2,1,0:T(8,128)S(1)}, u32[]{:S(2)}, u32[]{:S(2)}) collective-permute-start(f32[5,4,8,128]{3,2,1,0:T(8,128)} %get-tuple-element.33.edges), channel_id=1, source_target_pairs={{0,2},{2,4},{4,6},{6,8},{8,10},{10,12},{12,14},{16,18},{18,20},{20... | collective-permute-start | bytes 245768 | tf_op jit(solution)/shard_map/ppermute | solution.py:822
  13.7 0.0 copy-start
  13.7 1.2 %copy-done = f32[64,4,8,128]{3,2,1,0:T(8,128)S(1)} copy-done((f32[64,4,8,128]{3,2,1,0:T(8,128)S(1)}, f32[64,4,8,128]{3,2,1,0:T(8,128)}, u32[]{:S(2)}) %copy-start) | copy-done | bytes 1048600
  14.9 0.6 shard_map.73
  15.5 0.1 collective-permute-start.4
  15.6 0.0 collective-permute-done.1.right
  15.6 0.0 collective-permute-done.left
  15.6 0.1 copy-done.2
  15.7 0.6 shard_map.70
  16.3 2.9 %collective-permute-start.2 = (f32[18,8,128]{2,1,0:T(8,128)S(1)}, f32[18,8,128]{2,1,0:T(8,128)S(1)}, u32[]{:S(2)}, u32[]{:S(2)}) collective-permute-start(f32[18,8,128]{2,1,0:T(8,128)S(1)} %shard_map.70), channel_id=1, source_target_pairs={{0,16},{2,18},{4,20},{6,22},{8,24},{10,26},{12,28},{14,30},{16,0},... | collective-permute-start | bytes 221192 | tf_op jit(solution)/shard_map/ppermute | solution.py:350
  19.2 4.8 %shard_map.72 = (f32[64,4,8,128]{3,2,1,0:T(8,128)S(1)}, f32[64,4,8,128]{3,2,1,0:T(8,128)S(1)}, f32[4,2,4,8,128]{4,3,2,1,0:T(8,128)S(1)}, f32[512,128]{1,0:T(8,128)S(1)}, f32[512,128]{1,0:T(8,128)S(1)}) custom-call(s32[4]{0:T(128)S(1)} %copy-done.4, f32[4,4,8,128]{3,2,1,0:T(8,128)S(1)} %copy-done.2, f32[64,4,8,128]{3,2,1,0:T(8,128)S(1)} %copy-done.1, ...), custom_call_target="tpu_custom_call" | custom-call | flops 8000000000 | bytes 1048576 | tf_op jit(solution)/shard_map/pallas_call | solution.py:1024
  24.0 1.6 %collective-permute-start.7 = (f32[512,128]{1,0:T(8,128)S(1)}, f32[512,128]{1,0:T(8,128)S(1)}, u32[]{:S(2)}, u32[]{:S(2)}) collective-permute-start(f32[512,128]{1,0:T(8,128)S(1)} %get-tuple-element.47), channel_id=1, source_target_pairs={{0,1},{1,0},{2,3},{3,2},{4,5},{5,4},{6,7},{7,6},{8,9},{9,8},{10,11... | collective-permute-start | bytes 786440 | tf_op jit(solution)/shard_map/ppermute | solution.py:350
  25.6 0.0 collective-permute-done.3.rest_0_
  25.6 1.5 %collective-permute-done.4.rest_1_ = f32[8,4,8,128]{3,2,1,0:T(8,128)S(1)} collective-permute-done((f32[8,4,8,128]{3,2,1,0:T(8,128)S(1)}, f32[8,4,8,128]{3,2,1,0:T(8,128)S(1)}, u32[]{:S(2)}, u32[]{:S(2)}) %collective-permute-start.4) | collective-permute-done | bytes 131104 | tf_op jit(solution)/shard_map/ppermute | solution.py:350
  27.1 1.6 %collective-permute-done.2.rims = f32[18,8,128]{2,1,0:T(8,128)S(1)} collective-permute-done((f32[18,8,128]{2,1,0:T(8,128)S(1)}, f32[18,8,128]{2,1,0:T(8,128)S(1)}, u32[]{:S(2)}, u32[]{:S(2)}) %collective-permute-start.2) | collective-permute-done | bytes 73760 | tf_op jit(solution)/shard_map/ppermute | solution.py:350
  28.7 1.1 %shard_map.71 = (f32[7,4,8,128]{3,2,1,0:T(8,128)S(1)}, f32[2,7,4,8,128]{4,3,2,1,0:T(8,128)S(1)}) custom-call(s32[4]{0:T(128)S(1)} %copy-done.4, f32[4,4,8,128]{3,2,1,0:T(8,128)S(1)} %copy-done.2, f32[18,8,128]{2,1,0:T(8,128)S(1)} %collective-permute-done.2.rims, f32[5,4,8,128]{3,2,1,0:T(8,128)S(1)} %copy-done.3, ...), custom_call_target="tpu_custom_call" | custom-call | bytes 1048576 | tf_op jit(solution)/shard_map/pallas_call | solution.py:1036
  29.8 3.5 %shard_map.74 = (f32[64,4,8,128]{3,2,1,0:T(8,128)}, f32[256,128]{1,0:T(8,128)S(1)}, f32[256,128]{1,0:T(8,128)S(1)}) custom-call(s32[4]{0:T(128)S(1)} %copy-done.4, f32[64,4,8,128]{3,2,1,0:T(8,128)S(1)} %copy-done.1, s32[8,128]{1,0:T(8,128)S(1)} %copy-done.5, f32[8,128]{1,0:T(8,128)S(1)} %copy-done.6, f32[18,8,128]{2,1,0:T(8,128)S(1)} %collective-permute-done.2.rims, ...), custom_call_target="tpu_custom_call" | custom-call | flops 2000000000 | bytes 1048576 | tf_op jit(solution)/shard_map/pallas_call | solution.py:1060
  33.3 0.1 collective-permute-start.5
  33.3 2.9 %collective-permute-start.6 = (f32[8,4,8,128]{3,2,1,0:T(8,128)S(1)}, f32[8,4,8,128]{3,2,1,0:T(8,128)S(1)}, u32[]{:S(2)}, u32[]{:S(2)}) collective-permute-start(f32[8,4,8,128]{3,2,1,0:T(8,128)S(1)} %get-tuple-element.46), channel_id=1, source_target_pairs={{0,16},{2,18},{4,20},{6,22},{8,24},{10,26},{12,28},{14,30},{16,0},... | collective-permute-start | bytes 393224 | tf_op jit(solution)/shard_map/ppermute | solution.py:350
  36.3 1.5 %collective-permute-start.8 = (f32[256,128]{1,0:T(8,128)S(1)}, f32[256,128]{1,0:T(8,128)S(1)}, u32[]{:S(2)}, u32[]{:S(2)}) collective-permute-start(f32[256,128]{1,0:T(8,128)S(1)} %get-tuple-element.55), channel_id=1, source_target_pairs={{0,1},{1,0},{2,3},{3,2},{4,5},{5,4},{6,7},{7,6},{8,9},{9,8},{10,11... | collective-permute-start | bytes 393224 | tf_op jit(solution)/shard_map/ppermute | solution.py:350
  37.8 6.1 %collective-permute-done.5.rest_0_ = f32[8,4,8,128]{3,2,1,0:T(8,128)S(1)} collective-permute-done((f32[8,4,8,128]{3,2,1,0:T(8,128)S(1)}, f32[8,4,8,128]{3,2,1,0:T(8,128)S(1)}, u32[]{:S(2)}, u32[]{:S(2)}) %collective-permute-start.5) | collective-permute-done | bytes 131104 | tf_op jit(solution)/shard_map/ppermute | solution.py:350
  43.9 2.7 %collective-permute-done.6.rest_0_ = f32[8,4,8,128]{3,2,1,0:T(8,128)S(1)} collective-permute-done((f32[8,4,8,128]{3,2,1,0:T(8,128)S(1)}, f32[8,4,8,128]{3,2,1,0:T(8,128)S(1)}, u32[]{:S(2)}, u32[]{:S(2)}) %collective-permute-start.6) | collective-permute-done | bytes 131104 | tf_op jit(solution)/shard_map/ppermute | solution.py:350
  46.6 0.0 collective-permute-done.7.received
  46.6 2.3 %shard_map.75 = (f32[64,4,8,128]{3,2,1,0:T(8,128)}, f32[128,128]{1,0:T(8,128)S(1)}, f32[128,128]{1,0:T(8,128)S(1)}) custom-call(s32[4]{0:T(128)S(1)} %copy-done.4, f32[64,4,8,128]{3,2,1,0:T(8,128)S(1)} %copy-done.1, s32[8,128]{1,0:T(8,128)S(1)} %copy-done.5, f32[8,128]{1,0:T(8,128)S(1)} %copy-done.6, ...), custom_call_target="tpu_custom_call", output_to_operand_aliasing={{0}: (13, {})} | custom-call | flops 2000000000 | bytes 1048576 | tf_op jit(solution)/shard_map/pallas_call | solution.py:1060
  48.9 1.9 %collective-permute-start.9 = (f32[128,128]{1,0:T(8,128)S(1)}, f32[128,128]{1,0:T(8,128)S(1)}, u32[]{:S(2)}, u32[]{:S(2)}) collective-permute-start(f32[128,128]{1,0:T(8,128)S(1)} %get-tuple-element.56), channel_id=1, source_target_pairs={{0,1},{1,0},{2,3},{3,2},{4,5},{5,4},{6,7},{7,6},{8,9},{9,8},{10,11... | collective-permute-start | bytes 196616 | tf_op jit(solution)/shard_map/ppermute | solution.py:350
  50.8 2.3 %shard_map.76 = (f32[64,4,8,128]{3,2,1,0:T(8,128)}, f32[128,128]{1,0:T(8,128)S(1)}, f32[128,128]{1,0:T(8,128)S(1)}) custom-call(s32[4]{0:T(128)S(1)} %copy-done.4, f32[64,4,8,128]{3,2,1,0:T(8,128)S(1)} %copy-done.1, s32[8,128]{1,0:T(8,128)S(1)} %copy-done.5, f32[8,128]{1,0:T(8,128)S(1)} %copy-done.6, ...), custom_call_target="tpu_custom_call", output_to_operand_aliasing={{0}: (13, {})} | custom-call | flops 2000000000 | bytes 1048576 | tf_op jit(solution)/shard_map/pallas_call | solution.py:1060
  53.2 0.2 collective-permute-start.10
  53.4 0.4 shard_map.77.far
  53.8 3.7 %collective-permute-done.10.refs_5_ = f32[128,128]{1,0:T(8,128)S(1)} collective-permute-done((f32[128,128]{1,0:T(8,128)S(1)}, f32[128,128]{1,0:T(8,128)S(1)}, u32[]{:S(2)}, u32[]{:S(2)}) %collective-permute-start.10) | collective-permute-done | bytes 65568 | tf_op jit(solution)/shard_map/ppermute | solution.py:350
  57.5 1.1 %shard_map.78 = (f32[48,128]{1,0:T(8,128)S(1)}, f32[48,128]{1,0:T(8,128)S(1)}) custom-call(s32[4]{0:T(128)S(1)} %copy-done.4, f32[128,128]{1,0:T(8,128)S(1)} %shard_map.77.far, f32[256,128]{1,0:T(8,128)S(1)} %get-tuple-element.43.refs_0_, f32[128,128]{1,0:T(8,128)S(1)} %get-tuple-element.53.refs_1_, f32[128,128]{1,0:T(8,128)S(1)} %get-tuple-element.54.refs_2_, ...), custom_call_target="tpu_custom_call" | custom-call | bytes 1048576 | tf_op jit(solution)/shard_map/pallas_call | solution.py:1084
  58.6 0.1 collective-permute-start.11
  58.6 1.2 %collective-permute-done.11 = f32[48,128]{1,0:T(8,128)S(1)} collective-permute-done((f32[48,128]{1,0:T(8,128)S(1)}, f32[48,128]{1,0:T(8,128)S(1)}, u32[]{:S(2)}, u32[]{:S(2)}) %collective-permute-start.11) | collective-permute-done | bytes 24608 | tf_op jit(solution)/shard_map/ppermute | solution.py:350
  59.8 1.6 %collective-permute-start.13 = (f32[48,128]{1,0:T(8,128)S(1)}, f32[48,128]{1,0:T(8,128)S(1)}, u32[]{:S(2)}, u32[]{:S(2)}) collective-permute-start(f32[48,128]{1,0:T(8,128)S(1)} %add.27), channel_id=1, source_target_pairs={{0,4},{1,5},{2,6},{3,7},{4,0},{5,1},{6,2},{7,3},{8,12},{9,13},{10,... | collective-permute-start | bytes 73736 | tf_op jit(solution)/shard_map/ppermute | solution.py:356
  61.5 1.8 %collective-permute-start.12 = (f32[48,128]{1,0:T(8,128)S(1)}, f32[48,128]{1,0:T(8,128)S(1)}, u32[]{:S(2)}, u32[]{:S(2)}) collective-permute-start(f32[48,128]{1,0:T(8,128)S(1)} %add.27), channel_id=1, source_target_pairs={{0,1},{1,0},{2,3},{3,2},{4,5},{5,4},{6,7},{7,6},{8,9},{9,8},{10,11... | collective-permute-start | bytes 73736 | tf_op jit(solution)/shard_map/ppermute | solution.py:356
  63.3 1.2 %collective-permute-done.14 = f32[48,128]{1,0:T(8,128)S(1)} collective-permute-done((f32[48,128]{1,0:T(8,128)S(1)}, f32[48,128]{1,0:T(8,128)S(1)}, u32[]{:S(2)}, u32[]{:S(2)}) %collective-permute-start.14) | collective-permute-done | bytes 24608 | tf_op jit(solution)/shard_map/ppermute | solution.py:356
  64.6 0.7 collective-permute-done.12
  65.3 2.7 %collective-permute-start.17 = (f32[48,128]{1,0:T(8,128)S(1)}, f32[48,128]{1,0:T(8,128)S(1)}, u32[]{:S(2)}, u32[]{:S(2)}) collective-permute-start(f32[48,128]{1,0:T(8,128)S(1)} %add_add_fusion.1), channel_id=1, source_target_pairs={{0,24},{1,25},{2,26},{3,27},{4,28},{5,29},{6,30},{7,31},{8,16},{9,... | collective-permute-start | bytes 73736 | tf_op jit(solution)/shard_map/ppermute | solution.py:356
  68.0 1.8 %collective-permute-start.15 = (f32[48,128]{1,0:T(8,128)S(1)}, f32[48,128]{1,0:T(8,128)S(1)}, u32[]{:S(2)}, u32[]{:S(2)}) collective-permute-start(f32[48,128]{1,0:T(8,128)S(1)} %add_add_fusion.1), channel_id=1, source_target_pairs={{0,8},{1,9},{2,10},{3,11},{4,12},{5,13},{6,14},{7,15},{8,0},{9,1},... | collective-permute-start | bytes 73736 | tf_op jit(solution)/shard_map/ppermute | solution.py:356
  69.8 1.2 %collective-permute-done.17 = f32[48,128]{1,0:T(8,128)S(1)} collective-permute-done((f32[48,128]{1,0:T(8,128)S(1)}, f32[48,128]{1,0:T(8,128)S(1)}, u32[]{:S(2)}, u32[]{:S(2)}) %collective-permute-start.17) | collective-permute-done | bytes 24608 | tf_op jit(solution)/shard_map/ppermute | solution.py:356
  71.0 1.7 %collective-permute-done.16 = f32[48,128]{1,0:T(8,128)S(1)} collective-permute-done((f32[48,128]{1,0:T(8,128)S(1)}, f32[48,128]{1,0:T(8,128)S(1)}, u32[]{:S(2)}, u32[]{:S(2)}) %collective-permute-start.16) | collective-permute-done | bytes 24608 | tf_op jit(solution)/shard_map/ppermute | solution.py:356
  72.8 0.1 collective-permute-start.18
  72.8 1.2 %collective-permute-done.18.other = f32[48,128]{1,0:T(8,128)S(1)} collective-permute-done((f32[48,128]{1,0:T(8,128)S(1)}, f32[48,128]{1,0:T(8,128)S(1)}, u32[]{:S(2)}, u32[]{:S(2)}) %collective-permute-start.18) | collective-permute-done | bytes 24608 | tf_op jit(solution)/shard_map/ppermute | solution.py:350
  74.0 5.8 %shard_map.79 = f32[128,128]{1,0:T(8,128)} custom-call(s32[4]{0:T(128)S(1)} %copy-done.4, f32[48,128]{1,0:T(8,128)S(1)} %add_add_fusion.own, f32[48,128]{1,0:T(8,128)S(1)} %collective-permute-done.18.other), custom_call_target="tpu_custom_call" | custom-call | bytes 1048576 | tf_op jit(solution)/shard_map/pallas_call | solution.py:870
  (20 shorter events, 0.1 us)
Async XLA Ops:
  2.9 10.8 %copy-start.5 = (s32[8,128]{1,0:T(8,128)S(1)}, s32[8,128]{1,0:T(8,128)}, u32[]{:S(2)}) copy-start(s32[8,128]{1,0:T(8,128)} %wet.13) | copy-start | bytes 12292
  2.9 22.7 %collective-permute-start.3 = (f32[8,4,8,128]{3,2,1,0:T(8,128)}, f32[8,4,8,128]{3,2,1,0:T(8,128)S(1)}, u32[]{:S(2)}, u32[]{:S(2)}) collective-permute-start(f32[8,4,8,128]{3,2,1,0:T(8,128)} %shard_map.68), channel_id=1, source_target_pairs={{0,16},{2,18},{4,20},{6,22},{8,24},{10,26},{12,28},{14,30},{16,0},... | collective-permute-start | bytes 393224 | tf_op jit(solution)/shard_map/ppermute | solution.py:350
  9.2 4.5 %copy-start.4 = (s32[4]{0:T(128)S(1)}, s32[4]{0:T(128)}, u32[]{:S(2)}) copy-start(s32[4]{0:T(128)} %pad_add_fusion.meta) | copy-start | bytes 52
  9.2 6.4 %collective-permute-start.1 = (f32[5,4,8,128]{3,2,1,0:T(8,128)}, f32[5,4,8,128]{3,2,1,0:T(8,128)S(1)}, u32[]{:S(2)}, u32[]{:S(2)}) collective-permute-start(f32[5,4,8,128]{3,2,1,0:T(8,128)} %get-tuple-element.33.edges), channel_id=1, source_target_pairs={{2,0},{4,2},{6,4},{8,6},{10,8},{12,10},{14,12},{18,16},{20,18},{22... | collective-permute-start | bytes 245768 | tf_op jit(solution)/shard_map/ppermute | solution.py:822
  10.6 5.0 %collective-permute-start = (f32[5,4,8,128]{3,2,1,0:T(8,128)}, f32[5,4,8,128]{3,2,1,0:T(8,128)S(1)}, u32[]{:S(2)}, u32[]{:S(2)}) collective-permute-start(f32[5,4,8,128]{3,2,1,0:T(8,128)} %get-tuple-element.33.edges), channel_id=1, source_target_pairs={{0,2},{2,4},{4,6},{6,8},{8,10},{10,12},{12,14},{16,18},{18,20},{20... | collective-permute-start | bytes 245768 | tf_op jit(solution)/shard_map/ppermute | solution.py:822
  13.7 1.2 %copy-start = (f32[64,4,8,128]{3,2,1,0:T(8,128)S(1)}, f32[64,4,8,128]{3,2,1,0:T(8,128)}, u32[]{:S(2)}) copy-start(f32[64,4,8,128]{3,2,1,0:T(8,128)} %omega.13) | copy-start | bytes 3145732
  14.9 0.8 %copy-start.2 = (f32[4,4,8,128]{3,2,1,0:T(8,128)S(1)}, f32[4,4,8,128]{3,2,1,0:T(8,128)}, u32[]{:S(2)}) copy-start(f32[4,4,8,128]{3,2,1,0:T(8,128)} %get-tuple-element.32.statics) | copy-start | bytes 196612
  14.9 4.3 %copy-start.1 = (f32[64,4,8,128]{3,2,1,0:T(8,128)S(1)}, f32[64,4,8,128]{3,2,1,0:T(8,128)}, u32[]{:S(2)}) copy-start(f32[64,4,8,128]{3,2,1,0:T(8,128)} %omega.13) | copy-start | bytes 3145732
  15.5 11.6 %collective-permute-start.4 = (f32[8,4,8,128]{3,2,1,0:T(8,128)S(1)}, f32[8,4,8,128]{3,2,1,0:T(8,128)S(1)}, u32[]{:S(2)}, u32[]{:S(2)}) collective-permute-start(f32[8,4,8,128]{3,2,1,0:T(8,128)S(1)} %get-tuple-element.40), channel_id=1, source_target_pairs={{0,16},{2,18},{4,20},{6,22},{8,24},{10,26},{12,28},{14,30},{16,0},... | collective-permute-start | bytes 393224 | tf_op jit(solution)/shard_map/ppermute | solution.py:350
  15.7 3.5 %copy-start.3 = (f32[5,4,8,128]{3,2,1,0:T(8,128)S(1)}, f32[5,4,8,128]{3,2,1,0:T(8,128)}, u32[]{:S(2)}) copy-start(f32[5,4,8,128]{3,2,1,0:T(8,128)} %get-tuple-element.33.edges) | copy-start | bytes 245764
  15.7 3.5 %copy-start.6 = (f32[8,128]{1,0:T(8,128)S(1)}, f32[8,128]{1,0:T(8,128)}, u32[]{:S(2)}) copy-start(f32[8,128]{1,0:T(8,128)} %volume.7) | copy-start | bytes 12292
  16.3 12.4 %collective-permute-start.2 = (f32[18,8,128]{2,1,0:T(8,128)S(1)}, f32[18,8,128]{2,1,0:T(8,128)S(1)}, u32[]{:S(2)}, u32[]{:S(2)}) collective-permute-start(f32[18,8,128]{2,1,0:T(8,128)S(1)} %shard_map.70), channel_id=1, source_target_pairs={{0,16},{2,18},{4,20},{6,22},{8,24},{10,26},{12,28},{14,30},{16,0},... | collective-permute-start | bytes 221192 | tf_op jit(solution)/shard_map/ppermute | solution.py:350
  24.0 22.5 %collective-permute-start.7 = (f32[512,128]{1,0:T(8,128)S(1)}, f32[512,128]{1,0:T(8,128)S(1)}, u32[]{:S(2)}, u32[]{:S(2)}) collective-permute-start(f32[512,128]{1,0:T(8,128)S(1)} %get-tuple-element.47), channel_id=1, source_target_pairs={{0,1},{1,0},{2,3},{3,2},{4,5},{5,4},{6,7},{7,6},{8,9},{9,8},{10,11... | collective-permute-start | bytes 786440 | tf_op jit(solution)/shard_map/ppermute | solution.py:350
  33.3 10.6 %collective-permute-start.5 = (f32[8,4,8,128]{3,2,1,0:T(8,128)S(1)}, f32[8,4,8,128]{3,2,1,0:T(8,128)S(1)}, u32[]{:S(2)}, u32[]{:S(2)}) collective-permute-start(f32[8,4,8,128]{3,2,1,0:T(8,128)S(1)} %get-tuple-element.44), channel_id=1, source_target_pairs={{0,16},{2,18},{4,20},{6,22},{8,24},{10,26},{12,28},{14,30},{16,0},... | collective-permute-start | bytes 393224 | tf_op jit(solution)/shard_map/ppermute | solution.py:350
  33.3 13.2 %collective-permute-start.6 = (f32[8,4,8,128]{3,2,1,0:T(8,128)S(1)}, f32[8,4,8,128]{3,2,1,0:T(8,128)S(1)}, u32[]{:S(2)}, u32[]{:S(2)}) collective-permute-start(f32[8,4,8,128]{3,2,1,0:T(8,128)S(1)} %get-tuple-element.46), channel_id=1, source_target_pairs={{0,16},{2,18},{4,20},{6,22},{8,24},{10,26},{12,28},{14,30},{16,0},... | collective-permute-start | bytes 393224 | tf_op jit(solution)/shard_map/ppermute | solution.py:350
  36.3 17.5 %collective-permute-start.8 = (f32[256,128]{1,0:T(8,128)S(1)}, f32[256,128]{1,0:T(8,128)S(1)}, u32[]{:S(2)}, u32[]{:S(2)}) collective-permute-start(f32[256,128]{1,0:T(8,128)S(1)} %get-tuple-element.55), channel_id=1, source_target_pairs={{0,1},{1,0},{2,3},{3,2},{4,5},{5,4},{6,7},{7,6},{8,9},{9,8},{10,11... | collective-permute-start | bytes 393224 | tf_op jit(solution)/shard_map/ppermute | solution.py:350
  48.9 4.9 %collective-permute-start.9 = (f32[128,128]{1,0:T(8,128)S(1)}, f32[128,128]{1,0:T(8,128)S(1)}, u32[]{:S(2)}, u32[]{:S(2)}) collective-permute-start(f32[128,128]{1,0:T(8,128)S(1)} %get-tuple-element.56), channel_id=1, source_target_pairs={{0,1},{1,0},{2,3},{3,2},{4,5},{5,4},{6,7},{7,6},{8,9},{9,8},{10,11... | collective-permute-start | bytes 196616 | tf_op jit(solution)/shard_map/ppermute | solution.py:350
  53.2 4.3 %collective-permute-start.10 = (f32[128,128]{1,0:T(8,128)S(1)}, f32[128,128]{1,0:T(8,128)S(1)}, u32[]{:S(2)}, u32[]{:S(2)}) collective-permute-start(f32[128,128]{1,0:T(8,128)S(1)} %get-tuple-element.57), channel_id=1, source_target_pairs={{0,1},{1,0},{2,3},{3,2},{4,5},{5,4},{6,7},{7,6},{8,9},{9,8},{10,11... | collective-permute-start | bytes 196616 | tf_op jit(solution)/shard_map/ppermute | solution.py:350
  58.6 1.3 %collective-permute-start.11 = (f32[48,128]{1,0:T(8,128)S(1)}, f32[48,128]{1,0:T(8,128)S(1)}, u32[]{:S(2)}, u32[]{:S(2)}) collective-permute-start(f32[48,128]{1,0:T(8,128)S(1)} %get-tuple-element.59), channel_id=1, source_target_pairs={{0,2},{2,0},{4,6},{6,4},{8,10},{10,8},{12,14},{14,12},{16,18},{18,... | collective-permute-start | bytes 73736 | tf_op jit(solution)/shard_map/ppermute | solution.py:350
  59.8 4.7 %collective-permute-start.14 = (f32[48,128]{1,0:T(8,128)S(1)}, f32[48,128]{1,0:T(8,128)S(1)}, u32[]{:S(2)}, u32[]{:S(2)}) collective-permute-start(f32[48,128]{1,0:T(8,128)S(1)} %add.27), channel_id=1, source_target_pairs={{0,5},{1,4},{2,7},{3,6},{4,1},{5,0},{6,3},{7,2},{8,13},{9,12},{10,... | collective-permute-start | bytes 73736 | tf_op jit(solution)/shard_map/ppermute | solution.py:356
  59.8 4.7 %collective-permute-start.13 = (f32[48,128]{1,0:T(8,128)S(1)}, f32[48,128]{1,0:T(8,128)S(1)}, u32[]{:S(2)}, u32[]{:S(2)}) collective-permute-start(f32[48,128]{1,0:T(8,128)S(1)} %add.27), channel_id=1, source_target_pairs={{0,4},{1,5},{2,6},{3,7},{4,0},{5,1},{6,2},{7,3},{8,12},{9,13},{10,... | collective-permute-start | bytes 73736 | tf_op jit(solution)/shard_map/ppermute | solution.py:356
  61.5 3.8 %collective-permute-start.12 = (f32[48,128]{1,0:T(8,128)S(1)}, f32[48,128]{1,0:T(8,128)S(1)}, u32[]{:S(2)}, u32[]{:S(2)}) collective-permute-start(f32[48,128]{1,0:T(8,128)S(1)} %add.27), channel_id=1, source_target_pairs={{0,1},{1,0},{2,3},{3,2},{4,5},{5,4},{6,7},{7,6},{8,9},{9,8},{10,11... | collective-permute-start | bytes 73736 | tf_op jit(solution)/shard_map/ppermute | solution.py:356
  65.3 5.7 %collective-permute-start.17 = (f32[48,128]{1,0:T(8,128)S(1)}, f32[48,128]{1,0:T(8,128)S(1)}, u32[]{:S(2)}, u32[]{:S(2)}) collective-permute-start(f32[48,128]{1,0:T(8,128)S(1)} %add_add_fusion.1), channel_id=1, source_target_pairs={{0,24},{1,25},{2,26},{3,27},{4,28},{5,29},{6,30},{7,31},{8,16},{9,... | collective-permute-start | bytes 73736 | tf_op jit(solution)/shard_map/ppermute | solution.py:356
  68.0 4.7 %collective-permute-start.16 = (f32[48,128]{1,0:T(8,128)S(1)}, f32[48,128]{1,0:T(8,128)S(1)}, u32[]{:S(2)}, u32[]{:S(2)}) collective-permute-start(f32[48,128]{1,0:T(8,128)S(1)} %add_add_fusion.1), channel_id=1, source_target_pairs={{0,16},{1,17},{2,18},{3,19},{4,20},{5,21},{6,22},{7,23},{8,24},{9,... | collective-permute-start | bytes 73736 | tf_op jit(solution)/shard_map/ppermute | solution.py:356
  68.0 4.7 %collective-permute-start.15 = (f32[48,128]{1,0:T(8,128)S(1)}, f32[48,128]{1,0:T(8,128)S(1)}, u32[]{:S(2)}, u32[]{:S(2)}) collective-permute-start(f32[48,128]{1,0:T(8,128)S(1)} %add_add_fusion.1), channel_id=1, source_target_pairs={{0,8},{1,9},{2,10},{3,11},{4,12},{5,13},{6,14},{7,15},{8,0},{9,1},... | collective-permute-start | bytes 73736 | tf_op jit(solution)/shard_map/ppermute | solution.py:356
  72.8 1.3 %collective-permute-start.18 = (f32[48,128]{1,0:T(8,128)S(1)}, f32[48,128]{1,0:T(8,128)S(1)}, u32[]{:S(2)}, u32[]{:S(2)}) collective-permute-start(f32[48,128]{1,0:T(8,128)S(1)} %add_add_fusion.own), channel_id=1, source_target_pairs={{0,2},{2,0},{4,6},{6,4},{8,10},{10,8},{12,14},{14,12},{16,18},{18,... | collective-permute-start | bytes 73736 | tf_op jit(solution)/shard_map/ppermute | solution.py:350
